TPU v7x, 32 devices: a whole 2x2x4 slice. The times are simulated.
32 devices in a mesh: rep: 4 (over y, x), fsdp: 8 (over z, core).
Axes of the slice: x: 2, y: 2, z: 4, core: 2. Of those that a mesh axis runs over, the one named last changes fastest.
Arguments:
- images: bfloat16 [8, 1376, 1024], P('rep', 'fsdp'), may hold values from -6 to 6
- cotangent: bfloat16 [8, 1376, 1024], P('rep', 'fsdp'), may hold values from -6 to 6
- attn_norm_gain: bfloat16 [2, 1024], P(None, 'fsdp'), may hold values from 0.5 to 1.5
- attn_norm_bias: bfloat16 [2, 1024], P(None, 'fsdp'), may hold values from -1.5 to 1.5
- heads_weight: bfloat16 [2, 1024, 3072], P(None, 'fsdp'), may hold values from -0.1875 to 0.1875
- query_bias: bfloat16 [2, 1024], P(None, 'fsdp'), may hold values from -2.5 to 2.5
- value_bias: bfloat16 [2, 1024], P(None, 'fsdp'), may hold values from -2.5 to 2.5
- output_weight: bfloat16 [2, 1024, 1024], P(None, 'fsdp'), may hold values from -1.5 to 1.5
- output_bias: bfloat16 [2, 1024], P(None, 'fsdp'), may hold values from -1.5 to 1.5
- attn_layerscale: bfloat16 [2, 1024], P(None, 'fsdp'), may hold values from 0.29882812 to 1.5
- mlp_norm_gain: bfloat16 [2, 1024], P(None, 'fsdp'), may hold values from 0.5 to 1.5
- mlp_norm_bias: bfloat16 [2, 1024], P(None, 'fsdp'), may hold values from -1.5 to 1.5
- expand_weight: bfloat16 [2, 1024, 4096], P(None, 'fsdp'), may hold values from -0.1875 to 0.1875
- expand_bias: bfloat16 [2, 4096], P(None, 'fsdp'), may hold values from -2.5 to 2.5
- shrink_weight: bfloat16 [2, 4096, 1024], P(None, 'fsdp'), may hold values from -0.125 to 0.125
- shrink_bias: bfloat16 [2, 1024], P(None, 'fsdp'), may hold values from -1.5 to 1.5
- mlp_layerscale: bfloat16 [2, 1024], P(None, 'fsdp'), may hold values from 0.29882812 to 1.5
Outputs:
- activations: bfloat16 [8, 1376, 1024], P('rep', 'fsdp')
- grad_images: float32 [8, 1376, 1024], P('rep', 'fsdp')
- grad_attn_norm_gain: float32 [2, 1024], P(None, 'fsdp')
- grad_attn_norm_bias: float32 [2, 1024], P(None, 'fsdp')
- grad_heads_weight: float32 [2, 1024, 3072], P(None, 'fsdp')
- grad_query_bias: float32 [2, 1024], P(None, 'fsdp')
- grad_value_bias: float32 [2, 1024], P(None, 'fsdp')
- grad_output_weight: float32 [2, 1024, 1024], P(None, 'fsdp')
- grad_output_bias: float32 [2, 1024], P(None, 'fsdp')
- grad_attn_layerscale: float32 [2, 1024], P(None, 'fsdp')
- grad_mlp_norm_gain: float32 [2, 1024], P(None, 'fsdp')
- grad_mlp_norm_bias: float32 [2, 1024], P(None, 'fsdp')
- grad_expand_weight: float32 [2, 1024, 4096], P(None, 'fsdp')
- grad_expand_bias: float32 [2, 4096], P(None, 'fsdp')
- grad_shrink_weight: float32 [2, 4096, 1024], P(None, 'fsdp')
- grad_shrink_bias: float32 [2, 1024], P(None, 'fsdp')
- grad_mlp_layerscale: float32 [2, 1024], P(None, 'fsdp')
All inputs are finite; a program needn't handle non-finite values.
Results may differ from a plain program's by a relative error of at most 0.035.
Values may be sent and summed in bfloat16 or wider, within the bound.
A program may use at most 384 MiB of HBM per device.

v0:
```python
import jax
import jax.numpy as jnp
from jax import lax
from jax.sharding import PartitionSpec as P

HEADS = 16
LAYERS = 2


epsilon = 1e-06


def layer_norm(values_in, norm_gain, norm_shift):
    centre = jnp.mean(values_in, -1, keepdims=True)
    centered = values_in - centre
    spread = jnp.mean(centered * centered, -1, keepdims=True)
    return centered * lax.rsqrt(spread + epsilon) * norm_gain + norm_shift


def norm_back(values_in, norm_gain, norm_shift, grad):
    unused, pullback = jax.vjp(layer_norm, values_in, norm_gain, norm_shift)
    return pullback(grad)


def gelu_exact(hidden):
    return jax.nn.gelu(hidden, approximate=False)


def widen(tensor):
    return tensor.astype(jnp.float32)


def forward_dot(left, weight):
    return jnp.dot(left, weight, preferred_element_type=jnp.float32)


def weight_dot(left, grad):
    return lax.dot_general(left, grad, (((0,), (0,)), ((), ())), preferred_element_type=jnp.float32)


def input_dot(grad, weight):
    return lax.dot_general(
        grad, weight, (((1,), (1,)), ((), ())), preferred_element_type=jnp.float32
    )


def column_sum(grad):
    return jnp.sum(widen(grad), 0)


def fetch_forward(layer_params):
    (
        attn_norm_gain,
        attn_norm_bias,
        heads_weight,
        query_bias,
        value_bias,
        output_weight,
        output_bias,
        attn_layerscale,
        mlp_norm_gain,
        mlp_norm_bias,
        expand_weight,
        expand_bias,
        shrink_weight,
        shrink_bias,
        mlp_layerscale,
    ) = layer_params
    return (
        lax.all_gather(attn_norm_gain, "fsdp", axis=0, tiled=True),
        lax.all_gather(attn_norm_bias, "fsdp", axis=0, tiled=True),
        lax.all_gather(heads_weight, "fsdp", axis=0, tiled=True),
        lax.all_gather(query_bias, "fsdp", axis=0, tiled=True),
        lax.all_gather(value_bias, "fsdp", axis=0, tiled=True),
        lax.all_gather(output_weight, "fsdp", axis=0, tiled=True),
        lax.all_gather(output_bias, "fsdp", axis=0, tiled=True),
        lax.all_gather(attn_layerscale, "fsdp", axis=0, tiled=True),
        lax.all_gather(mlp_norm_gain, "fsdp", axis=0, tiled=True),
        lax.all_gather(mlp_norm_bias, "fsdp", axis=0, tiled=True),
        lax.all_gather(expand_weight, "fsdp", axis=0, tiled=True),
        lax.all_gather(expand_bias, "fsdp", axis=0, tiled=True),
        lax.all_gather(shrink_weight, "fsdp", axis=0, tiled=True),
        lax.all_gather(shrink_bias, "fsdp", axis=0, tiled=True),
        lax.all_gather(mlp_layerscale, "fsdp", axis=0, tiled=True),
    )


def fetch_backward(layer_params):
    (
        attn_norm_gain,
        attn_norm_bias,
        heads_weight,
        query_bias,
        value_bias,
        output_weight,
        output_bias,
        attn_layerscale,
        mlp_norm_gain,
        mlp_norm_bias,
        expand_weight,
        expand_bias,
        shrink_weight,
        shrink_bias,
        mlp_layerscale,
    ) = layer_params
    return (
        lax.all_gather(attn_norm_gain, "fsdp", axis=0, tiled=True),
        lax.all_gather(attn_norm_bias, "fsdp", axis=0, tiled=True),
        lax.all_gather(heads_weight, "fsdp", axis=0, tiled=True),
        lax.all_gather(query_bias, "fsdp", axis=0, tiled=True),
        lax.all_gather(value_bias, "fsdp", axis=0, tiled=True),
        lax.all_gather(output_weight, "fsdp", axis=0, tiled=True),
        lax.all_gather(output_bias, "fsdp", axis=0, tiled=True),
        lax.all_gather(attn_layerscale, "fsdp", axis=0, tiled=True),
        lax.all_gather(mlp_norm_gain, "fsdp", axis=0, tiled=True),
        lax.all_gather(mlp_norm_bias, "fsdp", axis=0, tiled=True),
        lax.all_gather(expand_weight, "fsdp", axis=0, tiled=True),
        lax.all_gather(expand_bias, "fsdp", axis=0, tiled=True),
        lax.all_gather(shrink_weight, "fsdp", axis=0, tiled=True),
        lax.all_gather(shrink_bias, "fsdp", axis=0, tiled=True),
        lax.all_gather(mlp_layerscale, "fsdp", axis=0, tiled=True),
    )


def reduce_grads(local_grads):
    (
        g_attn_gain,
        g_attn_shift,
        g_heads_weight,
        g_query_bias,
        g_value_bias,
        g_output_weight,
        g_output_bias,
        g_attn_scale,
        g_mlp_gain,
        g_mlp_shift,
        g_expand_weight,
        g_expand_bias,
        g_shrink_weight,
        g_shrink_bias,
        g_mlp_scale,
    ) = local_grads
    owned = (
        lax.psum_scatter(
            g_attn_gain.astype(jnp.bfloat16), "fsdp", scatter_dimension=0, tiled=True
        ).astype(jnp.float32),
        lax.psum_scatter(
            g_attn_shift.astype(jnp.bfloat16), "fsdp", scatter_dimension=0, tiled=True
        ).astype(jnp.float32),
        lax.psum_scatter(
            g_heads_weight.astype(jnp.bfloat16), "fsdp", scatter_dimension=0, tiled=True
        ).astype(jnp.float32),
        lax.psum_scatter(
            g_query_bias.astype(jnp.bfloat16), "fsdp", scatter_dimension=0, tiled=True
        ).astype(jnp.float32),
        lax.psum_scatter(
            g_value_bias.astype(jnp.bfloat16), "fsdp", scatter_dimension=0, tiled=True
        ).astype(jnp.float32),
        lax.psum_scatter(
            g_output_weight.astype(jnp.bfloat16), "fsdp", scatter_dimension=0, tiled=True
        ).astype(jnp.float32),
        lax.psum_scatter(
            g_output_bias.astype(jnp.bfloat16), "fsdp", scatter_dimension=0, tiled=True
        ).astype(jnp.float32),
        lax.psum_scatter(
            g_attn_scale.astype(jnp.bfloat16), "fsdp", scatter_dimension=0, tiled=True
        ).astype(jnp.float32),
        lax.psum_scatter(
            g_mlp_gain.astype(jnp.bfloat16), "fsdp", scatter_dimension=0, tiled=True
        ).astype(jnp.float32),
        lax.psum_scatter(
            g_mlp_shift.astype(jnp.bfloat16), "fsdp", scatter_dimension=0, tiled=True
        ).astype(jnp.float32),
        lax.psum_scatter(
            g_expand_weight.astype(jnp.bfloat16), "fsdp", scatter_dimension=0, tiled=True
        ).astype(jnp.float32),
        lax.psum_scatter(
            g_expand_bias.astype(jnp.bfloat16), "fsdp", scatter_dimension=0, tiled=True
        ).astype(jnp.float32),
        lax.psum_scatter(
            g_shrink_weight.astype(jnp.bfloat16), "fsdp", scatter_dimension=0, tiled=True
        ).astype(jnp.float32),
        lax.psum_scatter(
            g_shrink_bias.astype(jnp.bfloat16), "fsdp", scatter_dimension=0, tiled=True
        ).astype(jnp.float32),
        lax.psum_scatter(
            g_mlp_scale.astype(jnp.bfloat16), "fsdp", scatter_dimension=0, tiled=True
        ).astype(jnp.float32),
    )
    (
        o_attn_gain,
        o_attn_shift,
        o_heads_weight,
        o_query_bias,
        o_value_bias,
        o_output_weight,
        o_output_bias,
        o_attn_scale,
        o_mlp_gain,
        o_mlp_shift,
        o_expand_weight,
        o_expand_bias,
        o_shrink_weight,
        o_shrink_bias,
        o_mlp_scale,
    ) = owned
    return (
        lax.psum(o_attn_gain.astype(jnp.bfloat16), "rep").astype(jnp.float32),
        lax.psum(o_attn_shift.astype(jnp.bfloat16), "rep").astype(jnp.float32),
        lax.psum(o_heads_weight.astype(jnp.bfloat16), "rep").astype(jnp.float32),
        lax.psum(o_query_bias.astype(jnp.bfloat16), "rep").astype(jnp.float32),
        lax.psum(o_value_bias.astype(jnp.bfloat16), "rep").astype(jnp.float32),
        lax.psum(o_output_weight.astype(jnp.bfloat16), "rep").astype(jnp.float32),
        lax.psum(o_output_bias.astype(jnp.bfloat16), "rep").astype(jnp.float32),
        lax.psum(o_attn_scale.astype(jnp.bfloat16), "rep").astype(jnp.float32),
        lax.psum(o_mlp_gain.astype(jnp.bfloat16), "rep").astype(jnp.float32),
        lax.psum(o_mlp_shift.astype(jnp.bfloat16), "rep").astype(jnp.float32),
        lax.psum(o_expand_weight.astype(jnp.bfloat16), "rep").astype(jnp.float32),
        lax.psum(o_expand_bias.astype(jnp.bfloat16), "rep").astype(jnp.float32),
        lax.psum(o_shrink_weight.astype(jnp.bfloat16), "rep").astype(jnp.float32),
        lax.psum(o_shrink_bias.astype(jnp.bfloat16), "rep").astype(jnp.float32),
        lax.psum(o_mlp_scale.astype(jnp.bfloat16), "rep").astype(jnp.float32),
    )


def split_heads(queries, keys_values, groups):
    width = queries.shape[1]
    head_dim = width // HEADS
    query_blocks = queries.reshape(groups, -1, HEADS, head_dim)
    key_blocks = keys_values[:, :, :width].reshape(groups, -1, HEADS, head_dim)
    value_blocks = keys_values[:, :, width:].reshape(groups, -1, HEADS, head_dim)
    return (query_blocks, key_blocks, value_blocks, head_dim ** (-0.5))


def attend(queries, keys_values, groups):
    query_blocks, key_blocks, value_blocks, attn_factor = split_heads(queries, keys_values, groups)
    scores = (
        jnp.einsum("gqhd,gkhd->ghqk", query_blocks, key_blocks, preferred_element_type=jnp.float32)
        * attn_factor
    )
    largest = jnp.max(scores, -1, keepdims=True)
    log_total = largest + jnp.log(jnp.sum(jnp.exp(scores - largest), -1, keepdims=True))
    weights = jnp.exp(scores - log_total).astype(jnp.bfloat16)
    attended = jnp.einsum(
        "ghqk,gkhd->gqhd", weights, value_blocks, preferred_element_type=jnp.float32
    )
    return (attended.reshape(queries.shape), log_total)


def attend_back(queries, keys_values, log_total, d_attended, groups):
    width = queries.shape[1]
    query_blocks, key_blocks, value_blocks, attn_factor = split_heads(queries, keys_values, groups)
    scores = (
        jnp.einsum("gqhd,gkhd->ghqk", query_blocks, key_blocks, preferred_element_type=jnp.float32)
        * attn_factor
    )
    probs = jnp.exp(scores - log_total)
    d_blocks = d_attended.reshape(query_blocks.shape)
    d_probs = jnp.einsum(
        "gqhd,gkhd->ghqk", d_blocks, value_blocks, preferred_element_type=jnp.float32
    )
    inner = jnp.sum(probs * d_probs, -1, keepdims=True)
    d_scores = (probs * (d_probs - inner)).astype(jnp.bfloat16)
    d_query = (
        jnp.einsum("ghqk,gkhd->gqhd", d_scores, key_blocks, preferred_element_type=jnp.float32)
        * attn_factor
    )
    probs_low = probs.astype(jnp.bfloat16)
    d_key = (
        jnp.einsum("ghqk,gqhd->gkhd", d_scores, query_blocks, preferred_element_type=jnp.float32)
        * attn_factor
    )
    d_value = jnp.einsum("ghqk,gqhd->gkhd", probs_low, d_blocks, preferred_element_type=jnp.float32)
    d_keys_values = jnp.concatenate(
        [d_key.reshape(groups, -1, width), d_value.reshape(groups, -1, width)], 2
    )
    d_local_kv = lax.psum_scatter(
        d_keys_values.astype(jnp.bfloat16), "fsdp", scatter_dimension=1, tiled=True
    )
    return (d_query.reshape(queries.shape).astype(jnp.bfloat16), d_local_kv)


def forward_layer(tok_rows, gathered, groups):
    (
        attn_norm_gain,
        attn_norm_bias,
        heads_weight,
        query_bias,
        value_bias,
        output_weight,
        output_bias,
        attn_layerscale,
        mlp_norm_gain,
        mlp_norm_bias,
        expand_weight,
        expand_bias,
        shrink_weight,
        shrink_bias,
        mlp_layerscale,
    ) = gathered
    width = tok_rows.shape[1]
    normed = layer_norm(tok_rows, widen(attn_norm_gain), widen(attn_norm_bias)).astype(jnp.bfloat16)
    bias_row = jnp.concatenate(
        [widen(query_bias), jnp.zeros((width,), jnp.float32), widen(value_bias)]
    )
    projected = (forward_dot(normed, heads_weight) + bias_row).astype(jnp.bfloat16)
    queries = projected[:, :width]
    local_kv = projected[:, width:].reshape(groups, -1, 2 * width)
    keys_values = lax.all_gather(local_kv, "fsdp", axis=1, tiled=True)
    attended, log_total = attend(queries, keys_values, groups)
    attended_low = attended.astype(jnp.bfloat16)
    branch = forward_dot(attended_low, output_weight) + widen(output_bias)
    middle = tok_rows + widen(attn_layerscale) * branch
    normed_two = layer_norm(middle, widen(mlp_norm_gain), widen(mlp_norm_bias)).astype(jnp.bfloat16)
    hidden = forward_dot(normed_two, expand_weight) + widen(expand_bias)
    activated = gelu_exact(hidden).astype(jnp.bfloat16)
    mlp_out = forward_dot(activated, shrink_weight) + widen(shrink_bias)
    result = middle + widen(mlp_layerscale) * mlp_out
    saved = (
        tok_rows,
        normed,
        queries,
        keys_values,
        local_kv,
        log_total,
        attended_low,
        branch,
        middle,
        normed_two,
        hidden,
        activated,
        mlp_out,
    )
    return (result, saved)


def backward_layer(d_result, saved, gathered, groups):
    (
        attn_norm_gain,
        attn_norm_bias,
        heads_weight,
        query_bias,
        value_bias,
        output_weight,
        output_bias,
        attn_layerscale,
        mlp_norm_gain,
        mlp_norm_bias,
        expand_weight,
        expand_bias,
        shrink_weight,
        shrink_bias,
        mlp_layerscale,
    ) = gathered
    (
        tok_rows,
        normed,
        queries,
        keys_values,
        local_kv,
        log_total,
        attended_low,
        branch,
        middle,
        normed_two,
        hidden,
        activated,
        mlp_out,
    ) = saved
    width = tok_rows.shape[1]
    d_mlp = (d_result * widen(mlp_layerscale)).astype(jnp.bfloat16)
    g_mlp_scale = jnp.sum(d_result * mlp_out, 0)
    g_shrink_bias = column_sum(d_mlp)
    g_shrink_weight = weight_dot(activated, d_mlp)
    d_activated = input_dot(d_mlp, shrink_weight)
    unused, gelu_pull = jax.vjp(gelu_exact, hidden)
    d_hidden = gelu_pull(d_activated)[0].astype(jnp.bfloat16)
    g_expand_bias = column_sum(d_hidden)
    g_expand_weight = weight_dot(normed_two, d_hidden)
    d_normed_two = input_dot(d_hidden, expand_weight)
    d_middle_norm, g_mlp_gain, g_mlp_shift = norm_back(
        middle, widen(mlp_norm_gain), widen(mlp_norm_bias), d_normed_two
    )
    d_middle = d_result + d_middle_norm
    d_branch = (d_middle * widen(attn_layerscale)).astype(jnp.bfloat16)
    g_attn_scale = jnp.sum(d_middle * branch, 0)
    g_output_bias = column_sum(d_branch)
    g_output_weight = weight_dot(attended_low, d_branch)
    d_attended = input_dot(d_branch, output_weight).astype(jnp.bfloat16)
    d_query, d_local_kv = attend_back(queries, keys_values, log_total, d_attended, groups)
    d_projected = jnp.concatenate([d_query, d_local_kv.reshape(-1, 2 * width)], 1)
    g_query_bias = column_sum(d_query)
    g_value_bias = column_sum(d_projected[:, 2 * width :])
    g_heads_weight = weight_dot(normed, d_projected)
    d_normed = input_dot(d_projected, heads_weight)
    d_rows_norm, g_attn_gain, g_attn_shift = norm_back(
        tok_rows, widen(attn_norm_gain), widen(attn_norm_bias), d_normed
    )
    d_rows = d_middle + d_rows_norm
    local_grads = (
        g_attn_gain,
        g_attn_shift,
        g_heads_weight,
        g_query_bias,
        g_value_bias,
        g_output_weight,
        g_output_bias,
        g_attn_scale,
        g_mlp_gain,
        g_mlp_shift,
        g_expand_weight,
        g_expand_bias,
        g_shrink_weight,
        g_shrink_bias,
        g_mlp_scale,
    )
    return (d_rows, local_grads)


def local(
    images,
    cotangent,
    attn_norm_gain,
    attn_norm_bias,
    heads_weight,
    query_bias,
    value_bias,
    output_weight,
    output_bias,
    attn_layerscale,
    mlp_norm_gain,
    mlp_norm_bias,
    expand_weight,
    expand_bias,
    shrink_weight,
    shrink_bias,
    mlp_layerscale,
):
    groups = images.shape[0]
    width = images.shape[2]
    all_params = (
        attn_norm_gain,
        attn_norm_bias,
        heads_weight,
        query_bias,
        value_bias,
        output_weight,
        output_bias,
        attn_layerscale,
        mlp_norm_gain,
        mlp_norm_bias,
        expand_weight,
        expand_bias,
        shrink_weight,
        shrink_bias,
        mlp_layerscale,
    )
    tok_rows = widen(images).reshape(-1, width)
    saved_layers = []
    fetched = []
    for layer_idx in range(LAYERS):
        gathered = fetch_forward(tuple((param[layer_idx] for param in all_params)))
        fetched.append(gathered)
        tok_rows, saved = forward_layer(tok_rows, gathered, groups)
        saved_layers.append(saved)
    activations = tok_rows.astype(jnp.bfloat16).reshape(images.shape)
    d_rows = widen(cotangent).reshape(-1, width)
    layer_grads = [None] * LAYERS
    for layer_idx in reversed(range(LAYERS)):
        gathered = fetch_backward(tuple((param[layer_idx] for param in all_params)))
        d_rows, local_grads = backward_layer(d_rows, saved_layers[layer_idx], gathered, groups)
        layer_grads[layer_idx] = reduce_grads(local_grads)
    stacked = tuple(
        (
            jnp.stack([grads[position] for grads in layer_grads])
            for position in range(len(all_params))
        )
    )
    return (activations, d_rows.reshape(images.shape)) + stacked


def solution(mesh):
    in_specs = (
        P("rep", "fsdp", None),
        P("rep", "fsdp", None),
        P(None, "fsdp"),
        P(None, "fsdp"),
        P(None, "fsdp", None),
        P(None, "fsdp"),
        P(None, "fsdp"),
        P(None, "fsdp", None),
        P(None, "fsdp"),
        P(None, "fsdp"),
        P(None, "fsdp"),
        P(None, "fsdp"),
        P(None, "fsdp", None),
        P(None, "fsdp"),
        P(None, "fsdp", None),
        P(None, "fsdp"),
        P(None, "fsdp"),
    )
    out_specs = (
        P("rep", "fsdp", None),
        P("rep", "fsdp", None),
        P(None, "fsdp"),
        P(None, "fsdp"),
        P(None, "fsdp", None),
        P(None, "fsdp"),
        P(None, "fsdp"),
        P(None, "fsdp", None),
        P(None, "fsdp"),
        P(None, "fsdp"),
        P(None, "fsdp"),
        P(None, "fsdp"),
        P(None, "fsdp", None),
        P(None, "fsdp"),
        P(None, "fsdp", None),
        P(None, "fsdp"),
        P(None, "fsdp"),
    )
    return jax.shard_map(local, mesh=mesh, in_specs=in_specs, out_specs=out_specs, check_vma=False)
```

profile of v0, /device:TPU:0, one launch (start us, length us, event | category | flops | bytes accessed | tf_op | source)
XLA Modules:
  0.0 2299.8 jit_solution(15540597498499024753)
XLA Ops:
  238.6 15.1 copy.122
  253.7 17.8 multiply_reduce_fusion.3
  286.1 15.6 fusion.93
  312.5 19.7 multiply_convert_fusion.5
  332.3 62.8 %all-gather.51.cloned.1.call-done = bf16[1,4096,1024]{2,1,0:T(8,128)(2,1)} async-done(((bf16[1,512,1024]{2,1,0:T(8,128)(2,1)}), bf16[1,4096,1024]{2,1,0:T(8,128)(2,1)}) %all-gather.51.cloned.1.call-update) | async-done | bytes 8388624 | tf_op jit(solution)/shard_map/all_gather | solution.py:82
  404.0 56.0 %all-gather.53.cloned.1.call-done = bf16[1,1024,3072]{2,1,0:T(8,128)(2,1)} async-done(((bf16[1,128,3072]{2,1,0:T(8,128)(2,1)}), bf16[1,1024,3072]{2,1,0:T(8,128)(2,1)}) %all-gather.53.cloned.1.call-update) | async-done | bytes 6291472 | tf_op jit(solution)/shard_map/all_gather | solution.py:72
  587.9 15.1 copy.130
  603.0 15.1 copy.128
  618.1 17.9 multiply_reduce_fusion.2
  649.9 15.3 fusion.90
  690.5 19.2 multiply_convert_fusion.4
  709.6 62.9 %all-gather.59.cloned.1.call-done = bf16[1,4096,1024]{2,1,0:T(8,128)(2,1)} async-done(((bf16[1,512,1024]{2,1,0:T(8,128)(2,1)}), bf16[1,4096,1024]{2,1,0:T(8,128)(2,1)}) %all-gather.59.cloned.1.call-update) | async-done | bytes 8388624 | tf_op jit(solution)/shard_map/all_gather | solution.py:82
  805.8 15.6 convolution_convert_fusion.7
  821.4 22.7 multiply_reduce_fusion.1
  859.2 26.7 %multiply_convert_fusion.1 = bf16[2,16,172,1376]{3,2,1,0:T(8,128)(2,1)} fusion(f32[2,16,172,1376]{3,2,1,0:T(8,128)} %get-tuple-element.230, f32[2,16,172,1376]{3,2,1,0:T(8,128)} %get-tuple-element.225, f32[2,16,172]{2,1,0:T(8,128)S(1)} %get-tuple-element.229, f32[2,16,172]{2,1,0:T(8,128)S(1)} %log_add_fusion), kind=kLoop, calls=%fused_computation.2 | loop fusion | flops 37867520 | bytes 75779072 | tf_op jit(solution)/shard_map/convert_element_type | solution.py:263
  897.3 15.1 copy.139
  945.9 209.4 %all-reduce.31.cloned.1.call-done = bf16[2,1376,2048]{2,0,1:T(2,128)(2,1)} async-done(((bf16[2,1376,2048]{2,0,1:T(2,128)(2,1)}), bf16[2,1376,2048]{2,0,1:T(2,128)(2,1)}) %all-reduce.31.cloned.1.call-update) | async-done | bytes 11272208
  1205.8 16.2 convolution_convert_fusion.6
  1222.0 26.9 %multiply_reduce_fusion = (f32[2,16,172]{2,1,0:T(8,128)S(1)}, f32[2,16,172,1376]{3,2,1,0:T(8,128)}) fusion(f32[2,16,172,1376]{3,2,1,0:T(8,128)} %get-tuple-element.220, f32[2,16,172]{2,1,0:T(8,128)S(1)} %copy-done.33, bf16[2,172,16,64]{1,3,2,0:T(8,128)(2,1)} %copy.144, bf16[2,1376,16,64]{1,3,2,0:T(8,128)(2,1)} %bitcast.236), kind=kOutput, calls=%fused_computation.1 | convolution fusion | flops 999697024 | bytes 66972672 | tf_op jit(solution)/shard_map/gqhd,gkhd->ghqk/dot_general | solution.py:259
  1264.0 26.6 %multiply_convert_fusion = bf16[2,16,172,1376]{3,2,1,0:T(8,128)(2,1)} fusion(f32[2,16,172,1376]{3,2,1,0:T(8,128)} %get-tuple-element.234, f32[2,16,172,1376]{3,2,1,0:T(8,128)} %get-tuple-element.220, f32[2,16,172]{2,1,0:T(8,128)S(1)} %get-tuple-element.233, f32[2,16,172]{2,1,0:T(8,128)S(1)} %copy-done.33), kind=kLoop, calls=%fused_computation | loop fusion | flops 37867520 | bytes 75779072 | tf_op jit(solution)/shard_map/convert_element_type | solution.py:263
  1402.7 158.9 %all-reduce.33.cloned.1.call-done = bf16[2,1376,2048]{2,0,1:T(2,128)(2,1)} async-done(((bf16[2,1376,2048]{2,0,1:T(2,128)(2,1)}), bf16[2,1376,2048]{2,0,1:T(2,128)(2,1)}) %all-reduce.33.cloned.1.call-update) | async-done | bytes 11272208
  1576.0 24.0 %reduce-scatter.15.cloned.1.call-done = bf16[128,1024]{1,0:T(8,128)(2,1)} async-done(((bf16[1024,1024]{1,0:T(8,128)(2,1)}), bf16[128,1024]{1,0:T(8,128)(2,1)}) %reduce-scatter.15.cloned.1.call-update) | async-done | bytes 262160 | tf_op jit(solution)/shard_map/reduce_scatter | solution.py:159
  1599.9 36.6 %reduce-scatter.13.cloned.1.call-done = bf16[128,1024]{1,0:T(8,128)(2,1)} async-done(((bf16[1024,1024]{1,0:T(8,128)(2,1)}), bf16[128,1024]{1,0:T(8,128)(2,1)}) %reduce-scatter.13.cloned.1.call-update) | async-done | bytes 262160 | tf_op jit(solution)/shard_map/reduce_scatter | solution.py:159
  1636.6 90.5 %reduce-scatter.19.cloned.1.call-done = bf16[128,4096]{1,0:T(8,128)(2,1)} async-done(((bf16[1024,4096]{1,0:T(8,128)(2,1)}), bf16[128,4096]{1,0:T(8,128)(2,1)}) %reduce-scatter.19.cloned.1.call-update) | async-done | bytes 1048592 | tf_op jit(solution)/shard_map/reduce_scatter | solution.py:174
  1727.1 90.2 %reduce-scatter.23.cloned.1.call-done = bf16[512,1024]{1,0:T(8,128)(2,1)} async-done(((bf16[4096,1024]{1,0:T(8,128)(2,1)}), bf16[512,1024]{1,0:T(8,128)(2,1)}) %reduce-scatter.23.cloned.1.call-update) | async-done | bytes 1048592 | tf_op jit(solution)/shard_map/reduce_scatter | solution.py:180
  1817.3 70.3 %reduce-scatter.11.cloned.1.call-done = bf16[128,3072]{1,0:T(8,128)(2,1)} async-done(((bf16[1024,3072]{1,0:T(8,128)(2,1)}), bf16[128,3072]{1,0:T(8,128)(2,1)}) %reduce-scatter.11.cloned.1.call-update) | async-done | bytes 786448 | tf_op jit(solution)/shard_map/reduce_scatter | solution.py:150
  1887.6 90.2 %reduce-scatter.17.cloned.1.call-done = bf16[128,4096]{1,0:T(8,128)(2,1)} async-done(((bf16[1024,4096]{1,0:T(8,128)(2,1)}), bf16[128,4096]{1,0:T(8,128)(2,1)}) %reduce-scatter.17.cloned.1.call-update) | async-done | bytes 1048592 | tf_op jit(solution)/shard_map/reduce_scatter | solution.py:174
  1977.8 90.3 %reduce-scatter.21.cloned.1.call-done = bf16[512,1024]{1,0:T(8,128)(2,1)} async-done(((bf16[4096,1024]{1,0:T(8,128)(2,1)}), bf16[512,1024]{1,0:T(8,128)(2,1)}) %reduce-scatter.21.cloned.1.call-update) | async-done | bytes 1048592 | tf_op jit(solution)/shard_map/reduce_scatter | solution.py:180
  2068.0 70.3 %reduce-scatter.9.cloned.1.call-done = bf16[128,3072]{1,0:T(8,128)(2,1)} async-done(((bf16[1024,3072]{1,0:T(8,128)(2,1)}), bf16[128,3072]{1,0:T(8,128)(2,1)}) %reduce-scatter.9.cloned.1.call-update) | async-done | bytes 786448 | tf_op jit(solution)/shard_map/reduce_scatter | solution.py:150
  2154.0 26.8 %all-reduce.24 = (bf16[1024]{0:T(1024)(128)(2,1)S(1)}, bf16[1024]{0:T(1024)(128)(2,1)S(1)}, bf16[1024]{0:T(1024)(128)(2,1)S(1)}, bf16[1024]{0:T(1024)(128)(2,1)S...) all-reduce(bf16[1024]{0:T(1024)(128)(2,1)S(1)} %copy-done.106, ...), channel_id=35, replica_groups=mesh['rep'=4,'fsdp'=8] {'fsdp'}, use_global_device_ids=true, to_apply=%region_28.0.clone | all-reduce | flops 28672 | bytes 114688
  2188.7 16.5 all-reduce.25
  2211.5 71.0 %all-reduce.35.cloned.1.call-done = (bf16[1,128,3072]{2,1,0:T(8,128)(2,1)}, bf16[1,128,3072]{2,1,0:T(8,128)(2,1)}, bf16[1,128,1024]{2,1,0:T(8,128)(2,1)}, bf16[1...) async-done(((bf16[1,128,3072]{2,1,0:T(8,128)(2,1)}, ...) | async-done | bytes 6291472 | tf_op jit(solution)/shard_map/psum | solution.py:210
  (523 shorter events, 754.5 us)
Async XLA Ops:
  7.2 73.0 %all-gather.45.cloned.1.call-start = ((), (), s32[]{:S(2)}) async-start(), calls=%async_computation.18 | async-start | bytes 7077888 | tf_op jit(solution)/shard_map/all_gather | solution.py:72
  9.9 202.5 %all-gather.41.cloned.1.call-start = ((), (), s32[]{:S(2)}) async-start(), calls=%async_computation.8 | async-start | bytes 12681216 | tf_op jit(solution)/shard_map/all_gather | solution.py:309
  80.2 223.2 %copy-start.4 = (f32[344,1024]{1,0:T(8,128)}, f32[344,1024]{1,0:T(8,128)S(1)}, u32[]{:S(2)}) copy-start(f32[344,1024]{1,0:T(8,128)S(1)} %reshape.297) | copy-start | bytes 4227076
  95.3 208.2 %all-gather.47.cloned.1.call-start = ((), (), s32[]{:S(2)}) async-start(), calls=%async_computation.19 | async-start | bytes 2359296 | tf_op jit(solution)/shard_map/all_gather | solution.py:75
  96.3 216.2 %all-gather.49.cloned.1.call-start = ((), (), s32[]{:S(2)}) async-start(), calls=%async_computation.20 | async-start | bytes 9437184 | tf_op jit(solution)/shard_map/all_gather | solution.py:80
  99.5 295.7 %all-gather.51.cloned.1.call-start = ((), (), s32[]{:S(2)}) async-start(), calls=%async_computation.21 | async-start | bytes 9437184 | tf_op jit(solution)/shard_map/all_gather | solution.py:82
  102.8 357.1 %all-gather.53.cloned.1.call-start = ((), (), s32[]{:S(2)}) async-start(), calls=%async_computation.22 | async-start | bytes 7077888 | tf_op jit(solution)/shard_map/all_gather | solution.py:72
  103.4 473.7 %all-gather.43.cloned.1.call-start = ((), (), s32[]{:S(2)}) async-start(), calls=%async_computation.9 | async-start | bytes 12681216 | tf_op jit(solution)/shard_map/all_gather | solution.py:309
  126.0 334.0 %copy-start.59 = (f32[1,1024]{1,0:T(1,128)}, f32[1,1024]{1,0:T(1,128)S(1)}, u32[]{:S(2)}) copy-start(f32[1,1024]{1,0:T(1,128)S(1)} %convert_element_type.450) | copy-start | bytes 12292
  140.1 255.1 %copy-start.64 = (f32[1,1024]{1,0:T(1,128)}, f32[1,1024]{1,0:T(1,128)S(1)}, u32[]{:S(2)}) copy-start(f32[1,1024]{1,0:T(1,128)S(1)} %convert_element_type.444) | copy-start | bytes 12292
  403.6 267.6 %copy-start.9 = (f32[344,1024]{1,0:T(8,128)}, f32[344,1024]{1,0:T(8,128)S(1)}, u32[]{:S(2)}) copy-start(f32[344,1024]{1,0:T(8,128)S(1)} %get-tuple-element.174) | copy-start | bytes 4227076
  472.1 199.2 %all-gather.55.cloned.1.call-start = ((), (), s32[]{:S(2)}) async-start(), calls=%async_computation.23 | async-start | bytes 2359296 | tf_op jit(solution)/shard_map/all_gather | solution.py:75
  472.8 217.6 %all-gather.57.cloned.1.call-start = ((), (), s32[]{:S(2)}) async-start(), calls=%async_computation.24 | async-start | bytes 9437184 | tf_op jit(solution)/shard_map/all_gather | solution.py:80
  473.6 298.9 %all-gather.59.cloned.1.call-start = ((), (), s32[]{:S(2)}) async-start(), calls=%async_computation.25 | async-start | bytes 9437184 | tf_op jit(solution)/shard_map/all_gather | solution.py:82
  474.2 681.2 %all-reduce.31.cloned.1.call-start = ((), (), s32[]{:S(2)}) async-start(), calls=%async_computation.26 | async-start | bytes 22544384
  483.3 310.5 %copy-start.62 = (f32[1,1024]{1,0:T(1,128)}, f32[1,1024]{1,0:T(1,128)S(1)}, u32[]{:S(2)}) copy-start(f32[1,1024]{1,0:T(1,128)S(1)} %convert_element_type.455) | copy-start | bytes 12292
  926.7 634.9 %all-reduce.33.cloned.1.call-start = ((), (), s32[]{:S(2)}) async-start(), calls=%async_computation.27 | async-start | bytes 22544384
  945.9 218.8 %copy-start.46 = (f32[344]{0:T(512)S(1)}, f32[344]{0:T(512)}, u32[]{:S(2)}) copy-start(f32[344]{0:T(512)} %copy-done.45) | copy-start | bytes 4132
  945.9 218.8 %copy-start.60 = (f32[1,1024]{1,0:T(1,128)S(1)}, f32[1,1024]{1,0:T(1,128)}, u32[]{:S(2)}) copy-start(f32[1,1024]{1,0:T(1,128)} %copy-done.59) | copy-start | bytes 12292
  945.9 218.8 %copy-start.76 = (f32[344]{0:T(512)S(1)}, f32[344]{0:T(512)}, u32[]{:S(2)}) copy-start(f32[344]{0:T(512)} %copy-done.75) | copy-start | bytes 4132
  1331.4 268.5 %reduce-scatter.15.cloned.1.call-start = ((), (), s32[]{:S(2)}) async-start(), calls=%async_computation.13 | async-start | bytes 2359296 | tf_op jit(solution)/shard_map/reduce_scatter | solution.py:159
  1336.2 300.3 %reduce-scatter.13.cloned.1.call-start = ((), (), s32[]{:S(2)}) async-start(), calls=%async_computation.12 | async-start | bytes 2359296 | tf_op jit(solution)/shard_map/reduce_scatter | solution.py:159
  1340.7 386.4 %reduce-scatter.19.cloned.1.call-start = ((), (), s32[]{:S(2)}) async-start(), calls=%async_computation.15 | async-start | bytes 9437184 | tf_op jit(solution)/shard_map/reduce_scatter | solution.py:174
  1351.2 466.1 %reduce-scatter.23.cloned.1.call-start = ((), (), s32[]{:S(2)}) async-start(), calls=%async_computation.17 | async-start | bytes 9437184 | tf_op jit(solution)/shard_map/reduce_scatter | solution.py:180
  1362.0 525.6 %reduce-scatter.11.cloned.1.call-start = ((), (), s32[]{:S(2)}) async-start(), calls=%async_computation.11 | async-start | bytes 7077888 | tf_op jit(solution)/shard_map/reduce_scatter | solution.py:150
  1370.0 607.8 %reduce-scatter.17.cloned.1.call-start = ((), (), s32[]{:S(2)}) async-start(), calls=%async_computation.14 | async-start | bytes 9437184 | tf_op jit(solution)/shard_map/reduce_scatter | solution.py:174
  1379.7 688.3 %reduce-scatter.21.cloned.1.call-start = ((), (), s32[]{:S(2)}) async-start(), calls=%async_computation.16 | async-start | bytes 9437184 | tf_op jit(solution)/shard_map/reduce_scatter | solution.py:180
  1388.6 749.8 %reduce-scatter.9.cloned.1.call-start = ((), (), s32[]{:S(2)}) async-start(), calls=%async_computation.10 | async-start | bytes 7077888 | tf_op jit(solution)/shard_map/reduce_scatter | solution.py:150
  1575.9 563.8 %copy-start.22 = (bf16[2,172,1024]{2,0,1:T(2,128)(2,1)S(1)}, bf16[2,172,1024]{2,0,1:T(2,128)(2,1)}, u32[]{:S(2)}) copy-start(bf16[2,172,1024]{2,0,1:T(2,128)(2,1)} %param.18) | copy-start | bytes 2113540
  1575.9 568.0 %copy-start.66 = (bf16[16,64]{1,0:T(8,128)(2,1)S(1)}, bf16[16,64]{1,0:T(8,128)(2,1)}, u32[]{:S(2)}) copy-start(bf16[16,64]{1,0:T(8,128)(2,1)} %get-tuple-element.236) | copy-start | bytes 6148
  1575.9 568.2 %copy-start.13 = (bf16[344,2048]{1,0:T(8,128)(2,1)S(1)}, bf16[344,2048]{1,0:T(8,128)(2,1)}, u32[]{:S(2)}) copy-start(bf16[344,2048]{1,0:T(8,128)(2,1)} %reshape.311) | copy-start | bytes 4227076
  1575.9 706.6 %all-reduce.35.cloned.1.call-start = ((), (), s32[]{:S(2)}) async-start(), calls=%async_computation.28 | async-start | bytes 12582912 | tf_op jit(solution)/shard_map/psum | solution.py:210
  (121 other events, 3904.0 us)
Sparse Core Ops, SparseCore 0:
  10.2 67.5 all-gather.44
  95.4 104.4 all-gather.40
  201.4 27.3 all-gather.46
  230.9 81.5 all-gather.48
  314.5 80.5 all-gather.50
  396.6 63.2 all-gather.52
  472.2 104.8 all-gather.42
  579.3 27.3 all-gather.54
  608.9 81.5 all-gather.56
  691.9 80.5 all-gather.58
  926.9 228.4 all-reduce.30
  1331.5 230.0 all-reduce.32
  1563.9 35.9 reduce-scatter.14
  1602.1 34.4 reduce-scatter.12
  1638.7 88.3 reduce-scatter.18
  1729.2 87.9 reduce-scatter.22
  1819.4 68.1 reduce-scatter.10
  1889.7 87.9 reduce-scatter.16
  1980.0 87.9 reduce-scatter.20
  2070.2 68.1 reduce-scatter.8
  2142.8 139.6 all-reduce.34
where the time goes:
time: 2310 us; the launch traced here: 2300 us
  waiting for transfers between devices  1220 us (53%)
  matrix products  385 us (17%)
  blocking collectives  283 us (12%)
  local copies, waits for them, and re-layouts  250 us (11%)
  other arithmetic  144 us (6%)
    unnamed x23, waiting for transfers between devices  371 us
    reduce_scatter x2, waiting for transfers between devices, reduce_grads(): lax.psum_scatter(g_expand_weight.astype(jnp.bfloat16), 'fsdp', scatter_di...  181 us
    reduce_scatter x2, waiting for transfers between devices, reduce_grads(): lax.psum_scatter(g_shrink_weight.astype(jnp.bfloat16), 'fsdp', scatter_di...  180 us
    reduce_scatter x2, waiting for transfers between devices, reduce_grads(): lax.psum_scatter(g_heads_weight.astype(jnp.bfloat16), 'fsdp', scatter_dim...  141 us
    all_gather x2, waiting for transfers between devices, fetch_forward(): lax.all_gather(shrink_weight, 'fsdp', axis=0, tiled=True)  126 us
    dot_general x8, matrix products, forward_dot(): return jnp.dot(left, weight, preferred_element_type=jnp.float32)  71.2 us
    psum x1, waiting for transfers between devices, reduce_grads(): lax.psum(o_heads_weight.astype(jnp.bfloat16), 'rep').astype(jnp.float32)  71 us
    reduce_scatter x2, waiting for transfers between devices, reduce_grads(): lax.psum_scatter(g_output_weight.astype(jnp.bfloat16), 'fsdp', scatter_di...  60.6 us
  transfers between devices with their start and end apart: 21, of which 17 were waited for; matrix products, arithmetic and copies ran while one was open for 17% of the time, Pallas kernels for 0%

commit v1 on v0

v1 whole, which is shorter than its diff:
```python
import functools
import math

import jax
import jax.numpy as jnp
from jax import lax
from jax.experimental import pallas as pl
from jax.experimental.pallas import tpu as pltpu
from jax.sharding import PartitionSpec as P

HEADS = 16
LAYERS = 2
SMALL = (0, 1, 3, 4, 6, 7, 8, 9, 11, 13, 14)
MIB = 1 << 20

epsilon = 1e-06


def layer_norm(values_in, norm_gain, norm_shift):
    centre = jnp.mean(values_in, -1, keepdims=True)
    centered = values_in - centre
    spread = jnp.mean(centered * centered, -1, keepdims=True)
    return centered * lax.rsqrt(spread + epsilon) * norm_gain + norm_shift


def norm_back(values_in, norm_gain, norm_shift, grad):
    unused, pullback = jax.vjp(layer_norm, values_in, norm_gain, norm_shift)
    return pullback(grad)


def widen(tensor):
    return tensor.astype(jnp.float32)


def low(tensor):
    return tensor.astype(jnp.bfloat16)


def forward_dot(left, weight):
    return jnp.dot(left, weight, preferred_element_type=jnp.float32)


def weight_dot(left, grad):
    return lax.dot_general(left, grad, (((0,), (0,)), ((), ())), preferred_element_type=jnp.float32)


def input_dot(grad, weight):
    return lax.dot_general(
        grad, weight, (((1,), (1,)), ((), ())), preferred_element_type=jnp.float32
    )


def column_sum(grad):
    return jnp.sum(widen(grad), 0)


def pick(tensor, index, axis):
    return lax.dynamic_index_in_dim(tensor, index, axis, keepdims=False)


def swap(tensor, axis, offset):
    count = lax.axis_size(axis)
    return lax.ppermute(tensor, axis, [(i, i ^ offset) for i in range(count)])


def position():
    owner = lax.axis_index("fsdp")
    return owner // 2, owner % 2, lax.axis_index("rep")


def scalars(*values):
    return jnp.stack(values).astype(jnp.int32)


def estimate(microseconds, moved):
    return pl.CostEstimate(flops=1000, bytes_accessed=1000, transcendentals=0)


def params():
    return pltpu.CompilerParams(vmem_limit_bytes=60 * MIB)


def after(tensor, *earlier):
    return lax.optimization_barrier((tensor,) + earlier)[0]


def by_core(own, got, axis):
    core = position()[1]
    return jnp.where(
        core == 0, jnp.stack([own, got], axis), jnp.stack([got, own], axis)
    )


def columns_kernel(blocks, where_ref, *refs):
    ins, (own_ref, other_ref) = refs[:-2], refs[-2:]
    for side in range(2):

        @pl.when(where_ref[1] == side)
        def _():
            for out_ref, parity in ((own_ref, side), (other_ref, 1 - side)):
                start = 0
                for ref, block in zip(ins, blocks):
                    for i in range(parity, ref.shape[2] // block, 2):
                        out_ref[0, :, start : start + block] = ref[0, :, i * block : (i + 1) * block]
                        start += block


def column_pieces(shards):
    plane, core, member = position()
    owners, count = lax.axis_size("fsdp"), lax.axis_size("rep")
    rows = shards[0].shape[1] // count
    blocks = tuple(
        size // owners for size in (shards[0].shape[2] // 3, shards[1].shape[2])
    )
    columns = sum(shard.shape[2] for shard in shards) // 2
    shape = jax.ShapeDtypeStruct((LAYERS, rows, columns), jnp.bfloat16)
    out = pl.BlockSpec((1, rows, columns), lambda layer, where: (layer, 0, 0))
    own, other = pl.pallas_call(
        functools.partial(columns_kernel, blocks),
        out_shape=[shape, shape],
        grid_spec=pltpu.PrefetchScalarGridSpec(
            num_scalar_prefetch=1,
            grid=(LAYERS,),
            in_specs=[
                pl.BlockSpec((1, rows, shard.shape[2]), lambda layer, where: (layer, where[0], 0))
                for shard in shards
            ],
            out_specs=[out, out],
        ),
        compiler_params=params(),
        cost_estimate=estimate(0, 4 * LAYERS * rows * columns * 2),
    )(scalars(member, core), *shards)
    both = by_core(own, swap(other, "fsdp", 1), 1)
    split = shards[0].shape[2] // 2
    both = both.reshape(LAYERS, 2 * rows, columns)
    return both[..., :split], both[..., split:]


def place_kernel(half_rows, blocks, parts, where_ref, *refs):
    count = len(parts)
    pieces, outs, (in_sems, out_sems) = refs[:count], refs[count : -count - 2], refs[-2:]
    held = refs[-count - 2 : -2]
    plane, member = where_ref[0], where_ref[1]
    arrivals = []
    for i in range(count):
        arrivals.append(pltpu.make_async_copy(pieces[i], held[i], in_sems.at[i]))
        arrivals[-1].start()
    copies = []
    for i, (k, halves) in enumerate(parts):
        arrivals[i].wait()
        for j in range(pieces[0].shape[0]):
            for b, (row, rows, column, columns, put) in enumerate(blocks):
                if row // half_rows not in halves:
                    continue
                first = row - halves[0] * half_rows
                copy = pltpu.make_async_copy(
                    held[i].at[j, first : first + rows, column : column + columns],
                    put(outs, j ^ plane, k ^ member),
                    out_sems.at[b, i, j],
                )
                copy.start()
                copies.append(copy)
    for copy in copies:
        copy.wait()


def place(pieces, parts, shapes, blocks):
    plane, core, member = position()
    planes = pieces[0].shape[0]
    outs = pl.pallas_call(
        functools.partial(place_kernel, pieces[0].shape[1] // 2, blocks, parts),
        out_shape=[jax.ShapeDtypeStruct(shape, pieces[0].dtype) for shape in shapes],
        in_specs=[pl.BlockSpec(memory_space=pltpu.SMEM)]
        + [pl.BlockSpec(memory_space=pl.ANY)] * len(pieces),
        out_specs=[pl.BlockSpec(memory_space=pl.ANY)] * len(shapes),
        scratch_shapes=[pltpu.VMEM(piece.shape, piece.dtype) for piece in pieces]
        + [
            pltpu.SemaphoreType.DMA((len(pieces),)),
            pltpu.SemaphoreType.DMA((len(blocks), len(pieces), planes)),
        ],
        compiler_params=params(),
        cost_estimate=estimate(0, 4 * sum(piece.size for piece in pieces)),
    )(scalars(plane, member), *pieces)
    return [out.reshape(-1, out.shape[-1]) for out in outs]


def put_pair(side):
    return lambda outs, plane, member: outs[0].at[plane, side, member]


def place_first(pieces, parts, count, split):
    planes, rows, columns = pieces[0].shape
    half, rest = rows // 2, columns - split

    def put(side):
        return lambda outs, plane, member: outs[1].at[
            plane, member, :, side * rest : (side + 1) * rest
        ]

    shapes = [(planes, 2, count, half, split), (planes, count, half, 2 * rest)]
    blocks = [(side * half, half, 0, split, put_pair(side)) for side in range(2)]
    blocks += [(side * half, half, split, rest, put(side)) for side in range(2)]
    return place(pieces, parts, shapes, blocks)


def place_second(pieces, parts, count):
    planes, rows, columns = pieces[0].shape
    half, fine, width = rows // 2, rows // 4, columns // 2

    def put(side):
        return lambda outs, plane, member: outs[1].at[plane, member, side]

    shapes = [(planes, 2, count, fine, columns), (planes, count, 2, half, width)]
    blocks = [(side * fine, fine, 0, columns, put_pair(side)) for side in range(2)]
    blocks += [(half, half, side * width, width, put(side)) for side in range(2)]
    return place(pieces, parts, shapes, blocks)


def gather_planes(piece, *earlier, beside=()):
    column, sent, step = piece[None], list(earlier), lax.axis_size("fsdp") // 4
    while step:
        got = swap(after(column, *sent[-1:], *(beside if len(sent) > len(earlier) else ())), "fsdp", 2 * step)
        sent.append(got)
        column = jnp.stack([column, got], 1).reshape((-1,) + piece.shape)
        step //= 2
    return column, sent[len(earlier) :]


def gather_neighbours(column, earlier):
    held = {0: [column]}
    for bit in range(lax.axis_size("rep").bit_length() - 1):
        held[1 << bit] = [swap(after(column, *earlier), "rep", 1 << bit)]
    return held, [held[k][0] for k in held if k]


def gather_members(held, beside):
    count, rows = lax.axis_size("rep"), held[0][0].shape[1] // 2
    earlier = [held[k][0] for k in held if k] + list(beside)
    for level in range(1, count.bit_length() - 1):
        sent = []
        for k in range(1, count):
            if bin(k).count("1") != level + 1:
                continue
            held[k] = []
            for half, last in ((0, k & -k), (1, 1 << (k.bit_length() - 1))):
                source = held[k ^ last]
                if len(source) == 1:
                    source = source[0][:, half * rows : (half + 1) * rows]
                else:
                    source = source[half]
                held[k].append(swap(after(source, *earlier), "rep", last))
            sent += held[k]
        earlier = sent
    arrays, parts = [], []
    for k in range(count):
        for half, array in enumerate(held[k]):
            arrays.append(array)
            parts.append((k, (0, 1) if len(held[k]) == 1 else (half,)))
    return arrays, parts, earlier


def message_pieces(shards):
    heads, expand = column_pieces((shards[2], shards[10]))
    pieces = []
    for layer in range(LAYERS):
        output, shrink = quarter(shards[5][layer]), quarter(shards[12][layer])
        half = output.shape[1] // 2
        packed = jnp.concatenate([output[:, :half], output[:, half:]], 0)
        pieces.append(jnp.concatenate([heads[layer], packed], 1))
        half = shrink.shape[0] // 2
        packed = jnp.concatenate([shrink[:half], shrink[half:]], 1)
        pieces.append(jnp.concatenate([expand[layer], packed], 0))
    return pieces


def quarter(param):
    rows = param.shape[0] // lax.axis_size("rep")
    return lax.dynamic_slice_in_dim(param, lax.axis_index("rep") * rows, rows, 0)


def gather_small(all_params, token):
    packed = after(jnp.concatenate([all_params[i] for i in SMALL], 1), token)
    whole, owner, step = packed[None], lax.axis_index("fsdp"), 1
    while step < lax.axis_size("fsdp"):
        got = swap(whole, "fsdp", step)
        whole = jnp.where(
            (owner // step) % 2 == 0,
            jnp.concatenate([whole, got], 0),
            jnp.concatenate([got, whole], 0),
        )
        step *= 2
    vectors, start = [], 0
    for i in SMALL:
        size = all_params[i].shape[1]
        vectors.append(
            jnp.moveaxis(whole[:, :, start : start + size], 0, 1).reshape(LAYERS, -1)
        )
        start += size
    return vectors


def link_orders():
    bits = list(range(lax.axis_size("rep").bit_length() - 1))
    return [bits, bits[::-1]]


def divide(blocks, shapes, bits, outs):
    for side in range(len(shapes)):
        high, later = shapes[side]
        for i in range(high):
            for j in range(later):
                base = 2 * i * later + j
                for out_ref, index in (
                    (outs[2 * side], base + bits[side] * later),
                    (outs[2 * side + 1], base + (1 - bits[side]) * later),
                ):
                    for row, column, block in blocks(side, index):
                        out_ref[
                            0, i, j, row : row + block.shape[0], column : column + block.shape[1]
                        ] = block


def block_grad_kernel(shapes, where_ref, left_ref, grad_ref, more_ref, other_ref, *refs):
    outs, held, extra = refs[:-2], refs[-2], refs[-1]
    held[...] = low(weight_dot(left_ref[...], grad_ref[...])).reshape(held.shape)
    extra[...] = low(weight_dot(more_ref[...], other_ref[...])).reshape(extra.shape)
    rows, half, tall = held.shape[2], held.shape[3] // 2, extra.shape[1] // 2

    def blocks(side, index):
        return [
            (p * rows, 0, held[p, index, :, side * half : (side + 1) * half]) for p in range(2)
        ] + [(2 * rows, 0, extra[index, side * tall : (side + 1) * tall])]

    divide(blocks, shapes, (where_ref[0], where_ref[1]), outs)


def mixed_grad_kernel(shapes, where_ref, left_ref, grad_ref, more_ref, other_ref, *refs):
    outs, held, extra = refs[:4], refs[4], refs[5]
    held[...] = low(weight_dot(left_ref[...], grad_ref[...])).reshape(held.shape)
    extra[...] = low(weight_dot(more_ref[...], other_ref[...])).reshape(extra.shape)
    rows, rest = held.shape[2], extra.shape[2] // 2
    half = (held.shape[3] + rest) // 2

    def blocks(side, index):
        if side == 0:
            return [(p * rows, 0, held[p, index, :, :half]) for p in range(2)]
        return [(p * rows, 0, held[p, index, :, half:]) for p in range(2)] + [
            (p * rows, half - rest, extra[index, :, p * rest : (p + 1) * rest]) for p in range(2)
        ]

    divide(blocks, shapes, (where_ref[0], where_ref[1]), outs)


def grad_call(kernel, arrays, widths, rows, columns, scratch, orders):
    planes, count = lax.axis_size("fsdp") // 2, lax.axis_size("rep")
    member = lax.axis_index("rep")
    shapes = tuple((count >> (order[0] + 1), 1 << order[0]) for order in orders)
    tokens = arrays[0].shape[0]
    specs = []
    for array, width in zip(arrays, widths):
        if width is None:
            specs.append(pl.BlockSpec(array.shape, lambda z, where: (0, 0)))
        else:
            specs.append(pl.BlockSpec((tokens, width), lambda z, where: (0, z)))
    out_shapes, out_specs = [], []
    for high, later in shapes:
        block = (high, later, rows, columns // len(orders))
        out_specs += [pl.BlockSpec((1,) + block, lambda z, where: (z, 0, 0, 0, 0))] * 2
        out_shapes += [jax.ShapeDtypeStruct((planes,) + block, jnp.bfloat16)] * 2
    return pl.pallas_call(
        functools.partial(kernel, shapes),
        out_shape=out_shapes,
        grid_spec=pltpu.PrefetchScalarGridSpec(
            num_scalar_prefetch=1,
            grid=(planes,),
            in_specs=specs,
            out_specs=out_specs,
            scratch_shapes=[pltpu.VMEM(size, jnp.bfloat16) for size in scratch],
        ),
        compiler_params=params(),
        cost_estimate=estimate(5, 0),
    )(scalars(*[(member >> order[0]) & 1 for order in orders]), *arrays)


def block_grad(left, grad, more, other, orders):
    planes, count = lax.axis_size("fsdp") // 2, lax.axis_size("rep")
    widths = left.shape[1] // planes, more.shape[1] // planes
    columns = grad.shape[1]
    rows, tall = widths[0] // (2 * count), widths[1] // count
    return grad_call(
        block_grad_kernel, (left, grad, more, other), (widths[0], None, widths[1], None),
        2 * rows + tall // 2, columns,
        [(2, count, rows, columns), (count, tall, other.shape[1])], orders,
    )


def mixed_grad(left, grad, more, other, orders):
    planes, count = lax.axis_size("fsdp") // 2, lax.axis_size("rep")
    widths = left.shape[1] // planes, more.shape[1] // planes
    columns, rest = grad.shape[1], other.shape[1]
    rows = widths[1] // count
    if widths[1] % 128:
        first = low(weight_dot(left, grad)).reshape(planes, 2, count, rows, columns)
        second = low(weight_dot(more, other)).reshape(planes, count, rows, 2, rest // 2)
        total = jnp.concatenate([jnp.swapaxes(first, 1, 2), jnp.swapaxes(second, 2, 3)], 4)
        total = total.reshape(planes, count, 2 * rows, -1)
        half, member = total.shape[3] // 2, lax.axis_index("rep")
        top = count // 2
        left_part = total[..., :half].reshape(planes, top, 2, 1, 2 * rows, half)
        right_part = total[..., half:].reshape(planes, 1, 2, top, 2 * rows, half)
        sides = member % 2, member // top
        return [
            pick(part, side if kept else 1 - side, 2)
            for part, side in zip((left_part, right_part), sides)
            for kept in (True, False)
        ]
    return grad_call(
        mixed_grad_kernel, (left, grad, more, other), (widths[0], None, widths[1], None),
        2 * rows, columns + rest // 2,
        [(2, count, rows, columns), (count, rows, rest)], orders,
    )


def split_kernel(where_ref, *refs):
    count = len(refs) // 4
    for n in range(count):
        bit = where_ref[n]
        keep_in, got_ref = refs[2 * n], refs[2 * n + 1]
        keep_ref, send_ref = refs[2 * (count + n)], refs[2 * (count + n) + 1]
        keep_ref[0] = low(widen(keep_in[0, bit]) + widen(got_ref[0, bit]))
        send_ref[0] = low(widen(keep_in[0, 1 - bit]) + widen(got_ref[0, 1 - bit]))


def add_split(pairs, later, sides, rows):
    if len({pair[0].size // n for pair, n in zip(pairs, later)}) > 1:
        return [
            out
            for pair, n, side in zip(pairs, later, sides)
            for out in add_split([pair], [n], [side], rows)
        ]
    arrays, in_specs, out_specs, out_shapes = [], [], [], []
    for pair, n in zip(pairs, later):
        columns = pair[0].shape[-1]
        for array in pair:
            arrays.append(array.reshape(-1, 2, n, rows, columns))
            in_specs.append(
                pl.BlockSpec((1, 2, n, rows, columns), lambda i, where: (i, 0, 0, 0, 0))
            )
            out_specs.append(pl.BlockSpec((1, n, rows, columns), lambda i, where: (i, 0, 0, 0)))
            out_shapes.append(
                jax.ShapeDtypeStruct((arrays[-1].shape[0], n, rows, columns), jnp.bfloat16)
            )
    return pl.pallas_call(
        split_kernel,
        out_shape=out_shapes,
        grid_spec=pltpu.PrefetchScalarGridSpec(
            num_scalar_prefetch=1,
            grid=(arrays[0].shape[0],),
            in_specs=in_specs,
            out_specs=out_specs,
        ),
        compiler_params=params(),
        cost_estimate=estimate(0, sum(array.size for array in arrays) * 3),
    )(scalars(*sides), *arrays)


def merge_kernel(where_ref, *refs):
    arrays, (keep_ref, send_ref) = refs[:-2], refs[-2:]
    half = arrays[0].shape[-1]
    for out_ref, bit in ((keep_ref, where_ref[0]), (send_ref, 1 - where_ref[0])):
        start = 0
        for n in range(0, len(arrays), 4):
            left_ref, left_got, right_ref, right_got = arrays[n : n + 4]
            rows = slice(start, start + left_ref.shape[2])
            out_ref[0, rows, :half] = low(widen(left_ref[0, bit]) + widen(left_got[0, bit]))
            out_ref[0, rows, half:] = low(widen(right_ref[0, bit]) + widen(right_got[0, bit]))
            start += left_ref.shape[2]


def add_merge(messages, side):
    half = messages[0][0].shape[-1]
    arrays, specs, total = [], [], 0
    for message in messages:
        rows = message[0].shape[-2]
        arrays += [array.reshape(-1, 2, rows, half) for array in message]
        specs += [pl.BlockSpec((1, 2, rows, half), lambda i, where: (i, 0, 0, 0))] * 4
        total += rows
    high = arrays[0].shape[0]
    given = pl.BlockSpec((1, total, 2 * half), lambda i, where: (i, 0, 0))
    shape = jax.ShapeDtypeStruct((high, total, 2 * half), jnp.bfloat16)
    return pl.pallas_call(
        merge_kernel,
        out_shape=[shape, shape],
        grid_spec=pltpu.PrefetchScalarGridSpec(
            num_scalar_prefetch=1,
            grid=(high,),
            in_specs=specs,
            out_specs=[given, given],
        ),
        compiler_params=params(),
        cost_estimate=estimate(0, sum(array.size for array in arrays) * 3),
    )(scalars(side), *arrays)


def reduce_members(arrays):
    member, lanes = lax.axis_index("rep"), range(2)
    rows, orders = arrays[0].shape[-2], link_orders()
    bits = [sorted(order) for order in orders]
    keeps, sends = list(arrays[::2]), list(arrays[1::2])
    for n in range(len(orders[0])):
        gots = [swap(sends[i], "rep", 1 << orders[i][n]) for i in lanes]
        for i in lanes:
            bits[i].remove(orders[i][n])
        token = yield sends, gots
        gots = [after(got, token) for got in gots]
        if n + 1 < len(orders[0]):
            later = [1 << bits[i].index(orders[i][n + 1]) for i in lanes]
            sides = [(member >> orders[i][n + 1]) & 1 for i in lanes]
            outs = add_split(list(zip(keeps, gots)), later, sides, rows)
            keeps, sends = list(outs[::2]), list(outs[1::2])
    return [keeps[0], gots[0], keeps[1], gots[1]]


def reduce_planes(messages):
    plane, planes = position()[0], lax.axis_size("fsdp") // 2
    rows = sum(message[0].shape[-2] for message in messages)
    keep, send = add_merge(messages, plane % 2)
    step = 1
    while True:
        got = swap(send, "fsdp", 2 * step)
        token = yield [send], [got]
        got = after(got, token)
        step *= 2
        if step == planes:
            return low(widen(keep) + widen(got)).reshape(rows, -1)
        keep, send = add_split([(keep, got)], [1], [(plane // step) % 2], rows)


def finish_columns(total, columns):
    core = position()[1]
    rows = total.shape[0] // 2
    part = total[:, :columns].reshape(2, rows, columns)
    got = swap(pick(part, 1 - core, 0), "fsdp", 1)
    part = jnp.concatenate([pick(part, core, 0), got], 0)
    return jnp.concatenate([part, total[:, columns:]], 1)


def spread(own, low_last):
    pieces = [own]
    for k in range(1, lax.axis_size("rep")):
        last = k & -k if low_last else 1 << (k.bit_length() - 1)
        pieces.append(swap(pieces[k ^ last], "rep", last))
    return pieces


def column_out(out_ref, block, side, ref, start):
    rows = out_ref.shape[2]
    for i in range(out_ref.shape[3] // block):
        first = start if i % 2 == side else start + rows
        out_ref[0, 0, :, i * block : (i + 1) * block] = widen(
            ref[first : first + rows, (i // 2) * block : (i // 2 + 1) * block]
        )


def early_out_kernel(block, where_ref, *refs):
    expand_out, shrink_out = refs[-2:]
    for k, ref in enumerate(refs[:-4]):
        for side in range(2):

            @pl.when((pl.program_id(0) == k) & (where_ref[1] == side))
            def _():
                column_out(expand_out, block, side, ref, 0)

        @pl.when(pl.program_id(0) == k)
        def _():
            rows, columns = shrink_out.shape[2] // 2, shrink_out.shape[3]
            start = ref.shape[0] - rows
            shrink_out[0, 0, :rows] = widen(ref[start:, :columns])
            shrink_out[0, 0, rows:] = widen(ref[start:, columns:])


def late_out_kernel(block, where_ref, *refs):
    heads_out, output_out = refs[-2:]
    for k, ref in enumerate(refs[:-4]):
        for side in range(2):

            @pl.when((pl.program_id(0) == k) & (where_ref[1] == side))
            def _():
                column_out(heads_out, block, side, ref, 0)

        @pl.when(pl.program_id(0) == k)
        def _():
            rows, half = output_out.shape[2], output_out.shape[3] // 2
            start = ref.shape[1] - half
            output_out[0, 0, :, :half] = widen(ref[:rows, start:])
            output_out[0, 0, :, half:] = widen(ref[rows:, start:])


def write_out(kernel, layer, pieces, sizes, earlier):
    plane, core, member = position()
    count = len(pieces)
    shapes = [(LAYERS, count) + size for size in sizes]
    if earlier is None:
        earlier = [jnp.zeros((8, 128), jnp.float32)] * len(sizes)
        aliases = {}
    else:
        earlier = [array.reshape(shape) for array, shape in zip(earlier, shapes)]
        aliases = {1 + count + i: i for i in range(len(sizes))}
    return pl.pallas_call(
        kernel,
        out_shape=[jax.ShapeDtypeStruct(shape, jnp.float32) for shape in shapes],
        grid_spec=pltpu.PrefetchScalarGridSpec(
            num_scalar_prefetch=1,
            grid=(count,),
            in_specs=[pl.BlockSpec(piece.shape, lambda k, where: (0, 0)) for piece in pieces]
            + [pl.BlockSpec(memory_space=pl.ANY)] * len(sizes),
            out_specs=[
                pl.BlockSpec((1, 1) + size, lambda k, where: (layer, k ^ where[0], 0, 0))
                for size in sizes
            ],
        ),
        input_output_aliases=aliases,
        compiler_params=params(),
        cost_estimate=estimate(0, count * pieces[0].size * 6),
    )(scalars(member, core), *pieces, *earlier)


def reduce_small(grads):
    owners, count = lax.axis_size("fsdp"), lax.axis_size("rep")
    total = jnp.concatenate([g.reshape(LAYERS, owners, -1) for g in grads], 2)
    owner = lax.axis_index("fsdp")
    step = owners // 2
    while step:
        total = total.reshape(LAYERS, 2, step, -1)
        mine = (owner // step) % 2
        total = pick(total, mine, 1) + swap(pick(total, 1 - mine, 1), "fsdp", step)
        step //= 2
    step = 1
    while step < count:
        total = total + swap(total, "rep", step)
        step *= 2
    total = total.reshape(LAYERS, -1)
    outs, start = [], 0
    for g in grads:
        size = g.shape[1] // owners
        outs.append(total[:, start : start + size])
        start += size
    return outs


def other_half(rows):
    return swap(rows, "fsdp", lax.axis_size("fsdp") // 2)


def image_side():
    return lax.axis_index("fsdp") // (lax.axis_size("fsdp") // 2)


def regroup(blocks):
    side = image_side()
    return pick(blocks, side, 0), other_half(pick(blocks, 1 - side, 0))


def ungroup(rows, got):
    own, got = rows[: rows.shape[0] // 2], got.astype(rows.dtype)
    return jnp.where(image_side() == 0, jnp.stack([own, got]), jnp.stack([got, own]))


def chips_per_image():
    return lax.axis_size("fsdp") // 4


def share_rows(local_kv):
    shared = [local_kv]
    for k in range(1, chips_per_image()):
        low_bit = k & -k
        shared.append(swap(shared[k ^ low_bit], "fsdp", 2 * low_bit))
    return shared


def collect_rows(own, others):
    chips = chips_per_image()
    if chips == 2:
        got = swap(others, "fsdp", 2)
        return low(widen(own) + widen(got)), got
    total = jnp.concatenate([own, others], 1)
    while chips > 1:
        rows = total.shape[1] // 2
        got = swap(total[:, rows:], "fsdp", chips)
        total = low(widen(total[:, :rows]) + widen(got))
        chips //= 2
    return total, got


def both_cores(rows):
    return jnp.concatenate([rows, swap(rows, "fsdp", 1)], 0)


def one_head(tensor, head):
    half = tensor.shape[1] // 2
    lane = lax.broadcasted_iota(jnp.int32, tensor.shape, 1)
    keep = lane < half if head == 0 else lane >= half
    return jnp.where(keep, tensor, jnp.zeros_like(tensor))


def join(refs, held):
    start = 0
    for ref in refs:
        held[start : start + ref.shape[0], :] = ref[...]
        start += ref.shape[0]
    return held[...]


def attend_kernel(factor, parts, query_ref, *refs):
    out_ref, log_ref, held_keys, held_values = refs[2 * parts :]
    keys, values = join(refs[:parts], held_keys), join(refs[parts : 2 * parts], held_values)
    results, logs = [], []
    for head in range(2):
        scores = input_dot(one_head(query_ref[...], head), keys)
        largest = jnp.max(scores, -1, keepdims=True)
        weights = jnp.exp2((scores - largest) * factor)
        total = jnp.sum(weights, -1, keepdims=True)
        results.append(forward_dot(low(weights), values) / total)
        logs.append(largest * factor + jnp.log2(total))
    out_ref[...] = low(one_head(results[0], 0) + one_head(results[1], 1))
    shape = log_ref.shape
    log_ref[...] = one_head(jnp.broadcast_to(logs[0], shape), 0) + one_head(
        jnp.broadcast_to(logs[1], shape), 1
    )


def pair_block(rows, start):
    return pl.BlockSpec((rows, 128), lambda i: (0, start + i))


def kv_parts(projected, others):
    pairs = projected.shape[1] // 384
    if projected.shape[0] % 16:
        others = [jnp.concatenate([projected[:, 128 * pairs :]] + others, 0)]
        parts = []
    else:
        parts = [(projected, pairs, 2 * pairs)]
    return parts + [(other, 0, pairs) for other in others]


def kv_specs(parts, first=0):
    keys = [pair_block(array.shape[0], first + start) for array, start, unused in parts]
    values = [pair_block(array.shape[0], first + start) for array, unused, start in parts]
    rows = sum(array.shape[0] for array, unused, more in parts)
    held = [pltpu.VMEM((rows, 128), jnp.bfloat16)] * 2
    return keys + values, [array for array, unused, more in parts] * 2, held


def attend(projected, others, head_size):
    tokens, width = projected.shape[0], projected.shape[1] // 3
    pairs = width // 128
    parts = kv_parts(projected, others)
    specs, arrays, held = kv_specs(parts)
    factor = head_size ** (-0.5) * math.log2(math.e)
    return pl.pallas_call(
        functools.partial(attend_kernel, factor, len(parts)),
        out_shape=[
            jax.ShapeDtypeStruct((tokens, width), jnp.bfloat16),
            jax.ShapeDtypeStruct((tokens, width), jnp.float32),
        ],
        grid=(pairs,),
        in_specs=[pair_block(tokens, 0)] + specs,
        out_specs=[pair_block(tokens, 0), pair_block(tokens, 0)],
        scratch_shapes=held,
        compiler_params=params(),
        cost_estimate=estimate(18, 0),
    )(projected, *arrays)


def attend_back_kernel(factor, scale, parts, query_ref, *refs):
    log_ref, grad_ref, dq_ref, own_ref, others_ref, held_keys, held_values = refs[2 * parts :]
    keys, values = join(refs[:parts], held_keys), join(refs[parts : 2 * parts], held_values)
    d_query, d_key, d_value = [], 0.0, 0.0
    for head in range(2):
        query = one_head(query_ref[...], head)
        grad = one_head(grad_ref[...], head)
        half = query.shape[1] // 2
        log_total = log_ref[:, head * half : head * half + 1]
        probs = jnp.exp2(input_dot(query, keys) * factor - log_total)
        products = probs * input_dot(grad, values)
        d_scores = low(products - probs * jnp.sum(products, -1, keepdims=True))
        d_query.append(forward_dot(d_scores, keys))
        d_key = d_key + weight_dot(d_scores, query)
        d_value = d_value + weight_dot(low(probs), grad)
    dq_ref[...] = low((one_head(d_query[0], 0) + one_head(d_query[1], 1)) * scale)
    rows = own_ref.shape[1]
    for i, total in enumerate((low(d_key * scale), low(d_value))):
        own_ref[i] = total[:rows]
        others_ref[i] = total[rows:]


def attend_back(projected, others, log_total, d_attended, head_size, first, pairs):
    tokens, width = d_attended.shape[0], 128 * pairs
    parts = kv_parts(projected, others)
    specs, arrays, held = kv_specs(parts, first)
    rows = held[0].shape[0]
    scale = head_size ** (-0.5)
    own, taken = pair_block(tokens, 0), pair_block(tokens, first)
    return pl.pallas_call(
        functools.partial(attend_back_kernel, scale * math.log2(math.e), scale, len(parts)),
        out_shape=[
            jax.ShapeDtypeStruct((tokens, width), jnp.bfloat16),
            jax.ShapeDtypeStruct((2, tokens, width), jnp.bfloat16),
            jax.ShapeDtypeStruct((2, rows - tokens, width), jnp.bfloat16),
        ],
        grid=(pairs,),
        in_specs=[taken] + specs + [taken, taken],
        out_specs=[
            own,
            pl.BlockSpec((2, tokens, 128), lambda i: (0, 0, i)),
            pl.BlockSpec((2, rows - tokens, 128), lambda i: (0, 0, i)),
        ],
        scratch_shapes=held,
        compiler_params=params(),
        cost_estimate=estimate(8 * pairs, 0),
    )(projected, *arrays, log_total, d_attended)


def add_tile(part, own_ref, other_ref, total_ref):
    @pl.when(pl.program_id(0) == 0)
    def _():
        total_ref[...] = part

    @pl.when(pl.program_id(0) > 0)
    def _():
        total_ref[...] += part

    @pl.when(pl.program_id(0) == pl.num_programs(0) - 1)
    def _():
        half = own_ref.shape[0]
        own_ref[...] = total_ref[:half]
        other_ref[...] = low(total_ref[half:])


def expand_kernel(
    rows_ref, expand_ref, bias_ref, shrink_ref, active_ref, slope_ref, own_ref, other_ref, total_ref
):
    hidden = forward_dot(rows_ref[...], expand_ref[...]) + bias_ref[...]
    normal = 0.5 + 0.5 * lax.erf(hidden * math.sqrt(0.5))
    density = jnp.exp2(hidden * hidden * (-0.5 * math.log2(math.e)))
    slope_ref[...] = low(normal + hidden * density * (1.0 / math.sqrt(2.0 * math.pi)))
    active = low(hidden * normal)
    active_ref[...] = active
    add_tile(forward_dot(active, shrink_ref[...]), own_ref, other_ref, total_ref)


def feed_forward(rows_in, expand, expand_bias, shrink):
    tokens, width = rows_in.shape
    units = expand.shape[1]
    tile = 512
    whole = pl.BlockSpec((tokens, width), lambda i: (0, 0))
    half = pl.BlockSpec((tokens // 2, width), lambda i: (0, 0))
    part = pl.BlockSpec((tokens, tile), lambda i: (0, i))
    return pl.pallas_call(
        expand_kernel,
        out_shape=[
            jax.ShapeDtypeStruct((tokens, units), jnp.bfloat16),
            jax.ShapeDtypeStruct((tokens, units), jnp.bfloat16),
            jax.ShapeDtypeStruct((tokens // 2, width), jnp.float32),
            jax.ShapeDtypeStruct((tokens // 2, width), jnp.bfloat16),
        ],
        grid=(units // tile,),
        in_specs=[
            whole,
            pl.BlockSpec((width, tile), lambda i: (0, i)),
            pl.BlockSpec((1, tile), lambda i: (0, i)),
            pl.BlockSpec((tile, width), lambda i: (i, 0)),
        ],
        out_specs=[part, part, half, half],
        scratch_shapes=[pltpu.VMEM((tokens, width), jnp.float32)],
        compiler_params=params(),
        cost_estimate=estimate(14, 0),
    )(rows_in, expand, expand_bias[None], shrink)


def shrink_kernel(
    grad_ref, shrink_ref, slope_ref, expand_ref, hidden_ref, bias_ref, own_ref, other_ref, total_ref
):
    d_hidden = low(input_dot(grad_ref[...], shrink_ref[...]) * widen(slope_ref[...]))
    hidden_ref[...] = d_hidden
    bias_ref[...] = jnp.sum(widen(d_hidden), 0, keepdims=True)
    add_tile(input_dot(d_hidden, expand_ref[...]), own_ref, other_ref, total_ref)


def feed_back(d_mlp, shrink, slope, expand):
    tokens, width = d_mlp.shape
    units = expand.shape[1]
    tile = 512
    whole = pl.BlockSpec((tokens, width), lambda i: (0, 0))
    half = pl.BlockSpec((tokens // 2, width), lambda i: (0, 0))
    part = pl.BlockSpec((tokens, tile), lambda i: (0, i))
    return pl.pallas_call(
        shrink_kernel,
        out_shape=[
            jax.ShapeDtypeStruct((tokens, units), jnp.bfloat16),
            jax.ShapeDtypeStruct((1, units), jnp.float32),
            jax.ShapeDtypeStruct((tokens // 2, width), jnp.float32),
            jax.ShapeDtypeStruct((tokens // 2, width), jnp.bfloat16),
        ],
        grid=(units // tile,),
        in_specs=[
            whole,
            pl.BlockSpec((tile, width), lambda i: (i, 0)),
            part,
            pl.BlockSpec((width, tile), lambda i: (0, i)),
        ],
        out_specs=[part, pl.BlockSpec((1, tile), lambda i: (0, i)), half, half],
        scratch_shapes=[pltpu.VMEM((tokens, width), jnp.float32)],
        compiler_params=params(),
        cost_estimate=estimate(9, 0),
    )(d_mlp, shrink, slope, expand)


def core_half(vector):
    core = position()[1]
    return pick(widen(vector).reshape(lax.axis_size("fsdp") // 2, 2, -1), core, 1).reshape(-1)


def core_fill(half):
    parts = half.reshape(lax.axis_size("fsdp") // 2, -1)
    return by_core(parts, jnp.zeros_like(parts), 1).reshape(-1)


def normed_rows(tok_rows, gathered):
    return both_cores(low(layer_norm(tok_rows, widen(gathered[0]), widen(gathered[1]))))


def project(normed, gathered, token):
    heads_weight, query_bias, value_bias = gathered[2], gathered[3], gathered[4]
    width = normed.shape[1]
    bias_row = jnp.concatenate(
        [core_half(query_bias), jnp.zeros((width // 2,), jnp.float32), core_half(value_bias)]
    )
    projected = low(forward_dot(normed, heads_weight) + bias_row)
    return projected, share_rows(after(projected[:, width // 2 :], token))[1:]


def forward_layer(tok_rows, normed, projected, others, gathered, beside, neighbours, planes):
    (
        attn_norm_gain,
        attn_norm_bias,
        heads_weight,
        query_bias,
        value_bias,
        output_weight,
        output_bias,
        attn_layerscale,
        mlp_norm_gain,
        mlp_norm_bias,
        expand_weight,
        expand_bias,
        shrink_weight,
        shrink_bias,
        mlp_layerscale,
    ) = gathered
    tokens, width = tok_rows.shape
    attended, log_total = attend(projected, others, width // HEADS)
    attended = after(attended, *beside)
    got = swap(low(forward_dot(attended[tokens:], output_weight)), "fsdp", 1)
    branch = forward_dot(attended[:tokens], output_weight) + widen(got) + widen(output_bias)
    middle = tok_rows + widen(attn_layerscale) * branch
    normed_two = low(layer_norm(middle, widen(mlp_norm_gain), widen(mlp_norm_bias)))
    normed_two = both_cores(after(normed_two, *planes[:1]))
    activated, slope, own_sum, other_sum = feed_forward(
        normed_two, expand_weight, core_half(expand_bias), shrink_weight
    )
    other_sum = after(other_sum, *neighbours, *planes[1:])
    mlp_out = own_sum + widen(swap(other_sum, "fsdp", 1)) + widen(shrink_bias)
    result = middle + widen(mlp_layerscale) * mlp_out
    saved = (
        tok_rows,
        normed,
        projected,
        others,
        log_total,
        attended,
        branch,
        middle,
        normed_two,
        slope,
        activated,
        mlp_out,
    )
    return (result, saved)


class Later:
    def __init__(self):
        self.running, self.done, self.sends, self.gots = {}, {}, {}, {}

    def begin(self, name, kernel, arrays):
        self.running[name] = reduce_members(kernel(*arrays, link_orders()))
        self.step(name, None)

    def join(self, name, parts, token):
        for part in parts:
            while part in self.running:
                self.step(part, token)
        self.running[name] = reduce_planes([self.done[part] for part in parts])
        self.step(name, None)

    def step(self, name, token):
        try:
            self.sends[name], self.gots[name] = self.running[name].send(token)
        except StopIteration as end:
            self.done[name] = end.value
            self.sends[name] = self.gots[name] = []
            del self.running[name]

    def sent(self, value, *names):
        return after(value, *[array for name in names for array in self.sends[name]])

    def came(self, value, *names):
        return after(value, *[array for name in names for array in self.gots[name]])


def backward_layer(d_result, saved, gathered, later, new, old, activation_got):
    (
        attn_norm_gain,
        attn_norm_bias,
        heads_weight,
        query_bias,
        value_bias,
        output_weight,
        output_bias,
        attn_layerscale,
        mlp_norm_gain,
        mlp_norm_bias,
        expand_weight,
        expand_bias,
        shrink_weight,
        shrink_bias,
        mlp_layerscale,
    ) = gathered
    (
        tok_rows,
        normed,
        projected,
        others,
        log_total,
        attended,
        branch,
        middle,
        normed_two,
        slope,
        activated,
        mlp_out,
    ) = saved
    tokens, width = tok_rows.shape
    d_mlp = low(d_result * widen(mlp_layerscale))
    d_mlp_both = both_cores(d_mlp)
    g_mlp_scale = jnp.sum(d_result * mlp_out, 0)
    g_shrink_bias = column_sum(d_mlp)
    d_hidden, g_expand_bias, own_sum, other_sum = feed_back(
        d_mlp_both, shrink_weight, slope, expand_weight
    )
    block, mixed, block_planes, mixed_planes = new
    if old:
        other_sum = later.came(other_sum, old[0])
        later.join(old[2], [old[0]], other_sum)
        d_hidden = later.sent(d_hidden, old[2])
    got = swap(other_sum, "fsdp", 1)
    later.begin(block, block_grad, (normed_two, d_hidden, activated, d_mlp_both))
    own_sum = later.sent(own_sum, block)
    if old:
        own_sum = later.came(own_sum, old[1])
        later.step(old[1], own_sum)
        own_sum = later.sent(own_sum, old[1])
    d_middle_norm, g_mlp_gain, g_mlp_shift = norm_back(
        middle, widen(mlp_norm_gain), widen(mlp_norm_bias), own_sum + widen(got)
    )
    d_middle = d_result + d_middle_norm
    d_branch = low(d_middle * widen(attn_layerscale))
    d_branch_both = both_cores(d_branch)
    g_attn_scale = jnp.sum(d_middle * branch, 0)
    g_output_bias = column_sum(d_branch)
    d_attended = low(input_dot(d_branch_both, output_weight))
    pairs = d_attended.shape[1] // 128

    def back(first):
        return attend_back(
            projected, others, log_total, d_attended, width // HEADS, first, pairs // 2
        )

    first_query, d_own, d_others = back(0)
    first_kv, first_got = collect_rows(d_own, d_others)
    if old:
        d_attended = later.came(d_attended, old[1], old[2])
        later.join(old[3], [old[1]], first_query)
        later.step(old[2], first_query)
        d_attended = later.sent(d_attended, old[3], old[2])
    else:
        d_attended = after(d_attended, activation_got)
    second_query, d_own, d_others = back(pairs // 2)
    d_others = after(d_others, first_got)
    second_kv, second_got = collect_rows(d_own, d_others)
    second_query = later.came(second_query, block)
    later.step(block, second_query)
    second_query = later.sent(second_query, block)
    if old:
        later.step(old[3], second_query)
    d_query = jnp.concatenate([first_query, second_query], 1)
    d_key = jnp.concatenate([first_kv[0], second_kv[0]], 1)
    d_value = jnp.concatenate([first_kv[1], second_kv[1]], 1)
    d_projected = jnp.concatenate([d_query, d_key, d_value], 1)
    g_query_bias = column_sum(d_query)
    g_value_bias = column_sum(d_value)
    got = swap(low(input_dot(d_projected[tokens:], heads_weight)), "fsdp", 1)
    later.begin(mixed, mixed_grad, (normed, d_projected, attended, d_branch_both))
    d_projected = later.sent(d_projected, mixed)
    if old:
        later.join(block_planes, [block], d_projected)
        d_projected = later.sent(d_projected, block_planes)
    d_normed = input_dot(d_projected[:tokens], heads_weight) + widen(got)
    d_rows_norm, g_attn_gain, g_attn_shift = norm_back(
        tok_rows, widen(attn_norm_gain), widen(attn_norm_bias), d_normed
    )
    d_rows = d_middle + d_rows_norm
    small_grads = (
        g_attn_gain,
        g_attn_shift,
        core_fill(g_query_bias),
        core_fill(g_value_bias),
        g_output_bias,
        g_attn_scale,
        g_mlp_gain,
        g_mlp_shift,
        core_fill(g_expand_bias),
        g_shrink_bias,
        g_mlp_scale,
    )
    return (d_rows, small_grads)


def local(images, cotangent, *all_params):
    owners, count = lax.axis_size("fsdp"), lax.axis_size("rep")
    pieces = message_pieces(all_params)
    column, planes = gather_planes(pieces[0])
    own, got = regroup(after(images, planes[0]))
    tok_rows = widen(jnp.concatenate([own, got], 0))
    column = after(column, got)
    next_column, next_planes = gather_planes(pieces[1], got)
    small = gather_small(all_params, got)
    held, neighbours = gather_neighbours(column, [])
    saved_layers, fetched = [], []
    for layer in range(LAYERS):
        gathered = [None] * len(all_params)
        for i, vector in zip(SMALL, small):
            gathered[i] = vector[layer]
        normed = normed_rows(tok_rows, gathered)
        arrays, parts, earlier = gather_members(held, [])
        arrays[0] = after(arrays[0], next_planes[-1])
        gathered[2], gathered[5] = place_first(
            arrays, parts, count, all_params[2].shape[2] // 2
        )
        projected, others = project(normed, gathered, next_planes[-1])
        held, neighbours = gather_neighbours(next_column, earlier)
        if layer + 1 < LAYERS:
            column, planes = gather_planes(pieces[2 * layer + 2], others[-1])
            beside = planes[:1]
        else:
            own, got = regroup(after(cotangent, others[-1]))
            d_rows = widen(jnp.concatenate([own, got], 0))
            beside, planes, neighbours, next_planes = [got], [], [], []
        arrays, parts, earlier = gather_members(held, [])
        arrays[0] = after(arrays[0], *planes[-1:])
        if layer + 1 < LAYERS:
            next_column, next_planes = gather_planes(pieces[2 * layer + 3], planes[-1])
            held, neighbours = gather_neighbours(column, earlier)
        gathered[10], gathered[12] = place_second(arrays, parts, count)
        fetched.append(tuple(gathered))
        tok_rows, saved = forward_layer(
            tok_rows, normed, projected, others, gathered, beside, neighbours, next_planes
        )
        saved_layers.append(saved)
    activation_rows = low(tok_rows)
    small_grads = [None] * LAYERS
    outs = {}

    def size(i):
        return (all_params[i].shape[1] // count, all_params[i].shape[2])

    def block_piece(later, layer):
        total = later.done[layer, 2]
        half = total.shape[0] // 2
        return jnp.concatenate([finish_columns(total[:half], total.shape[1]), total[half:]], 0)

    def mixed_piece(later, layer):
        return finish_columns(later.done[layer, 3], size(2)[1] // 2)

    def write_block(layer, pieces):
        outs["block"] = write_out(
            functools.partial(early_out_kernel, size(10)[1] // owners),
            layer, pieces, [size(10), size(12)], outs.get("block"),
        )

    def write_mixed(layer, pieces):
        outs["mixed"] = write_out(
            functools.partial(late_out_kernel, size(2)[1] // 3 // owners),
            layer, pieces, [size(2), size(5)], outs.get("mixed"),
        )

    later = Later()
    for layer in reversed(range(LAYERS)):
        new = [(layer, n) for n in range(4)]
        old = [(layer + 1, n) for n in range(4)] if layer + 1 < LAYERS else None
        if not old:
            activation_got = other_half(activation_rows[activation_rows.shape[0] // 2 :])
        d_rows, small_grads[layer] = backward_layer(
            d_rows, saved_layers[layer], fetched[layer], later, new, old, activation_got
        )
    activations = ungroup(activation_rows, activation_got)
    image_got = other_half(low(d_rows[d_rows.shape[0] // 2 :]))
    d_images = ungroup(d_rows, image_got)
    for name in (old[2], old[3]):
        while name in later.running:
            later.step(name, d_rows)
    first = block_piece(later, layer + 1)
    rows = first.shape[0]
    first = after(jnp.concatenate([first, mixed_piece(later, layer + 1)], 0), d_rows)
    later.step(new[1], d_rows)
    pieces = spread(later.sent(first, new[1]), True)
    write_block(layer + 1, [piece[:rows] for piece in pieces])
    write_mixed(layer + 1, [piece[rows:] for piece in pieces])
    later.join(new[3], [new[1]], d_rows)
    for name in (new[3], new[2]):
        while name in later.running:
            later.step(name, image_got)
    write_block(layer, spread(block_piece(later, layer), False))
    write_mixed(layer, spread(mixed_piece(later, layer), False))
    stacked = [None] * len(all_params)
    for i, out in zip((10, 12, 2, 5), list(outs["block"]) + list(outs["mixed"])):
        stacked[i] = out.reshape(all_params[i].shape)
    reduced = reduce_small(
        [jnp.stack([grads[n] for grads in small_grads]) for n in range(len(SMALL))]
    )
    for i, vector in zip(SMALL, reduced):
        stacked[i] = vector
    return (activations, d_images) + tuple(stacked)


def solution(mesh):
    in_specs = (
        P("rep", "fsdp", None),
        P("rep", "fsdp", None),
        P(None, "fsdp"),
        P(None, "fsdp"),
        P(None, "fsdp", None),
        P(None, "fsdp"),
        P(None, "fsdp"),
        P(None, "fsdp", None),
        P(None, "fsdp"),
        P(None, "fsdp"),
        P(None, "fsdp"),
        P(None, "fsdp"),
        P(None, "fsdp", None),
        P(None, "fsdp"),
        P(None, "fsdp", None),
        P(None, "fsdp"),
        P(None, "fsdp"),
    )
    out_specs = (
        P("rep", "fsdp", None),
        P("rep", "fsdp", None),
        P(None, "fsdp"),
        P(None, "fsdp"),
        P(None, "fsdp", None),
        P(None, "fsdp"),
        P(None, "fsdp"),
        P(None, "fsdp", None),
        P(None, "fsdp"),
        P(None, "fsdp"),
        P(None, "fsdp"),
        P(None, "fsdp"),
        P(None, "fsdp", None),
        P(None, "fsdp"),
        P(None, "fsdp", None),
        P(None, "fsdp"),
        P(None, "fsdp"),
    )
    return jax.shard_map(local, mesh=mesh, in_specs=in_specs, out_specs=out_specs, check_vma=False)
```

time: 2310 us -> 854 us (0.37)
  waiting for transfers between devices: 1220 us -> 290 us
  matrix products: 385 us -> 33.5 us
  Pallas kernels: 0 us -> 283 us
  blocking collectives: 283 us -> 0 us
  local copies, waits for them, and re-layouts: 250 us -> 66.9 us
  starting transfers between devices: 1.43 us -> 94.8 us
  other arithmetic: 144 us -> 71.4 us
    reduce_scatter x8 -> x0, waiting for transfers between devices: 562 us -> none  [the longest x2 181 us: reduce_grads(): lax.psum_scatter(g_expand_weight.astype(jnp.bfloat16), 'fsdp', scatter_di...]
    unnamed x23 -> x0, waiting for transfers between devices: 371 us -> none
    ppermute x0 -> x96, waiting for transfers between devices: none -> 290 us  [swap(): return lax.ppermute(tensor, axis, [(i, i ^ offset) for i in range(count)])]
    pallas_call x0 -> x35, Pallas kernels: none -> 283 us  [the longest x4 65.6 us: attend_back(): pl.pallas_call(functools.partial(attend_back_kernel, scale * math.log2(ma...]
    dot_general x20 -> x0, matrix products: 254 us -> none  [the longest x8 59.2 us: weight_dot(): lax.dot_general(left, grad, (((0,), (0,)), ((), ())), preferred_element_t...]
    all_gather x22 -> x0, blocking collectives: 240 us -> none  [the longest x2 27.7 us: fetch_forward(): lax.all_gather(expand_bias, 'fsdp', axis=0, tiled=True)]
    all_gather x10 -> x0, waiting for transfers between devices: 214 us -> none  [the longest x2 126 us: fetch_forward(): lax.all_gather(shrink_weight, 'fsdp', axis=0, tiled=True)]
    reshape x22 -> x2, local copies, waits for them, and re-layouts: 102 us -> 0.08 us  [reduce_small(): total = total.reshape(LAYERS, 2, step, -1)]
  transfers between devices with their start and end apart: 21 -> 96, of which waited for: 17 -> 35; matrix products, arithmetic and copies ran while one was open for 17% -> 16% of each run, Pallas kernels for 0% -> 30%
where the time goes in v1:
time: 854 us; the launch traced here: 843 us
  waiting for transfers between devices  290 us (34%)
  Pallas kernels  283 us (33%)
  starting transfers between devices  94.8 us (11%)
  other arithmetic  71.4 us (8%)
  local copies, waits for them, and re-layouts  66.9 us (8%)
  matrix products  33.5 us (4%)
    ppermute x96, waiting for transfers between devices, swap(): return lax.ppermute(tensor, axis, [(i, i ^ offset) for i in range(count)])  290 us
    ppermute x96, starting transfers between devices, swap(): return lax.ppermute(tensor, axis, [(i, i ^ offset) for i in range(count)])  94.8 us
    pallas_call x4, Pallas kernels, attend_back(): pl.pallas_call(functools.partial(attend_back_kernel, scale * math.log2(ma...  65.6 us
    pallas_call x4, Pallas kernels, grad_call(): pl.pallas_call(functools.partial(kernel, shapes), out_shape=out_shapes, g...  41.5 us
    pallas_call x2, Pallas kernels, attend(): pl.pallas_call(functools.partial(attend_kernel, factor, len(parts)), out_...  36.8 us
    pallas_call x8, Pallas kernels, add_split(): pl.pallas_call(split_kernel, out_shape=out_shapes, grid_spec=pltpu.Prefet...  32.4 us
    pallas_call x2, Pallas kernels, feed_forward(): pl.pallas_call(expand_kernel, out_shape=[jax.ShapeDtypeStruct((tokens, un...  25.7 us
    unnamed x339, local copies, waits for them, and re-layouts  25.3 us
  transfers between devices with their start and end apart: 96, of which 35 were waited for; matrix products, arithmetic and copies ran while one was open for 16% of the time, Pallas kernels for 30%

profile of v1, /device:TPU:0, one launch (start us, length us, event | category | flops | bytes accessed | tf_op | source)
XLA Modules:
  0.0 843.2 jit_solution(11829175516954721275)
XLA Ops:
  15.9 11.8 %collective-permute-done.1 = bf16[1,64,2048]{2,1,0:T(8,128)(2,1)S(1)} collective-permute-done((bf16[1,64,2048]{2,1,0:T(8,128)(2,1)S(1)}, bf16[1,64,2048]{2,1,0:T(8,128)(2,1)S(1)}, u32[]{:S(2)}, u32[]{:S(2)}) %collective-permute-start.1) | collective-permute-done | bytes 262176 | tf_op jit(solution)/shard_map/ppermute | solution.py:63
  32.3 14.7 %collective-permute-done.2 = bf16[172,1024]{1,0:T(8,128)(2,1)S(1)} collective-permute-done((bf16[172,1024]{1,0:T(8,128)(2,1)S(1)}, bf16[172,1024]{1,0:T(8,128)(2,1)S(1)}, u32[]{:S(2)}, u32[]{:S(2)}) %collective-permute-start.2) | collective-permute-done | bytes 352288 | tf_op jit(solution)/shard_map/ppermute | solution.py:63
  55.0 13.3 %collective-permute-done.5 = bf16[4,2,1792]{2,1,0:T(2,128)(2,1)S(1)} collective-permute-done((bf16[4,2,1792]{2,1,0:T(2,128)(2,1)S(1)}, bf16[4,2,1792]{2,1,0:T(2,128)(2,1)S(1)}, u32[]{:S(2)}, u32[]{:S(2)}) %collective-permute-start.5) | collective-permute-done | bytes 28704 | tf_op jit(solution)/shard_map/ppermute | solution.py:63
  90.2 12.3 %collective-permute-done.9 = bf16[2,128,2048]{2,1,0:T(8,128)(2,1)S(1)} collective-permute-done((bf16[2,128,2048]{2,1,0:T(8,128)(2,1)S(1)}, bf16[2,128,2048]{2,1,0:T(8,128)(2,1)S(1)}, u32[]{:S(2)}, u32[]{:S(2)}) %collective-permute-start.9) | collective-permute-done | bytes 1048608 | tf_op jit(solution)/shard_map/ppermute | solution.py:63
  121.8 23.5 %collective-permute-done.14.refs_1_.refs_3_ = bf16[688,1024]{1,0:T(8,128)(2,1)S(1)} collective-permute-done((bf16[688,1024]{1,0:T(8,128)(2,1)S(1)}, bf16[688,1024]{1,0:T(8,128)(2,1)S(1)}, u32[]{:S(2)}, u32[]{:S(2)}) %collective-permute-start.14) | collective-permute-done | bytes 1409056 | tf_op jit(solution)/shard_map/ppermute | solution.py:63
  146.8 18.3 %shard_map.298 = (bf16[688,512]{1,0:T(8,128)(2,1)}, f32[688,512]{1,0:T(8,128)}) custom-call(bf16[688,1536]{1,0:T(8,128)(2,1)} %copy-done, bf16[688,1536]{1,0:T(8,128)(2,1)} %copy-done, bf16[688,1024]{1,0:T(8,128)(2,1)} %copy-done.2, bf16[688,1536]{1,0:T(8,128)(2,1)} %copy-done, bf16[688,1024]{1,0:T(8,128)(2,1)} %copy-done.2), custom_call_target="tpu_custom_call" | custom-call | flops 1000 | bytes 1000 | tf_op jit(solution)/shard_map/pallas_call | solution.py:760
  182.9 19.3 %collective-permute-done.18 = bf16[1,128,2048]{2,1,0:T(8,128)(2,1)S(1)} collective-permute-done((bf16[1,128,2048]{2,1,0:T(8,128)(2,1)S(1)}, bf16[1,128,2048]{2,1,0:T(8,128)(2,1)S(1)}, u32[]{:S(2)}, u32[]{:S(2)}) %collective-permute-start.18) | collective-permute-done | bytes 524320 | tf_op jit(solution)/shard_map/ppermute | solution.py:63
  219.2 12.9 %shard_map.300 = (bf16[688,2048]{1,0:T(8,128)(2,1)}, bf16[688,2048]{1,0:T(8,128)(2,1)}, f32[344,1024]{1,0:T(8,128)}, bf16[344,1024]{1,0:T(8,128)(2,1)}) custom-call(bf16[688,1024]{1,0:T(8,128)(2,1)} %copy-done.10, bf16[1024,2048]{1,0:T(8,128)(2,1)} %bitcast.302, f32[1,2048]{1,0:T(1,128)} %bitcast.380, bf16[2048,1024]{1,0:T(8,128)(2,1)} %bitcast.304), custom_call_target="tpu_custom_call" | custom-call | flops 1000 | bytes 1000 | tf_op jit(solution)/shard_map/pallas_call | solution.py:859
  243.6 9.9 %collective-permute-done.30.refs_4_ = bf16[4,32,2048]{2,1,0:T(8,128)(2,1)S(1)} collective-permute-done((bf16[4,32,2048]{2,1,0:T(8,128)(2,1)S(1)}, bf16[4,32,2048]{2,1,0:T(8,128)(2,1)S(1)}, u32[]{:S(2)}, u32[]{:S(2)}) %collective-permute-start.30) | collective-permute-done | bytes 524320 | tf_op jit(solution)/shard_map/ppermute | solution.py:63
  273.3 25.3 %collective-permute-done.31.refs_1_.refs_3_ = bf16[688,1024]{1,0:T(8,128)(2,1)S(1)} collective-permute-done((bf16[688,1024]{1,0:T(8,128)(2,1)S(1)}, bf16[688,1024]{1,0:T(8,128)(2,1)S(1)}, u32[]{:S(2)}, u32[]{:S(2)}) %collective-permute-start.31) | collective-permute-done | bytes 1409056 | tf_op jit(solution)/shard_map/ppermute | solution.py:63
  302.5 18.5 %shard_map.302 = (bf16[688,512]{1,0:T(8,128)(2,1)}, f32[688,512]{1,0:T(8,128)}) custom-call(bf16[688,1536]{1,0:T(8,128)(2,1)} %copy-done.1, bf16[688,1536]{1,0:T(8,128)(2,1)} %copy-done.1, bf16[688,1024]{1,0:T(8,128)(2,1)} %copy-done.3, bf16[688,1536]{1,0:T(8,128)(2,1)} %copy-done.1, bf16[688,1024]{1,0:T(8,128)(2,1)} %copy-done.3), custom_call_target="tpu_custom_call" | custom-call | flops 1000 | bytes 1000 | tf_op jit(solution)/shard_map/pallas_call | solution.py:760
  339.3 11.7 %collective-permute-done.38.refs_4_ = bf16[4,64,2048]{2,1,0:T(8,128)(2,1)} collective-permute-done((bf16[4,64,2048]{2,1,0:T(8,128)(2,1)}, bf16[4,64,2048]{2,1,0:T(8,128)(2,1)}, u32[]{:S(2)}, u32[]{:S(2)}) %collective-permute-start.38) | collective-permute-done | bytes 1048608 | tf_op jit(solution)/shard_map/ppermute | solution.py:63
  353.5 7.9 shard_map.303
  366.5 12.9 %shard_map.304 = (bf16[688,2048]{1,0:T(8,128)(2,1)}, bf16[688,2048]{1,0:T(8,128)(2,1)}, f32[344,1024]{1,0:T(8,128)}, bf16[344,1024]{1,0:T(8,128)(2,1)}) custom-call(bf16[688,1024]{1,0:T(8,128)(2,1)} %pad_maximum_fusion.4.rows_ref.left_ref, bf16[1024,2048]{1,0:T(8,128)(2,1)} %bitcast.306, f32[1,2048]{1,0:T(1,128)} %bitcast.379, bf16[2048,1024]{1,0:T(8,128)(2,1)} %bitcast.308), custom_call_target="tpu_custom_call" | custom-call | flops 1000 | bytes 1000 | tf_op jit(solution)/shard_map/pallas_call | solution.py:859
  379.3 12.0 %shard_map.305 = (bf16[688,2048]{1,0:T(8,128)(2,1)}, f32[1,2048]{1,0:T(1,128)}, f32[344,1024]{1,0:T(8,128)}, bf16[344,1024]{1,0:T(8,128)(2,1)}) custom-call(bf16[688,1024]{1,0:T(8,128)(2,1)} %pad_maximum_fusion.5.grad_ref.other_ref, bf16[2048,1024]{1,0:T(8,128)(2,1)} %bitcast.309, bf16[688,2048]{1,0:T(8,128)(2,1)} %get-tuple-element.237.slope_ref, ...), custom_call_target="tpu_custom_call" | custom-call | flops 1000 | bytes 1000 | tf_op jit(solution)/shard_map/pallas_call | solution.py:897
  392.5 12.6 %shard_map.306 = (bf16[4,2,1,128,1024]{4,3,2,1,0:T(8,128)(2,1)}, bf16[4,2,1,128,1024]{4,3,2,1,0:T(8,128)(2,1)}, bf16[4,1,2,128,1024]{4,3,2,1,0:T(8,128)(2,1)}, bf16[4,1,2,128,1024]{4,3,2,1,0:T(8,128)(2,1)}) custom-call(s32[2]{0:T(128)} %pad_add_fusion.2.where_ref, bf16[688,1024]{1,0:T(8,128)(2,1)} %pad_maximum_fusion.4.rows_ref.left_ref, ...), custom_call_target="tpu_custom_call" | custom-call | flops 1000 | bytes 1000 | tf_op jit(solution)/shard_map/pallas_call | solution.py:370
  420.0 16.2 %shard_map.307 = (bf16[688,256]{1,0:T(8,128)(2,1)}, bf16[2,688,256]{2,1,0:T(8,128)(2,1)}, bf16[2,688,256]{2,1,0:T(8,128)(2,1)}) custom-call(bf16[688,1536]{1,0:T(8,128)(2,1)} %copy-done.1, bf16[688,1536]{1,0:T(8,128)(2,1)} %copy-done.1, bf16[688,1024]{1,0:T(8,128)(2,1)} %copy-done.3, bf16[688,1536]{1,0:T(8,128)(2,1)} %copy-done.1, ...), custom_call_target="tpu_custom_call" | custom-call | flops 1000 | bytes 1000 | tf_op jit(solution)/shard_map/pallas_call | solution.py:804
  440.2 19.7 %collective-permute-done.40 = bf16[172,1024]{1,0:T(8,128)(2,1)} collective-permute-done((bf16[172,1024]{1,0:T(8,128)(2,1)S(1)}, bf16[172,1024]{1,0:T(8,128)(2,1)}, u32[]{:S(2)}, u32[]{:S(2)}) %collective-permute-start.40) | collective-permute-done | bytes 352288 | tf_op jit(solution)/shard_map/ppermute | solution.py:63
  459.8 16.4 %shard_map.308 = (bf16[688,256]{1,0:T(8,128)(2,1)}, bf16[2,688,256]{2,1,0:T(8,128)(2,1)}, bf16[2,688,256]{2,1,0:T(8,128)(2,1)}) custom-call(bf16[688,1536]{1,0:T(8,128)(2,1)} %copy-done.1, bf16[688,1536]{1,0:T(8,128)(2,1)} %copy-done.1, bf16[688,1024]{1,0:T(8,128)(2,1)} %copy-done.3, bf16[688,1536]{1,0:T(8,128)(2,1)} %copy-done.1, ...), custom_call_target="tpu_custom_call" | custom-call | flops 1000 | bytes 1000 | tf_op jit(solution)/shard_map/pallas_call | solution.py:804
  503.4 8.5 %shard_map.310 = (bf16[4,2,1,64,1024]{4,3,2,1,0:T(8,128)(2,1)}, bf16[4,2,1,64,1024]{4,3,2,1,0:T(8,128)(2,1)}, bf16[4,1,2,64,1024]{4,3,2,1,0:T(8,128)(2,1)}, bf16[4,1,2,64,1024]{4,3,2,1,0:T(8,128)(2,1)}) custom-call(s32[2]{0:T(128)} %pad_add_fusion.2.where_ref, bf16[688,1024]{1,0:T(8,128)(2,1)} %pad_maximum_fusion.3.left_ref, bf16[688,1536]{1,0:T(8,128)(2,1)} %copy-done.36, ...), custom_call_target="tpu_custom_call" | custom-call | flops 1000 | bytes 1000 | tf_op jit(solution)/shard_map/pallas_call | solution.py:370
  526.4 12.0 %shard_map.311 = (bf16[688,2048]{1,0:T(8,128)(2,1)}, f32[1,2048]{1,0:T(1,128)}, f32[344,1024]{1,0:T(8,128)}, bf16[344,1024]{1,0:T(8,128)(2,1)}) custom-call(bf16[688,1024]{1,0:T(8,128)(2,1)} %pad_maximum_fusion.7.grad_ref.other_ref, bf16[2048,1024]{1,0:T(8,128)(2,1)} %bitcast.305, bf16[688,2048]{1,0:T(8,128)(2,1)} %get-tuple-element.265.slope_ref, ...), custom_call_target="tpu_custom_call" | custom-call | flops 1000 | bytes 1000 | tf_op jit(solution)/shard_map/pallas_call | solution.py:897
  541.8 12.3 %shard_map.313 = (bf16[4,2,1,128,1024]{4,3,2,1,0:T(8,128)(2,1)}, bf16[4,2,1,128,1024]{4,3,2,1,0:T(8,128)(2,1)}, bf16[4,1,2,128,1024]{4,3,2,1,0:T(8,128)(2,1)}, bf16[4,1,2,128,1024]{4,3,2,1,0:T(8,128)(2,1)}) custom-call(s32[2]{0:T(128)} %pad_add_fusion.2.where_ref, bf16[688,1024]{1,0:T(8,128)(2,1)} %copy-done.10, ...), custom_call_target="tpu_custom_call" | custom-call | flops 1000 | bytes 1000 | tf_op jit(solution)/shard_map/pallas_call | solution.py:370
  580.3 16.5 %shard_map.315 = (bf16[688,256]{1,0:T(8,128)(2,1)}, bf16[2,688,256]{2,1,0:T(8,128)(2,1)}, bf16[2,688,256]{2,1,0:T(8,128)(2,1)}) custom-call(bf16[688,1536]{1,0:T(8,128)(2,1)} %copy-done, bf16[688,1536]{1,0:T(8,128)(2,1)} %copy-done, bf16[688,1024]{1,0:T(8,128)(2,1)} %copy-done.2, bf16[688,1536]{1,0:T(8,128)(2,1)} %copy-done, bf16[688,1024]{1,0:T(8,128)(2,1)} %copy-done.2, ...), custom_call_target="tpu_custom_call" | custom-call | flops 1000 | bytes 1000 | tf_op jit(solution)/shard_map/pallas_call | solution.py:804
  596.8 16.8 %collective-permute-done.57 = bf16[4,1,64,1024]{3,2,1,0:T(8,128)(2,1)} collective-permute-done((bf16[4,1,64,1024]{3,2,1,0:T(8,128)(2,1)}, bf16[4,1,64,1024]{3,2,1,0:T(8,128)(2,1)}, u32[]{:S(2)}, u32[]{:S(2)}) %collective-permute-start.57) | collective-permute-done | bytes 524320 | tf_op jit(solution)/shard_map/ppermute | solution.py:63
  628.1 16.4 %shard_map.318 = (bf16[688,256]{1,0:T(8,128)(2,1)}, bf16[2,688,256]{2,1,0:T(8,128)(2,1)}, bf16[2,688,256]{2,1,0:T(8,128)(2,1)}) custom-call(bf16[688,1536]{1,0:T(8,128)(2,1)} %copy-done, bf16[688,1536]{1,0:T(8,128)(2,1)} %copy-done, bf16[688,1024]{1,0:T(8,128)(2,1)} %copy-done.2, bf16[688,1536]{1,0:T(8,128)(2,1)} %copy-done, bf16[688,1024]{1,0:T(8,128)(2,1)} %copy-done.2, ...), custom_call_target="tpu_custom_call" | custom-call | flops 1000 | bytes 1000 | tf_op jit(solution)/shard_map/pallas_call | solution.py:804
  663.2 11.3 %collective-permute-done.62 = bf16[2,688,256]{2,1,0:T(8,128)(2,1)} collective-permute-done((bf16[2,688,256]{2,1,0:T(8,128)(2,1)}, bf16[2,688,256]{2,1,0:T(8,128)(2,1)}, u32[]{:S(2)}, u32[]{:S(2)}) %collective-permute-start.62) | collective-permute-done | bytes 704544 | tf_op jit(solution)/shard_map/ppermute | solution.py:63
  678.9 8.1 shard_map.320
  704.5 12.8 %collective-permute-done.67 = f32[2,4,1792]{2,1,0:T(4,128)S(1)} collective-permute-done((f32[2,4,1792]{2,1,0:T(4,128)S(1)}, f32[2,4,1792]{2,1,0:T(4,128)S(1)}, u32[]{:S(2)}, u32[]{:S(2)}) %collective-permute-start.67) | collective-permute-done | bytes 57376 | tf_op jit(solution)/shard_map/ppermute | solution.py:63
  733.1 10.4 %collective-permute-done.66 = bf16[172,1024]{1,0:T(8,128)(2,1)} collective-permute-done((bf16[172,1024]{1,0:T(8,128)(2,1)}, bf16[172,1024]{1,0:T(8,128)(2,1)}, u32[]{:S(2)}, u32[]{:S(2)}) %collective-permute-start.66) | collective-permute-done | bytes 352288 | tf_op jit(solution)/shard_map/ppermute | solution.py:63
  764.4 10.1 %collective-permute-done.91 = bf16[1,1,128,2048]{3,2,1,0:T(8,128)(2,1)S(1)} collective-permute-done((bf16[1,1,128,2048]{3,2,1,0:T(8,128)(2,1)}, bf16[1,1,128,2048]{3,2,1,0:T(8,128)(2,1)S(1)}, u32[]{:S(2)}, u32[]{:S(2)}) %collective-permute-start.91) | collective-permute-done | bytes 524320 | tf_op jit(solution)/shard_map/ppermute | solution.py:63
  781.1 11.9 %collective-permute-done.77 = bf16[1,1,64,2048]{3,2,1,0:T(8,128)(2,1)S(1)} collective-permute-done((bf16[1,1,64,2048]{3,2,1,0:T(8,128)(2,1)}, bf16[1,1,64,2048]{3,2,1,0:T(8,128)(2,1)S(1)}, u32[]{:S(2)}, u32[]{:S(2)}) %collective-permute-start.77) | collective-permute-done | bytes 262176 | tf_op jit(solution)/shard_map/ppermute | solution.py:63
  798.0 10.2 %collective-permute-done.93.refs_1_ = bf16[128,2048]{1,0:T(8,128)(2,1)} collective-permute-done((bf16[128,2048]{1,0:T(8,128)(2,1)S(1)}, bf16[128,2048]{1,0:T(8,128)(2,1)}, u32[]{:S(2)}, u32[]{:S(2)}) %collective-permute-start.93) | collective-permute-done | bytes 524320 | tf_op jit(solution)/shard_map/ppermute | solution.py:63
  (741 shorter events, 393.0 us)
Async XLA Ops:
  28.2 40.9 %collective-permute-start.7 = (bf16[2,64,2048]{2,1,0:T(8,128)(2,1)S(1)}, bf16[2,64,2048]{2,1,0:T(8,128)(2,1)S(1)}, u32[]{:S(2)}, u32[]{:S(2)}) collective-permute-start(bf16[2,64,2048]{2,1,0:T(8,128)(2,1)S(1)} %get-tuple-element.194), channel_id=1, source_target_pairs={{0,2},{1,3},{2,0},{3,1},{4,6},{5,7},{6,4},{7,5},{8,10},{9,11},{10,... | collective-permute-start | bytes 1572872 | tf_op jit(solution)/shard_map/ppermute | solution.py:63
  114.5 30.9 %collective-permute-start.14 = (bf16[688,1024]{1,0:T(8,128)(2,1)S(1)}, bf16[688,1024]{1,0:T(8,128)(2,1)S(1)}, u32[]{:S(2)}, u32[]{:S(2)}) collective-permute-start(bf16[688,1024]{1,0:T(8,128)(2,1)S(1)} %slice.495), channel_id=1, source_target_pairs={{0,2},{1,3},{2,0},{3,1},{4,6},{5,7},{6,4},{7,5},{8,10},{9,11},{10,... | collective-permute-start | bytes 4227080 | tf_op jit(solution)/shard_map/ppermute | solution.py:63
  118.0 52.6 %collective-permute-start.20 = (bf16[4,128,2048]{2,1,0:T(8,128)(2,1)}, bf16[4,128,2048]{2,1,0:T(8,128)(2,1)}, u32[]{:S(2)}, u32[]{:S(2)}) collective-permute-start(bf16[4,128,2048]{2,1,0:T(8,128)(2,1)} %bitcast.59.refs_0_), channel_id=1, source_target_pairs={{0,8},{8,0},{16,24},{24,16},{1,9},{9,1},{17,25},{25,17},{2,10},{10... | collective-permute-start | bytes 6291464 | tf_op jit(solution)/shard_map/ppermute | solution.py:63
  119.6 52.3 %collective-permute-start.21 = (bf16[4,128,2048]{2,1,0:T(8,128)(2,1)}, bf16[4,128,2048]{2,1,0:T(8,128)(2,1)}, u32[]{:S(2)}, u32[]{:S(2)}) collective-permute-start(bf16[4,128,2048]{2,1,0:T(8,128)(2,1)} %bitcast.59.refs_0_), channel_id=1, source_target_pairs={{0,16},{8,24},{16,0},{24,8},{1,17},{9,25},{17,1},{25,9},{2,18},{10... | collective-permute-start | bytes 6291464 | tf_op jit(solution)/shard_map/ppermute | solution.py:63
  171.8 31.8 %collective-permute-start.23 = (bf16[4,64,2048]{2,1,0:T(8,128)(2,1)S(1)}, bf16[4,64,2048]{2,1,0:T(8,128)(2,1)}, u32[]{:S(2)}, u32[]{:S(2)}) collective-permute-start(bf16[4,64,2048]{2,1,0:T(8,128)(2,1)S(1)} %slice.509), channel_id=1, source_target_pairs={{0,16},{8,24},{16,0},{24,8},{1,17},{9,25},{17,1},{25,9},{2,18},{10... | collective-permute-start | bytes 3145736 | tf_op jit(solution)/shard_map/ppermute | solution.py:63
  266.5 32.1 %collective-permute-start.31 = (bf16[688,1024]{1,0:T(8,128)(2,1)S(1)}, bf16[688,1024]{1,0:T(8,128)(2,1)S(1)}, u32[]{:S(2)}, u32[]{:S(2)}) collective-permute-start(bf16[688,1024]{1,0:T(8,128)(2,1)S(1)} %slice.521), channel_id=1, source_target_pairs={{0,2},{1,3},{2,0},{3,1},{4,6},{5,7},{6,4},{7,5},{8,10},{9,11},{10,... | collective-permute-start | bytes 4227080 | tf_op jit(solution)/shard_map/ppermute | solution.py:63
  271.3 51.4 %collective-permute-start.35 = (bf16[4,128,2048]{2,1,0:T(8,128)(2,1)}, bf16[4,128,2048]{2,1,0:T(8,128)(2,1)}, u32[]{:S(2)}, u32[]{:S(2)}) collective-permute-start(bf16[4,128,2048]{2,1,0:T(8,128)(2,1)} %bitcast.87.refs_0_), channel_id=1, source_target_pairs={{0,8},{8,0},{16,24},{24,16},{1,9},{9,1},{17,25},{25,17},{2,10},{10... | collective-permute-start | bytes 6291464 | tf_op jit(solution)/shard_map/ppermute | solution.py:63
  272.8 52.3 %collective-permute-start.36 = (bf16[4,128,2048]{2,1,0:T(8,128)(2,1)}, bf16[4,128,2048]{2,1,0:T(8,128)(2,1)}, u32[]{:S(2)}, u32[]{:S(2)}) collective-permute-start(bf16[4,128,2048]{2,1,0:T(8,128)(2,1)} %bitcast.87.refs_0_), channel_id=1, source_target_pairs={{0,16},{8,24},{16,0},{24,8},{1,17},{9,25},{17,1},{25,9},{2,18},{10... | collective-permute-start | bytes 6291464 | tf_op jit(solution)/shard_map/ppermute | solution.py:63
  405.1 75.6 %collective-permute-start.44 = (bf16[4,2,1,128,1024]{4,3,2,1,0:T(8,128)(2,1)}, bf16[4,2,1,128,1024]{4,3,2,1,0:T(8,128)(2,1)}, u32[]{:S(2)}, u32[]{:S(2)}) collective-permute-start(bf16[4,2,1,128,1024]{4,3,2,1,0:T(8,128)(2,1)} %get-tuple-element.241), channel_id=1, source_target_pairs={{0,8},{8,0},{16,24},{24,16},{1,9},{9,1},{17,25},{25,17},{2,10},{10... | collective-permute-start | bytes 6291464 | tf_op jit(solution)/shard_map/ppermute | solution.py:63
  406.8 73.9 %collective-permute-start.45 = (bf16[4,1,2,128,1024]{4,3,2,0,1:T(8,128)(2,1)}, bf16[4,1,2,128,1024]{4,3,2,0,1:T(8,128)(2,1)}, u32[]{:S(2)}, u32[]{:S(2)}) collective-permute-start(bf16[4,1,2,128,1024]{4,3,2,0,1:T(8,128)(2,1)} %bitcast.431), channel_id=1, source_target_pairs={{0,16},{8,24},{16,0},{24,8},{1,17},{9,25},{17,1},{25,9},{2,18},{10... | collective-permute-start | bytes 6291464 | tf_op jit(solution)/shard_map/ppermute | solution.py:63
  436.3 40.0 %collective-permute-start.46 = (bf16[2,688,256]{2,1,0:T(8,128)(2,1)}, bf16[2,688,256]{2,1,0:T(8,128)(2,1)}, u32[]{:S(2)}, u32[]{:S(2)}) collective-permute-start(bf16[2,688,256]{2,1,0:T(8,128)(2,1)} %get-tuple-element.258), channel_id=1, source_target_pairs={{0,2},{1,3},{2,0},{3,1},{4,6},{5,7},{6,4},{7,5},{8,10},{9,11},{10,... | collective-permute-start | bytes 2113544 | tf_op jit(solution)/shard_map/ppermute | solution.py:63
  502.1 36.3 %collective-permute-start.50 = (bf16[4,1,128,1024]{3,2,1,0:T(8,128)(2,1)}, bf16[4,1,128,1024]{3,2,1,0:T(8,128)(2,1)}, u32[]{:S(2)}, u32[]{:S(2)}) collective-permute-start(bf16[4,1,128,1024]{3,2,1,0:T(8,128)(2,1)} %get-tuple-element.254), channel_id=1, source_target_pairs={{0,16},{8,24},{16,0},{24,8},{1,17},{9,25},{17,1},{25,9},{2,18},{10... | collective-permute-start | bytes 3145736 | tf_op jit(solution)/shard_map/ppermute | solution.py:63
  502.9 35.5 %collective-permute-start.51 = (bf16[4,1,128,1024]{3,2,1,0:T(8,128)(2,1)}, bf16[4,1,128,1024]{3,2,1,0:T(8,128)(2,1)}, u32[]{:S(2)}, u32[]{:S(2)}) collective-permute-start(bf16[4,1,128,1024]{3,2,1,0:T(8,128)(2,1)} %get-tuple-element.255), channel_id=1, source_target_pairs={{0,8},{8,0},{16,24},{24,16},{1,9},{9,1},{17,25},{25,17},{2,10},{10... | collective-permute-start | bytes 3145736 | tf_op jit(solution)/shard_map/ppermute | solution.py:63
  522.5 32.6 %collective-permute-start.52 = (bf16[4,2,1,64,1024]{4,3,2,1,0:T(8,128)(2,1)}, bf16[4,2,1,64,1024]{4,3,2,1,0:T(8,128)(2,1)}, u32[]{:S(2)}, u32[]{:S(2)}) collective-permute-start(bf16[4,2,1,64,1024]{4,3,2,1,0:T(8,128)(2,1)} %get-tuple-element.262), channel_id=1, source_target_pairs={{0,8},{8,0},{16,24},{24,16},{1,9},{9,1},{17,25},{25,17},{2,10},{10... | collective-permute-start | bytes 3145736 | tf_op jit(solution)/shard_map/ppermute | solution.py:63
  524.0 31.2 %collective-permute-start.53 = (bf16[4,1,2,64,1024]{4,3,2,0,1:T(8,128)(2,1)}, bf16[4,1,2,64,1024]{4,3,2,0,1:T(8,128)(2,1)}, u32[]{:S(2)}, u32[]{:S(2)}) collective-permute-start(bf16[4,1,2,64,1024]{4,3,2,0,1:T(8,128)(2,1)} %bitcast.108), channel_id=1, source_target_pairs={{0,16},{8,24},{16,0},{24,8},{1,17},{9,25},{17,1},{25,9},{2,18},{10... | collective-permute-start | bytes 3145736 | tf_op jit(solution)/shard_map/ppermute | solution.py:63
  554.1 95.5 %collective-permute-start.59 = (bf16[4,2,1,128,1024]{4,3,2,1,0:T(8,128)(2,1)}, bf16[4,2,1,128,1024]{4,3,2,1,0:T(8,128)(2,1)}, u32[]{:S(2)}, u32[]{:S(2)}) collective-permute-start(bf16[4,2,1,128,1024]{4,3,2,1,0:T(8,128)(2,1)} %get-tuple-element.277), channel_id=1, source_target_pairs={{0,8},{8,0},{16,24},{24,16},{1,9},{9,1},{17,25},{25,17},{2,10},{10... | collective-permute-start | bytes 6291464 | tf_op jit(solution)/shard_map/ppermute | solution.py:63
  560.0 89.5 %collective-permute-start.60 = (bf16[4,1,2,128,1024]{4,3,2,0,1:T(8,128)(2,1)}, bf16[4,1,2,128,1024]{4,3,2,0,1:T(8,128)(2,1)}, u32[]{:S(2)}, u32[]{:S(2)}) collective-permute-start(bf16[4,1,2,128,1024]{4,3,2,0,1:T(8,128)(2,1)} %bitcast.430), channel_id=1, source_target_pairs={{0,16},{8,24},{16,0},{24,8},{1,17},{9,25},{17,1},{25,9},{2,18},{10... | collective-permute-start | bytes 6291464 | tf_op jit(solution)/shard_map/ppermute | solution.py:63
  571.2 42.4 %collective-permute-start.57 = (bf16[4,1,64,1024]{3,2,1,0:T(8,128)(2,1)}, bf16[4,1,64,1024]{3,2,1,0:T(8,128)(2,1)}, u32[]{:S(2)}, u32[]{:S(2)}) collective-permute-start(bf16[4,1,64,1024]{3,2,1,0:T(8,128)(2,1)} %get-tuple-element.286), channel_id=1, source_target_pairs={{0,8},{8,0},{16,24},{24,16},{1,9},{9,1},{17,25},{25,17},{2,10},{10... | collective-permute-start | bytes 1572872 | tf_op jit(solution)/shard_map/ppermute | solution.py:63
  573.6 50.6 %collective-permute-start.58 = (bf16[2,128,2048]{2,1,0:T(8,128)(2,1)}, bf16[2,128,2048]{2,1,0:T(8,128)(2,1)}, u32[]{:S(2)}, u32[]{:S(2)}) collective-permute-start(bf16[2,128,2048]{2,1,0:T(8,128)(2,1)} %get-tuple-element.274), channel_id=1, source_target_pairs={{0,2},{1,3},{2,0},{3,1},{4,6},{5,7},{6,4},{7,5},{8,10},{9,11},{10,... | collective-permute-start | bytes 3145736 | tf_op jit(solution)/shard_map/ppermute | solution.py:63
  575.9 43.3 %collective-permute-start.56 = (bf16[4,1,64,1024]{3,2,1,0:T(8,128)(2,1)}, bf16[4,1,64,1024]{3,2,1,0:T(8,128)(2,1)}, u32[]{:S(2)}, u32[]{:S(2)}) collective-permute-start(bf16[4,1,64,1024]{3,2,1,0:T(8,128)(2,1)} %get-tuple-element.285), channel_id=1, source_target_pairs={{0,16},{8,24},{16,0},{24,8},{1,17},{9,25},{17,1},{25,9},{2,18},{10... | collective-permute-start | bytes 1572872 | tf_op jit(solution)/shard_map/ppermute | solution.py:63
  613.7 31.6 %collective-permute-start.61 = (bf16[2,688,256]{2,1,0:T(8,128)(2,1)}, bf16[2,688,256]{2,1,0:T(8,128)(2,1)}, u32[]{:S(2)}, u32[]{:S(2)}) collective-permute-start(bf16[2,688,256]{2,1,0:T(8,128)(2,1)} %get-tuple-element.310), channel_id=1, source_target_pairs={{0,2},{1,3},{2,0},{3,1},{4,6},{5,7},{6,4},{7,5},{8,10},{9,11},{10,... | collective-permute-start | bytes 2113544 | tf_op jit(solution)/shard_map/ppermute | solution.py:63
  621.7 36.5 %collective-permute-start.84 = (bf16[2,64,2048]{2,1,0:T(8,128)(2,1)}, bf16[2,64,2048]{2,1,0:T(8,128)(2,1)}, u32[]{:S(2)}, u32[]{:S(2)}) collective-permute-start(bf16[2,64,2048]{2,1,0:T(8,128)(2,1)} %get-tuple-element.295), channel_id=1, source_target_pairs={{0,2},{1,3},{2,0},{3,1},{4,6},{5,7},{6,4},{7,5},{8,10},{9,11},{10,... | collective-permute-start | bytes 1572872 | tf_op jit(solution)/shard_map/ppermute | solution.py:63
  626.9 71.5 %collective-permute-start.82 = (bf16[1,1,128,2048]{3,2,1,0:T(8,128)(2,1)}, bf16[1,1,128,2048]{3,2,1,0:T(8,128)(2,1)}, u32[]{:S(2)}, u32[]{:S(2)}) collective-permute-start(bf16[1,1,128,2048]{3,2,1,0:T(8,128)(2,1)} %get-tuple-element.298), channel_id=1, source_target_pairs={{0,4},{1,5},{2,6},{3,7},{4,0},{5,1},{6,2},{7,3},{8,12},{9,13},{10,... | collective-permute-start | bytes 1572872 | tf_op jit(solution)/shard_map/ppermute | solution.py:63
  656.2 31.1 %collective-permute-start.64 = (bf16[4,1,128,1024]{3,2,1,0:T(8,128)(2,1)}, bf16[4,1,128,1024]{3,2,1,0:T(8,128)(2,1)}, u32[]{:S(2)}, u32[]{:S(2)}) collective-permute-start(bf16[4,1,128,1024]{3,2,1,0:T(8,128)(2,1)} %get-tuple-element.307), channel_id=1, source_target_pairs={{0,8},{8,0},{16,24},{24,16},{1,9},{9,1},{17,25},{25,17},{2,10},{10... | collective-permute-start | bytes 3145736 | tf_op jit(solution)/shard_map/ppermute | solution.py:63
  660.2 39.7 %collective-permute-start.85 = (bf16[1,1,64,2048]{3,2,1,0:T(8,128)(2,1)}, bf16[1,1,64,2048]{3,2,1,0:T(8,128)(2,1)}, u32[]{:S(2)}, u32[]{:S(2)}) collective-permute-start(bf16[1,1,64,2048]{3,2,1,0:T(8,128)(2,1)} %get-tuple-element.346), channel_id=1, source_target_pairs={{0,4},{1,5},{2,6},{3,7},{4,0},{5,1},{6,2},{7,3},{8,12},{9,13},{10,... | collective-permute-start | bytes 786440 | tf_op jit(solution)/shard_map/ppermute | solution.py:63
  687.3 38.8 %collective-permute-start.72 = (bf16[4,2,1,64,1024]{4,3,2,1,0:T(8,128)(2,1)}, bf16[4,2,1,64,1024]{4,3,2,1,0:T(8,128)(2,1)}, u32[]{:S(2)}, u32[]{:S(2)}) collective-permute-start(bf16[4,2,1,64,1024]{4,3,2,1,0:T(8,128)(2,1)} %get-tuple-element.314), channel_id=1, source_target_pairs={{0,8},{8,0},{16,24},{24,16},{1,9},{9,1},{17,25},{25,17},{2,10},{10... | collective-permute-start | bytes 3145736 | tf_op jit(solution)/shard_map/ppermute | solution.py:63
  688.1 37.9 %collective-permute-start.73 = (bf16[4,1,2,64,1024]{4,3,2,0,1:T(8,128)(2,1)}, bf16[4,1,2,64,1024]{4,3,2,0,1:T(8,128)(2,1)}, u32[]{:S(2)}, u32[]{:S(2)}) collective-permute-start(bf16[4,1,2,64,1024]{4,3,2,0,1:T(8,128)(2,1)} %bitcast.166), channel_id=1, source_target_pairs={{0,16},{8,24},{16,0},{24,8},{1,17},{9,25},{17,1},{25,9},{2,18},{10... | collective-permute-start | bytes 3145736 | tf_op jit(solution)/shard_map/ppermute | solution.py:63
  692.9 54.1 %collective-permute-start.90 = (bf16[2,128,2048]{2,1,0:T(8,128)(2,1)}, bf16[2,128,2048]{2,1,0:T(8,128)(2,1)}, u32[]{:S(2)}, u32[]{:S(2)}) collective-permute-start(bf16[2,128,2048]{2,1,0:T(8,128)(2,1)} %get-tuple-element.321), channel_id=1, source_target_pairs={{0,2},{1,3},{2,0},{3,1},{4,6},{5,7},{6,4},{7,5},{8,10},{9,11},{10,... | collective-permute-start | bytes 3145736 | tf_op jit(solution)/shard_map/ppermute | solution.py:63
  757.2 38.3 %collective-permute-start.71 = (f32[2,1,1792]{2,0,1:T(2,128)}, f32[2,1,1792]{2,0,1:T(2,128)}, u32[]{:S(2)}, u32[]{:S(2)}) collective-permute-start(f32[2,1,1792]{2,0,1:T(2,128)} %add.406), channel_id=1, source_target_pairs={{0,16},{8,24},{16,0},{24,8},{1,17},{9,25},{17,1},{25,9},{2,18},{10... | collective-permute-start | bytes 43016 | tf_op jit(solution)/shard_map/ppermute | solution.py:63
  758.0 53.1 %collective-permute-start.87 = (bf16[192,2048]{1,0:T(8,128)(2,1)S(1)}, bf16[192,2048]{1,0:T(8,128)(2,1)S(1)}, u32[]{:S(2)}, u32[]{:S(2)}) collective-permute-start(bf16[192,2048]{1,0:T(8,128)(2,1)S(1)} %maximum_maximum_fusion), channel_id=1, source_target_pairs={{0,8},{8,0},{16,24},{24,16},{1,9},{9,1},{17,25},{25,17},{2,10},{10... | collective-permute-start | bytes 2359304 | tf_op jit(solution)/shard_map/ppermute | solution.py:63
  763.2 59.5 %collective-permute-start.89 = (bf16[192,2048]{1,0:T(8,128)(2,1)}, bf16[192,2048]{1,0:T(8,128)(2,1)S(1)}, u32[]{:S(2)}, u32[]{:S(2)}) collective-permute-start(bf16[192,2048]{1,0:T(8,128)(2,1)} %collective-permute-done.88), channel_id=1, source_target_pairs={{0,8},{8,0},{16,24},{24,16},{1,9},{9,1},{17,25},{25,17},{2,10},{10... | collective-permute-start | bytes 2359304 | tf_op jit(solution)/shard_map/ppermute | solution.py:63
  796.9 41.1 %collective-permute-start.94 = (bf16[128,2048]{1,0:T(8,128)(2,1)S(1)}, bf16[128,2048]{1,0:T(8,128)(2,1)}, u32[]{:S(2)}, u32[]{:S(2)}) collective-permute-start(bf16[128,2048]{1,0:T(8,128)(2,1)S(1)} %pad_maximum_fusion.17.refs_0_), channel_id=1, source_target_pairs={{0,16},{8,24},{16,0},{24,8},{1,17},{9,25},{17,1},{25,9},{2,18},{10... | collective-permute-start | bytes 1572872 | tf_op jit(solution)/shard_map/ppermute | solution.py:63
  (222 other events, 2421.2 us)

commit v2 on v1

--- a/solution.py
+++ b/solution.py
@@ -76,8 +76,8 @@
     return pl.CostEstimate(flops=1000, bytes_accessed=1000, transcendentals=0)
 
 
-def params():
-    return pltpu.CompilerParams(vmem_limit_bytes=60 * MIB)
+def params(mib):
+    return pltpu.CompilerParams(vmem_limit_bytes=mib * MIB)
 
 
 def after(tensor, *earlier):
@@ -127,7 +127,6 @@
             ],
             out_specs=[out, out],
         ),
-        compiler_params=params(),
         cost_estimate=estimate(0, 4 * LAYERS * rows * columns * 2),
     )(scalars(member, core), *shards)
     both = by_core(own, swap(other, "fsdp", 1), 1)
@@ -178,7 +177,7 @@
             pltpu.SemaphoreType.DMA((len(pieces),)),
             pltpu.SemaphoreType.DMA((len(blocks), len(pieces), planes)),
         ],
-        compiler_params=params(),
+        compiler_params=params(20),
         cost_estimate=estimate(0, 4 * sum(piece.size for piece in pieces)),
     )(scalars(plane, member), *pieces)
     return [out.reshape(-1, out.shape[-1]) for out in outs]
@@ -377,7 +376,7 @@
             out_specs=out_specs,
             scratch_shapes=[pltpu.VMEM(size, jnp.bfloat16) for size in scratch],
         ),
-        compiler_params=params(),
+        compiler_params=params(40),
         cost_estimate=estimate(5, 0),
     )(scalars(*[(member >> order[0]) & 1 for order in orders]), *arrays)
 
@@ -459,7 +458,7 @@
             in_specs=in_specs,
             out_specs=out_specs,
         ),
-        compiler_params=params(),
+        compiler_params=params(24),
         cost_estimate=estimate(0, sum(array.size for array in arrays) * 3),
     )(scalars(*sides), *arrays)
 
@@ -497,7 +496,7 @@
             in_specs=specs,
             out_specs=[given, given],
         ),
-        compiler_params=params(),
+        compiler_params=params(24),
         cost_estimate=estimate(0, sum(array.size for array in arrays) * 3),
     )(scalars(side), *arrays)
 
@@ -620,14 +619,15 @@
             ],
         ),
         input_output_aliases=aliases,
-        compiler_params=params(),
+        compiler_params=params(24),
         cost_estimate=estimate(0, count * pieces[0].size * 6),
     )(scalars(member, core), *pieces, *earlier)
 
 
-def reduce_small(grads):
+def reduce_small(grads, earlier):
     owners, count = lax.axis_size("fsdp"), lax.axis_size("rep")
     total = jnp.concatenate([g.reshape(LAYERS, owners, -1) for g in grads], 2)
+    total = after(total, *earlier)
     owner = lax.axis_index("fsdp")
     step = owners // 2
     while step:
@@ -767,7 +767,7 @@
         in_specs=[pair_block(tokens, 0)] + specs,
         out_specs=[pair_block(tokens, 0), pair_block(tokens, 0)],
         scratch_shapes=held,
-        compiler_params=params(),
+        compiler_params=params(56),
         cost_estimate=estimate(18, 0),
     )(projected, *arrays)
 
@@ -816,7 +816,7 @@
             pl.BlockSpec((2, rows - tokens, 128), lambda i: (0, 0, i)),
         ],
         scratch_shapes=held,
-        compiler_params=params(),
+        compiler_params=params(60),
         cost_estimate=estimate(8 * pairs, 0),
     )(projected, *arrays, log_total, d_attended)
 
@@ -873,7 +873,7 @@
         ],
         out_specs=[part, part, half, half],
         scratch_shapes=[pltpu.VMEM((tokens, width), jnp.float32)],
-        compiler_params=params(),
+        compiler_params=params(32),
         cost_estimate=estimate(14, 0),
     )(rows_in, expand, expand_bias[None], shrink)
 
@@ -911,7 +911,7 @@
         ],
         out_specs=[part, pl.BlockSpec((1, tile), lambda i: (0, i)), half, half],
         scratch_shapes=[pltpu.VMEM((tokens, width), jnp.float32)],
-        compiler_params=params(),
+        compiler_params=params(32),
         cost_estimate=estimate(9, 0),
     )(d_mlp, shrink, slope, expand)
 
@@ -1067,6 +1067,8 @@
     got = swap(other_sum, "fsdp", 1)
     later.begin(block, block_grad, (normed_two, d_hidden, activated, d_mlp_both))
     own_sum = later.sent(own_sum, block)
+    if not old:
+        own_sum = after(own_sum, activation_got)
     if old:
         own_sum = later.came(own_sum, old[1])
         later.step(old[1], own_sum)
@@ -1090,12 +1092,9 @@
     first_query, d_own, d_others = back(0)
     first_kv, first_got = collect_rows(d_own, d_others)
     if old:
-        d_attended = later.came(d_attended, old[1], old[2])
-        later.join(old[3], [old[1]], first_query)
+        d_attended = later.came(d_attended, old[2])
         later.step(old[2], first_query)
-        d_attended = later.sent(d_attended, old[3], old[2])
-    else:
-        d_attended = after(d_attended, activation_got)
+        d_attended = later.sent(d_attended, old[2])
     second_query, d_own, d_others = back(pairs // 2)
     d_others = after(d_others, first_got)
     second_kv, second_got = collect_rows(d_own, d_others)
@@ -1103,7 +1102,9 @@
     later.step(block, second_query)
     second_query = later.sent(second_query, block)
     if old:
-        later.step(old[3], second_query)
+        second_query = later.came(second_query, old[1])
+        later.join(old[3], [old[1]], second_query)
+        second_query = later.sent(second_query, old[3])
     d_query = jnp.concatenate([first_query, second_query], 1)
     d_key = jnp.concatenate([first_kv[0], second_kv[0]], 1)
     d_value = jnp.concatenate([first_kv[1], second_kv[1]], 1)
@@ -1227,17 +1228,19 @@
     pieces = spread(later.sent(first, new[1]), True)
     write_block(layer + 1, [piece[:rows] for piece in pieces])
     write_mixed(layer + 1, [piece[rows:] for piece in pieces])
+    last_sends = later.sends[new[1]]
     later.join(new[3], [new[1]], d_rows)
-    for name in (new[3], new[2]):
-        while name in later.running:
-            later.step(name, image_got)
+    while new[3] in later.running:
+        later.step(new[3], d_rows)
+    while new[2] in later.running:
+        later.step(new[2], image_got)
     write_block(layer, spread(block_piece(later, layer), False))
     write_mixed(layer, spread(mixed_piece(later, layer), False))
     stacked = [None] * len(all_params)
     for i, out in zip((10, 12, 2, 5), list(outs["block"]) + list(outs["mixed"])):
         stacked[i] = out.reshape(all_params[i].shape)
     reduced = reduce_small(
-        [jnp.stack([grads[n] for grads in small_grads]) for n in range(len(SMALL))]
+        [jnp.stack([grads[n] for grads in small_grads]) for n in range(len(SMALL))], last_sends
     )
     for i, vector in zip(SMALL, reduced):
         stacked[i] = vector

time: 854 us -> 782 us (0.916)
  Pallas kernels: 283 us -> 227 us
  waiting for transfers between devices: 290 us -> 318 us
  other arithmetic: 71.4 us -> 45.7 us
  starting transfers between devices: 94.8 us -> 83 us
  matrix products: 33.5 us -> 24.5 us
    ppermute x96, waiting for transfers between devices: 290 us -> 318 us  [swap(): return lax.ppermute(tensor, axis, [(i, i ^ offset) for i in range(count)])]
    pallas_call x8, Pallas kernels: 32.4 us -> 13 us  [add_split(): pl.pallas_call(split_kernel, out_shape=out_shapes, grid_spec=pltpu.Prefet...]
    unnamed x339 -> x411, local copies, waits for them, and re-layouts: 25.3 us -> 42.7 us
    ppermute x96, starting transfers between devices: 94.8 us -> 83 us  [swap(): return lax.ppermute(tensor, axis, [(i, i ^ offset) for i in range(count)])]
    pallas_call x4, Pallas kernels: 41.5 us -> 32.3 us  [grad_call(): pl.pallas_call(functools.partial(kernel, shapes), out_shape=out_shapes, g...]
    concatenate x7, other arithmetic: 13.8 us -> 4.73 us  [both_cores(): return jnp.concatenate([rows, swap(rows, 'fsdp', 1)], 0)]
  transfers between devices with their start and end apart: 96 -> 96, of which waited for: 35 -> 42; matrix products, arithmetic and copies ran while one was open for 16% -> 12% of each run, Pallas kernels for 30% -> 26%
where the time goes in v2:
time: 782 us; the launch traced here: 772 us
  waiting for transfers between devices  318 us (41%)
  Pallas kernels  227 us (29%)
  starting transfers between devices  83 us (11%)
  local copies, waits for them, and re-layouts  69 us (9%)
  other arithmetic  45.7 us (6%)
  matrix products  24.5 us (3%)
    ppermute x96, waiting for transfers between devices, swap(): return lax.ppermute(tensor, axis, [(i, i ^ offset) for i in range(count)])  318 us
    ppermute x96, starting transfers between devices, swap(): return lax.ppermute(tensor, axis, [(i, i ^ offset) for i in range(count)])  83 us
    pallas_call x4, Pallas kernels, attend_back(): pl.pallas_call(functools.partial(attend_back_kernel, scale * math.log2(ma...  65.6 us
    unnamed x411, local copies, waits for them, and re-layouts  42.7 us
    pallas_call x2, Pallas kernels, attend(): pl.pallas_call(functools.partial(attend_kernel, factor, len(parts)), out_...  36.8 us
    pallas_call x4, Pallas kernels, grad_call(): pl.pallas_call(functools.partial(kernel, shapes), out_shape=out_shapes, g...  32.3 us
    pallas_call x4, Pallas kernels, place(): pl.pallas_call(functools.partial(place_kernel, pieces[0].shape[1] // 2, b...  23.2 us
    pallas_call x2, Pallas kernels, feed_forward(): pl.pallas_call(expand_kernel, out_shape=[jax.ShapeDtypeStruct((tokens, un...  19.7 us
  transfers between devices with their start and end apart: 96, of which 42 were waited for; matrix products, arithmetic and copies ran while one was open for 12% of the time, Pallas kernels for 26%

profile of v2, /device:TPU:0, one launch (start us, length us, event | category | flops | bytes accessed | tf_op | source)
XLA Modules:
  0.0 771.7 jit_solution(664944008412981550)
XLA Ops:
  14.0 12.5 %collective-permute-done.1 = bf16[1,64,2048]{2,1,0:T(8,128)(2,1)S(1)} collective-permute-done((bf16[1,64,2048]{2,1,0:T(8,128)(2,1)S(1)}, bf16[1,64,2048]{2,1,0:T(8,128)(2,1)S(1)}, u32[]{:S(2)}, u32[]{:S(2)}) %collective-permute-start.1) | collective-permute-done | bytes 262176 | tf_op jit(solution)/shard_map/ppermute | solution.py:63
  31.2 14.6 %collective-permute-done.2 = bf16[172,1024]{1,0:T(8,128)(2,1)S(1)} collective-permute-done((bf16[172,1024]{1,0:T(8,128)(2,1)S(1)}, bf16[172,1024]{1,0:T(8,128)(2,1)S(1)}, u32[]{:S(2)}, u32[]{:S(2)}) %collective-permute-start.2) | collective-permute-done | bytes 352288 | tf_op jit(solution)/shard_map/ppermute | solution.py:63
  53.9 13.3 %collective-permute-done.5 = bf16[4,2,1792]{2,1,0:T(2,128)(2,1)S(1)} collective-permute-done((bf16[4,2,1792]{2,1,0:T(2,128)(2,1)S(1)}, bf16[4,2,1792]{2,1,0:T(2,128)(2,1)S(1)}, u32[]{:S(2)}, u32[]{:S(2)}) %collective-permute-start.5) | collective-permute-done | bytes 28704 | tf_op jit(solution)/shard_map/ppermute | solution.py:63
  71.1 6.1 collective-permute-done.8
  89.8 11.5 %collective-permute-done.9 = bf16[2,128,2048]{2,1,0:T(8,128)(2,1)S(1)} collective-permute-done((bf16[2,128,2048]{2,1,0:T(8,128)(2,1)S(1)}, bf16[2,128,2048]{2,1,0:T(8,128)(2,1)S(1)}, u32[]{:S(2)}, u32[]{:S(2)}) %collective-permute-start.9) | collective-permute-done | bytes 1048608 | tf_op jit(solution)/shard_map/ppermute | solution.py:63
  113.4 25.5 %collective-permute-done.14.refs_1_.refs_3_ = bf16[688,1024]{1,0:T(8,128)(2,1)} collective-permute-done((bf16[688,1024]{1,0:T(8,128)(2,1)S(1)}, bf16[688,1024]{1,0:T(8,128)(2,1)}, u32[]{:S(2)}, u32[]{:S(2)}) %collective-permute-start.14) | collective-permute-done | bytes 1409056 | tf_op jit(solution)/shard_map/ppermute | solution.py:63
  140.8 18.3 %shard_map.298 = (bf16[688,512]{1,0:T(8,128)(2,1)}, f32[688,512]{1,0:T(8,128)}) custom-call(bf16[688,1536]{1,0:T(8,128)(2,1)} %copy-done.54, bf16[688,1536]{1,0:T(8,128)(2,1)} %copy-done.54, bf16[688,1024]{1,0:T(8,128)(2,1)} %collective-permute-done.14.refs_1_.refs_3_, bf16[688,1536]{1,0:T(8,128)(2,1)} %copy-done.54, ...), custom_call_target="tpu_custom_call" | custom-call | flops 1000 | bytes 1000 | tf_op jit(solution)/shard_map/pallas_call | solution.py:760
  178.0 15.2 %collective-permute-done.18 = bf16[1,128,2048]{2,1,0:T(8,128)(2,1)S(1)} collective-permute-done((bf16[1,128,2048]{2,1,0:T(8,128)(2,1)S(1)}, bf16[1,128,2048]{2,1,0:T(8,128)(2,1)S(1)}, u32[]{:S(2)}, u32[]{:S(2)}) %collective-permute-start.18) | collective-permute-done | bytes 524320 | tf_op jit(solution)/shard_map/ppermute | solution.py:63
  208.5 8.1 %shard_map.299 = (bf16[4,2,4,32,2048]{4,3,2,1,0:T(8,128)(2,1)S(1)}, bf16[4,4,2,64,1024]{4,3,2,1,0:T(8,128)(2,1)S(1)}) custom-call(s32[2]{0:T(128)S(1)} %pad_add_fusion.1.where_ref, bf16[4,128,2048]{2,1,0:T(8,128)(2,1)S(1)} %bitcast.312, bf16[4,128,2048]{2,1,0:T(8,128)(2,1)S(1)} %copy-done.7, bf16[4,128,2048]{2,1,0:T(8,128)(2,1)S(1)} %copy-done.9, ...), custom_call_target="tpu_custom_call" | custom-call | flops 1000 | bytes 1000 | tf_op jit(solution)/shard_map/pallas_call | solution.py:169
  218.4 9.8 %shard_map.300 = (bf16[688,2048]{1,0:T(8,128)(2,1)S(1)}, bf16[688,2048]{1,0:T(8,128)(2,1)S(1)}, f32[344,1024]{1,0:T(8,128)S(1)}, bf16[344,1024]{1,0:T(8,128)(2,1)S(1)}) custom-call(bf16[688,1024]{1,0:T(8,128)(2,1)S(1)} %constant_dynamic-update-slice_fusion.11.rows_ref.left_ref, bf16[1024,2048]{1,0:T(8,128)(2,1)S(1)} %bitcast.302, f32[1,2048]{1,0:T(1,128)S(1)} %bitcast.353, ...), custom_call_target="tpu_custom_call" | custom-call | flops 1000 | bytes 1000 | tf_op jit(solution)/shard_map/pallas_call | solution.py:859
  238.0 11.9 %collective-permute-done.30.refs_4_ = bf16[4,32,2048]{2,1,0:T(8,128)(2,1)S(1)} collective-permute-done((bf16[4,32,2048]{2,1,0:T(8,128)(2,1)S(1)}, bf16[4,32,2048]{2,1,0:T(8,128)(2,1)S(1)}, u32[]{:S(2)}, u32[]{:S(2)}) %collective-permute-start.30) | collective-permute-done | bytes 524320 | tf_op jit(solution)/shard_map/ppermute | solution.py:63
  265.6 26.5 %collective-permute-done.31.refs_1_.refs_3_ = bf16[688,1024]{1,0:T(8,128)(2,1)S(1)} collective-permute-done((bf16[688,1024]{1,0:T(8,128)(2,1)S(1)}, bf16[688,1024]{1,0:T(8,128)(2,1)S(1)}, u32[]{:S(2)}, u32[]{:S(2)}) %collective-permute-start.31) | collective-permute-done | bytes 1409056 | tf_op jit(solution)/shard_map/ppermute | solution.py:63
  296.3 18.5 %shard_map.302 = (bf16[688,512]{1,0:T(8,128)(2,1)}, f32[688,512]{1,0:T(8,128)}) custom-call(bf16[688,1536]{1,0:T(8,128)(2,1)} %copy-done.55, bf16[688,1536]{1,0:T(8,128)(2,1)} %copy-done.55, bf16[688,1024]{1,0:T(8,128)(2,1)} %copy-done.59, bf16[688,1536]{1,0:T(8,128)(2,1)} %copy-done.55, bf16[688,1024]{1,0:T(8,128)(2,1)} %copy-done.59), custom_call_target="tpu_custom_call" | custom-call | flops 1000 | bytes 1000 | tf_op jit(solution)/shard_map/pallas_call | solution.py:760
  326.5 17.6 %collective-permute-done.38.refs_4_ = bf16[4,64,2048]{2,1,0:T(8,128)(2,1)} collective-permute-done((bf16[4,64,2048]{2,1,0:T(8,128)(2,1)}, bf16[4,64,2048]{2,1,0:T(8,128)(2,1)}, u32[]{:S(2)}, u32[]{:S(2)}) %collective-permute-start.38) | collective-permute-done | bytes 1048608 | tf_op jit(solution)/shard_map/ppermute | solution.py:63
  349.6 8.0 %shard_map.303 = (bf16[4,2,4,32,2048]{4,3,2,1,0:T(8,128)(2,1)S(1)}, bf16[4,4,2,64,1024]{4,3,2,1,0:T(8,128)(2,1)S(1)}) custom-call(s32[2]{0:T(128)S(1)} %pad_add_fusion.1.where_ref, bf16[4,128,2048]{2,1,0:T(8,128)(2,1)S(1)} %bitcast.315, bf16[4,128,2048]{2,1,0:T(8,128)(2,1)S(1)} %copy-done.11, bf16[4,128,2048]{2,1,0:T(8,128)(2,1)S(1)} %copy-done.13, ...), custom_call_target="tpu_custom_call" | custom-call | flops 1000 | bytes 1000 | tf_op jit(solution)/shard_map/pallas_call | solution.py:169
  359.0 9.9 %shard_map.304 = (bf16[688,2048]{1,0:T(8,128)(2,1)S(1)}, bf16[688,2048]{1,0:T(8,128)(2,1)S(1)}, f32[344,1024]{1,0:T(8,128)S(1)}, bf16[344,1024]{1,0:T(8,128)(2,1)S(1)}) custom-call(bf16[688,1024]{1,0:T(8,128)(2,1)S(1)} %pad_maximum_fusion.4.rows_ref.left_ref, bf16[1024,2048]{1,0:T(8,128)(2,1)S(1)} %bitcast.306, f32[1,2048]{1,0:T(1,128)S(1)} %bitcast.352, ...), custom_call_target="tpu_custom_call" | custom-call | flops 1000 | bytes 1000 | tf_op jit(solution)/shard_map/pallas_call | solution.py:859
  374.7 8.8 %shard_map.305 = (bf16[688,2048]{1,0:T(8,128)(2,1)S(1)}, f32[1,2048]{1,0:T(1,128)S(1)}, f32[344,1024]{1,0:T(8,128)S(1)}, bf16[344,1024]{1,0:T(8,128)(2,1)S(1)}) custom-call(bf16[688,1024]{1,0:T(8,128)(2,1)S(1)} %pad_maximum_fusion.5.grad_ref.other_ref, bf16[2048,1024]{1,0:T(8,128)(2,1)S(1)} %bitcast.309, bf16[688,2048]{1,0:T(8,128)(2,1)S(1)} %get-tuple-element.240.slope_ref, ...), custom_call_target="tpu_custom_call" | custom-call | flops 1000 | bytes 1000 | tf_op jit(solution)/shard_map/pallas_call | solution.py:897
  384.0 10.6 %shard_map.306 = (bf16[4,2,1,128,1024]{4,3,2,1,0:T(8,128)(2,1)S(1)}, bf16[4,2,1,128,1024]{4,3,2,1,0:T(8,128)(2,1)}, bf16[4,1,2,128,1024]{4,3,2,1,0:T(8,128)(2,1)S(1)}, bf16[4,1,2,128,1024]{4,3,2,1,0:T(8,128)(2,1)}) custom-call(s32[2]{0:T(128)S(1)} %pad_add_fusion.2.where_ref, bf16[688,1024]{1,0:T(8,128)(2,1)S(1)} %pad_maximum_fusion.4.rows_ref.left_ref, ...), custom_call_target="tpu_custom_call" | custom-call | flops 1000 | bytes 1000 | tf_op jit(solution)/shard_map/pallas_call | solution.py:369
  396.4 6.5 collective-permute-done.40
  410.4 16.2 %shard_map.307 = (bf16[688,256]{1,0:T(8,128)(2,1)}, bf16[2,688,256]{2,1,0:T(8,128)(2,1)}, bf16[2,688,256]{2,1,0:T(8,128)(2,1)}) custom-call(bf16[688,1536]{1,0:T(8,128)(2,1)} %copy-done.55, bf16[688,1536]{1,0:T(8,128)(2,1)} %copy-done.55, bf16[688,1024]{1,0:T(8,128)(2,1)} %copy-done.59, bf16[688,1536]{1,0:T(8,128)(2,1)} %copy-done.55, ...), custom_call_target="tpu_custom_call" | custom-call | flops 1000 | bytes 1000 | tf_op jit(solution)/shard_map/pallas_call | solution.py:804
  426.6 16.5 %shard_map.308 = (bf16[688,256]{1,0:T(8,128)(2,1)}, bf16[2,688,256]{2,1,0:T(8,128)(2,1)}, bf16[2,688,256]{2,1,0:T(8,128)(2,1)}) custom-call(bf16[688,1536]{1,0:T(8,128)(2,1)} %copy-done.55, bf16[688,1536]{1,0:T(8,128)(2,1)} %copy-done.55, bf16[688,1024]{1,0:T(8,128)(2,1)} %copy-done.59, bf16[688,1536]{1,0:T(8,128)(2,1)} %copy-done.55, ...), custom_call_target="tpu_custom_call" | custom-call | flops 1000 | bytes 1000 | tf_op jit(solution)/shard_map/pallas_call | solution.py:804
  487.2 8.7 %shard_map.311 = (bf16[688,2048]{1,0:T(8,128)(2,1)S(1)}, f32[1,2048]{1,0:T(1,128)S(1)}, f32[344,1024]{1,0:T(8,128)S(1)}, bf16[344,1024]{1,0:T(8,128)(2,1)S(1)}) custom-call(bf16[688,1024]{1,0:T(8,128)(2,1)S(1)} %pad_maximum_fusion.7.grad_ref.other_ref, bf16[2048,1024]{1,0:T(8,128)(2,1)S(1)} %bitcast.305, bf16[688,2048]{1,0:T(8,128)(2,1)S(1)} %copy-done.22, ...), custom_call_target="tpu_custom_call" | custom-call | flops 1000 | bytes 1000 | tf_op jit(solution)/shard_map/pallas_call | solution.py:897
  497.2 10.6 %shard_map.313 = (bf16[4,2,1,128,1024]{4,3,2,1,0:T(8,128)(2,1)S(1)}, bf16[4,2,1,128,1024]{4,3,2,1,0:T(8,128)(2,1)}, bf16[4,1,2,128,1024]{4,3,2,1,0:T(8,128)(2,1)S(1)}, bf16[4,1,2,128,1024]{4,3,2,1,0:T(8,128)(2,1)}) custom-call(s32[2]{0:T(128)S(1)} %pad_add_fusion.2.where_ref, bf16[688,1024]{1,0:T(8,128)(2,1)S(1)} %constant_dynamic-update-slice_fusion.11.rows_ref.left_ref, ...), custom_call_target="tpu_custom_call" | custom-call | flops 1000 | bytes 1000 | tf_op jit(solution)/shard_map/pallas_call | solution.py:369
  509.3 8.6 %collective-permute-done.52.refs_1_ = bf16[4,2,1,64,1024]{4,3,2,1,0:T(8,128)(2,1)S(1)} collective-permute-done((bf16[4,2,1,64,1024]{4,3,2,1,0:T(8,128)(2,1)}, bf16[4,2,1,64,1024]{4,3,2,1,0:T(8,128)(2,1)S(1)}, u32[]{:S(2)}, u32[]{:S(2)}) %collective-permute-start.52) | collective-permute-done | bytes 1048608 | tf_op jit(solution)/shard_map/ppermute | solution.py:63
  536.6 16.4 %shard_map.315 = (bf16[688,256]{1,0:T(8,128)(2,1)}, bf16[2,688,256]{2,1,0:T(8,128)(2,1)}, bf16[2,688,256]{2,1,0:T(8,128)(2,1)}) custom-call(bf16[688,1536]{1,0:T(8,128)(2,1)} %copy-done.54, bf16[688,1536]{1,0:T(8,128)(2,1)} %copy-done.54, bf16[688,1024]{1,0:T(8,128)(2,1)} %collective-permute-done.14.refs_1_.refs_3_, bf16[688,1536]{1,0:T(8,128)(2,1)} %copy-done.54, ...), custom_call_target="tpu_custom_call" | custom-call | flops 1000 | bytes 1000 | tf_op jit(solution)/shard_map/pallas_call | solution.py:804
  560.3 16.6 %shard_map.317 = (bf16[688,256]{1,0:T(8,128)(2,1)}, bf16[2,688,256]{2,1,0:T(8,128)(2,1)}, bf16[2,688,256]{2,1,0:T(8,128)(2,1)}) custom-call(bf16[688,1536]{1,0:T(8,128)(2,1)} %copy-done.54, bf16[688,1536]{1,0:T(8,128)(2,1)} %copy-done.54, bf16[688,1024]{1,0:T(8,128)(2,1)} %collective-permute-done.14.refs_1_.refs_3_, bf16[688,1536]{1,0:T(8,128)(2,1)} %copy-done.54, ...), custom_call_target="tpu_custom_call" | custom-call | flops 1000 | bytes 1000 | tf_op jit(solution)/shard_map/pallas_call | solution.py:804
  591.7 17.0 %collective-permute-done.62 = bf16[2,688,256]{2,1,0:T(8,128)(2,1)S(1)} collective-permute-done((bf16[2,688,256]{2,1,0:T(8,128)(2,1)}, bf16[2,688,256]{2,1,0:T(8,128)(2,1)S(1)}, u32[]{:S(2)}, u32[]{:S(2)}) %collective-permute-start.62) | collective-permute-done | bytes 704544 | tf_op jit(solution)/shard_map/ppermute | solution.py:63
  631.6 18.0 %collective-permute-done.85 = bf16[1,1,64,2048]{3,2,1,0:T(8,128)(2,1)S(1)} collective-permute-done((bf16[1,1,64,2048]{3,2,1,0:T(8,128)(2,1)S(1)}, bf16[1,1,64,2048]{3,2,1,0:T(8,128)(2,1)S(1)}, u32[]{:S(2)}, u32[]{:S(2)}) %collective-permute-start.85) | collective-permute-done | bytes 262176 | tf_op jit(solution)/shard_map/ppermute | solution.py:63
  660.6 10.7 %collective-permute-done.69 = f32[2,4,1792]{2,1,0:T(4,128)S(1)} collective-permute-done((f32[2,4,1792]{2,1,0:T(4,128)S(1)}, f32[2,4,1792]{2,1,0:T(4,128)S(1)}, u32[]{:S(2)}, u32[]{:S(2)}) %collective-permute-start.69) | collective-permute-done | bytes 57376 | tf_op jit(solution)/shard_map/ppermute | solution.py:63
  693.6 12.1 %collective-permute-done.91 = bf16[1,1,128,2048]{3,2,1,0:T(8,128)(2,1)S(1)} collective-permute-done((bf16[1,1,128,2048]{3,2,1,0:T(8,128)(2,1)S(1)}, bf16[1,1,128,2048]{3,2,1,0:T(8,128)(2,1)S(1)}, u32[]{:S(2)}, u32[]{:S(2)}) %collective-permute-start.91) | collective-permute-done | bytes 524320 | tf_op jit(solution)/shard_map/ppermute | solution.py:63
  712.0 8.9 %collective-permute-done.77 = bf16[1,1,64,2048]{3,2,1,0:T(8,128)(2,1)S(1)} collective-permute-done((bf16[1,1,64,2048]{3,2,1,0:T(8,128)(2,1)S(1)}, bf16[1,1,64,2048]{3,2,1,0:T(8,128)(2,1)S(1)}, u32[]{:S(2)}, u32[]{:S(2)}) %collective-permute-start.77) | collective-permute-done | bytes 262176 | tf_op jit(solution)/shard_map/ppermute | solution.py:63
  744.7 13.3 %collective-permute-done.89 = bf16[192,2048]{1,0:T(8,128)(2,1)S(1)} collective-permute-done((bf16[192,2048]{1,0:T(8,128)(2,1)S(1)}, bf16[192,2048]{1,0:T(8,128)(2,1)S(1)}, u32[]{:S(2)}, u32[]{:S(2)}) %collective-permute-start.89) | collective-permute-done | bytes 786464 | tf_op jit(solution)/shard_map/ppermute | solution.py:63
  (814 shorter events, 340.7 us)
Async XLA Ops:
  27.1 40.3 %collective-permute-start.7 = (bf16[2,64,2048]{2,1,0:T(8,128)(2,1)S(1)}, bf16[2,64,2048]{2,1,0:T(8,128)(2,1)S(1)}, u32[]{:S(2)}, u32[]{:S(2)}) collective-permute-start(bf16[2,64,2048]{2,1,0:T(8,128)(2,1)S(1)} %get-tuple-element.197), channel_id=1, source_target_pairs={{0,2},{1,3},{2,0},{3,1},{4,6},{5,7},{6,4},{7,5},{8,10},{9,11},{10,... | collective-permute-start | bytes 1572872 | tf_op jit(solution)/shard_map/ppermute | solution.py:63
  109.4 54.2 %collective-permute-start.20 = (bf16[4,128,2048]{2,1,0:T(8,128)(2,1)S(1)}, bf16[4,128,2048]{2,1,0:T(8,128)(2,1)S(1)}, u32[]{:S(2)}, u32[]{:S(2)}) collective-permute-start(bf16[4,128,2048]{2,1,0:T(8,128)(2,1)S(1)} %bitcast.310), channel_id=1, source_target_pairs={{0,8},{8,0},{16,24},{24,16},{1,9},{9,1},{17,25},{25,17},{2,10},{10... | collective-permute-start | bytes 6291464 | tf_op jit(solution)/shard_map/ppermute | solution.py:63
  111.1 52.7 %collective-permute-start.21 = (bf16[4,128,2048]{2,1,0:T(8,128)(2,1)S(1)}, bf16[4,128,2048]{2,1,0:T(8,128)(2,1)S(1)}, u32[]{:S(2)}, u32[]{:S(2)}) collective-permute-start(bf16[4,128,2048]{2,1,0:T(8,128)(2,1)S(1)} %bitcast.311), channel_id=1, source_target_pairs={{0,16},{8,24},{16,0},{24,8},{1,17},{9,25},{17,1},{25,9},{2,18},{10... | collective-permute-start | bytes 6291464 | tf_op jit(solution)/shard_map/ppermute | solution.py:63
  194.7 35.1 %collective-permute-start.26 = (bf16[2,128,2048]{2,1,0:T(8,128)(2,1)}, bf16[2,128,2048]{2,1,0:T(8,128)(2,1)}, u32[]{:S(2)}, u32[]{:S(2)}) collective-permute-start(bf16[2,128,2048]{2,1,0:T(8,128)(2,1)} %get-tuple-element.222), channel_id=1, source_target_pairs={{0,2},{1,3},{2,0},{3,1},{4,6},{5,7},{6,4},{7,5},{8,10},{9,11},{10,... | collective-permute-start | bytes 3145736 | tf_op jit(solution)/shard_map/ppermute | solution.py:63
  196.7 33.2 %collective-permute-start.24 = (bf16[4,64,2048]{2,1,0:T(8,128)(2,1)}, bf16[4,64,2048]{2,1,0:T(8,128)(2,1)}, u32[]{:S(2)}, u32[]{:S(2)}) collective-permute-start(bf16[4,64,2048]{2,1,0:T(8,128)(2,1)} %bitcast.65.refs_0_), channel_id=1, source_target_pairs={{0,8},{8,0},{16,24},{24,16},{1,9},{9,1},{17,25},{25,17},{2,10},{10... | collective-permute-start | bytes 3145736 | tf_op jit(solution)/shard_map/ppermute | solution.py:63
  198.2 31.7 %collective-permute-start.25 = (bf16[4,64,2048]{2,1,0:T(8,128)(2,1)}, bf16[4,64,2048]{2,1,0:T(8,128)(2,1)}, u32[]{:S(2)}, u32[]{:S(2)}) collective-permute-start(bf16[4,64,2048]{2,1,0:T(8,128)(2,1)} %bitcast.65.refs_0_), channel_id=1, source_target_pairs={{0,16},{8,24},{16,0},{24,8},{1,17},{9,25},{17,1},{25,9},{2,18},{10... | collective-permute-start | bytes 3145736 | tf_op jit(solution)/shard_map/ppermute | solution.py:63
  259.9 32.2 %collective-permute-start.31 = (bf16[688,1024]{1,0:T(8,128)(2,1)S(1)}, bf16[688,1024]{1,0:T(8,128)(2,1)S(1)}, u32[]{:S(2)}, u32[]{:S(2)}) collective-permute-start(bf16[688,1024]{1,0:T(8,128)(2,1)S(1)} %slice.521), channel_id=1, source_target_pairs={{0,2},{1,3},{2,0},{3,1},{4,6},{5,7},{6,4},{7,5},{8,10},{9,11},{10,... | collective-permute-start | bytes 4227080 | tf_op jit(solution)/shard_map/ppermute | solution.py:63
  263.5 53.4 %collective-permute-start.35 = (bf16[4,128,2048]{2,1,0:T(8,128)(2,1)S(1)}, bf16[4,128,2048]{2,1,0:T(8,128)(2,1)S(1)}, u32[]{:S(2)}, u32[]{:S(2)}) collective-permute-start(bf16[4,128,2048]{2,1,0:T(8,128)(2,1)S(1)} %bitcast.313), channel_id=1, source_target_pairs={{0,8},{8,0},{16,24},{24,16},{1,9},{9,1},{17,25},{25,17},{2,10},{10... | collective-permute-start | bytes 6291464 | tf_op jit(solution)/shard_map/ppermute | solution.py:63
  264.1 54.0 %collective-permute-start.36 = (bf16[4,128,2048]{2,1,0:T(8,128)(2,1)S(1)}, bf16[4,128,2048]{2,1,0:T(8,128)(2,1)S(1)}, u32[]{:S(2)}, u32[]{:S(2)}) collective-permute-start(bf16[4,128,2048]{2,1,0:T(8,128)(2,1)S(1)} %bitcast.314), channel_id=1, source_target_pairs={{0,16},{8,24},{16,0},{24,8},{1,17},{9,25},{17,1},{25,9},{2,18},{10... | collective-permute-start | bytes 6291464 | tf_op jit(solution)/shard_map/ppermute | solution.py:63
  325.0 32.5 %collective-permute-start.34 = (bf16[344,1024]{1,0:T(8,128)(2,1)}, bf16[344,1024]{1,0:T(8,128)(2,1)}, u32[]{:S(2)}, u32[]{:S(2)}) collective-permute-start(bf16[344,1024]{1,0:T(8,128)(2,1)} %add_convert_fusion.7), channel_id=1, source_target_pairs={{0,1},{1,0},{2,3},{3,2},{4,5},{5,4},{6,7},{7,6},{8,9},{9,8},{10,11... | collective-permute-start | bytes 2113544 | tf_op jit(solution)/shard_map/ppermute | solution.py:63
  395.9 50.2 %collective-permute-start.44 = (bf16[4,2,1,128,1024]{4,3,2,1,0:T(8,128)(2,1)}, bf16[4,2,1,128,1024]{4,3,2,1,0:T(8,128)(2,1)}, u32[]{:S(2)}, u32[]{:S(2)}) collective-permute-start(bf16[4,2,1,128,1024]{4,3,2,1,0:T(8,128)(2,1)} %get-tuple-element.244), channel_id=1, source_target_pairs={{0,8},{8,0},{16,24},{24,16},{1,9},{9,1},{17,25},{25,17},{2,10},{10... | collective-permute-start | bytes 6291464 | tf_op jit(solution)/shard_map/ppermute | solution.py:63
  402.9 47.9 %collective-permute-start.45 = (bf16[4,1,2,128,1024]{4,3,2,0,1:T(8,128)(2,1)}, bf16[4,1,2,128,1024]{4,3,2,0,1:T(8,128)(2,1)}, u32[]{:S(2)}, u32[]{:S(2)}) collective-permute-start(bf16[4,1,2,128,1024]{4,3,2,0,1:T(8,128)(2,1)} %bitcast.96), channel_id=1, source_target_pairs={{0,16},{8,24},{16,0},{24,8},{1,17},{9,25},{17,1},{25,9},{2,18},{10... | collective-permute-start | bytes 6291464 | tf_op jit(solution)/shard_map/ppermute | solution.py:63
  484.4 33.5 %collective-permute-start.52 = (bf16[4,2,1,64,1024]{4,3,2,1,0:T(8,128)(2,1)}, bf16[4,2,1,64,1024]{4,3,2,1,0:T(8,128)(2,1)S(1)}, u32[]{:S(2)}, u32[]{:S(2)}) collective-permute-start(bf16[4,2,1,64,1024]{4,3,2,1,0:T(8,128)(2,1)} %get-tuple-element.265), channel_id=1, source_target_pairs={{0,8},{8,0},{16,24},{24,16},{1,9},{9,1},{17,25},{25,17},{2,10},{10... | collective-permute-start | bytes 3145736 | tf_op jit(solution)/shard_map/ppermute | solution.py:63
  485.9 32.0 %collective-permute-start.53 = (bf16[4,1,2,64,1024]{4,3,2,0,1:T(8,128)(2,1)S(1)}, bf16[4,1,2,64,1024]{4,3,2,0,1:T(8,128)(2,1)S(1)}, u32[]{:S(2)}, u32[]{:S(2)}) collective-permute-start(bf16[4,1,2,64,1024]{4,3,2,0,1:T(8,128)(2,1)S(1)} %bitcast.363), channel_id=1, source_target_pairs={{0,16},{8,24},{16,0},{24,8},{1,17},{9,25},{17,1},{25,9},{2,18},{10... | collective-permute-start | bytes 3145736 | tf_op jit(solution)/shard_map/ppermute | solution.py:63
  507.8 72.6 %collective-permute-start.57 = (bf16[4,2,1,128,1024]{4,3,2,1,0:T(8,128)(2,1)}, bf16[4,2,1,128,1024]{4,3,2,1,0:T(8,128)(2,1)}, u32[]{:S(2)}, u32[]{:S(2)}) collective-permute-start(bf16[4,2,1,128,1024]{4,3,2,1,0:T(8,128)(2,1)} %get-tuple-element.280), channel_id=1, source_target_pairs={{0,8},{8,0},{16,24},{24,16},{1,9},{9,1},{17,25},{25,17},{2,10},{10... | collective-permute-start | bytes 6291464 | tf_op jit(solution)/shard_map/ppermute | solution.py:63
  520.2 61.5 %collective-permute-start.58 = (bf16[4,1,2,128,1024]{4,3,2,0,1:T(8,128)(2,1)}, bf16[4,1,2,128,1024]{4,3,2,0,1:T(8,128)(2,1)}, u32[]{:S(2)}, u32[]{:S(2)}) collective-permute-start(bf16[4,1,2,128,1024]{4,3,2,0,1:T(8,128)(2,1)} %bitcast.114), channel_id=1, source_target_pairs={{0,16},{8,24},{16,0},{24,8},{1,17},{9,25},{17,1},{25,9},{2,18},{10... | collective-permute-start | bytes 6291464 | tf_op jit(solution)/shard_map/ppermute | solution.py:63
  555.1 32.0 %collective-permute-start.59 = (bf16[4,1,64,1024]{3,2,1,0:T(8,128)(2,1)}, bf16[4,1,64,1024]{3,2,1,0:T(8,128)(2,1)}, u32[]{:S(2)}, u32[]{:S(2)}) collective-permute-start(bf16[4,1,64,1024]{3,2,1,0:T(8,128)(2,1)} %get-tuple-element.288), channel_id=1, source_target_pairs={{0,16},{8,24},{16,0},{24,8},{1,17},{9,25},{17,1},{25,9},{2,18},{10... | collective-permute-start | bytes 1572872 | tf_op jit(solution)/shard_map/ppermute | solution.py:63
  580.5 44.9 %collective-permute-start.82 = (bf16[1,1,128,2048]{3,2,1,0:T(8,128)(2,1)S(1)}, bf16[1,1,128,2048]{3,2,1,0:T(8,128)(2,1)}, u32[]{:S(2)}, u32[]{:S(2)}) collective-permute-start(bf16[1,1,128,2048]{3,2,1,0:T(8,128)(2,1)S(1)} %copy-done.51), channel_id=1, source_target_pairs={{0,4},{1,5},{2,6},{3,7},{4,0},{5,1},{6,2},{7,3},{8,12},{9,13},{10,... | collective-permute-start | bytes 1572872 | tf_op jit(solution)/shard_map/ppermute | solution.py:63
  585.5 31.8 %collective-permute-start.64 = (bf16[4,1,128,1024]{3,2,1,0:T(8,128)(2,1)S(1)}, bf16[4,1,128,1024]{3,2,1,0:T(8,128)(2,1)S(1)}, u32[]{:S(2)}, u32[]{:S(2)}) collective-permute-start(bf16[4,1,128,1024]{3,2,1,0:T(8,128)(2,1)S(1)} %get-tuple-element.305), channel_id=1, source_target_pairs={{0,8},{8,0},{16,24},{24,16},{1,9},{9,1},{17,25},{25,17},{2,10},{10... | collective-permute-start | bytes 3145736 | tf_op jit(solution)/shard_map/ppermute | solution.py:63
  587.1 31.8 %collective-permute-start.63 = (bf16[4,1,128,1024]{3,2,1,0:T(8,128)(2,1)S(1)}, bf16[4,1,128,1024]{3,2,1,0:T(8,128)(2,1)S(1)}, u32[]{:S(2)}, u32[]{:S(2)}) collective-permute-start(bf16[4,1,128,1024]{3,2,1,0:T(8,128)(2,1)S(1)} %get-tuple-element.304), channel_id=1, source_target_pairs={{0,16},{8,24},{16,0},{24,8},{1,17},{9,25},{17,1},{25,9},{2,18},{10... | collective-permute-start | bytes 3145736 | tf_op jit(solution)/shard_map/ppermute | solution.py:63
  589.0 39.2 %collective-permute-start.84 = (bf16[2,64,2048]{2,1,0:T(8,128)(2,1)S(1)}, bf16[2,64,2048]{2,1,0:T(8,128)(2,1)S(1)}, u32[]{:S(2)}, u32[]{:S(2)}) collective-permute-start(bf16[2,64,2048]{2,1,0:T(8,128)(2,1)S(1)} %get-tuple-element.312), channel_id=1, source_target_pairs={{0,2},{1,3},{2,0},{3,1},{4,6},{5,7},{6,4},{7,5},{8,10},{9,11},{10,... | collective-permute-start | bytes 1572872 | tf_op jit(solution)/shard_map/ppermute | solution.py:63
  617.4 35.7 %collective-permute-start.67 = (bf16[4,2,1,64,1024]{4,3,2,1,0:T(8,128)(2,1)S(1)}, bf16[4,2,1,64,1024]{4,3,2,1,0:T(8,128)(2,1)S(1)}, u32[]{:S(2)}, u32[]{:S(2)}) collective-permute-start(bf16[4,2,1,64,1024]{4,3,2,1,0:T(8,128)(2,1)S(1)} %get-tuple-element.319), channel_id=1, source_target_pairs={{0,8},{8,0},{16,24},{24,16},{1,9},{9,1},{17,25},{25,17},{2,10},{10... | collective-permute-start | bytes 3145736 | tf_op jit(solution)/shard_map/ppermute | solution.py:63
  618.9 34.1 %collective-permute-start.68 = (bf16[4,1,2,64,1024]{4,3,2,0,1:T(8,128)(2,1)S(1)}, bf16[4,1,2,64,1024]{4,3,2,0,1:T(8,128)(2,1)S(1)}, u32[]{:S(2)}, u32[]{:S(2)}) collective-permute-start(bf16[4,1,2,64,1024]{4,3,2,0,1:T(8,128)(2,1)S(1)} %bitcast.362), channel_id=1, source_target_pairs={{0,16},{8,24},{16,0},{24,8},{1,17},{9,25},{17,1},{25,9},{2,18},{10... | collective-permute-start | bytes 3145736 | tf_op jit(solution)/shard_map/ppermute | solution.py:63
  620.9 58.4 %collective-permute-start.90 = (bf16[2,128,2048]{2,1,0:T(8,128)(2,1)}, bf16[2,128,2048]{2,1,0:T(8,128)(2,1)S(1)}, u32[]{:S(2)}, u32[]{:S(2)}) collective-permute-start(bf16[2,128,2048]{2,1,0:T(8,128)(2,1)} %get-tuple-element.326), channel_id=1, source_target_pairs={{0,2},{1,3},{2,0},{3,1},{4,6},{5,7},{6,4},{7,5},{8,10},{9,11},{10,... | collective-permute-start | bytes 3145736 | tf_op jit(solution)/shard_map/ppermute | solution.py:63
  628.2 51.9 %collective-permute-start.83 = (bf16[32,2048]{1,0:T(8,128)(2,1)}, bf16[32,2048]{1,0:T(8,128)(2,1)}, u32[]{:S(2)}, u32[]{:S(2)}) collective-permute-start(bf16[32,2048]{1,0:T(8,128)(2,1)} %get-tuple-element.500), channel_id=1, source_target_pairs={{0,1},{1,0},{2,3},{3,2},{4,5},{5,4},{6,7},{7,6},{8,9},{9,8},{10,11... | collective-permute-start | bytes 393224 | tf_op jit(solution)/shard_map/ppermute | solution.py:63
  681.6 44.7 %collective-permute-start.88 = (bf16[192,2048]{1,0:T(8,128)(2,1)S(1)}, bf16[192,2048]{1,0:T(8,128)(2,1)S(1)}, u32[]{:S(2)}, u32[]{:S(2)}) collective-permute-start(bf16[192,2048]{1,0:T(8,128)(2,1)S(1)} %maximum_maximum_fusion), channel_id=1, source_target_pairs={{0,16},{8,24},{16,0},{24,8},{1,17},{9,25},{17,1},{25,9},{2,18},{10... | collective-permute-start | bytes 2359304 | tf_op jit(solution)/shard_map/ppermute | solution.py:63
  686.8 43.4 %collective-permute-start.87 = (bf16[192,2048]{1,0:T(8,128)(2,1)S(1)}, bf16[192,2048]{1,0:T(8,128)(2,1)S(1)}, u32[]{:S(2)}, u32[]{:S(2)}) collective-permute-start(bf16[192,2048]{1,0:T(8,128)(2,1)S(1)} %maximum_maximum_fusion), channel_id=1, source_target_pairs={{0,8},{8,0},{16,24},{24,16},{1,9},{9,1},{17,25},{25,17},{2,10},{10... | collective-permute-start | bytes 2359304 | tf_op jit(solution)/shard_map/ppermute | solution.py:63
  693.1 31.3 %collective-permute-start.72 = (f32[2,1,1792]{2,0,1:T(2,128)S(1)}, f32[2,1,1792]{2,0,1:T(2,128)S(1)}, u32[]{:S(2)}, u32[]{:S(2)}) collective-permute-start(f32[2,1,1792]{2,0,1:T(2,128)S(1)} %dynamic-slice_add_fusion), channel_id=1, source_target_pairs={{0,8},{8,0},{16,24},{24,16},{1,9},{9,1},{17,25},{25,17},{2,10},{10... | collective-permute-start | bytes 43016 | tf_op jit(solution)/shard_map/ppermute | solution.py:63
  726.3 31.7 %collective-permute-start.89 = (bf16[192,2048]{1,0:T(8,128)(2,1)S(1)}, bf16[192,2048]{1,0:T(8,128)(2,1)S(1)}, u32[]{:S(2)}, u32[]{:S(2)}) collective-permute-start(bf16[192,2048]{1,0:T(8,128)(2,1)S(1)} %collective-permute-done.88), channel_id=1, source_target_pairs={{0,8},{8,0},{16,24},{24,16},{1,9},{9,1},{17,25},{25,17},{2,10},{10... | collective-permute-start | bytes 2359304 | tf_op jit(solution)/shard_map/ppermute | solution.py:63
  729.9 38.2 %collective-permute-start.94 = (bf16[128,2048]{1,0:T(8,128)(2,1)S(1)}, bf16[128,2048]{1,0:T(8,128)(2,1)S(1)}, u32[]{:S(2)}, u32[]{:S(2)}) collective-permute-start(bf16[128,2048]{1,0:T(8,128)(2,1)S(1)} %pad_maximum_fusion.17.refs_0_), channel_id=1, source_target_pairs={{0,16},{8,24},{16,0},{24,8},{1,17},{9,25},{17,1},{25,9},{2,18},{10... | collective-permute-start | bytes 1572872 | tf_op jit(solution)/shard_map/ppermute | solution.py:63
  730.2 33.6 %collective-permute-start.80 = (bf16[64,2048]{1,0:T(8,128)(2,1)S(1)}, bf16[64,2048]{1,0:T(8,128)(2,1)S(1)}, u32[]{:S(2)}, u32[]{:S(2)}) collective-permute-start(bf16[64,2048]{1,0:T(8,128)(2,1)S(1)} %pad_maximum_fusion.18.refs_0_), channel_id=1, source_target_pairs={{0,16},{8,24},{16,0},{24,8},{1,17},{9,25},{17,1},{25,9},{2,18},{10... | collective-permute-start | bytes 786440 | tf_op jit(solution)/shard_map/ppermute | solution.py:63
  735.9 32.1 %collective-permute-start.95 = (bf16[128,2048]{1,0:T(8,128)(2,1)S(1)}, bf16[128,2048]{1,0:T(8,128)(2,1)S(1)}, u32[]{:S(2)}, u32[]{:S(2)}) collective-permute-start(bf16[128,2048]{1,0:T(8,128)(2,1)S(1)} %collective-permute-done.93.refs_1_), channel_id=1, source_target_pairs={{0,16},{8,24},{16,0},{24,8},{1,17},{9,25},{17,1},{25,9},{2,18},{10... | collective-permute-start | bytes 1572872 | tf_op jit(solution)/shard_map/ppermute | solution.py:63
  (259 other events, 3129.7 us)

commit v3 on v2

--- a/solution.py
+++ b/solution.py
@@ -277,8 +277,8 @@
     return lax.dynamic_slice_in_dim(param, lax.axis_index("rep") * rows, rows, 0)
 
 
-def gather_small(all_params, token):
-    packed = after(jnp.concatenate([all_params[i] for i in SMALL], 1), token)
+def gather_small(all_params):
+    packed = jnp.concatenate([all_params[i] for i in SMALL], 1)
     whole, owner, step = packed[None], lax.axis_index("fsdp"), 1
     while step < lax.axis_size("fsdp"):
         got = swap(whole, "fsdp", step)
@@ -295,7 +295,7 @@
             jnp.moveaxis(whole[:, :, start : start + size], 0, 1).reshape(LAYERS, -1)
         )
         start += size
-    return vectors
+    return vectors, got
 
 
 def link_orders():
@@ -940,7 +940,9 @@
     return projected, share_rows(after(projected[:, width // 2 :], token))[1:]
 
 
-def forward_layer(tok_rows, normed, projected, others, gathered, beside, neighbours, planes):
+def forward_layer(
+    tok_rows, normed, projected, others, gathered, beside, neighbours, following
+):
     (
         attn_norm_gain,
         attn_norm_bias,
@@ -965,11 +967,11 @@
     branch = forward_dot(attended[:tokens], output_weight) + widen(got) + widen(output_bias)
     middle = tok_rows + widen(attn_layerscale) * branch
     normed_two = low(layer_norm(middle, widen(mlp_norm_gain), widen(mlp_norm_bias)))
-    normed_two = both_cores(after(normed_two, *planes[:1]))
+    normed_two = after(both_cores(normed_two), *neighbours)
     activated, slope, own_sum, other_sum = feed_forward(
         normed_two, expand_weight, core_half(expand_bias), shrink_weight
     )
-    other_sum = after(other_sum, *neighbours, *planes[1:])
+    other_sum = after(other_sum, *following)
     mlp_out = own_sum + widen(swap(other_sum, "fsdp", 1)) + widen(shrink_bias)
     result = middle + widen(mlp_layerscale) * mlp_out
     saved = (
@@ -1069,10 +1071,6 @@
     own_sum = later.sent(own_sum, block)
     if not old:
         own_sum = after(own_sum, activation_got)
-    if old:
-        own_sum = later.came(own_sum, old[1])
-        later.step(old[1], own_sum)
-        own_sum = later.sent(own_sum, old[1])
     d_middle_norm, g_mlp_gain, g_mlp_shift = norm_back(
         middle, widen(mlp_norm_gain), widen(mlp_norm_bias), own_sum + widen(got)
     )
@@ -1082,6 +1080,9 @@
     g_attn_scale = jnp.sum(d_middle * branch, 0)
     g_output_bias = column_sum(d_branch)
     d_attended = low(input_dot(d_branch_both, output_weight))
+    if old:
+        later.step(old[1], d_attended)
+        d_attended = later.sent(d_attended, old[1])
     pairs = d_attended.shape[1] // 128
 
     def back(first):
@@ -1101,10 +1102,6 @@
     second_query = later.came(second_query, block)
     later.step(block, second_query)
     second_query = later.sent(second_query, block)
-    if old:
-        second_query = later.came(second_query, old[1])
-        later.join(old[3], [old[1]], second_query)
-        second_query = later.sent(second_query, old[3])
     d_query = jnp.concatenate([first_query, second_query], 1)
     d_key = jnp.concatenate([first_kv[0], second_kv[0]], 1)
     d_value = jnp.concatenate([first_kv[1], second_kv[1]], 1)
@@ -1115,6 +1112,8 @@
     later.begin(mixed, mixed_grad, (normed, d_projected, attended, d_branch_both))
     d_projected = later.sent(d_projected, mixed)
     if old:
+        later.join(old[3], [old[1]], d_projected)
+        d_projected = later.sent(d_projected, old[3])
         later.join(block_planes, [block], d_projected)
         d_projected = later.sent(d_projected, block_planes)
     d_normed = input_dot(d_projected[:tokens], heads_weight) + widen(got)
@@ -1141,20 +1140,21 @@
 def local(images, cotangent, *all_params):
     owners, count = lax.axis_size("fsdp"), lax.axis_size("rep")
     pieces = message_pieces(all_params)
-    column, planes = gather_planes(pieces[0])
+    small, small_got = gather_small(all_params)
+    column, planes = gather_planes(pieces[0], beside=[small_got])
     own, got = regroup(after(images, planes[0]))
     tok_rows = widen(jnp.concatenate([own, got], 0))
     column = after(column, got)
     next_column, next_planes = gather_planes(pieces[1], got)
-    small = gather_small(all_params, got)
     held, neighbours = gather_neighbours(column, [])
+    members = gather_members(held, [])
     saved_layers, fetched = [], []
     for layer in range(LAYERS):
         gathered = [None] * len(all_params)
         for i, vector in zip(SMALL, small):
             gathered[i] = vector[layer]
         normed = normed_rows(tok_rows, gathered)
-        arrays, parts, earlier = gather_members(held, [])
+        arrays, parts, earlier = members
         arrays[0] = after(arrays[0], next_planes[-1])
         gathered[2], gathered[5] = place_first(
             arrays, parts, count, all_params[2].shape[2] // 2
@@ -1167,16 +1167,24 @@
         else:
             own, got = regroup(after(cotangent, others[-1]))
             d_rows = widen(jnp.concatenate([own, got], 0))
-            beside, planes, neighbours, next_planes = [got], [], [], []
+            beside, planes, neighbours, next_planes, members = [got], [], [], [], [[]] * 3
         arrays, parts, earlier = gather_members(held, [])
-        arrays[0] = after(arrays[0], *planes[-1:])
         if layer + 1 < LAYERS:
             next_column, next_planes = gather_planes(pieces[2 * layer + 3], planes[-1])
             held, neighbours = gather_neighbours(column, earlier)
+            members = gather_members(held, [])
+        arrays[0] = after(arrays[0], *planes[-1:], *next_planes[:1])
         gathered[10], gathered[12] = place_second(arrays, parts, count)
         fetched.append(tuple(gathered))
         tok_rows, saved = forward_layer(
-            tok_rows, normed, projected, others, gathered, beside, neighbours, next_planes
+            tok_rows,
+            normed,
+            projected,
+            others,
+            gathered,
+            beside,
+            neighbours,
+            next_planes[1:] + members[2],
         )
         saved_layers.append(saved)
     activation_rows = low(tok_rows)
@@ -1228,19 +1236,19 @@
     pieces = spread(later.sent(first, new[1]), True)
     write_block(layer + 1, [piece[:rows] for piece in pieces])
     write_mixed(layer + 1, [piece[rows:] for piece in pieces])
-    last_sends = later.sends[new[1]]
+    last_gots = later.gots[new[1]] + [image_got]
     later.join(new[3], [new[1]], d_rows)
     while new[3] in later.running:
         later.step(new[3], d_rows)
     while new[2] in later.running:
-        later.step(new[2], image_got)
+        later.step(new[2], d_rows)
     write_block(layer, spread(block_piece(later, layer), False))
     write_mixed(layer, spread(mixed_piece(later, layer), False))
     stacked = [None] * len(all_params)
     for i, out in zip((10, 12, 2, 5), list(outs["block"]) + list(outs["mixed"])):
         stacked[i] = out.reshape(all_params[i].shape)
     reduced = reduce_small(
-        [jnp.stack([grads[n] for grads in small_grads]) for n in range(len(SMALL))], last_sends
+        [jnp.stack([grads[n] for grads in small_grads]) for n in range(len(SMALL))], last_gots
     )
     for i, vector in zip(SMALL, reduced):
         stacked[i] = vector

time: 782 us -> 845 us (1.081)
  waiting for transfers between devices: 318 us -> 355 us
  local copies, waits for them, and re-layouts: 69 us -> 85.2 us
    ppermute x96, waiting for transfers between devices: 318 us -> 355 us  [swap(): return lax.ppermute(tensor, axis, [(i, i ^ offset) for i in range(count)])]
    unnamed x411 -> x484, local copies, waits for them, and re-layouts: 42.7 us -> 55.7 us
  transfers between devices with their start and end apart: 96 -> 96, of which waited for: 42 -> 44; matrix products, arithmetic and copies ran while one was open for 12% -> 11% of each run, Pallas kernels for 26% -> 24%
where the time goes in v3:
time: 845 us; the launch traced here: 835 us
  waiting for transfers between devices  355 us (42%)
  Pallas kernels  227 us (27%)
  starting transfers between devices  91 us (11%)
  local copies, waits for them, and re-layouts  85.2 us (10%)
  other arithmetic  45.2 us (5%)
  matrix products  26.6 us (3%)
    ppermute x96, waiting for transfers between devices, swap(): return lax.ppermute(tensor, axis, [(i, i ^ offset) for i in range(count)])  355 us
    ppermute x96, starting transfers between devices, swap(): return lax.ppermute(tensor, axis, [(i, i ^ offset) for i in range(count)])  91 us
    pallas_call x4, Pallas kernels, attend_back(): pl.pallas_call(functools.partial(attend_back_kernel, scale * math.log2(ma...  65.5 us
    unnamed x484, local copies, waits for them, and re-layouts  55.7 us
    pallas_call x2, Pallas kernels, attend(): pl.pallas_call(functools.partial(attend_kernel, factor, len(parts)), out_...  36.8 us
    pallas_call x4, Pallas kernels, grad_call(): pl.pallas_call(functools.partial(kernel, shapes), out_shape=out_shapes, g...  33.2 us
    pallas_call x4, Pallas kernels, place(): pl.pallas_call(functools.partial(place_kernel, pieces[0].shape[1] // 2, b...  22.1 us
    pallas_call x2, Pallas kernels, feed_forward(): pl.pallas_call(expand_kernel, out_shape=[jax.ShapeDtypeStruct((tokens, un...  19.6 us
  transfers between devices with their start and end apart: 96, of which 44 were waited for; matrix products, arithmetic and copies ran while one was open for 11% of the time, Pallas kernels for 24%

profile of v3, /device:TPU:0, one launch (start us, length us, event | category | flops | bytes accessed | tf_op | source)
XLA Modules:
  0.0 834.9 jit_solution(271971833298450264)
XLA Ops:
  24.2 9.1 %collective-permute-done.1 = bf16[1,64,2048]{2,1,0:T(8,128)(2,1)S(1)} collective-permute-done((bf16[1,64,2048]{2,1,0:T(8,128)(2,1)S(1)}, bf16[1,64,2048]{2,1,0:T(8,128)(2,1)S(1)}, u32[]{:S(2)}, u32[]{:S(2)}) %collective-permute-start.1) | collective-permute-done | bytes 262176 | tf_op jit(solution)/shard_map/ppermute | solution.py:63
  38.4 13.7 %collective-permute-done.2 = bf16[172,1024]{1,0:T(8,128)(2,1)S(1)} collective-permute-done((bf16[172,1024]{1,0:T(8,128)(2,1)S(1)}, bf16[172,1024]{1,0:T(8,128)(2,1)S(1)}, u32[]{:S(2)}, u32[]{:S(2)}) %collective-permute-start.2) | collective-permute-done | bytes 352288 | tf_op jit(solution)/shard_map/ppermute | solution.py:63
  61.1 16.0 %collective-permute-done.8 = bf16[1,128,2048]{2,1,0:T(8,128)(2,1)S(1)} collective-permute-done((bf16[1,128,2048]{2,1,0:T(8,128)(2,1)S(1)}, bf16[1,128,2048]{2,1,0:T(8,128)(2,1)S(1)}, u32[]{:S(2)}, u32[]{:S(2)}) %collective-permute-start.8) | collective-permute-done | bytes 524320 | tf_op jit(solution)/shard_map/ppermute | solution.py:63
  83.8 17.3 %collective-permute-done.9 = bf16[2,128,2048]{2,1,0:T(8,128)(2,1)S(1)} collective-permute-done((bf16[2,128,2048]{2,1,0:T(8,128)(2,1)S(1)}, bf16[2,128,2048]{2,1,0:T(8,128)(2,1)S(1)}, u32[]{:S(2)}, u32[]{:S(2)}) %collective-permute-start.9) | collective-permute-done | bytes 1048608 | tf_op jit(solution)/shard_map/ppermute | solution.py:63
  112.4 25.3 %collective-permute-done.14.refs_1_.refs_3_ = bf16[688,1024]{1,0:T(8,128)(2,1)} collective-permute-done((bf16[688,1024]{1,0:T(8,128)(2,1)S(1)}, bf16[688,1024]{1,0:T(8,128)(2,1)}, u32[]{:S(2)}, u32[]{:S(2)}) %collective-permute-start.14) | collective-permute-done | bytes 1409056 | tf_op jit(solution)/shard_map/ppermute | solution.py:63
  140.8 18.3 %shard_map.298 = (bf16[688,512]{1,0:T(8,128)(2,1)}, f32[688,512]{1,0:T(8,128)}) custom-call(bf16[688,1536]{1,0:T(8,128)(2,1)} %copy-done.82, bf16[688,1536]{1,0:T(8,128)(2,1)} %copy-done.82, bf16[688,1024]{1,0:T(8,128)(2,1)} %collective-permute-done.14.refs_1_.refs_3_, bf16[688,1536]{1,0:T(8,128)(2,1)} %copy-done.82, ...), custom_call_target="tpu_custom_call" | custom-call | flops 1000 | bytes 1000 | tf_op jit(solution)/shard_map/pallas_call | solution.py:760
  175.3 13.4 %collective-permute-done.22.refs_4_ = bf16[4,64,2048]{2,1,0:T(8,128)(2,1)S(1)} collective-permute-done((bf16[4,64,2048]{2,1,0:T(8,128)(2,1)S(1)}, bf16[4,64,2048]{2,1,0:T(8,128)(2,1)S(1)}, u32[]{:S(2)}, u32[]{:S(2)}) %collective-permute-start.22) | collective-permute-done | bytes 1048608 | tf_op jit(solution)/shard_map/ppermute | solution.py:63
  196.9 18.7 %collective-permute-done.23.refs_1_ = bf16[4,64,2048]{2,1,0:T(8,128)(2,1)S(1)} collective-permute-done((bf16[4,64,2048]{2,1,0:T(8,128)(2,1)S(1)}, bf16[4,64,2048]{2,1,0:T(8,128)(2,1)S(1)}, u32[]{:S(2)}, u32[]{:S(2)}) %collective-permute-start.23) | collective-permute-done | bytes 1048608 | tf_op jit(solution)/shard_map/ppermute | solution.py:63
  231.2 8.1 shard_map.299
  239.4 9.8 %shard_map.300 = (bf16[688,2048]{1,0:T(8,128)(2,1)S(1)}, bf16[688,2048]{1,0:T(8,128)(2,1)S(1)}, f32[344,1024]{1,0:T(8,128)S(1)}, bf16[344,1024]{1,0:T(8,128)(2,1)S(1)}) custom-call(bf16[688,1024]{1,0:T(8,128)(2,1)S(1)} %pad_maximum_fusion.3.rows_ref.left_ref, bf16[1024,2048]{1,0:T(8,128)(2,1)S(1)} %bitcast.302, f32[1,2048]{1,0:T(1,128)S(1)} %bitcast.355, ...), custom_call_target="tpu_custom_call" | custom-call | flops 1000 | bytes 1000 | tf_op jit(solution)/shard_map/pallas_call | solution.py:859
  267.6 29.3 %collective-permute-done.31.refs_1_.refs_3_ = bf16[688,1024]{1,0:T(8,128)(2,1)S(1)} collective-permute-done((bf16[688,1024]{1,0:T(8,128)(2,1)S(1)}, bf16[688,1024]{1,0:T(8,128)(2,1)S(1)}, u32[]{:S(2)}, u32[]{:S(2)}) %collective-permute-start.31) | collective-permute-done | bytes 1409056 | tf_op jit(solution)/shard_map/ppermute | solution.py:63
  298.1 18.5 %shard_map.302 = (bf16[688,512]{1,0:T(8,128)(2,1)}, f32[688,512]{1,0:T(8,128)}) custom-call(bf16[688,1536]{1,0:T(8,128)(2,1)} %copy-done.83, bf16[688,1536]{1,0:T(8,128)(2,1)} %copy-done.83, bf16[688,1024]{1,0:T(8,128)(2,1)} %copy-done.87, bf16[688,1536]{1,0:T(8,128)(2,1)} %copy-done.83, bf16[688,1024]{1,0:T(8,128)(2,1)} %copy-done.87), custom_call_target="tpu_custom_call" | custom-call | flops 1000 | bytes 1000 | tf_op jit(solution)/shard_map/pallas_call | solution.py:760
  328.1 17.4 %collective-permute-done.38.refs_4_ = bf16[4,64,2048]{2,1,0:T(8,128)(2,1)} collective-permute-done((bf16[4,64,2048]{2,1,0:T(8,128)(2,1)}, bf16[4,64,2048]{2,1,0:T(8,128)(2,1)}, u32[]{:S(2)}, u32[]{:S(2)}) %collective-permute-start.38) | collective-permute-done | bytes 1048608 | tf_op jit(solution)/shard_map/ppermute | solution.py:63
  351.6 7.8 shard_map.303
  359.6 9.8 %shard_map.304 = (bf16[688,2048]{1,0:T(8,128)(2,1)S(1)}, bf16[688,2048]{1,0:T(8,128)(2,1)S(1)}, f32[344,1024]{1,0:T(8,128)S(1)}, bf16[344,1024]{1,0:T(8,128)(2,1)S(1)}) custom-call(bf16[688,1024]{1,0:T(8,128)(2,1)S(1)} %pad_maximum_fusion.5.rows_ref.left_ref, bf16[1024,2048]{1,0:T(8,128)(2,1)S(1)} %bitcast.306, f32[1,2048]{1,0:T(1,128)S(1)} %bitcast.354, ...), custom_call_target="tpu_custom_call" | custom-call | flops 1000 | bytes 1000 | tf_op jit(solution)/shard_map/pallas_call | solution.py:859
  375.1 9.7 %shard_map.305 = (bf16[688,2048]{1,0:T(8,128)(2,1)S(1)}, f32[1,2048]{1,0:T(1,128)S(1)}, f32[344,1024]{1,0:T(8,128)S(1)}, bf16[344,1024]{1,0:T(8,128)(2,1)}) custom-call(bf16[688,1024]{1,0:T(8,128)(2,1)S(1)} %pad_maximum_fusion.6.grad_ref.other_ref, bf16[2048,1024]{1,0:T(8,128)(2,1)S(1)} %bitcast.309, bf16[688,2048]{1,0:T(8,128)(2,1)S(1)} %get-tuple-element.236.slope_ref, ...), custom_call_target="tpu_custom_call" | custom-call | flops 1000 | bytes 1000 | tf_op jit(solution)/shard_map/pallas_call | solution.py:897
  394.8 10.7 %shard_map.306 = (bf16[4,2,1,128,1024]{4,3,2,1,0:T(8,128)(2,1)S(1)}, bf16[4,2,1,128,1024]{4,3,2,1,0:T(8,128)(2,1)}, bf16[4,1,2,128,1024]{4,3,2,1,0:T(8,128)(2,1)S(1)}, bf16[4,1,2,128,1024]{4,3,2,1,0:T(8,128)(2,1)}) custom-call(s32[2]{0:T(128)S(1)} %pad_add_fusion.2.where_ref, bf16[688,1024]{1,0:T(8,128)(2,1)S(1)} %copy-done.5, ...), custom_call_target="tpu_custom_call" | custom-call | flops 1000 | bytes 1000 | tf_op jit(solution)/shard_map/pallas_call | solution.py:369
  419.0 16.2 %shard_map.307 = (bf16[688,256]{1,0:T(8,128)(2,1)}, bf16[2,688,256]{2,1,0:T(8,128)(2,1)}, bf16[2,688,256]{2,1,0:T(8,128)(2,1)}) custom-call(bf16[688,1536]{1,0:T(8,128)(2,1)} %copy-done.83, bf16[688,1536]{1,0:T(8,128)(2,1)} %copy-done.83, bf16[688,1024]{1,0:T(8,128)(2,1)} %copy-done.87, bf16[688,1536]{1,0:T(8,128)(2,1)} %copy-done.83, ...), custom_call_target="tpu_custom_call" | custom-call | flops 1000 | bytes 1000 | tf_op jit(solution)/shard_map/pallas_call | solution.py:804
  435.3 16.4 %shard_map.308 = (bf16[688,256]{1,0:T(8,128)(2,1)}, bf16[2,688,256]{2,1,0:T(8,128)(2,1)}, bf16[2,688,256]{2,1,0:T(8,128)(2,1)}) custom-call(bf16[688,1536]{1,0:T(8,128)(2,1)} %copy-done.83, bf16[688,1536]{1,0:T(8,128)(2,1)} %copy-done.83, bf16[688,1024]{1,0:T(8,128)(2,1)} %copy-done.87, bf16[688,1536]{1,0:T(8,128)(2,1)} %copy-done.83, ...), custom_call_target="tpu_custom_call" | custom-call | flops 1000 | bytes 1000 | tf_op jit(solution)/shard_map/pallas_call | solution.py:804
  463.5 7.0 collective-permute-done.47
  478.1 6.2 shard_map.310
  495.7 8.7 %shard_map.311 = (bf16[688,2048]{1,0:T(8,128)(2,1)S(1)}, f32[1,2048]{1,0:T(1,128)S(1)}, f32[344,1024]{1,0:T(8,128)S(1)}, bf16[344,1024]{1,0:T(8,128)(2,1)S(1)}) custom-call(bf16[688,1024]{1,0:T(8,128)(2,1)S(1)} %pad_maximum_fusion.8.grad_ref.other_ref, bf16[2048,1024]{1,0:T(8,128)(2,1)S(1)} %bitcast.305, bf16[688,2048]{1,0:T(8,128)(2,1)S(1)} %copy-done.32, ...), custom_call_target="tpu_custom_call" | custom-call | flops 1000 | bytes 1000 | tf_op jit(solution)/shard_map/pallas_call | solution.py:897
  505.1 11.1 %shard_map.313 = (bf16[4,2,1,128,1024]{4,3,2,1,0:T(8,128)(2,1)S(1)}, bf16[4,2,1,128,1024]{4,3,2,1,0:T(8,128)(2,1)}, bf16[4,1,2,128,1024]{4,3,2,1,0:T(8,128)(2,1)S(1)}, bf16[4,1,2,128,1024]{4,3,2,1,0:T(8,128)(2,1)}) custom-call(s32[2]{0:T(128)S(1)} %pad_add_fusion.2.where_ref, bf16[688,1024]{1,0:T(8,128)(2,1)S(1)} %pad_maximum_fusion.3.rows_ref.left_ref, ...), custom_call_target="tpu_custom_call" | custom-call | flops 1000 | bytes 1000 | tf_op jit(solution)/shard_map/pallas_call | solution.py:369
  540.3 55.1 %collective-permute-done.55 = bf16[4,1,2,64,1024]{4,3,2,0,1:T(8,128)(2,1)} collective-permute-done((bf16[4,1,2,64,1024]{4,3,2,0,1:T(8,128)(2,1)}, bf16[4,1,2,64,1024]{4,3,2,0,1:T(8,128)(2,1)}, u32[]{:S(2)}, u32[]{:S(2)}) %collective-permute-start.55) | collective-permute-done | bytes 1048608 | tf_op jit(solution)/shard_map/ppermute | solution.py:63
  601.8 16.4 %shard_map.315 = (bf16[688,256]{1,0:T(8,128)(2,1)}, bf16[2,688,256]{2,1,0:T(8,128)(2,1)}, bf16[2,688,256]{2,1,0:T(8,128)(2,1)}) custom-call(bf16[688,1536]{1,0:T(8,128)(2,1)} %copy-done.82, bf16[688,1536]{1,0:T(8,128)(2,1)} %copy-done.82, bf16[688,1024]{1,0:T(8,128)(2,1)} %collective-permute-done.14.refs_1_.refs_3_, bf16[688,1536]{1,0:T(8,128)(2,1)} %copy-done.82, ...), custom_call_target="tpu_custom_call" | custom-call | flops 1000 | bytes 1000 | tf_op jit(solution)/shard_map/pallas_call | solution.py:804
  626.5 16.4 %shard_map.317 = (bf16[688,256]{1,0:T(8,128)(2,1)}, bf16[2,688,256]{2,1,0:T(8,128)(2,1)}, bf16[2,688,256]{2,1,0:T(8,128)(2,1)}) custom-call(bf16[688,1536]{1,0:T(8,128)(2,1)} %copy-done.82, bf16[688,1536]{1,0:T(8,128)(2,1)} %copy-done.82, bf16[688,1024]{1,0:T(8,128)(2,1)} %collective-permute-done.14.refs_1_.refs_3_, bf16[688,1536]{1,0:T(8,128)(2,1)} %copy-done.82, ...), custom_call_target="tpu_custom_call" | custom-call | flops 1000 | bytes 1000 | tf_op jit(solution)/shard_map/pallas_call | solution.py:804
  684.0 10.9 %collective-permute-done.82 = bf16[1,1,128,2048]{3,2,1,0:T(8,128)(2,1)S(1)} collective-permute-done((bf16[1,1,128,2048]{3,2,1,0:T(8,128)(2,1)S(1)}, bf16[1,1,128,2048]{3,2,1,0:T(8,128)(2,1)S(1)}, u32[]{:S(2)}, u32[]{:S(2)}) %collective-permute-start.82) | collective-permute-done | bytes 524320 | tf_op jit(solution)/shard_map/ppermute | solution.py:63
  708.2 14.0 %collective-permute-done.85 = bf16[1,1,64,2048]{3,2,1,0:T(8,128)(2,1)S(1)} collective-permute-done((bf16[1,1,64,2048]{3,2,1,0:T(8,128)(2,1)S(1)}, bf16[1,1,64,2048]{3,2,1,0:T(8,128)(2,1)S(1)}, u32[]{:S(2)}, u32[]{:S(2)}) %collective-permute-start.85) | collective-permute-done | bytes 262176 | tf_op jit(solution)/shard_map/ppermute | solution.py:63
  722.2 7.3 collective-permute-done.66
  750.4 18.6 %collective-permute-done.91 = bf16[1,1,128,2048]{3,2,1,0:T(8,128)(2,1)S(1)} collective-permute-done((bf16[1,1,128,2048]{3,2,1,0:T(8,128)(2,1)S(1)}, bf16[1,1,128,2048]{3,2,1,0:T(8,128)(2,1)S(1)}, u32[]{:S(2)}, u32[]{:S(2)}) %collective-permute-start.91) | collective-permute-done | bytes 524320 | tf_op jit(solution)/shard_map/ppermute | solution.py:63
  772.8 12.9 %collective-permute-done.77 = bf16[1,1,64,2048]{3,2,1,0:T(8,128)(2,1)S(1)} collective-permute-done((bf16[1,1,64,2048]{3,2,1,0:T(8,128)(2,1)S(1)}, bf16[1,1,64,2048]{3,2,1,0:T(8,128)(2,1)S(1)}, u32[]{:S(2)}, u32[]{:S(2)}) %collective-permute-start.77) | collective-permute-done | bytes 262176 | tf_op jit(solution)/shard_map/ppermute | solution.py:63
  808.9 13.9 %collective-permute-done.89 = bf16[192,2048]{1,0:T(8,128)(2,1)S(1)} collective-permute-done((bf16[192,2048]{1,0:T(8,128)(2,1)S(1)}, bf16[192,2048]{1,0:T(8,128)(2,1)S(1)}, u32[]{:S(2)}, u32[]{:S(2)}) %collective-permute-start.89) | collective-permute-done | bytes 786464 | tf_op jit(solution)/shard_map/ppermute | solution.py:63
  (883 shorter events, 346.5 us)
Async XLA Ops:
  106.9 30.8 %collective-permute-start.14 = (bf16[688,1024]{1,0:T(8,128)(2,1)S(1)}, bf16[688,1024]{1,0:T(8,128)(2,1)}, u32[]{:S(2)}, u32[]{:S(2)}) collective-permute-start(bf16[688,1024]{1,0:T(8,128)(2,1)S(1)} %slice.495), channel_id=1, source_target_pairs={{0,2},{1,3},{2,0},{3,1},{4,6},{5,7},{6,4},{7,5},{8,10},{9,11},{10,... | collective-permute-start | bytes 4227080 | tf_op jit(solution)/shard_map/ppermute | solution.py:63
  108.5 54.5 %collective-permute-start.20 = (bf16[4,128,2048]{2,1,0:T(8,128)(2,1)S(1)}, bf16[4,128,2048]{2,1,0:T(8,128)(2,1)S(1)}, u32[]{:S(2)}, u32[]{:S(2)}) collective-permute-start(bf16[4,128,2048]{2,1,0:T(8,128)(2,1)S(1)} %bitcast.310), channel_id=1, source_target_pairs={{0,8},{8,0},{16,24},{24,16},{1,9},{9,1},{17,25},{25,17},{2,10},{10... | collective-permute-start | bytes 6291464 | tf_op jit(solution)/shard_map/ppermute | solution.py:63
  110.1 53.0 %collective-permute-start.19 = (bf16[4,128,2048]{2,1,0:T(8,128)(2,1)S(1)}, bf16[4,128,2048]{2,1,0:T(8,128)(2,1)S(1)}, u32[]{:S(2)}, u32[]{:S(2)}) collective-permute-start(bf16[4,128,2048]{2,1,0:T(8,128)(2,1)S(1)} %bitcast.311), channel_id=1, source_target_pairs={{0,16},{8,24},{16,0},{24,8},{1,17},{9,25},{17,1},{25,9},{2,18},{10... | collective-permute-start | bytes 6291464 | tf_op jit(solution)/shard_map/ppermute | solution.py:63
  196.5 54.4 %collective-permute-start.26 = (bf16[2,128,2048]{2,1,0:T(8,128)(2,1)}, bf16[2,128,2048]{2,1,0:T(8,128)(2,1)}, u32[]{:S(2)}, u32[]{:S(2)}) collective-permute-start(bf16[2,128,2048]{2,1,0:T(8,128)(2,1)} %get-tuple-element.218), channel_id=1, source_target_pairs={{0,2},{1,3},{2,0},{3,1},{4,6},{5,7},{6,4},{7,5},{8,10},{9,11},{10,... | collective-permute-start | bytes 3145736 | tf_op jit(solution)/shard_map/ppermute | solution.py:63
  216.8 34.1 %collective-permute-start.28 = (bf16[4,32,2048]{2,1,0:T(8,128)(2,1)}, bf16[4,32,2048]{2,1,0:T(8,128)(2,1)}, u32[]{:S(2)}, u32[]{:S(2)}) collective-permute-start(bf16[4,32,2048]{2,1,0:T(8,128)(2,1)} %slice.513), channel_id=1, source_target_pairs={{0,16},{8,24},{16,0},{24,8},{1,17},{9,25},{17,1},{25,9},{2,18},{10... | collective-permute-start | bytes 1572872 | tf_op jit(solution)/shard_map/ppermute | solution.py:63
  220.2 30.7 %collective-permute-start.27 = (bf16[4,32,2048]{2,1,0:T(8,128)(2,1)}, bf16[4,32,2048]{2,1,0:T(8,128)(2,1)}, u32[]{:S(2)}, u32[]{:S(2)}) collective-permute-start(bf16[4,32,2048]{2,1,0:T(8,128)(2,1)} %slice.512), channel_id=1, source_target_pairs={{0,8},{8,0},{16,24},{24,16},{1,9},{9,1},{17,25},{25,17},{2,10},{10... | collective-permute-start | bytes 1572872 | tf_op jit(solution)/shard_map/ppermute | solution.py:63
  263.9 32.9 %collective-permute-start.31 = (bf16[688,1024]{1,0:T(8,128)(2,1)S(1)}, bf16[688,1024]{1,0:T(8,128)(2,1)S(1)}, u32[]{:S(2)}, u32[]{:S(2)}) collective-permute-start(bf16[688,1024]{1,0:T(8,128)(2,1)S(1)} %slice.521), channel_id=1, source_target_pairs={{0,2},{1,3},{2,0},{3,1},{4,6},{5,7},{6,4},{7,5},{8,10},{9,11},{10,... | collective-permute-start | bytes 4227080 | tf_op jit(solution)/shard_map/ppermute | solution.py:63
  266.2 52.1 %collective-permute-start.35 = (bf16[4,128,2048]{2,1,0:T(8,128)(2,1)S(1)}, bf16[4,128,2048]{2,1,0:T(8,128)(2,1)S(1)}, u32[]{:S(2)}, u32[]{:S(2)}) collective-permute-start(bf16[4,128,2048]{2,1,0:T(8,128)(2,1)S(1)} %bitcast.313), channel_id=1, source_target_pairs={{0,8},{8,0},{16,24},{24,16},{1,9},{9,1},{17,25},{25,17},{2,10},{10... | collective-permute-start | bytes 6291464 | tf_op jit(solution)/shard_map/ppermute | solution.py:63
  267.1 52.4 %collective-permute-start.36 = (bf16[4,128,2048]{2,1,0:T(8,128)(2,1)S(1)}, bf16[4,128,2048]{2,1,0:T(8,128)(2,1)}, u32[]{:S(2)}, u32[]{:S(2)}) collective-permute-start(bf16[4,128,2048]{2,1,0:T(8,128)(2,1)S(1)} %bitcast.314), channel_id=1, source_target_pairs={{0,16},{8,24},{16,0},{24,8},{1,17},{9,25},{17,1},{25,9},{2,18},{10... | collective-permute-start | bytes 6291464 | tf_op jit(solution)/shard_map/ppermute | solution.py:63
  326.5 32.9 %collective-permute-start.34 = (bf16[344,1024]{1,0:T(8,128)(2,1)S(1)}, bf16[344,1024]{1,0:T(8,128)(2,1)S(1)}, u32[]{:S(2)}, u32[]{:S(2)}) collective-permute-start(bf16[344,1024]{1,0:T(8,128)(2,1)S(1)} %add_convert_fusion.7), channel_id=1, source_target_pairs={{0,1},{1,0},{2,3},{3,2},{4,5},{5,4},{6,7},{7,6},{8,9},{9,8},{10,11... | collective-permute-start | bytes 2113544 | tf_op jit(solution)/shard_map/ppermute | solution.py:63
  406.8 47.9 %collective-permute-start.44 = (bf16[4,2,1,128,1024]{4,3,2,1,0:T(8,128)(2,1)}, bf16[4,2,1,128,1024]{4,3,2,1,0:T(8,128)(2,1)}, u32[]{:S(2)}, u32[]{:S(2)}) collective-permute-start(bf16[4,2,1,128,1024]{4,3,2,1,0:T(8,128)(2,1)} %get-tuple-element.240), channel_id=1, source_target_pairs={{0,8},{8,0},{16,24},{24,16},{1,9},{9,1},{17,25},{25,17},{2,10},{10... | collective-permute-start | bytes 6291464 | tf_op jit(solution)/shard_map/ppermute | solution.py:63
  408.5 47.6 %collective-permute-start.45 = (bf16[4,1,2,128,1024]{4,3,2,0,1:T(8,128)(2,1)}, bf16[4,1,2,128,1024]{4,3,2,0,1:T(8,128)(2,1)}, u32[]{:S(2)}, u32[]{:S(2)}) collective-permute-start(bf16[4,1,2,128,1024]{4,3,2,0,1:T(8,128)(2,1)} %bitcast.96), channel_id=1, source_target_pairs={{0,16},{8,24},{16,0},{24,8},{1,17},{9,25},{17,1},{25,9},{2,18},{10... | collective-permute-start | bytes 6291464 | tf_op jit(solution)/shard_map/ppermute | solution.py:63
  476.4 28.0 %collective-permute-start.50 = (bf16[4,1,128,1024]{3,2,1,0:T(8,128)(2,1)S(1)}, bf16[4,1,128,1024]{3,2,1,0:T(8,128)(2,1)S(1)}, u32[]{:S(2)}, u32[]{:S(2)}) collective-permute-start(bf16[4,1,128,1024]{3,2,1,0:T(8,128)(2,1)S(1)} %get-tuple-element.253), channel_id=1, source_target_pairs={{0,16},{8,24},{16,0},{24,8},{1,17},{9,25},{17,1},{25,9},{2,18},{10... | collective-permute-start | bytes 3145736 | tf_op jit(solution)/shard_map/ppermute | solution.py:63
  477.3 27.2 %collective-permute-start.51 = (bf16[4,1,128,1024]{3,2,1,0:T(8,128)(2,1)S(1)}, bf16[4,1,128,1024]{3,2,1,0:T(8,128)(2,1)S(1)}, u32[]{:S(2)}, u32[]{:S(2)}) collective-permute-start(bf16[4,1,128,1024]{3,2,1,0:T(8,128)(2,1)S(1)} %get-tuple-element.254), channel_id=1, source_target_pairs={{0,8},{8,0},{16,24},{24,16},{1,9},{9,1},{17,25},{25,17},{2,10},{10... | collective-permute-start | bytes 3145736 | tf_op jit(solution)/shard_map/ppermute | solution.py:63
  524.2 121.3 %collective-permute-start.57 = (bf16[4,2,1,128,1024]{4,3,2,1,0:T(8,128)(2,1)}, bf16[4,2,1,128,1024]{4,3,2,1,0:T(8,128)(2,1)}, u32[]{:S(2)}, u32[]{:S(2)}) collective-permute-start(bf16[4,2,1,128,1024]{4,3,2,1,0:T(8,128)(2,1)} %get-tuple-element.276), channel_id=1, source_target_pairs={{0,8},{8,0},{16,24},{24,16},{1,9},{9,1},{17,25},{25,17},{2,10},{10... | collective-permute-start | bytes 6291464 | tf_op jit(solution)/shard_map/ppermute | solution.py:63
  525.4 120.1 %collective-permute-start.58 = (bf16[4,1,2,128,1024]{4,3,2,0,1:T(8,128)(2,1)}, bf16[4,1,2,128,1024]{4,3,2,0,1:T(8,128)(2,1)}, u32[]{:S(2)}, u32[]{:S(2)}) collective-permute-start(bf16[4,1,2,128,1024]{4,3,2,0,1:T(8,128)(2,1)} %bitcast.114), channel_id=1, source_target_pairs={{0,16},{8,24},{16,0},{24,8},{1,17},{9,25},{17,1},{25,9},{2,18},{10... | collective-permute-start | bytes 6291464 | tf_op jit(solution)/shard_map/ppermute | solution.py:63
  526.6 68.9 %collective-permute-start.55 = (bf16[4,1,2,64,1024]{4,3,2,0,1:T(8,128)(2,1)}, bf16[4,1,2,64,1024]{4,3,2,0,1:T(8,128)(2,1)}, u32[]{:S(2)}, u32[]{:S(2)}) collective-permute-start(bf16[4,1,2,64,1024]{4,3,2,0,1:T(8,128)(2,1)} %bitcast.109), channel_id=1, source_target_pairs={{0,16},{8,24},{16,0},{24,8},{1,17},{9,25},{17,1},{25,9},{2,18},{10... | collective-permute-start | bytes 3145736 | tf_op jit(solution)/shard_map/ppermute | solution.py:63
  527.4 68.1 %collective-permute-start.54 = (bf16[4,2,1,64,1024]{4,3,2,1,0:T(8,128)(2,1)}, bf16[4,2,1,64,1024]{4,3,2,1,0:T(8,128)(2,1)}, u32[]{:S(2)}, u32[]{:S(2)}) collective-permute-start(bf16[4,2,1,64,1024]{4,3,2,1,0:T(8,128)(2,1)} %get-tuple-element.261), channel_id=1, source_target_pairs={{0,8},{8,0},{16,24},{24,16},{1,9},{9,1},{17,25},{25,17},{2,10},{10... | collective-permute-start | bytes 3145736 | tf_op jit(solution)/shard_map/ppermute | solution.py:63
  535.4 87.6 %collective-permute-start.56 = (bf16[2,128,2048]{2,1,0:T(8,128)(2,1)}, bf16[2,128,2048]{2,1,0:T(8,128)(2,1)}, u32[]{:S(2)}, u32[]{:S(2)}) collective-permute-start(bf16[2,128,2048]{2,1,0:T(8,128)(2,1)} %copy-done.77), channel_id=1, source_target_pairs={{0,2},{1,3},{2,0},{3,1},{4,6},{5,7},{6,4},{7,5},{8,10},{9,11},{10,... | collective-permute-start | bytes 3145736 | tf_op jit(solution)/shard_map/ppermute | solution.py:63
  622.1 46.2 %collective-permute-start.62 = (bf16[4,1,64,1024]{3,2,1,0:T(8,128)(2,1)}, bf16[4,1,64,1024]{3,2,1,0:T(8,128)(2,1)}, u32[]{:S(2)}, u32[]{:S(2)}) collective-permute-start(bf16[4,1,64,1024]{3,2,1,0:T(8,128)(2,1)} %copy-done.81), channel_id=1, source_target_pairs={{0,8},{8,0},{16,24},{24,16},{1,9},{9,1},{17,25},{25,17},{2,10},{10... | collective-permute-start | bytes 1572872 | tf_op jit(solution)/shard_map/ppermute | solution.py:63
  623.0 47.6 %collective-permute-start.61 = (bf16[4,1,64,1024]{3,2,1,0:T(8,128)(2,1)}, bf16[4,1,64,1024]{3,2,1,0:T(8,128)(2,1)}, u32[]{:S(2)}, u32[]{:S(2)}) collective-permute-start(bf16[4,1,64,1024]{3,2,1,0:T(8,128)(2,1)} %copy-done.80), channel_id=1, source_target_pairs={{0,16},{8,24},{16,0},{24,8},{1,17},{9,25},{17,1},{25,9},{2,18},{10... | collective-permute-start | bytes 1572872 | tf_op jit(solution)/shard_map/ppermute | solution.py:63
  673.8 28.5 %collective-permute-start.67 = (bf16[4,2,1,64,1024]{4,3,2,1,0:T(8,128)(2,1)S(1)}, bf16[4,2,1,64,1024]{4,3,2,1,0:T(8,128)(2,1)S(1)}, u32[]{:S(2)}, u32[]{:S(2)}) collective-permute-start(bf16[4,2,1,64,1024]{4,3,2,1,0:T(8,128)(2,1)S(1)} %get-tuple-element.307), channel_id=1, source_target_pairs={{0,8},{8,0},{16,24},{24,16},{1,9},{9,1},{17,25},{25,17},{2,10},{10... | collective-permute-start | bytes 3145736 | tf_op jit(solution)/shard_map/ppermute | solution.py:63
  675.0 27.3 %collective-permute-start.68 = (bf16[4,1,2,64,1024]{4,3,2,0,1:T(8,128)(2,1)S(1)}, bf16[4,1,2,64,1024]{4,3,2,0,1:T(8,128)(2,1)S(1)}, u32[]{:S(2)}, u32[]{:S(2)}) collective-permute-start(bf16[4,1,2,64,1024]{4,3,2,0,1:T(8,128)(2,1)S(1)} %bitcast.364), channel_id=1, source_target_pairs={{0,16},{8,24},{16,0},{24,8},{1,17},{9,25},{17,1},{25,9},{2,18},{10... | collective-permute-start | bytes 3145736 | tf_op jit(solution)/shard_map/ppermute | solution.py:63
  678.2 63.9 %collective-permute-start.90 = (bf16[2,128,2048]{2,1,0:T(8,128)(2,1)}, bf16[2,128,2048]{2,1,0:T(8,128)(2,1)S(1)}, u32[]{:S(2)}, u32[]{:S(2)}) collective-permute-start(bf16[2,128,2048]{2,1,0:T(8,128)(2,1)} %get-tuple-element.320), channel_id=1, source_target_pairs={{0,2},{1,3},{2,0},{3,1},{4,6},{5,7},{6,4},{7,5},{8,10},{9,11},{10,... | collective-permute-start | bytes 3145736 | tf_op jit(solution)/shard_map/ppermute | solution.py:63
  697.6 31.8 %collective-permute-start.66 = (bf16[172,1024]{1,0:T(8,128)(2,1)S(1)}, bf16[172,1024]{1,0:T(8,128)(2,1)S(1)}, u32[]{:S(2)}, u32[]{:S(2)}) collective-permute-start(bf16[172,1024]{1,0:T(8,128)(2,1)S(1)} %slice.655), channel_id=1, source_target_pairs={{0,4},{1,5},{2,6},{3,7},{4,0},{5,1},{6,2},{7,3},{8,12},{9,13},{10,... | collective-permute-start | bytes 1056776 | tf_op jit(solution)/shard_map/ppermute | solution.py:63
  745.0 44.5 %collective-permute-start.88 = (bf16[192,2048]{1,0:T(8,128)(2,1)S(1)}, bf16[192,2048]{1,0:T(8,128)(2,1)S(1)}, u32[]{:S(2)}, u32[]{:S(2)}) collective-permute-start(bf16[192,2048]{1,0:T(8,128)(2,1)S(1)} %maximum_maximum_fusion), channel_id=1, source_target_pairs={{0,16},{8,24},{16,0},{24,8},{1,17},{9,25},{17,1},{25,9},{2,18},{10... | collective-permute-start | bytes 2359304 | tf_op jit(solution)/shard_map/ppermute | solution.py:63
  745.9 48.1 %collective-permute-start.87 = (bf16[192,2048]{1,0:T(8,128)(2,1)S(1)}, bf16[192,2048]{1,0:T(8,128)(2,1)S(1)}, u32[]{:S(2)}, u32[]{:S(2)}) collective-permute-start(bf16[192,2048]{1,0:T(8,128)(2,1)S(1)} %maximum_maximum_fusion), channel_id=1, source_target_pairs={{0,8},{8,0},{16,24},{24,16},{1,9},{9,1},{17,25},{25,17},{2,10},{10... | collective-permute-start | bytes 2359304 | tf_op jit(solution)/shard_map/ppermute | solution.py:63
  749.5 38.7 %collective-permute-start.74 = (f32[2,1,1792]{2,0,1:T(2,128)S(1)}, f32[2,1,1792]{2,0,1:T(2,128)S(1)}, u32[]{:S(2)}, u32[]{:S(2)}) collective-permute-start(f32[2,1,1792]{2,0,1:T(2,128)S(1)} %dynamic-slice_add_fusion), channel_id=1, source_target_pairs={{0,8},{8,0},{16,24},{24,16},{1,9},{9,1},{17,25},{25,17},{2,10},{10... | collective-permute-start | bytes 43016 | tf_op jit(solution)/shard_map/ppermute | solution.py:63
  789.5 33.3 %collective-permute-start.89 = (bf16[192,2048]{1,0:T(8,128)(2,1)S(1)}, bf16[192,2048]{1,0:T(8,128)(2,1)S(1)}, u32[]{:S(2)}, u32[]{:S(2)}) collective-permute-start(bf16[192,2048]{1,0:T(8,128)(2,1)S(1)} %collective-permute-done.88), channel_id=1, source_target_pairs={{0,8},{8,0},{16,24},{24,16},{1,9},{9,1},{17,25},{25,17},{2,10},{10... | collective-permute-start | bytes 2359304 | tf_op jit(solution)/shard_map/ppermute | solution.py:63
  793.1 38.2 %collective-permute-start.94 = (bf16[128,2048]{1,0:T(8,128)(2,1)S(1)}, bf16[128,2048]{1,0:T(8,128)(2,1)S(1)}, u32[]{:S(2)}, u32[]{:S(2)}) collective-permute-start(bf16[128,2048]{1,0:T(8,128)(2,1)S(1)} %pad_maximum_fusion.18.refs_0_), channel_id=1, source_target_pairs={{0,16},{8,24},{16,0},{24,8},{1,17},{9,25},{17,1},{25,9},{2,18},{10... | collective-permute-start | bytes 1572872 | tf_op jit(solution)/shard_map/ppermute | solution.py:63
  794.0 34.5 %collective-permute-start.80 = (bf16[64,2048]{1,0:T(8,128)(2,1)S(1)}, bf16[64,2048]{1,0:T(8,128)(2,1)S(1)}, u32[]{:S(2)}, u32[]{:S(2)}) collective-permute-start(bf16[64,2048]{1,0:T(8,128)(2,1)S(1)} %pad_maximum_fusion.19.refs_0_), channel_id=1, source_target_pairs={{0,16},{8,24},{16,0},{24,8},{1,17},{9,25},{17,1},{25,9},{2,18},{10... | collective-permute-start | bytes 786440 | tf_op jit(solution)/shard_map/ppermute | solution.py:63
  800.7 30.6 %collective-permute-start.95 = (bf16[128,2048]{1,0:T(8,128)(2,1)S(1)}, bf16[128,2048]{1,0:T(8,128)(2,1)S(1)}, u32[]{:S(2)}, u32[]{:S(2)}) collective-permute-start(bf16[128,2048]{1,0:T(8,128)(2,1)S(1)} %collective-permute-done.93.refs_1_), channel_id=1, source_target_pairs={{0,16},{8,24},{16,0},{24,8},{1,17},{9,25},{17,1},{25,9},{2,18},{10... | collective-permute-start | bytes 1572872 | tf_op jit(solution)/shard_map/ppermute | solution.py:63
  (296 other events, 2880.5 us)

commit v4 on v3

--- a/solution.py
+++ b/solution.py
@@ -941,7 +941,7 @@
 
 
 def forward_layer(
-    tok_rows, normed, projected, others, gathered, beside, neighbours, following
+    tok_rows, normed, projected, others, gathered, beside, following
 ):
     (
         attn_norm_gain,
@@ -967,7 +967,7 @@
     branch = forward_dot(attended[:tokens], output_weight) + widen(got) + widen(output_bias)
     middle = tok_rows + widen(attn_layerscale) * branch
     normed_two = low(layer_norm(middle, widen(mlp_norm_gain), widen(mlp_norm_bias)))
-    normed_two = after(both_cores(normed_two), *neighbours)
+    normed_two = both_cores(normed_two)
     activated, slope, own_sum, other_sum = feed_forward(
         normed_two, expand_weight, core_half(expand_bias), shrink_weight
     )
@@ -1071,6 +1071,10 @@
     own_sum = later.sent(own_sum, block)
     if not old:
         own_sum = after(own_sum, activation_got)
+    else:
+        own_sum = later.came(own_sum, old[1])
+        later.step(old[1], own_sum)
+        own_sum = later.sent(own_sum, old[1])
     d_middle_norm, g_mlp_gain, g_mlp_shift = norm_back(
         middle, widen(mlp_norm_gain), widen(mlp_norm_bias), own_sum + widen(got)
     )
@@ -1080,9 +1084,6 @@
     g_attn_scale = jnp.sum(d_middle * branch, 0)
     g_output_bias = column_sum(d_branch)
     d_attended = low(input_dot(d_branch_both, output_weight))
-    if old:
-        later.step(old[1], d_attended)
-        d_attended = later.sent(d_attended, old[1])
     pairs = d_attended.shape[1] // 128
 
     def back(first):
@@ -1102,6 +1103,10 @@
     second_query = later.came(second_query, block)
     later.step(block, second_query)
     second_query = later.sent(second_query, block)
+    if old:
+        second_query = later.came(second_query, old[1])
+        later.join(old[3], [old[1]], second_query)
+        second_query = later.sent(second_query, old[3])
     d_query = jnp.concatenate([first_query, second_query], 1)
     d_key = jnp.concatenate([first_kv[0], second_kv[0]], 1)
     d_value = jnp.concatenate([first_kv[1], second_kv[1]], 1)
@@ -1112,8 +1117,6 @@
     later.begin(mixed, mixed_grad, (normed, d_projected, attended, d_branch_both))
     d_projected = later.sent(d_projected, mixed)
     if old:
-        later.join(old[3], [old[1]], d_projected)
-        d_projected = later.sent(d_projected, old[3])
         later.join(block_planes, [block], d_projected)
         d_projected = later.sent(d_projected, block_planes)
     d_normed = input_dot(d_projected[:tokens], heads_weight) + widen(got)
@@ -1175,6 +1178,7 @@
             members = gather_members(held, [])
         arrays[0] = after(arrays[0], *planes[-1:], *next_planes[:1])
         gathered[10], gathered[12] = place_second(arrays, parts, count)
+        gathered[10] = after(gathered[10], *neighbours)
         fetched.append(tuple(gathered))
         tok_rows, saved = forward_layer(
             tok_rows,
@@ -1183,7 +1187,6 @@
             others,
             gathered,
             beside,
-            neighbours,
             next_planes[1:] + members[2],
         )
         saved_layers.append(saved)

time: 845 us -> 787 us (0.931)
  waiting for transfers between devices: 355 us -> 306 us
    ppermute x96, waiting for transfers between devices: 355 us -> 306 us  [swap(): return lax.ppermute(tensor, axis, [(i, i ^ offset) for i in range(count)])]
    unnamed x484 -> x462, local copies, waits for them, and re-layouts: 55.7 us -> 50 us
  transfers between devices with their start and end apart: 96 -> 96, of which waited for: 44 -> 42; matrix products, arithmetic and copies ran while one was open for 11% -> 12% of each run, Pallas kernels for 24% -> 26%
where the time goes in v4:
time: 787 us; the launch traced here: 776 us
  waiting for transfers between devices  306 us (39%)
  Pallas kernels  229 us (29%)
  starting transfers between devices  86.8 us (11%)
  local copies, waits for them, and re-layouts  79.4 us (10%)
  other arithmetic  47.7 us (6%)
  matrix products  23.2 us (3%)
    ppermute x96, waiting for transfers between devices, swap(): return lax.ppermute(tensor, axis, [(i, i ^ offset) for i in range(count)])  306 us
    ppermute x96, starting transfers between devices, swap(): return lax.ppermute(tensor, axis, [(i, i ^ offset) for i in range(count)])  86.8 us
    pallas_call x4, Pallas kernels, attend_back(): pl.pallas_call(functools.partial(attend_back_kernel, scale * math.log2(ma...  65.5 us
    unnamed x462, local copies, waits for them, and re-layouts  50 us
    pallas_call x2, Pallas kernels, attend(): pl.pallas_call(functools.partial(attend_kernel, factor, len(parts)), out_...  36.8 us
    pallas_call x4, Pallas kernels, grad_call(): pl.pallas_call(functools.partial(kernel, shapes), out_shape=out_shapes, g...  32.6 us
    pallas_call x4, Pallas kernels, place(): pl.pallas_call(functools.partial(place_kernel, pieces[0].shape[1] // 2, b...  22.1 us
    pallas_call x2, Pallas kernels, feed_forward(): pl.pallas_call(expand_kernel, out_shape=[jax.ShapeDtypeStruct((tokens, un...  19.6 us
  transfers between devices with their start and end apart: 96, of which 42 were waited for; matrix products, arithmetic and copies ran while one was open for 12% of the time, Pallas kernels for 26%

profile of v4, /device:TPU:0, one launch (start us, length us, event | category | flops | bytes accessed | tf_op | source)
XLA Modules:
  0.0 776.4 jit_solution(7071984506549355177)
XLA Ops:
  24.3 9.1 %collective-permute-done.1 = bf16[1,64,2048]{2,1,0:T(8,128)(2,1)S(1)} collective-permute-done((bf16[1,64,2048]{2,1,0:T(8,128)(2,1)S(1)}, bf16[1,64,2048]{2,1,0:T(8,128)(2,1)S(1)}, u32[]{:S(2)}, u32[]{:S(2)}) %collective-permute-start.1) | collective-permute-done | bytes 262176 | tf_op jit(solution)/shard_map/ppermute | solution.py:63
  38.4 13.7 %collective-permute-done.2 = bf16[172,1024]{1,0:T(8,128)(2,1)S(1)} collective-permute-done((bf16[172,1024]{1,0:T(8,128)(2,1)S(1)}, bf16[172,1024]{1,0:T(8,128)(2,1)S(1)}, u32[]{:S(2)}, u32[]{:S(2)}) %collective-permute-start.2) | collective-permute-done | bytes 352288 | tf_op jit(solution)/shard_map/ppermute | solution.py:63
  61.1 16.1 %collective-permute-done.8 = bf16[1,128,2048]{2,1,0:T(8,128)(2,1)S(1)} collective-permute-done((bf16[1,128,2048]{2,1,0:T(8,128)(2,1)S(1)}, bf16[1,128,2048]{2,1,0:T(8,128)(2,1)S(1)}, u32[]{:S(2)}, u32[]{:S(2)}) %collective-permute-start.8) | collective-permute-done | bytes 524320 | tf_op jit(solution)/shard_map/ppermute | solution.py:63
  83.9 17.5 %collective-permute-done.9 = bf16[2,128,2048]{2,1,0:T(8,128)(2,1)S(1)} collective-permute-done((bf16[2,128,2048]{2,1,0:T(8,128)(2,1)S(1)}, bf16[2,128,2048]{2,1,0:T(8,128)(2,1)S(1)}, u32[]{:S(2)}, u32[]{:S(2)}) %collective-permute-start.9) | collective-permute-done | bytes 1048608 | tf_op jit(solution)/shard_map/ppermute | solution.py:63
  112.7 25.3 %collective-permute-done.14.refs_1_.refs_3_ = bf16[688,1024]{1,0:T(8,128)(2,1)} collective-permute-done((bf16[688,1024]{1,0:T(8,128)(2,1)S(1)}, bf16[688,1024]{1,0:T(8,128)(2,1)}, u32[]{:S(2)}, u32[]{:S(2)}) %collective-permute-start.14) | collective-permute-done | bytes 1409056 | tf_op jit(solution)/shard_map/ppermute | solution.py:63
  140.9 18.3 %shard_map.298 = (bf16[688,512]{1,0:T(8,128)(2,1)}, f32[688,512]{1,0:T(8,128)}) custom-call(bf16[688,1536]{1,0:T(8,128)(2,1)} %copy-done.75, bf16[688,1536]{1,0:T(8,128)(2,1)} %copy-done.75, bf16[688,1024]{1,0:T(8,128)(2,1)} %collective-permute-done.14.refs_1_.refs_3_, bf16[688,1536]{1,0:T(8,128)(2,1)} %copy-done.75, ...), custom_call_target="tpu_custom_call" | custom-call | flops 1000 | bytes 1000 | tf_op jit(solution)/shard_map/pallas_call | solution.py:760
  175.5 13.4 %collective-permute-done.23.refs_4_ = bf16[4,64,2048]{2,1,0:T(8,128)(2,1)S(1)} collective-permute-done((bf16[4,64,2048]{2,1,0:T(8,128)(2,1)S(1)}, bf16[4,64,2048]{2,1,0:T(8,128)(2,1)S(1)}, u32[]{:S(2)}, u32[]{:S(2)}) %collective-permute-start.23) | collective-permute-done | bytes 1048608 | tf_op jit(solution)/shard_map/ppermute | solution.py:63
  197.1 18.7 %collective-permute-done.24.refs_1_ = bf16[4,64,2048]{2,1,0:T(8,128)(2,1)S(1)} collective-permute-done((bf16[4,64,2048]{2,1,0:T(8,128)(2,1)S(1)}, bf16[4,64,2048]{2,1,0:T(8,128)(2,1)S(1)}, u32[]{:S(2)}, u32[]{:S(2)}) %collective-permute-start.24) | collective-permute-done | bytes 1048608 | tf_op jit(solution)/shard_map/ppermute | solution.py:63
  231.4 8.1 %shard_map.299 = (bf16[4,2,4,32,2048]{4,3,2,1,0:T(8,128)(2,1)S(1)}, bf16[4,4,2,64,1024]{4,3,2,1,0:T(8,128)(2,1)S(1)}) custom-call(s32[2]{0:T(128)S(1)} %pad_add_fusion.1.where_ref, bf16[4,128,2048]{2,1,0:T(8,128)(2,1)S(1)} %bitcast.312, bf16[4,128,2048]{2,1,0:T(8,128)(2,1)S(1)} %copy-done.17, bf16[4,128,2048]{2,1,0:T(8,128)(2,1)S(1)} %copy-done.19, ...), custom_call_target="tpu_custom_call" | custom-call | flops 1000 | bytes 1000 | tf_op jit(solution)/shard_map/pallas_call | solution.py:169
  239.5 9.8 %shard_map.300 = (bf16[688,2048]{1,0:T(8,128)(2,1)S(1)}, bf16[688,2048]{1,0:T(8,128)(2,1)S(1)}, f32[344,1024]{1,0:T(8,128)S(1)}, bf16[344,1024]{1,0:T(8,128)(2,1)S(1)}) custom-call(bf16[688,1024]{1,0:T(8,128)(2,1)S(1)} %pad_maximum_fusion.3.rows_ref.left_ref, bf16[1024,2048]{1,0:T(8,128)(2,1)S(1)} %bitcast.302, f32[1,2048]{1,0:T(1,128)S(1)} %bitcast.355, ...), custom_call_target="tpu_custom_call" | custom-call | flops 1000 | bytes 1000 | tf_op jit(solution)/shard_map/pallas_call | solution.py:859
  267.6 29.2 %collective-permute-done.31.refs_1_.refs_3_ = bf16[688,1024]{1,0:T(8,128)(2,1)S(1)} collective-permute-done((bf16[688,1024]{1,0:T(8,128)(2,1)S(1)}, bf16[688,1024]{1,0:T(8,128)(2,1)S(1)}, u32[]{:S(2)}, u32[]{:S(2)}) %collective-permute-start.31) | collective-permute-done | bytes 1409056 | tf_op jit(solution)/shard_map/ppermute | solution.py:63
  298.1 18.5 %shard_map.302 = (bf16[688,512]{1,0:T(8,128)(2,1)}, f32[688,512]{1,0:T(8,128)}) custom-call(bf16[688,1536]{1,0:T(8,128)(2,1)} %copy-done.76, bf16[688,1536]{1,0:T(8,128)(2,1)} %copy-done.76, bf16[688,1024]{1,0:T(8,128)(2,1)} %copy-done.80, bf16[688,1536]{1,0:T(8,128)(2,1)} %copy-done.76, bf16[688,1024]{1,0:T(8,128)(2,1)} %copy-done.80), custom_call_target="tpu_custom_call" | custom-call | flops 1000 | bytes 1000 | tf_op jit(solution)/shard_map/pallas_call | solution.py:760
  328.1 17.2 %collective-permute-done.38.refs_4_ = bf16[4,64,2048]{2,1,0:T(8,128)(2,1)} collective-permute-done((bf16[4,64,2048]{2,1,0:T(8,128)(2,1)}, bf16[4,64,2048]{2,1,0:T(8,128)(2,1)}, u32[]{:S(2)}, u32[]{:S(2)}) %collective-permute-start.38) | collective-permute-done | bytes 1048608 | tf_op jit(solution)/shard_map/ppermute | solution.py:63
  351.5 7.8 %shard_map.303 = (bf16[4,2,4,32,2048]{4,3,2,1,0:T(8,128)(2,1)S(1)}, bf16[4,4,2,64,1024]{4,3,2,1,0:T(8,128)(2,1)S(1)}) custom-call(s32[2]{0:T(128)S(1)} %pad_add_fusion.1.where_ref, bf16[4,128,2048]{2,1,0:T(8,128)(2,1)S(1)} %bitcast.315, bf16[4,128,2048]{2,1,0:T(8,128)(2,1)S(1)} %copy-done.21, bf16[4,128,2048]{2,1,0:T(8,128)(2,1)} %collective-permute-done.36.refs_2_, ...), custom_call_target="tpu_custom_call" | custom-call | flops 1000 | bytes 1000 | tf_op jit(solution)/shard_map/pallas_call | solution.py:169
  359.5 9.8 %shard_map.304 = (bf16[688,2048]{1,0:T(8,128)(2,1)S(1)}, bf16[688,2048]{1,0:T(8,128)(2,1)S(1)}, f32[344,1024]{1,0:T(8,128)S(1)}, bf16[344,1024]{1,0:T(8,128)(2,1)S(1)}) custom-call(bf16[688,1024]{1,0:T(8,128)(2,1)S(1)} %pad_maximum_fusion.5.rows_ref.left_ref, bf16[1024,2048]{1,0:T(8,128)(2,1)S(1)} %bitcast.306, f32[1,2048]{1,0:T(1,128)S(1)} %bitcast.354, ...), custom_call_target="tpu_custom_call" | custom-call | flops 1000 | bytes 1000 | tf_op jit(solution)/shard_map/pallas_call | solution.py:859
  375.1 9.6 %shard_map.305 = (bf16[688,2048]{1,0:T(8,128)(2,1)S(1)}, f32[1,2048]{1,0:T(1,128)S(1)}, f32[344,1024]{1,0:T(8,128)S(1)}, bf16[344,1024]{1,0:T(8,128)(2,1)}) custom-call(bf16[688,1024]{1,0:T(8,128)(2,1)S(1)} %pad_maximum_fusion.6.grad_ref.other_ref, bf16[2048,1024]{1,0:T(8,128)(2,1)S(1)} %bitcast.309, bf16[688,2048]{1,0:T(8,128)(2,1)S(1)} %get-tuple-element.238.slope_ref, ...), custom_call_target="tpu_custom_call" | custom-call | flops 1000 | bytes 1000 | tf_op jit(solution)/shard_map/pallas_call | solution.py:897
  394.7 10.7 %shard_map.306 = (bf16[4,2,1,128,1024]{4,3,2,1,0:T(8,128)(2,1)S(1)}, bf16[4,2,1,128,1024]{4,3,2,1,0:T(8,128)(2,1)}, bf16[4,1,2,128,1024]{4,3,2,1,0:T(8,128)(2,1)S(1)}, bf16[4,1,2,128,1024]{4,3,2,1,0:T(8,128)(2,1)}) custom-call(s32[2]{0:T(128)S(1)} %pad_add_fusion.2.where_ref, bf16[688,1024]{1,0:T(8,128)(2,1)S(1)} %copy-done.5, ...), custom_call_target="tpu_custom_call" | custom-call | flops 1000 | bytes 1000 | tf_op jit(solution)/shard_map/pallas_call | solution.py:369
  418.9 16.2 %shard_map.307 = (bf16[688,256]{1,0:T(8,128)(2,1)}, bf16[2,688,256]{2,1,0:T(8,128)(2,1)}, bf16[2,688,256]{2,1,0:T(8,128)(2,1)}) custom-call(bf16[688,1536]{1,0:T(8,128)(2,1)} %copy-done.76, bf16[688,1536]{1,0:T(8,128)(2,1)} %copy-done.76, bf16[688,1024]{1,0:T(8,128)(2,1)} %copy-done.80, bf16[688,1536]{1,0:T(8,128)(2,1)} %copy-done.76, ...), custom_call_target="tpu_custom_call" | custom-call | flops 1000 | bytes 1000 | tf_op jit(solution)/shard_map/pallas_call | solution.py:804
  435.2 16.4 %shard_map.308 = (bf16[688,256]{1,0:T(8,128)(2,1)}, bf16[2,688,256]{2,1,0:T(8,128)(2,1)}, bf16[2,688,256]{2,1,0:T(8,128)(2,1)}) custom-call(bf16[688,1536]{1,0:T(8,128)(2,1)} %copy-done.76, bf16[688,1536]{1,0:T(8,128)(2,1)} %copy-done.76, bf16[688,1024]{1,0:T(8,128)(2,1)} %copy-done.80, bf16[688,1536]{1,0:T(8,128)(2,1)} %copy-done.76, ...), custom_call_target="tpu_custom_call" | custom-call | flops 1000 | bytes 1000 | tf_op jit(solution)/shard_map/pallas_call | solution.py:804
  477.1 6.2 shard_map.310
  494.4 8.7 %shard_map.311 = (bf16[688,2048]{1,0:T(8,128)(2,1)S(1)}, f32[1,2048]{1,0:T(1,128)S(1)}, f32[344,1024]{1,0:T(8,128)S(1)}, bf16[344,1024]{1,0:T(8,128)(2,1)S(1)}) custom-call(bf16[688,1024]{1,0:T(8,128)(2,1)S(1)} %pad_maximum_fusion.8.grad_ref.other_ref, bf16[2048,1024]{1,0:T(8,128)(2,1)S(1)} %bitcast.305, bf16[688,2048]{1,0:T(8,128)(2,1)S(1)} %copy-done.32, ...), custom_call_target="tpu_custom_call" | custom-call | flops 1000 | bytes 1000 | tf_op jit(solution)/shard_map/pallas_call | solution.py:897
  505.5 10.5 %shard_map.313 = (bf16[4,2,1,128,1024]{4,3,2,1,0:T(8,128)(2,1)S(1)}, bf16[4,2,1,128,1024]{4,3,2,1,0:T(8,128)(2,1)}, bf16[4,1,2,128,1024]{4,3,2,1,0:T(8,128)(2,1)S(1)}, bf16[4,1,2,128,1024]{4,3,2,1,0:T(8,128)(2,1)}) custom-call(s32[2]{0:T(128)S(1)} %pad_add_fusion.2.where_ref, bf16[688,1024]{1,0:T(8,128)(2,1)S(1)} %pad_maximum_fusion.3.rows_ref.left_ref, ...), custom_call_target="tpu_custom_call" | custom-call | flops 1000 | bytes 1000 | tf_op jit(solution)/shard_map/pallas_call | solution.py:369
  517.1 7.9 %collective-permute-done.52.refs_1_ = bf16[4,2,1,64,1024]{4,3,2,1,0:T(8,128)(2,1)S(1)} collective-permute-done((bf16[4,2,1,64,1024]{4,3,2,1,0:T(8,128)(2,1)}, bf16[4,2,1,64,1024]{4,3,2,1,0:T(8,128)(2,1)S(1)}, u32[]{:S(2)}, u32[]{:S(2)}) %collective-permute-start.52) | collective-permute-done | bytes 1048608 | tf_op jit(solution)/shard_map/ppermute | solution.py:63
  548.2 16.4 %shard_map.315 = (bf16[688,256]{1,0:T(8,128)(2,1)}, bf16[2,688,256]{2,1,0:T(8,128)(2,1)}, bf16[2,688,256]{2,1,0:T(8,128)(2,1)}) custom-call(bf16[688,1536]{1,0:T(8,128)(2,1)} %copy-done.75, bf16[688,1536]{1,0:T(8,128)(2,1)} %copy-done.75, bf16[688,1024]{1,0:T(8,128)(2,1)} %collective-permute-done.14.refs_1_.refs_3_, bf16[688,1536]{1,0:T(8,128)(2,1)} %copy-done.75, ...), custom_call_target="tpu_custom_call" | custom-call | flops 1000 | bytes 1000 | tf_op jit(solution)/shard_map/pallas_call | solution.py:804
  572.5 16.4 %shard_map.317 = (bf16[688,256]{1,0:T(8,128)(2,1)}, bf16[2,688,256]{2,1,0:T(8,128)(2,1)}, bf16[2,688,256]{2,1,0:T(8,128)(2,1)}) custom-call(bf16[688,1536]{1,0:T(8,128)(2,1)} %copy-done.75, bf16[688,1536]{1,0:T(8,128)(2,1)} %copy-done.75, bf16[688,1024]{1,0:T(8,128)(2,1)} %collective-permute-done.14.refs_1_.refs_3_, bf16[688,1536]{1,0:T(8,128)(2,1)} %copy-done.75, ...), custom_call_target="tpu_custom_call" | custom-call | flops 1000 | bytes 1000 | tf_op jit(solution)/shard_map/pallas_call | solution.py:804
  605.9 14.8 %collective-permute-done.62 = bf16[2,688,256]{2,1,0:T(8,128)(2,1)S(1)} collective-permute-done((bf16[2,688,256]{2,1,0:T(8,128)(2,1)}, bf16[2,688,256]{2,1,0:T(8,128)(2,1)S(1)}, u32[]{:S(2)}, u32[]{:S(2)}) %collective-permute-start.62) | collective-permute-done | bytes 704544 | tf_op jit(solution)/shard_map/ppermute | solution.py:63
  643.4 12.5 %collective-permute-done.68 = bf16[4,1,2,64,1024]{4,3,2,0,1:T(8,128)(2,1)S(1)} collective-permute-done((bf16[4,1,2,64,1024]{4,3,2,0,1:T(8,128)(2,1)S(1)}, bf16[4,1,2,64,1024]{4,3,2,0,1:T(8,128)(2,1)S(1)}, u32[]{:S(2)}, u32[]{:S(2)}) %collective-permute-start.68) | collective-permute-done | bytes 1048608 | tf_op jit(solution)/shard_map/ppermute | solution.py:63
  662.8 7.0 collective-permute-done.66
  691.3 19.4 %collective-permute-done.91 = bf16[1,1,128,2048]{3,2,1,0:T(8,128)(2,1)S(1)} collective-permute-done((bf16[1,1,128,2048]{3,2,1,0:T(8,128)(2,1)S(1)}, bf16[1,1,128,2048]{3,2,1,0:T(8,128)(2,1)S(1)}, u32[]{:S(2)}, u32[]{:S(2)}) %collective-permute-start.91) | collective-permute-done | bytes 524320 | tf_op jit(solution)/shard_map/ppermute | solution.py:63
  715.0 12.4 %collective-permute-done.77 = bf16[1,1,64,2048]{3,2,1,0:T(8,128)(2,1)S(1)} collective-permute-done((bf16[1,1,64,2048]{3,2,1,0:T(8,128)(2,1)S(1)}, bf16[1,1,64,2048]{3,2,1,0:T(8,128)(2,1)S(1)}, u32[]{:S(2)}, u32[]{:S(2)}) %collective-permute-start.77) | collective-permute-done | bytes 262176 | tf_op jit(solution)/shard_map/ppermute | solution.py:63
  736.6 5.8 collective-permute-done.93.refs_1_
  750.3 14.2 %collective-permute-done.89 = bf16[192,2048]{1,0:T(8,128)(2,1)S(1)} collective-permute-done((bf16[192,2048]{1,0:T(8,128)(2,1)S(1)}, bf16[192,2048]{1,0:T(8,128)(2,1)S(1)}, u32[]{:S(2)}, u32[]{:S(2)}) %collective-permute-start.89) | collective-permute-done | bytes 786464 | tf_op jit(solution)/shard_map/ppermute | solution.py:63
  (861 shorter events, 334.1 us)
Async XLA Ops:
  107.1 30.9 %collective-permute-start.14 = (bf16[688,1024]{1,0:T(8,128)(2,1)S(1)}, bf16[688,1024]{1,0:T(8,128)(2,1)}, u32[]{:S(2)}, u32[]{:S(2)}) collective-permute-start(bf16[688,1024]{1,0:T(8,128)(2,1)S(1)} %slice.495), channel_id=1, source_target_pairs={{0,2},{1,3},{2,0},{3,1},{4,6},{5,7},{6,4},{7,5},{8,10},{9,11},{10,... | collective-permute-start | bytes 4227080 | tf_op jit(solution)/shard_map/ppermute | solution.py:63
  108.8 54.3 %collective-permute-start.20 = (bf16[4,128,2048]{2,1,0:T(8,128)(2,1)S(1)}, bf16[4,128,2048]{2,1,0:T(8,128)(2,1)S(1)}, u32[]{:S(2)}, u32[]{:S(2)}) collective-permute-start(bf16[4,128,2048]{2,1,0:T(8,128)(2,1)S(1)} %bitcast.310), channel_id=1, source_target_pairs={{0,8},{8,0},{16,24},{24,16},{1,9},{9,1},{17,25},{25,17},{2,10},{10... | collective-permute-start | bytes 6291464 | tf_op jit(solution)/shard_map/ppermute | solution.py:63
  110.3 52.9 %collective-permute-start.21 = (bf16[4,128,2048]{2,1,0:T(8,128)(2,1)S(1)}, bf16[4,128,2048]{2,1,0:T(8,128)(2,1)S(1)}, u32[]{:S(2)}, u32[]{:S(2)}) collective-permute-start(bf16[4,128,2048]{2,1,0:T(8,128)(2,1)S(1)} %bitcast.311), channel_id=1, source_target_pairs={{0,16},{8,24},{16,0},{24,8},{1,17},{9,25},{17,1},{25,9},{2,18},{10... | collective-permute-start | bytes 6291464 | tf_op jit(solution)/shard_map/ppermute | solution.py:63
  196.7 54.3 %collective-permute-start.26 = (bf16[2,128,2048]{2,1,0:T(8,128)(2,1)}, bf16[2,128,2048]{2,1,0:T(8,128)(2,1)}, u32[]{:S(2)}, u32[]{:S(2)}) collective-permute-start(bf16[2,128,2048]{2,1,0:T(8,128)(2,1)} %get-tuple-element.220), channel_id=1, source_target_pairs={{0,2},{1,3},{2,0},{3,1},{4,6},{5,7},{6,4},{7,5},{8,10},{9,11},{10,... | collective-permute-start | bytes 3145736 | tf_op jit(solution)/shard_map/ppermute | solution.py:63
  216.9 34.0 %collective-permute-start.28 = (bf16[4,32,2048]{2,1,0:T(8,128)(2,1)}, bf16[4,32,2048]{2,1,0:T(8,128)(2,1)}, u32[]{:S(2)}, u32[]{:S(2)}) collective-permute-start(bf16[4,32,2048]{2,1,0:T(8,128)(2,1)} %slice.513), channel_id=1, source_target_pairs={{0,16},{8,24},{16,0},{24,8},{1,17},{9,25},{17,1},{25,9},{2,18},{10... | collective-permute-start | bytes 1572872 | tf_op jit(solution)/shard_map/ppermute | solution.py:63
  220.3 30.6 %collective-permute-start.27 = (bf16[4,32,2048]{2,1,0:T(8,128)(2,1)}, bf16[4,32,2048]{2,1,0:T(8,128)(2,1)}, u32[]{:S(2)}, u32[]{:S(2)}) collective-permute-start(bf16[4,32,2048]{2,1,0:T(8,128)(2,1)} %slice.512), channel_id=1, source_target_pairs={{0,8},{8,0},{16,24},{24,16},{1,9},{9,1},{17,25},{25,17},{2,10},{10... | collective-permute-start | bytes 1572872 | tf_op jit(solution)/shard_map/ppermute | solution.py:63
  263.9 32.9 %collective-permute-start.31 = (bf16[688,1024]{1,0:T(8,128)(2,1)S(1)}, bf16[688,1024]{1,0:T(8,128)(2,1)S(1)}, u32[]{:S(2)}, u32[]{:S(2)}) collective-permute-start(bf16[688,1024]{1,0:T(8,128)(2,1)S(1)} %slice.521), channel_id=1, source_target_pairs={{0,2},{1,3},{2,0},{3,1},{4,6},{5,7},{6,4},{7,5},{8,10},{9,11},{10,... | collective-permute-start | bytes 4227080 | tf_op jit(solution)/shard_map/ppermute | solution.py:63
  266.3 52.0 %collective-permute-start.35 = (bf16[4,128,2048]{2,1,0:T(8,128)(2,1)S(1)}, bf16[4,128,2048]{2,1,0:T(8,128)(2,1)S(1)}, u32[]{:S(2)}, u32[]{:S(2)}) collective-permute-start(bf16[4,128,2048]{2,1,0:T(8,128)(2,1)S(1)} %bitcast.313), channel_id=1, source_target_pairs={{0,8},{8,0},{16,24},{24,16},{1,9},{9,1},{17,25},{25,17},{2,10},{10... | collective-permute-start | bytes 6291464 | tf_op jit(solution)/shard_map/ppermute | solution.py:63
  267.2 52.2 %collective-permute-start.36 = (bf16[4,128,2048]{2,1,0:T(8,128)(2,1)S(1)}, bf16[4,128,2048]{2,1,0:T(8,128)(2,1)}, u32[]{:S(2)}, u32[]{:S(2)}) collective-permute-start(bf16[4,128,2048]{2,1,0:T(8,128)(2,1)S(1)} %bitcast.314), channel_id=1, source_target_pairs={{0,16},{8,24},{16,0},{24,8},{1,17},{9,25},{17,1},{25,9},{2,18},{10... | collective-permute-start | bytes 6291464 | tf_op jit(solution)/shard_map/ppermute | solution.py:63
  326.5 32.8 %collective-permute-start.34 = (bf16[344,1024]{1,0:T(8,128)(2,1)S(1)}, bf16[344,1024]{1,0:T(8,128)(2,1)S(1)}, u32[]{:S(2)}, u32[]{:S(2)}) collective-permute-start(bf16[344,1024]{1,0:T(8,128)(2,1)S(1)} %add_convert_fusion.7), channel_id=1, source_target_pairs={{0,1},{1,0},{2,3},{3,2},{4,5},{5,4},{6,7},{7,6},{8,9},{9,8},{10,11... | collective-permute-start | bytes 2113544 | tf_op jit(solution)/shard_map/ppermute | solution.py:63
  406.7 47.9 %collective-permute-start.44 = (bf16[4,2,1,128,1024]{4,3,2,1,0:T(8,128)(2,1)}, bf16[4,2,1,128,1024]{4,3,2,1,0:T(8,128)(2,1)}, u32[]{:S(2)}, u32[]{:S(2)}) collective-permute-start(bf16[4,2,1,128,1024]{4,3,2,1,0:T(8,128)(2,1)} %get-tuple-element.242), channel_id=1, source_target_pairs={{0,8},{8,0},{16,24},{24,16},{1,9},{9,1},{17,25},{25,17},{2,10},{10... | collective-permute-start | bytes 6291464 | tf_op jit(solution)/shard_map/ppermute | solution.py:63
  408.5 47.7 %collective-permute-start.45 = (bf16[4,1,2,128,1024]{4,3,2,0,1:T(8,128)(2,1)}, bf16[4,1,2,128,1024]{4,3,2,0,1:T(8,128)(2,1)}, u32[]{:S(2)}, u32[]{:S(2)}) collective-permute-start(bf16[4,1,2,128,1024]{4,3,2,0,1:T(8,128)(2,1)} %bitcast.96), channel_id=1, source_target_pairs={{0,16},{8,24},{16,0},{24,8},{1,17},{9,25},{17,1},{25,9},{2,18},{10... | collective-permute-start | bytes 6291464 | tf_op jit(solution)/shard_map/ppermute | solution.py:63
  491.9 33.0 %collective-permute-start.52 = (bf16[4,2,1,64,1024]{4,3,2,1,0:T(8,128)(2,1)}, bf16[4,2,1,64,1024]{4,3,2,1,0:T(8,128)(2,1)S(1)}, u32[]{:S(2)}, u32[]{:S(2)}) collective-permute-start(bf16[4,2,1,64,1024]{4,3,2,1,0:T(8,128)(2,1)} %get-tuple-element.263), channel_id=1, source_target_pairs={{0,8},{8,0},{16,24},{24,16},{1,9},{9,1},{17,25},{25,17},{2,10},{10... | collective-permute-start | bytes 3145736 | tf_op jit(solution)/shard_map/ppermute | solution.py:63
  493.1 31.9 %collective-permute-start.53 = (bf16[4,1,2,64,1024]{4,3,2,0,1:T(8,128)(2,1)}, bf16[4,1,2,64,1024]{4,3,2,0,1:T(8,128)(2,1)}, u32[]{:S(2)}, u32[]{:S(2)}) collective-permute-start(bf16[4,1,2,64,1024]{4,3,2,0,1:T(8,128)(2,1)} %bitcast.108), channel_id=1, source_target_pairs={{0,16},{8,24},{16,0},{24,8},{1,17},{9,25},{17,1},{25,9},{2,18},{10... | collective-permute-start | bytes 3145736 | tf_op jit(solution)/shard_map/ppermute | solution.py:63
  516.0 75.7 %collective-permute-start.57 = (bf16[4,2,1,128,1024]{4,3,2,1,0:T(8,128)(2,1)}, bf16[4,2,1,128,1024]{4,3,2,1,0:T(8,128)(2,1)}, u32[]{:S(2)}, u32[]{:S(2)}) collective-permute-start(bf16[4,2,1,128,1024]{4,3,2,1,0:T(8,128)(2,1)} %get-tuple-element.278), channel_id=1, source_target_pairs={{0,8},{8,0},{16,24},{24,16},{1,9},{9,1},{17,25},{25,17},{2,10},{10... | collective-permute-start | bytes 6291464 | tf_op jit(solution)/shard_map/ppermute | solution.py:63
  529.0 65.0 %collective-permute-start.58 = (bf16[4,1,2,128,1024]{4,3,2,0,1:T(8,128)(2,1)}, bf16[4,1,2,128,1024]{4,3,2,0,1:T(8,128)(2,1)}, u32[]{:S(2)}, u32[]{:S(2)}) collective-permute-start(bf16[4,1,2,128,1024]{4,3,2,0,1:T(8,128)(2,1)} %bitcast.114), channel_id=1, source_target_pairs={{0,16},{8,24},{16,0},{24,8},{1,17},{9,25},{17,1},{25,9},{2,18},{10... | collective-permute-start | bytes 6291464 | tf_op jit(solution)/shard_map/ppermute | solution.py:63
  537.5 31.1 %collective-permute-start.56 = (bf16[2,128,2048]{2,1,0:T(8,128)(2,1)}, bf16[2,128,2048]{2,1,0:T(8,128)(2,1)}, u32[]{:S(2)}, u32[]{:S(2)}) collective-permute-start(bf16[2,128,2048]{2,1,0:T(8,128)(2,1)} %get-tuple-element.275), channel_id=1, source_target_pairs={{0,2},{1,3},{2,0},{3,1},{4,6},{5,7},{6,4},{7,5},{8,10},{9,11},{10,... | collective-permute-start | bytes 3145736 | tf_op jit(solution)/shard_map/ppermute | solution.py:63
  567.7 33.1 %collective-permute-start.59 = (bf16[4,1,64,1024]{3,2,1,0:T(8,128)(2,1)}, bf16[4,1,64,1024]{3,2,1,0:T(8,128)(2,1)}, u32[]{:S(2)}, u32[]{:S(2)}) collective-permute-start(bf16[4,1,64,1024]{3,2,1,0:T(8,128)(2,1)} %get-tuple-element.286), channel_id=1, source_target_pairs={{0,16},{8,24},{16,0},{24,8},{1,17},{9,25},{17,1},{25,9},{2,18},{10... | collective-permute-start | bytes 1572872 | tf_op jit(solution)/shard_map/ppermute | solution.py:63
  568.6 33.2 %collective-permute-start.60 = (bf16[4,1,64,1024]{3,2,1,0:T(8,128)(2,1)}, bf16[4,1,64,1024]{3,2,1,0:T(8,128)(2,1)}, u32[]{:S(2)}, u32[]{:S(2)}) collective-permute-start(bf16[4,1,64,1024]{3,2,1,0:T(8,128)(2,1)} %get-tuple-element.287), channel_id=1, source_target_pairs={{0,8},{8,0},{16,24},{24,16},{1,9},{9,1},{17,25},{25,17},{2,10},{10... | collective-permute-start | bytes 1572872 | tf_op jit(solution)/shard_map/ppermute | solution.py:63
  590.6 30.2 %collective-permute-start.62 = (bf16[2,688,256]{2,1,0:T(8,128)(2,1)}, bf16[2,688,256]{2,1,0:T(8,128)(2,1)S(1)}, u32[]{:S(2)}, u32[]{:S(2)}) collective-permute-start(bf16[2,688,256]{2,1,0:T(8,128)(2,1)} %get-tuple-element.316), channel_id=1, source_target_pairs={{0,2},{1,3},{2,0},{3,1},{4,6},{5,7},{6,4},{7,5},{8,10},{9,11},{10,... | collective-permute-start | bytes 2113544 | tf_op jit(solution)/shard_map/ppermute | solution.py:63
  591.7 45.4 %collective-permute-start.82 = (bf16[1,1,128,2048]{3,2,1,0:T(8,128)(2,1)S(1)}, bf16[1,1,128,2048]{3,2,1,0:T(8,128)(2,1)}, u32[]{:S(2)}, u32[]{:S(2)}) collective-permute-start(bf16[1,1,128,2048]{3,2,1,0:T(8,128)(2,1)S(1)} %copy-done.74), channel_id=1, source_target_pairs={{0,4},{1,5},{2,6},{3,7},{4,0},{5,1},{6,2},{7,3},{8,12},{9,13},{10,... | collective-permute-start | bytes 1572872 | tf_op jit(solution)/shard_map/ppermute | solution.py:63
  599.5 30.0 %collective-permute-start.64 = (bf16[4,1,128,1024]{3,2,1,0:T(8,128)(2,1)S(1)}, bf16[4,1,128,1024]{3,2,1,0:T(8,128)(2,1)S(1)}, u32[]{:S(2)}, u32[]{:S(2)}) collective-permute-start(bf16[4,1,128,1024]{3,2,1,0:T(8,128)(2,1)S(1)} %get-tuple-element.303), channel_id=1, source_target_pairs={{0,8},{8,0},{16,24},{24,16},{1,9},{9,1},{17,25},{25,17},{2,10},{10... | collective-permute-start | bytes 3145736 | tf_op jit(solution)/shard_map/ppermute | solution.py:63
  600.7 30.0 %collective-permute-start.63 = (bf16[4,1,128,1024]{3,2,1,0:T(8,128)(2,1)S(1)}, bf16[4,1,128,1024]{3,2,1,0:T(8,128)(2,1)S(1)}, u32[]{:S(2)}, u32[]{:S(2)}) collective-permute-start(bf16[4,1,128,1024]{3,2,1,0:T(8,128)(2,1)S(1)} %get-tuple-element.302), channel_id=1, source_target_pairs={{0,16},{8,24},{16,0},{24,8},{1,17},{9,25},{17,1},{25,9},{2,18},{10... | collective-permute-start | bytes 3145736 | tf_op jit(solution)/shard_map/ppermute | solution.py:63
  603.3 33.9 %collective-permute-start.84 = (bf16[2,64,2048]{2,1,0:T(8,128)(2,1)S(1)}, bf16[2,64,2048]{2,1,0:T(8,128)(2,1)S(1)}, u32[]{:S(2)}, u32[]{:S(2)}) collective-permute-start(bf16[2,64,2048]{2,1,0:T(8,128)(2,1)S(1)} %get-tuple-element.310), channel_id=1, source_target_pairs={{0,2},{1,3},{2,0},{3,1},{4,6},{5,7},{6,4},{7,5},{8,10},{9,11},{10,... | collective-permute-start | bytes 1572872 | tf_op jit(solution)/shard_map/ppermute | solution.py:63
  633.3 50.5 %collective-permute-start.90 = (bf16[2,128,2048]{2,1,0:T(8,128)(2,1)}, bf16[2,128,2048]{2,1,0:T(8,128)(2,1)S(1)}, u32[]{:S(2)}, u32[]{:S(2)}) collective-permute-start(bf16[2,128,2048]{2,1,0:T(8,128)(2,1)} %get-tuple-element.324), channel_id=1, source_target_pairs={{0,2},{1,3},{2,0},{3,1},{4,6},{5,7},{6,4},{7,5},{8,10},{9,11},{10,... | collective-permute-start | bytes 3145736 | tf_op jit(solution)/shard_map/ppermute | solution.py:63
  687.3 43.6 %collective-permute-start.88 = (bf16[192,2048]{1,0:T(8,128)(2,1)S(1)}, bf16[192,2048]{1,0:T(8,128)(2,1)S(1)}, u32[]{:S(2)}, u32[]{:S(2)}) collective-permute-start(bf16[192,2048]{1,0:T(8,128)(2,1)S(1)} %maximum_maximum_fusion), channel_id=1, source_target_pairs={{0,16},{8,24},{16,0},{24,8},{1,17},{9,25},{17,1},{25,9},{2,18},{10... | collective-permute-start | bytes 2359304 | tf_op jit(solution)/shard_map/ppermute | solution.py:63
  688.3 47.4 %collective-permute-start.87 = (bf16[192,2048]{1,0:T(8,128)(2,1)S(1)}, bf16[192,2048]{1,0:T(8,128)(2,1)S(1)}, u32[]{:S(2)}, u32[]{:S(2)}) collective-permute-start(bf16[192,2048]{1,0:T(8,128)(2,1)S(1)} %maximum_maximum_fusion), channel_id=1, source_target_pairs={{0,8},{8,0},{16,24},{24,16},{1,9},{9,1},{17,25},{25,17},{2,10},{10... | collective-permute-start | bytes 2359304 | tf_op jit(solution)/shard_map/ppermute | solution.py:63
  690.1 39.8 %collective-permute-start.74 = (f32[2,1,1792]{2,0,1:T(2,128)S(1)}, f32[2,1,1792]{2,0,1:T(2,128)S(1)}, u32[]{:S(2)}, u32[]{:S(2)}) collective-permute-start(f32[2,1,1792]{2,0,1:T(2,128)S(1)} %dynamic-slice_add_fusion), channel_id=1, source_target_pairs={{0,8},{8,0},{16,24},{24,16},{1,9},{9,1},{17,25},{25,17},{2,10},{10... | collective-permute-start | bytes 43016 | tf_op jit(solution)/shard_map/ppermute | solution.py:63
  730.9 33.6 %collective-permute-start.89 = (bf16[192,2048]{1,0:T(8,128)(2,1)S(1)}, bf16[192,2048]{1,0:T(8,128)(2,1)S(1)}, u32[]{:S(2)}, u32[]{:S(2)}) collective-permute-start(bf16[192,2048]{1,0:T(8,128)(2,1)S(1)} %collective-permute-done.88), channel_id=1, source_target_pairs={{0,8},{8,0},{16,24},{24,16},{1,9},{9,1},{17,25},{25,17},{2,10},{10... | collective-permute-start | bytes 2359304 | tf_op jit(solution)/shard_map/ppermute | solution.py:63
  734.5 38.3 %collective-permute-start.94 = (bf16[128,2048]{1,0:T(8,128)(2,1)S(1)}, bf16[128,2048]{1,0:T(8,128)(2,1)S(1)}, u32[]{:S(2)}, u32[]{:S(2)}) collective-permute-start(bf16[128,2048]{1,0:T(8,128)(2,1)S(1)} %pad_maximum_fusion.18.refs_0_), channel_id=1, source_target_pairs={{0,16},{8,24},{16,0},{24,8},{1,17},{9,25},{17,1},{25,9},{2,18},{10... | collective-permute-start | bytes 1572872 | tf_op jit(solution)/shard_map/ppermute | solution.py:63
  735.7 34.5 %collective-permute-start.80 = (bf16[64,2048]{1,0:T(8,128)(2,1)S(1)}, bf16[64,2048]{1,0:T(8,128)(2,1)S(1)}, u32[]{:S(2)}, u32[]{:S(2)}) collective-permute-start(bf16[64,2048]{1,0:T(8,128)(2,1)S(1)} %pad_maximum_fusion.19.refs_0_), channel_id=1, source_target_pairs={{0,16},{8,24},{16,0},{24,8},{1,17},{9,25},{17,1},{25,9},{2,18},{10... | collective-permute-start | bytes 786440 | tf_op jit(solution)/shard_map/ppermute | solution.py:63
  742.4 30.3 %collective-permute-start.95 = (bf16[128,2048]{1,0:T(8,128)(2,1)S(1)}, bf16[128,2048]{1,0:T(8,128)(2,1)S(1)}, u32[]{:S(2)}, u32[]{:S(2)}) collective-permute-start(bf16[128,2048]{1,0:T(8,128)(2,1)S(1)} %collective-permute-done.93.refs_1_), channel_id=1, source_target_pairs={{0,16},{8,24},{16,0},{24,8},{1,17},{9,25},{17,1},{25,9},{2,18},{10... | collective-permute-start | bytes 1572872 | tf_op jit(solution)/shard_map/ppermute | solution.py:63
  (285 other events, 2565.9 us)

commit v5 on v4

--- a/solution.py
+++ b/solution.py
@@ -1170,7 +1170,7 @@
         else:
             own, got = regroup(after(cotangent, others[-1]))
             d_rows = widen(jnp.concatenate([own, got], 0))
-            beside, planes, neighbours, next_planes, members = [got], [], [], [], [[]] * 3
+            beside, planes, neighbours, next_planes = [got], [], [], []
         arrays, parts, earlier = gather_members(held, [])
         if layer + 1 < LAYERS:
             next_column, next_planes = gather_planes(pieces[2 * layer + 3], planes[-1])
@@ -1178,7 +1178,6 @@
             members = gather_members(held, [])
         arrays[0] = after(arrays[0], *planes[-1:], *next_planes[:1])
         gathered[10], gathered[12] = place_second(arrays, parts, count)
-        gathered[10] = after(gathered[10], *neighbours)
         fetched.append(tuple(gathered))
         tok_rows, saved = forward_layer(
             tok_rows,
@@ -1187,7 +1186,7 @@
             others,
             gathered,
             beside,
-            next_planes[1:] + members[2],
+            next_planes[1:] + neighbours,
         )
         saved_layers.append(saved)
     activation_rows = low(tok_rows)
@@ -1237,14 +1236,15 @@
     first = after(jnp.concatenate([first, mixed_piece(later, layer + 1)], 0), d_rows)
     later.step(new[1], d_rows)
     pieces = spread(later.sent(first, new[1]), True)
+    last_gots = later.gots[new[1]] + [image_got]
+    later.step(new[2], later.sends[new[1]][0])
+    later.join(new[3], [new[1]], later.gots[new[2]][0])
+    while new[2] in later.running:
+        later.step(new[2], d_rows)
+    while new[3] in later.running:
+        later.step(new[3], pieces[1])
     write_block(layer + 1, [piece[:rows] for piece in pieces])
     write_mixed(layer + 1, [piece[rows:] for piece in pieces])
-    last_gots = later.gots[new[1]] + [image_got]
-    later.join(new[3], [new[1]], d_rows)
-    while new[3] in later.running:
-        later.step(new[3], d_rows)
-    while new[2] in later.running:
-        later.step(new[2], d_rows)
     write_block(layer, spread(block_piece(later, layer), False))
     write_mixed(layer, spread(mixed_piece(later, layer), False))
     stacked = [None] * len(all_params)

time: 787 us -> 795 us (1.010)
  waiting for transfers between devices: 306 us -> 318 us
    ppermute x96, waiting for transfers between devices: 306 us -> 318 us  [swap(): return lax.ppermute(tensor, axis, [(i, i ^ offset) for i in range(count)])]
    unnamed x462 -> x454, local copies, waits for them, and re-layouts: 50 us -> 45.4 us
  transfers between devices with their start and end apart: 96 -> 96, of which waited for: 42 -> 41; matrix products, arithmetic and copies ran while one was open for 12% -> 12% of each run, Pallas kernels for 26% -> 26%
where the time goes in v5:
time: 795 us; the launch traced here: 784 us
  waiting for transfers between devices  318 us (40%)
  Pallas kernels  230 us (29%)
  starting transfers between devices  86.4 us (11%)
  local copies, waits for them, and re-layouts  74.5 us (9%)
  other arithmetic  47.7 us (6%)
  matrix products  23.3 us (3%)
    ppermute x96, waiting for transfers between devices, swap(): return lax.ppermute(tensor, axis, [(i, i ^ offset) for i in range(count)])  318 us
    ppermute x96, starting transfers between devices, swap(): return lax.ppermute(tensor, axis, [(i, i ^ offset) for i in range(count)])  86.4 us
    pallas_call x4, Pallas kernels, attend_back(): pl.pallas_call(functools.partial(attend_back_kernel, scale * math.log2(ma...  65.5 us
    unnamed x454, local copies, waits for them, and re-layouts  45.4 us
    pallas_call x2, Pallas kernels, attend(): pl.pallas_call(functools.partial(attend_kernel, factor, len(parts)), out_...  36.7 us
    pallas_call x4, Pallas kernels, grad_call(): pl.pallas_call(functools.partial(kernel, shapes), out_shape=out_shapes, g...  32.6 us
    pallas_call x4, Pallas kernels, place(): pl.pallas_call(functools.partial(place_kernel, pieces[0].shape[1] // 2, b...  23 us
    pallas_call x2, Pallas kernels, feed_forward(): pl.pallas_call(expand_kernel, out_shape=[jax.ShapeDtypeStruct((tokens, un...  19.6 us
  transfers between devices with their start and end apart: 96, of which 41 were waited for; matrix products, arithmetic and copies ran while one was open for 12% of the time, Pallas kernels for 26%

profile of v5, /device:TPU:0, one launch (start us, length us, event | category | flops | bytes accessed | tf_op | source)
XLA Modules:
  0.0 784.5 jit_solution(9971316683614233901)
XLA Ops:
  24.2 9.1 %collective-permute-done.1 = bf16[1,64,2048]{2,1,0:T(8,128)(2,1)S(1)} collective-permute-done((bf16[1,64,2048]{2,1,0:T(8,128)(2,1)S(1)}, bf16[1,64,2048]{2,1,0:T(8,128)(2,1)S(1)}, u32[]{:S(2)}, u32[]{:S(2)}) %collective-permute-start.1) | collective-permute-done | bytes 262176 | tf_op jit(solution)/shard_map/ppermute | solution.py:63
  38.3 13.7 %collective-permute-done.2 = bf16[172,1024]{1,0:T(8,128)(2,1)S(1)} collective-permute-done((bf16[172,1024]{1,0:T(8,128)(2,1)S(1)}, bf16[172,1024]{1,0:T(8,128)(2,1)S(1)}, u32[]{:S(2)}, u32[]{:S(2)}) %collective-permute-start.2) | collective-permute-done | bytes 352288 | tf_op jit(solution)/shard_map/ppermute | solution.py:63
  61.0 16.1 %collective-permute-done.8 = bf16[1,128,2048]{2,1,0:T(8,128)(2,1)S(1)} collective-permute-done((bf16[1,128,2048]{2,1,0:T(8,128)(2,1)S(1)}, bf16[1,128,2048]{2,1,0:T(8,128)(2,1)S(1)}, u32[]{:S(2)}, u32[]{:S(2)}) %collective-permute-start.8) | collective-permute-done | bytes 524320 | tf_op jit(solution)/shard_map/ppermute | solution.py:63
  83.8 17.5 %collective-permute-done.9 = bf16[2,128,2048]{2,1,0:T(8,128)(2,1)S(1)} collective-permute-done((bf16[2,128,2048]{2,1,0:T(8,128)(2,1)S(1)}, bf16[2,128,2048]{2,1,0:T(8,128)(2,1)S(1)}, u32[]{:S(2)}, u32[]{:S(2)}) %collective-permute-start.9) | collective-permute-done | bytes 1048608 | tf_op jit(solution)/shard_map/ppermute | solution.py:63
  112.7 25.4 %collective-permute-done.14.refs_1_.refs_3_ = bf16[688,1024]{1,0:T(8,128)(2,1)} collective-permute-done((bf16[688,1024]{1,0:T(8,128)(2,1)S(1)}, bf16[688,1024]{1,0:T(8,128)(2,1)}, u32[]{:S(2)}, u32[]{:S(2)}) %collective-permute-start.14) | collective-permute-done | bytes 1409056 | tf_op jit(solution)/shard_map/ppermute | solution.py:63
  140.9 18.3 %shard_map.298 = (bf16[688,512]{1,0:T(8,128)(2,1)}, f32[688,512]{1,0:T(8,128)}) custom-call(bf16[688,1536]{1,0:T(8,128)(2,1)} %copy-done.72, bf16[688,1536]{1,0:T(8,128)(2,1)} %copy-done.72, bf16[688,1024]{1,0:T(8,128)(2,1)} %collective-permute-done.14.refs_1_.refs_3_, bf16[688,1536]{1,0:T(8,128)(2,1)} %copy-done.72, ...), custom_call_target="tpu_custom_call" | custom-call | flops 1000 | bytes 1000 | tf_op jit(solution)/shard_map/pallas_call | solution.py:760
  176.1 19.0 %collective-permute-done.19 = bf16[1,128,2048]{2,1,0:T(8,128)(2,1)S(1)} collective-permute-done((bf16[1,128,2048]{2,1,0:T(8,128)(2,1)S(1)}, bf16[1,128,2048]{2,1,0:T(8,128)(2,1)S(1)}, u32[]{:S(2)}, u32[]{:S(2)}) %collective-permute-start.19) | collective-permute-done | bytes 524320 | tf_op jit(solution)/shard_map/ppermute | solution.py:63
  212.4 8.1 %shard_map.299 = (bf16[4,2,4,32,2048]{4,3,2,1,0:T(8,128)(2,1)S(1)}, bf16[4,4,2,64,1024]{4,3,2,1,0:T(8,128)(2,1)S(1)}) custom-call(s32[2]{0:T(128)S(1)} %pad_add_fusion.1.where_ref, bf16[4,128,2048]{2,1,0:T(8,128)(2,1)S(1)} %bitcast.312, bf16[4,128,2048]{2,1,0:T(8,128)(2,1)S(1)} %copy-done.17, bf16[4,128,2048]{2,1,0:T(8,128)(2,1)S(1)} %copy-done.19, ...), custom_call_target="tpu_custom_call" | custom-call | flops 1000 | bytes 1000 | tf_op jit(solution)/shard_map/pallas_call | solution.py:169
  220.5 9.8 %shard_map.300 = (bf16[688,2048]{1,0:T(8,128)(2,1)S(1)}, bf16[688,2048]{1,0:T(8,128)(2,1)S(1)}, f32[344,1024]{1,0:T(8,128)S(1)}, bf16[344,1024]{1,0:T(8,128)(2,1)S(1)}) custom-call(bf16[688,1024]{1,0:T(8,128)(2,1)S(1)} %pad_maximum_fusion.3.rows_ref.left_ref, bf16[1024,2048]{1,0:T(8,128)(2,1)S(1)} %bitcast.302, f32[1,2048]{1,0:T(1,128)S(1)} %bitcast.352, ...), custom_call_target="tpu_custom_call" | custom-call | flops 1000 | bytes 1000 | tf_op jit(solution)/shard_map/pallas_call | solution.py:859
  238.3 12.0 %collective-permute-done.30.refs_4_ = bf16[4,32,2048]{2,1,0:T(8,128)(2,1)S(1)} collective-permute-done((bf16[4,32,2048]{2,1,0:T(8,128)(2,1)S(1)}, bf16[4,32,2048]{2,1,0:T(8,128)(2,1)S(1)}, u32[]{:S(2)}, u32[]{:S(2)}) %collective-permute-start.30) | collective-permute-done | bytes 524320 | tf_op jit(solution)/shard_map/ppermute | solution.py:63
  265.3 26.5 %collective-permute-done.31.refs_1_.refs_3_ = bf16[688,1024]{1,0:T(8,128)(2,1)S(1)} collective-permute-done((bf16[688,1024]{1,0:T(8,128)(2,1)S(1)}, bf16[688,1024]{1,0:T(8,128)(2,1)S(1)}, u32[]{:S(2)}, u32[]{:S(2)}) %collective-permute-start.31) | collective-permute-done | bytes 1409056 | tf_op jit(solution)/shard_map/ppermute | solution.py:63
  294.2 18.5 %shard_map.302 = (bf16[688,512]{1,0:T(8,128)(2,1)}, f32[688,512]{1,0:T(8,128)}) custom-call(bf16[688,1536]{1,0:T(8,128)(2,1)} %copy-done.73, bf16[688,1536]{1,0:T(8,128)(2,1)} %copy-done.73, bf16[688,1024]{1,0:T(8,128)(2,1)} %copy-done.77, bf16[688,1536]{1,0:T(8,128)(2,1)} %copy-done.73, bf16[688,1024]{1,0:T(8,128)(2,1)} %copy-done.77), custom_call_target="tpu_custom_call" | custom-call | flops 1000 | bytes 1000 | tf_op jit(solution)/shard_map/pallas_call | solution.py:760
  324.7 16.8 %collective-permute-done.38.refs_4_ = bf16[4,64,2048]{2,1,0:T(8,128)(2,1)} collective-permute-done((bf16[4,64,2048]{2,1,0:T(8,128)(2,1)}, bf16[4,64,2048]{2,1,0:T(8,128)(2,1)}, u32[]{:S(2)}, u32[]{:S(2)}) %collective-permute-start.38) | collective-permute-done | bytes 1048608 | tf_op jit(solution)/shard_map/ppermute | solution.py:63
  348.2 7.8 shard_map.303
  356.2 9.8 %shard_map.304 = (bf16[688,2048]{1,0:T(8,128)(2,1)S(1)}, bf16[688,2048]{1,0:T(8,128)(2,1)S(1)}, f32[344,1024]{1,0:T(8,128)S(1)}, bf16[344,1024]{1,0:T(8,128)(2,1)S(1)}) custom-call(bf16[688,1024]{1,0:T(8,128)(2,1)S(1)} %pad_maximum_fusion.5.rows_ref.left_ref, bf16[1024,2048]{1,0:T(8,128)(2,1)S(1)} %bitcast.306, f32[1,2048]{1,0:T(1,128)S(1)} %bitcast.351, ...), custom_call_target="tpu_custom_call" | custom-call | flops 1000 | bytes 1000 | tf_op jit(solution)/shard_map/pallas_call | solution.py:859
  371.8 9.6 %shard_map.305 = (bf16[688,2048]{1,0:T(8,128)(2,1)S(1)}, f32[1,2048]{1,0:T(1,128)S(1)}, f32[344,1024]{1,0:T(8,128)S(1)}, bf16[344,1024]{1,0:T(8,128)(2,1)}) custom-call(bf16[688,1024]{1,0:T(8,128)(2,1)S(1)} %pad_maximum_fusion.6.grad_ref.other_ref, bf16[2048,1024]{1,0:T(8,128)(2,1)S(1)} %bitcast.309, bf16[688,2048]{1,0:T(8,128)(2,1)S(1)} %get-tuple-element.236.slope_ref, ...), custom_call_target="tpu_custom_call" | custom-call | flops 1000 | bytes 1000 | tf_op jit(solution)/shard_map/pallas_call | solution.py:897
  390.3 10.7 %shard_map.306 = (bf16[4,2,1,128,1024]{4,3,2,1,0:T(8,128)(2,1)S(1)}, bf16[4,2,1,128,1024]{4,3,2,1,0:T(8,128)(2,1)}, bf16[4,1,2,128,1024]{4,3,2,1,0:T(8,128)(2,1)S(1)}, bf16[4,1,2,128,1024]{4,3,2,1,0:T(8,128)(2,1)}) custom-call(s32[2]{0:T(128)S(1)} %pad_add_fusion.2.where_ref, bf16[688,1024]{1,0:T(8,128)(2,1)S(1)} %copy-done.5, ...), custom_call_target="tpu_custom_call" | custom-call | flops 1000 | bytes 1000 | tf_op jit(solution)/shard_map/pallas_call | solution.py:369
  415.0 16.2 %shard_map.307 = (bf16[688,256]{1,0:T(8,128)(2,1)}, bf16[2,688,256]{2,1,0:T(8,128)(2,1)}, bf16[2,688,256]{2,1,0:T(8,128)(2,1)}) custom-call(bf16[688,1536]{1,0:T(8,128)(2,1)} %copy-done.73, bf16[688,1536]{1,0:T(8,128)(2,1)} %copy-done.73, bf16[688,1024]{1,0:T(8,128)(2,1)} %copy-done.77, bf16[688,1536]{1,0:T(8,128)(2,1)} %copy-done.73, ...), custom_call_target="tpu_custom_call" | custom-call | flops 1000 | bytes 1000 | tf_op jit(solution)/shard_map/pallas_call | solution.py:804
  431.3 16.5 %shard_map.308 = (bf16[688,256]{1,0:T(8,128)(2,1)}, bf16[2,688,256]{2,1,0:T(8,128)(2,1)}, bf16[2,688,256]{2,1,0:T(8,128)(2,1)}) custom-call(bf16[688,1536]{1,0:T(8,128)(2,1)} %copy-done.73, bf16[688,1536]{1,0:T(8,128)(2,1)} %copy-done.73, bf16[688,1024]{1,0:T(8,128)(2,1)} %copy-done.77, bf16[688,1536]{1,0:T(8,128)(2,1)} %copy-done.73, ...), custom_call_target="tpu_custom_call" | custom-call | flops 1000 | bytes 1000 | tf_op jit(solution)/shard_map/pallas_call | solution.py:804
  490.4 8.7 %shard_map.311 = (bf16[688,2048]{1,0:T(8,128)(2,1)S(1)}, f32[1,2048]{1,0:T(1,128)S(1)}, f32[344,1024]{1,0:T(8,128)S(1)}, bf16[344,1024]{1,0:T(8,128)(2,1)S(1)}) custom-call(bf16[688,1024]{1,0:T(8,128)(2,1)S(1)} %pad_maximum_fusion.8.grad_ref.other_ref, bf16[2048,1024]{1,0:T(8,128)(2,1)S(1)} %bitcast.305, bf16[688,2048]{1,0:T(8,128)(2,1)S(1)} %copy-done.31, ...), custom_call_target="tpu_custom_call" | custom-call | flops 1000 | bytes 1000 | tf_op jit(solution)/shard_map/pallas_call | solution.py:897
  501.5 10.5 %shard_map.313 = (bf16[4,2,1,128,1024]{4,3,2,1,0:T(8,128)(2,1)S(1)}, bf16[4,2,1,128,1024]{4,3,2,1,0:T(8,128)(2,1)}, bf16[4,1,2,128,1024]{4,3,2,1,0:T(8,128)(2,1)S(1)}, bf16[4,1,2,128,1024]{4,3,2,1,0:T(8,128)(2,1)}) custom-call(s32[2]{0:T(128)S(1)} %pad_add_fusion.2.where_ref, bf16[688,1024]{1,0:T(8,128)(2,1)S(1)} %pad_maximum_fusion.3.rows_ref.left_ref, ...), custom_call_target="tpu_custom_call" | custom-call | flops 1000 | bytes 1000 | tf_op jit(solution)/shard_map/pallas_call | solution.py:369
  513.4 7.9 %collective-permute-done.52.refs_1_ = bf16[4,2,1,64,1024]{4,3,2,1,0:T(8,128)(2,1)S(1)} collective-permute-done((bf16[4,2,1,64,1024]{4,3,2,1,0:T(8,128)(2,1)}, bf16[4,2,1,64,1024]{4,3,2,1,0:T(8,128)(2,1)S(1)}, u32[]{:S(2)}, u32[]{:S(2)}) %collective-permute-start.52) | collective-permute-done | bytes 1048608 | tf_op jit(solution)/shard_map/ppermute | solution.py:63
  544.4 16.4 %shard_map.315 = (bf16[688,256]{1,0:T(8,128)(2,1)}, bf16[2,688,256]{2,1,0:T(8,128)(2,1)}, bf16[2,688,256]{2,1,0:T(8,128)(2,1)}) custom-call(bf16[688,1536]{1,0:T(8,128)(2,1)} %copy-done.72, bf16[688,1536]{1,0:T(8,128)(2,1)} %copy-done.72, bf16[688,1024]{1,0:T(8,128)(2,1)} %collective-permute-done.14.refs_1_.refs_3_, bf16[688,1536]{1,0:T(8,128)(2,1)} %copy-done.72, ...), custom_call_target="tpu_custom_call" | custom-call | flops 1000 | bytes 1000 | tf_op jit(solution)/shard_map/pallas_call | solution.py:804
  568.7 16.5 %shard_map.317 = (bf16[688,256]{1,0:T(8,128)(2,1)}, bf16[2,688,256]{2,1,0:T(8,128)(2,1)}, bf16[2,688,256]{2,1,0:T(8,128)(2,1)}) custom-call(bf16[688,1536]{1,0:T(8,128)(2,1)} %copy-done.72, bf16[688,1536]{1,0:T(8,128)(2,1)} %copy-done.72, bf16[688,1024]{1,0:T(8,128)(2,1)} %collective-permute-done.14.refs_1_.refs_3_, bf16[688,1536]{1,0:T(8,128)(2,1)} %copy-done.72, ...), custom_call_target="tpu_custom_call" | custom-call | flops 1000 | bytes 1000 | tf_op jit(solution)/shard_map/pallas_call | solution.py:804
  602.3 14.7 %collective-permute-done.62 = bf16[2,688,256]{2,1,0:T(8,128)(2,1)S(1)} collective-permute-done((bf16[2,688,256]{2,1,0:T(8,128)(2,1)}, bf16[2,688,256]{2,1,0:T(8,128)(2,1)S(1)}, u32[]{:S(2)}, u32[]{:S(2)}) %collective-permute-start.62) | collective-permute-done | bytes 704544 | tf_op jit(solution)/shard_map/ppermute | solution.py:63
  639.8 12.7 %collective-permute-done.68 = bf16[4,1,2,64,1024]{4,3,2,0,1:T(8,128)(2,1)S(1)} collective-permute-done((bf16[4,1,2,64,1024]{4,3,2,0,1:T(8,128)(2,1)S(1)}, bf16[4,1,2,64,1024]{4,3,2,0,1:T(8,128)(2,1)S(1)}, u32[]{:S(2)}, u32[]{:S(2)}) %collective-permute-start.68) | collective-permute-done | bytes 1048608 | tf_op jit(solution)/shard_map/ppermute | solution.py:63
  659.0 7.0 collective-permute-done.66
  685.9 21.2 %collective-permute-done.77 = bf16[1,1,128,2048]{3,2,1,0:T(8,128)(2,1)S(1)} collective-permute-done((bf16[1,1,128,2048]{3,2,1,0:T(8,128)(2,1)S(1)}, bf16[1,1,128,2048]{3,2,1,0:T(8,128)(2,1)S(1)}, u32[]{:S(2)}, u32[]{:S(2)}) %collective-permute-start.77) | collective-permute-done | bytes 524320 | tf_op jit(solution)/shard_map/ppermute | solution.py:63
  708.4 12.9 %collective-permute-done.78 = bf16[2,64,2048]{2,1,0:T(8,128)(2,1)S(1)} collective-permute-done((bf16[2,64,2048]{2,1,0:T(8,128)(2,1)S(1)}, bf16[2,64,2048]{2,1,0:T(8,128)(2,1)S(1)}, u32[]{:S(2)}, u32[]{:S(2)}) %collective-permute-start.78) | collective-permute-done | bytes 524320 | tf_op jit(solution)/shard_map/ppermute | solution.py:63
  721.7 13.8 %collective-permute-done.85 = bf16[1,1,64,2048]{3,2,1,0:T(8,128)(2,1)S(1)} collective-permute-done((bf16[1,1,64,2048]{3,2,1,0:T(8,128)(2,1)S(1)}, bf16[1,1,64,2048]{3,2,1,0:T(8,128)(2,1)S(1)}, u32[]{:S(2)}, u32[]{:S(2)}) %collective-permute-start.85) | collective-permute-done | bytes 262176 | tf_op jit(solution)/shard_map/ppermute | solution.py:63
  743.8 6.8 collective-permute-done.93.refs_1_
  758.7 13.9 %collective-permute-done.91 = bf16[192,2048]{1,0:T(8,128)(2,1)S(1)} collective-permute-done((bf16[192,2048]{1,0:T(8,128)(2,1)S(1)}, bf16[192,2048]{1,0:T(8,128)(2,1)S(1)}, u32[]{:S(2)}, u32[]{:S(2)}) %collective-permute-start.91) | collective-permute-done | bytes 786464 | tf_op jit(solution)/shard_map/ppermute | solution.py:63
  (853 shorter events, 335.5 us)
Async XLA Ops:
  107.1 30.9 %collective-permute-start.14 = (bf16[688,1024]{1,0:T(8,128)(2,1)S(1)}, bf16[688,1024]{1,0:T(8,128)(2,1)}, u32[]{:S(2)}, u32[]{:S(2)}) collective-permute-start(bf16[688,1024]{1,0:T(8,128)(2,1)S(1)} %slice.495), channel_id=1, source_target_pairs={{0,2},{1,3},{2,0},{3,1},{4,6},{5,7},{6,4},{7,5},{8,10},{9,11},{10,... | collective-permute-start | bytes 4227080 | tf_op jit(solution)/shard_map/ppermute | solution.py:63
  108.7 54.5 %collective-permute-start.20 = (bf16[4,128,2048]{2,1,0:T(8,128)(2,1)S(1)}, bf16[4,128,2048]{2,1,0:T(8,128)(2,1)S(1)}, u32[]{:S(2)}, u32[]{:S(2)}) collective-permute-start(bf16[4,128,2048]{2,1,0:T(8,128)(2,1)S(1)} %bitcast.310), channel_id=1, source_target_pairs={{0,8},{8,0},{16,24},{24,16},{1,9},{9,1},{17,25},{25,17},{2,10},{10... | collective-permute-start | bytes 6291464 | tf_op jit(solution)/shard_map/ppermute | solution.py:63
  110.3 53.1 %collective-permute-start.21 = (bf16[4,128,2048]{2,1,0:T(8,128)(2,1)S(1)}, bf16[4,128,2048]{2,1,0:T(8,128)(2,1)S(1)}, u32[]{:S(2)}, u32[]{:S(2)}) collective-permute-start(bf16[4,128,2048]{2,1,0:T(8,128)(2,1)S(1)} %bitcast.311), channel_id=1, source_target_pairs={{0,16},{8,24},{16,0},{24,8},{1,17},{9,25},{17,1},{25,9},{2,18},{10... | collective-permute-start | bytes 6291464 | tf_op jit(solution)/shard_map/ppermute | solution.py:63
  163.4 33.3 %collective-permute-start.23 = (bf16[4,64,2048]{2,1,0:T(8,128)(2,1)S(1)}, bf16[4,64,2048]{2,1,0:T(8,128)(2,1)S(1)}, u32[]{:S(2)}, u32[]{:S(2)}) collective-permute-start(bf16[4,64,2048]{2,1,0:T(8,128)(2,1)S(1)} %slice.509), channel_id=1, source_target_pairs={{0,16},{8,24},{16,0},{24,8},{1,17},{9,25},{17,1},{25,9},{2,18},{10... | collective-permute-start | bytes 3145736 | tf_op jit(solution)/shard_map/ppermute | solution.py:63
  165.0 32.6 %collective-permute-start.22 = (bf16[4,64,2048]{2,1,0:T(8,128)(2,1)S(1)}, bf16[4,64,2048]{2,1,0:T(8,128)(2,1)S(1)}, u32[]{:S(2)}, u32[]{:S(2)}) collective-permute-start(bf16[4,64,2048]{2,1,0:T(8,128)(2,1)S(1)} %slice.508), channel_id=1, source_target_pairs={{0,8},{8,0},{16,24},{24,16},{1,9},{9,1},{17,25},{25,17},{2,10},{10... | collective-permute-start | bytes 3145736 | tf_op jit(solution)/shard_map/ppermute | solution.py:63
  196.6 35.3 %collective-permute-start.24 = (bf16[2,128,2048]{2,1,0:T(8,128)(2,1)}, bf16[2,128,2048]{2,1,0:T(8,128)(2,1)}, u32[]{:S(2)}, u32[]{:S(2)}) collective-permute-start(bf16[2,128,2048]{2,1,0:T(8,128)(2,1)} %get-tuple-element.217), channel_id=1, source_target_pairs={{0,2},{1,3},{2,0},{3,1},{4,6},{5,7},{6,4},{7,5},{8,10},{9,11},{10,... | collective-permute-start | bytes 3145736 | tf_op jit(solution)/shard_map/ppermute | solution.py:63
  198.6 33.3 %collective-permute-start.25 = (bf16[4,64,2048]{2,1,0:T(8,128)(2,1)}, bf16[4,64,2048]{2,1,0:T(8,128)(2,1)S(1)}, u32[]{:S(2)}, u32[]{:S(2)}) collective-permute-start(bf16[4,64,2048]{2,1,0:T(8,128)(2,1)} %bitcast.68.refs_0_), channel_id=1, source_target_pairs={{0,8},{8,0},{16,24},{24,16},{1,9},{9,1},{17,25},{25,17},{2,10},{10... | collective-permute-start | bytes 3145736 | tf_op jit(solution)/shard_map/ppermute | solution.py:63
  200.1 31.9 %collective-permute-start.26 = (bf16[4,64,2048]{2,1,0:T(8,128)(2,1)}, bf16[4,64,2048]{2,1,0:T(8,128)(2,1)}, u32[]{:S(2)}, u32[]{:S(2)}) collective-permute-start(bf16[4,64,2048]{2,1,0:T(8,128)(2,1)} %bitcast.68.refs_0_), channel_id=1, source_target_pairs={{0,16},{8,24},{16,0},{24,8},{1,17},{9,25},{17,1},{25,9},{2,18},{10... | collective-permute-start | bytes 3145736 | tf_op jit(solution)/shard_map/ppermute | solution.py:63
  259.5 32.3 %collective-permute-start.31 = (bf16[688,1024]{1,0:T(8,128)(2,1)S(1)}, bf16[688,1024]{1,0:T(8,128)(2,1)S(1)}, u32[]{:S(2)}, u32[]{:S(2)}) collective-permute-start(bf16[688,1024]{1,0:T(8,128)(2,1)S(1)} %slice.521), channel_id=1, source_target_pairs={{0,2},{1,3},{2,0},{3,1},{4,6},{5,7},{6,4},{7,5},{8,10},{9,11},{10,... | collective-permute-start | bytes 4227080 | tf_op jit(solution)/shard_map/ppermute | solution.py:63
  263.2 51.2 %collective-permute-start.35 = (bf16[4,128,2048]{2,1,0:T(8,128)(2,1)S(1)}, bf16[4,128,2048]{2,1,0:T(8,128)(2,1)S(1)}, u32[]{:S(2)}, u32[]{:S(2)}) collective-permute-start(bf16[4,128,2048]{2,1,0:T(8,128)(2,1)S(1)} %bitcast.313), channel_id=1, source_target_pairs={{0,8},{8,0},{16,24},{24,16},{1,9},{9,1},{17,25},{25,17},{2,10},{10... | collective-permute-start | bytes 6291464 | tf_op jit(solution)/shard_map/ppermute | solution.py:63
  263.8 51.8 %collective-permute-start.36 = (bf16[4,128,2048]{2,1,0:T(8,128)(2,1)S(1)}, bf16[4,128,2048]{2,1,0:T(8,128)(2,1)}, u32[]{:S(2)}, u32[]{:S(2)}) collective-permute-start(bf16[4,128,2048]{2,1,0:T(8,128)(2,1)S(1)} %bitcast.314), channel_id=1, source_target_pairs={{0,16},{8,24},{16,0},{24,8},{1,17},{9,25},{17,1},{25,9},{2,18},{10... | collective-permute-start | bytes 6291464 | tf_op jit(solution)/shard_map/ppermute | solution.py:63
  323.3 32.8 %collective-permute-start.34 = (bf16[344,1024]{1,0:T(8,128)(2,1)S(1)}, bf16[344,1024]{1,0:T(8,128)(2,1)S(1)}, u32[]{:S(2)}, u32[]{:S(2)}) collective-permute-start(bf16[344,1024]{1,0:T(8,128)(2,1)S(1)} %add_convert_fusion.7), channel_id=1, source_target_pairs={{0,1},{1,0},{2,3},{3,2},{4,5},{5,4},{6,7},{7,6},{8,9},{9,8},{10,11... | collective-permute-start | bytes 2113544 | tf_op jit(solution)/shard_map/ppermute | solution.py:63
  402.3 47.9 %collective-permute-start.44 = (bf16[4,2,1,128,1024]{4,3,2,1,0:T(8,128)(2,1)}, bf16[4,2,1,128,1024]{4,3,2,1,0:T(8,128)(2,1)}, u32[]{:S(2)}, u32[]{:S(2)}) collective-permute-start(bf16[4,2,1,128,1024]{4,3,2,1,0:T(8,128)(2,1)} %get-tuple-element.240), channel_id=1, source_target_pairs={{0,8},{8,0},{16,24},{24,16},{1,9},{9,1},{17,25},{25,17},{2,10},{10... | collective-permute-start | bytes 6291464 | tf_op jit(solution)/shard_map/ppermute | solution.py:63
  404.8 47.5 %collective-permute-start.45 = (bf16[4,1,2,128,1024]{4,3,2,0,1:T(8,128)(2,1)}, bf16[4,1,2,128,1024]{4,3,2,0,1:T(8,128)(2,1)}, u32[]{:S(2)}, u32[]{:S(2)}) collective-permute-start(bf16[4,1,2,128,1024]{4,3,2,0,1:T(8,128)(2,1)} %bitcast.96), channel_id=1, source_target_pairs={{0,16},{8,24},{16,0},{24,8},{1,17},{9,25},{17,1},{25,9},{2,18},{10... | collective-permute-start | bytes 6291464 | tf_op jit(solution)/shard_map/ppermute | solution.py:63
  488.0 33.4 %collective-permute-start.52 = (bf16[4,2,1,64,1024]{4,3,2,1,0:T(8,128)(2,1)}, bf16[4,2,1,64,1024]{4,3,2,1,0:T(8,128)(2,1)S(1)}, u32[]{:S(2)}, u32[]{:S(2)}) collective-permute-start(bf16[4,2,1,64,1024]{4,3,2,1,0:T(8,128)(2,1)} %get-tuple-element.261), channel_id=1, source_target_pairs={{0,8},{8,0},{16,24},{24,16},{1,9},{9,1},{17,25},{25,17},{2,10},{10... | collective-permute-start | bytes 3145736 | tf_op jit(solution)/shard_map/ppermute | solution.py:63
  489.5 31.9 %collective-permute-start.53 = (bf16[4,1,2,64,1024]{4,3,2,0,1:T(8,128)(2,1)}, bf16[4,1,2,64,1024]{4,3,2,0,1:T(8,128)(2,1)}, u32[]{:S(2)}, u32[]{:S(2)}) collective-permute-start(bf16[4,1,2,64,1024]{4,3,2,0,1:T(8,128)(2,1)} %bitcast.108), channel_id=1, source_target_pairs={{0,16},{8,24},{16,0},{24,8},{1,17},{9,25},{17,1},{25,9},{2,18},{10... | collective-permute-start | bytes 3145736 | tf_op jit(solution)/shard_map/ppermute | solution.py:63
  512.0 75.9 %collective-permute-start.57 = (bf16[4,2,1,128,1024]{4,3,2,1,0:T(8,128)(2,1)}, bf16[4,2,1,128,1024]{4,3,2,1,0:T(8,128)(2,1)}, u32[]{:S(2)}, u32[]{:S(2)}) collective-permute-start(bf16[4,2,1,128,1024]{4,3,2,1,0:T(8,128)(2,1)} %get-tuple-element.276), channel_id=1, source_target_pairs={{0,8},{8,0},{16,24},{24,16},{1,9},{9,1},{17,25},{25,17},{2,10},{10... | collective-permute-start | bytes 6291464 | tf_op jit(solution)/shard_map/ppermute | solution.py:63
  525.4 64.9 %collective-permute-start.58 = (bf16[4,1,2,128,1024]{4,3,2,0,1:T(8,128)(2,1)}, bf16[4,1,2,128,1024]{4,3,2,0,1:T(8,128)(2,1)}, u32[]{:S(2)}, u32[]{:S(2)}) collective-permute-start(bf16[4,1,2,128,1024]{4,3,2,0,1:T(8,128)(2,1)} %bitcast.114), channel_id=1, source_target_pairs={{0,16},{8,24},{16,0},{24,8},{1,17},{9,25},{17,1},{25,9},{2,18},{10... | collective-permute-start | bytes 6291464 | tf_op jit(solution)/shard_map/ppermute | solution.py:63
  533.6 31.5 %collective-permute-start.56 = (bf16[2,128,2048]{2,1,0:T(8,128)(2,1)}, bf16[2,128,2048]{2,1,0:T(8,128)(2,1)}, u32[]{:S(2)}, u32[]{:S(2)}) collective-permute-start(bf16[2,128,2048]{2,1,0:T(8,128)(2,1)} %get-tuple-element.273), channel_id=1, source_target_pairs={{0,2},{1,3},{2,0},{3,1},{4,6},{5,7},{6,4},{7,5},{8,10},{9,11},{10,... | collective-permute-start | bytes 3145736 | tf_op jit(solution)/shard_map/ppermute | solution.py:63
  563.8 33.5 %collective-permute-start.59 = (bf16[4,1,64,1024]{3,2,1,0:T(8,128)(2,1)}, bf16[4,1,64,1024]{3,2,1,0:T(8,128)(2,1)}, u32[]{:S(2)}, u32[]{:S(2)}) collective-permute-start(bf16[4,1,64,1024]{3,2,1,0:T(8,128)(2,1)} %get-tuple-element.284), channel_id=1, source_target_pairs={{0,16},{8,24},{16,0},{24,8},{1,17},{9,25},{17,1},{25,9},{2,18},{10... | collective-permute-start | bytes 1572872 | tf_op jit(solution)/shard_map/ppermute | solution.py:63
  565.1 33.1 %collective-permute-start.60 = (bf16[4,1,64,1024]{3,2,1,0:T(8,128)(2,1)}, bf16[4,1,64,1024]{3,2,1,0:T(8,128)(2,1)}, u32[]{:S(2)}, u32[]{:S(2)}) collective-permute-start(bf16[4,1,64,1024]{3,2,1,0:T(8,128)(2,1)} %get-tuple-element.285), channel_id=1, source_target_pairs={{0,8},{8,0},{16,24},{24,16},{1,9},{9,1},{17,25},{25,17},{2,10},{10... | collective-permute-start | bytes 1572872 | tf_op jit(solution)/shard_map/ppermute | solution.py:63
  586.8 30.2 %collective-permute-start.62 = (bf16[2,688,256]{2,1,0:T(8,128)(2,1)}, bf16[2,688,256]{2,1,0:T(8,128)(2,1)S(1)}, u32[]{:S(2)}, u32[]{:S(2)}) collective-permute-start(bf16[2,688,256]{2,1,0:T(8,128)(2,1)} %get-tuple-element.314), channel_id=1, source_target_pairs={{0,2},{1,3},{2,0},{3,1},{4,6},{5,7},{6,4},{7,5},{8,10},{9,11},{10,... | collective-permute-start | bytes 2113544 | tf_op jit(solution)/shard_map/ppermute | solution.py:63
  587.9 45.4 %collective-permute-start.79 = (bf16[1,1,128,2048]{3,2,1,0:T(8,128)(2,1)S(1)}, bf16[1,1,128,2048]{3,2,1,0:T(8,128)(2,1)}, u32[]{:S(2)}, u32[]{:S(2)}) collective-permute-start(bf16[1,1,128,2048]{3,2,1,0:T(8,128)(2,1)S(1)} %copy-done.71), channel_id=1, source_target_pairs={{0,4},{1,5},{2,6},{3,7},{4,0},{5,1},{6,2},{7,3},{8,12},{9,13},{10,... | collective-permute-start | bytes 1572872 | tf_op jit(solution)/shard_map/ppermute | solution.py:63
  595.8 29.9 %collective-permute-start.64 = (bf16[4,1,128,1024]{3,2,1,0:T(8,128)(2,1)S(1)}, bf16[4,1,128,1024]{3,2,1,0:T(8,128)(2,1)S(1)}, u32[]{:S(2)}, u32[]{:S(2)}) collective-permute-start(bf16[4,1,128,1024]{3,2,1,0:T(8,128)(2,1)S(1)} %get-tuple-element.301), channel_id=1, source_target_pairs={{0,8},{8,0},{16,24},{24,16},{1,9},{9,1},{17,25},{25,17},{2,10},{10... | collective-permute-start | bytes 3145736 | tf_op jit(solution)/shard_map/ppermute | solution.py:63
  597.4 29.9 %collective-permute-start.63 = (bf16[4,1,128,1024]{3,2,1,0:T(8,128)(2,1)S(1)}, bf16[4,1,128,1024]{3,2,1,0:T(8,128)(2,1)S(1)}, u32[]{:S(2)}, u32[]{:S(2)}) collective-permute-start(bf16[4,1,128,1024]{3,2,1,0:T(8,128)(2,1)S(1)} %get-tuple-element.300), channel_id=1, source_target_pairs={{0,16},{8,24},{16,0},{24,8},{1,17},{9,25},{17,1},{25,9},{2,18},{10... | collective-permute-start | bytes 3145736 | tf_op jit(solution)/shard_map/ppermute | solution.py:63
  599.7 33.7 %collective-permute-start.81 = (bf16[2,64,2048]{2,1,0:T(8,128)(2,1)S(1)}, bf16[2,64,2048]{2,1,0:T(8,128)(2,1)S(1)}, u32[]{:S(2)}, u32[]{:S(2)}) collective-permute-start(bf16[2,64,2048]{2,1,0:T(8,128)(2,1)S(1)} %get-tuple-element.308), channel_id=1, source_target_pairs={{0,2},{1,3},{2,0},{3,1},{4,6},{5,7},{6,4},{7,5},{8,10},{9,11},{10,... | collective-permute-start | bytes 1572872 | tf_op jit(solution)/shard_map/ppermute | solution.py:63
  629.6 50.7 %collective-permute-start.76 = (bf16[2,128,2048]{2,1,0:T(8,128)(2,1)}, bf16[2,128,2048]{2,1,0:T(8,128)(2,1)S(1)}, u32[]{:S(2)}, u32[]{:S(2)}) collective-permute-start(bf16[2,128,2048]{2,1,0:T(8,128)(2,1)} %get-tuple-element.322), channel_id=1, source_target_pairs={{0,2},{1,3},{2,0},{3,1},{4,6},{5,7},{6,4},{7,5},{8,10},{9,11},{10,... | collective-permute-start | bytes 3145736 | tf_op jit(solution)/shard_map/ppermute | solution.py:63
  683.6 55.7 %collective-permute-start.90 = (bf16[192,2048]{1,0:T(8,128)(2,1)S(1)}, bf16[192,2048]{1,0:T(8,128)(2,1)S(1)}, u32[]{:S(2)}, u32[]{:S(2)}) collective-permute-start(bf16[192,2048]{1,0:T(8,128)(2,1)S(1)} %maximum_maximum_fusion), channel_id=1, source_target_pairs={{0,16},{8,24},{16,0},{24,8},{1,17},{9,25},{17,1},{25,9},{2,18},{10... | collective-permute-start | bytes 2359304 | tf_op jit(solution)/shard_map/ppermute | solution.py:63
  707.5 30.6 %collective-permute-start.74 = (f32[2,1,1792]{2,0,1:T(2,128)S(1)}, f32[2,1,1792]{2,0,1:T(2,128)S(1)}, u32[]{:S(2)}, u32[]{:S(2)}) collective-permute-start(f32[2,1,1792]{2,0,1:T(2,128)S(1)} %dynamic-slice_add_fusion), channel_id=1, source_target_pairs={{0,8},{8,0},{16,24},{24,16},{1,9},{9,1},{17,25},{25,17},{2,10},{10... | collective-permute-start | bytes 43016 | tf_op jit(solution)/shard_map/ppermute | solution.py:63
  739.3 33.3 %collective-permute-start.91 = (bf16[192,2048]{1,0:T(8,128)(2,1)S(1)}, bf16[192,2048]{1,0:T(8,128)(2,1)S(1)}, u32[]{:S(2)}, u32[]{:S(2)}) collective-permute-start(bf16[192,2048]{1,0:T(8,128)(2,1)S(1)} %collective-permute-done.90), channel_id=1, source_target_pairs={{0,8},{8,0},{16,24},{24,16},{1,9},{9,1},{17,25},{25,17},{2,10},{10... | collective-permute-start | bytes 2359304 | tf_op jit(solution)/shard_map/ppermute | solution.py:63
  742.8 35.5 %collective-permute-start.94 = (bf16[128,2048]{1,0:T(8,128)(2,1)S(1)}, bf16[128,2048]{1,0:T(8,128)(2,1)S(1)}, u32[]{:S(2)}, u32[]{:S(2)}) collective-permute-start(bf16[128,2048]{1,0:T(8,128)(2,1)S(1)} %pad_maximum_fusion.18.refs_0_), channel_id=1, source_target_pairs={{0,16},{8,24},{16,0},{24,8},{1,17},{9,25},{17,1},{25,9},{2,18},{10... | collective-permute-start | bytes 1572872 | tf_op jit(solution)/shard_map/ppermute | solution.py:63
  751.7 29.8 %collective-permute-start.88 = (bf16[64,2048]{1,0:T(8,128)(2,1)S(1)}, bf16[64,2048]{1,0:T(8,128)(2,1)S(1)}, u32[]{:S(2)}, u32[]{:S(2)}) collective-permute-start(bf16[64,2048]{1,0:T(8,128)(2,1)S(1)} %pad_maximum_fusion.19.refs_0_), channel_id=1, source_target_pairs={{0,16},{8,24},{16,0},{24,8},{1,17},{9,25},{17,1},{25,9},{2,18},{10... | collective-permute-start | bytes 786440 | tf_op jit(solution)/shard_map/ppermute | solution.py:63
  (281 other events, 2709.4 us)

commit v6 on v2

--- a/solution.py
+++ b/solution.py
@@ -177,7 +177,7 @@
             pltpu.SemaphoreType.DMA((len(pieces),)),
             pltpu.SemaphoreType.DMA((len(blocks), len(pieces), planes)),
         ],
-        compiler_params=params(20),
+        compiler_params=params(60),
         cost_estimate=estimate(0, 4 * sum(piece.size for piece in pieces)),
     )(scalars(plane, member), *pieces)
     return [out.reshape(-1, out.shape[-1]) for out in outs]
@@ -1228,19 +1228,19 @@
     pieces = spread(later.sent(first, new[1]), True)
     write_block(layer + 1, [piece[:rows] for piece in pieces])
     write_mixed(layer + 1, [piece[rows:] for piece in pieces])
-    last_sends = later.sends[new[1]]
+    last_gots = later.gots[new[1]] + [image_got]
     later.join(new[3], [new[1]], d_rows)
     while new[3] in later.running:
         later.step(new[3], d_rows)
     while new[2] in later.running:
-        later.step(new[2], image_got)
+        later.step(new[2], d_rows)
     write_block(layer, spread(block_piece(later, layer), False))
     write_mixed(layer, spread(mixed_piece(later, layer), False))
     stacked = [None] * len(all_params)
     for i, out in zip((10, 12, 2, 5), list(outs["block"]) + list(outs["mixed"])):
         stacked[i] = out.reshape(all_params[i].shape)
     reduced = reduce_small(
-        [jnp.stack([grads[n] for grads in small_grads]) for n in range(len(SMALL))], last_sends
+        [jnp.stack([grads[n] for grads in small_grads]) for n in range(len(SMALL))], last_gots
     )
     for i, vector in zip(SMALL, reduced):
         stacked[i] = vector

time: 782 us -> 785 us (level)
  waiting for transfers between devices: 318 us -> 306 us
    ppermute x96, waiting for transfers between devices: 318 us -> 306 us  [swap(): return lax.ppermute(tensor, axis, [(i, i ^ offset) for i in range(count)])]
    unnamed x411 -> x435, local copies, waits for them, and re-layouts: 42.7 us -> 41.3 us
  transfers between devices with their start and end apart: 96 -> 96, of which waited for: 42 -> 43; matrix products, arithmetic and copies ran while one was open for 12% -> 12% of each run, Pallas kernels for 26% -> 27%
where the time goes in v6:
time: 785 us; the launch traced here: 775 us
  waiting for transfers between devices  306 us (39%)
  Pallas kernels  232 us (30%)
  starting transfers between devices  84.3 us (11%)
  local copies, waits for them, and re-layouts  73.8 us (9%)
  other arithmetic  47.8 us (6%)
  matrix products  26.2 us (3%)
    ppermute x96, waiting for transfers between devices, swap(): return lax.ppermute(tensor, axis, [(i, i ^ offset) for i in range(count)])  306 us
    ppermute x96, starting transfers between devices, swap(): return lax.ppermute(tensor, axis, [(i, i ^ offset) for i in range(count)])  84.3 us
    pallas_call x4, Pallas kernels, attend_back(): pl.pallas_call(functools.partial(attend_back_kernel, scale * math.log2(ma...  65.5 us
    unnamed x435, local copies, waits for them, and re-layouts  41.3 us
    pallas_call x2, Pallas kernels, attend(): pl.pallas_call(functools.partial(attend_kernel, factor, len(parts)), out_...  36.8 us
    pallas_call x4, Pallas kernels, grad_call(): pl.pallas_call(functools.partial(kernel, shapes), out_shape=out_shapes, g...  32.7 us
    pallas_call x4, Pallas kernels, place(): pl.pallas_call(functools.partial(place_kernel, pieces[0].shape[1] // 2, b...  25 us
    pallas_call x2, Pallas kernels, feed_forward(): pl.pallas_call(expand_kernel, out_shape=[jax.ShapeDtypeStruct((tokens, un...  19.7 us
  transfers between devices with their start and end apart: 96, of which 43 were waited for; matrix products, arithmetic and copies ran while one was open for 12% of the time, Pallas kernels for 27%

profile of v6, /device:TPU:0, one launch (start us, length us, event | category | flops | bytes accessed | tf_op | source)
XLA Modules:
  0.0 774.8 jit_solution(17720547740150950311)
XLA Ops:
  17.2 11.8 %collective-permute-done.1 = bf16[1,64,2048]{2,1,0:T(8,128)(2,1)S(1)} collective-permute-done((bf16[1,64,2048]{2,1,0:T(8,128)(2,1)S(1)}, bf16[1,64,2048]{2,1,0:T(8,128)(2,1)S(1)}, u32[]{:S(2)}, u32[]{:S(2)}) %collective-permute-start.1) | collective-permute-done | bytes 262176 | tf_op jit(solution)/shard_map/ppermute | solution.py:63
  33.7 14.6 %collective-permute-done.2 = bf16[172,1024]{1,0:T(8,128)(2,1)S(1)} collective-permute-done((bf16[172,1024]{1,0:T(8,128)(2,1)S(1)}, bf16[172,1024]{1,0:T(8,128)(2,1)S(1)}, u32[]{:S(2)}, u32[]{:S(2)}) %collective-permute-start.2) | collective-permute-done | bytes 352288 | tf_op jit(solution)/shard_map/ppermute | solution.py:63
  56.3 13.3 %collective-permute-done.5 = bf16[4,2,1792]{2,1,0:T(2,128)(2,1)S(1)} collective-permute-done((bf16[4,2,1792]{2,1,0:T(2,128)(2,1)S(1)}, bf16[4,2,1792]{2,1,0:T(2,128)(2,1)S(1)}, u32[]{:S(2)}, u32[]{:S(2)}) %collective-permute-start.5) | collective-permute-done | bytes 28704 | tf_op jit(solution)/shard_map/ppermute | solution.py:63
  92.8 11.0 %collective-permute-done.9 = bf16[2,128,2048]{2,1,0:T(8,128)(2,1)S(1)} collective-permute-done((bf16[2,128,2048]{2,1,0:T(8,128)(2,1)S(1)}, bf16[2,128,2048]{2,1,0:T(8,128)(2,1)S(1)}, u32[]{:S(2)}, u32[]{:S(2)}) %collective-permute-start.9) | collective-permute-done | bytes 1048608 | tf_op jit(solution)/shard_map/ppermute | solution.py:63
  121.2 24.6 %collective-permute-done.14.refs_1_.refs_3_ = bf16[688,1024]{1,0:T(8,128)(2,1)S(1)} collective-permute-done((bf16[688,1024]{1,0:T(8,128)(2,1)S(1)}, bf16[688,1024]{1,0:T(8,128)(2,1)S(1)}, u32[]{:S(2)}, u32[]{:S(2)}) %collective-permute-start.14) | collective-permute-done | bytes 1409056 | tf_op jit(solution)/shard_map/ppermute | solution.py:63
  148.3 18.4 %shard_map.298 = (bf16[688,512]{1,0:T(8,128)(2,1)}, f32[688,512]{1,0:T(8,128)}) custom-call(bf16[688,1536]{1,0:T(8,128)(2,1)} %copy-done.42, bf16[688,1536]{1,0:T(8,128)(2,1)} %copy-done.42, bf16[688,1024]{1,0:T(8,128)(2,1)} %copy-done.44, bf16[688,1536]{1,0:T(8,128)(2,1)} %copy-done.42, bf16[688,1024]{1,0:T(8,128)(2,1)} %copy-done.44), custom_call_target="tpu_custom_call" | custom-call | flops 1000 | bytes 1000 | tf_op jit(solution)/shard_map/pallas_call | solution.py:760
  185.1 16.6 %collective-permute-done.18 = bf16[1,128,2048]{2,1,0:T(8,128)(2,1)S(1)} collective-permute-done((bf16[1,128,2048]{2,1,0:T(8,128)(2,1)S(1)}, bf16[1,128,2048]{2,1,0:T(8,128)(2,1)S(1)}, u32[]{:S(2)}, u32[]{:S(2)}) %collective-permute-start.18) | collective-permute-done | bytes 524320 | tf_op jit(solution)/shard_map/ppermute | solution.py:63
  207.0 7.9 %shard_map.299 = (bf16[4,2,4,32,2048]{4,3,2,1,0:T(8,128)(2,1)}, bf16[4,4,2,64,1024]{4,3,2,1,0:T(8,128)(2,1)}) custom-call(s32[2]{0:T(128)} %pad_add_fusion.1.where_ref, bf16[4,128,2048]{2,1,0:T(8,128)(2,1)} %bitcast.343, bf16[4,128,2048]{2,1,0:T(8,128)(2,1)} %copy-done.70, bf16[4,128,2048]{2,1,0:T(8,128)(2,1)} %collective-permute-done.21.refs_2_, ...), custom_call_target="tpu_custom_call" | custom-call | flops 1000 | bytes 1000 | tf_op jit(solution)/shard_map/pallas_call | solution.py:169
  219.3 9.8 %shard_map.300 = (bf16[688,2048]{1,0:T(8,128)(2,1)S(1)}, bf16[688,2048]{1,0:T(8,128)(2,1)S(1)}, f32[344,1024]{1,0:T(8,128)S(1)}, bf16[344,1024]{1,0:T(8,128)(2,1)S(1)}) custom-call(bf16[688,1024]{1,0:T(8,128)(2,1)S(1)} %constant_dynamic-update-slice_fusion.11.rows_ref.left_ref, bf16[1024,2048]{1,0:T(8,128)(2,1)S(1)} %bitcast.302, f32[1,2048]{1,0:T(1,128)S(1)} %bitcast.337, ...), custom_call_target="tpu_custom_call" | custom-call | flops 1000 | bytes 1000 | tf_op jit(solution)/shard_map/pallas_call | solution.py:859
  240.6 11.1 %collective-permute-done.30.refs_4_ = bf16[4,32,2048]{2,1,0:T(8,128)(2,1)S(1)} collective-permute-done((bf16[4,32,2048]{2,1,0:T(8,128)(2,1)S(1)}, bf16[4,32,2048]{2,1,0:T(8,128)(2,1)S(1)}, u32[]{:S(2)}, u32[]{:S(2)}) %collective-permute-start.30) | collective-permute-done | bytes 524320 | tf_op jit(solution)/shard_map/ppermute | solution.py:63
  269.8 26.1 %collective-permute-done.31.refs_1_.refs_3_ = bf16[688,1024]{1,0:T(8,128)(2,1)S(1)} collective-permute-done((bf16[688,1024]{1,0:T(8,128)(2,1)S(1)}, bf16[688,1024]{1,0:T(8,128)(2,1)S(1)}, u32[]{:S(2)}, u32[]{:S(2)}) %collective-permute-start.31) | collective-permute-done | bytes 1409056 | tf_op jit(solution)/shard_map/ppermute | solution.py:63
  300.1 18.5 %shard_map.302 = (bf16[688,512]{1,0:T(8,128)(2,1)}, f32[688,512]{1,0:T(8,128)}) custom-call(bf16[688,1536]{1,0:T(8,128)(2,1)} %copy-done.43, bf16[688,1536]{1,0:T(8,128)(2,1)} %copy-done.43, bf16[688,1024]{1,0:T(8,128)(2,1)} %copy-done.48, bf16[688,1536]{1,0:T(8,128)(2,1)} %copy-done.43, bf16[688,1024]{1,0:T(8,128)(2,1)} %copy-done.48), custom_call_target="tpu_custom_call" | custom-call | flops 1000 | bytes 1000 | tf_op jit(solution)/shard_map/pallas_call | solution.py:760
  332.3 16.5 %collective-permute-done.38.refs_4_ = bf16[4,64,2048]{2,1,0:T(8,128)(2,1)} collective-permute-done((bf16[4,64,2048]{2,1,0:T(8,128)(2,1)}, bf16[4,64,2048]{2,1,0:T(8,128)(2,1)}, u32[]{:S(2)}, u32[]{:S(2)}) %collective-permute-start.38) | collective-permute-done | bytes 1048608 | tf_op jit(solution)/shard_map/ppermute | solution.py:63
  352.3 7.9 %shard_map.303 = (bf16[4,2,4,32,2048]{4,3,2,1,0:T(8,128)(2,1)}, bf16[4,4,2,64,1024]{4,3,2,1,0:T(8,128)(2,1)}) custom-call(s32[2]{0:T(128)} %pad_add_fusion.1.where_ref, bf16[4,128,2048]{2,1,0:T(8,128)(2,1)} %bitcast.346, bf16[4,128,2048]{2,1,0:T(8,128)(2,1)} %collective-permute-done.35.refs_1_, bf16[4,128,2048]{2,1,0:T(8,128)(2,1)} %collective-permute-done.36.refs_2_, ...), custom_call_target="tpu_custom_call" | custom-call | flops 1000 | bytes 1000 | tf_op jit(solution)/shard_map/pallas_call | solution.py:169
  366.0 9.9 %shard_map.304 = (bf16[688,2048]{1,0:T(8,128)(2,1)S(1)}, bf16[688,2048]{1,0:T(8,128)(2,1)S(1)}, f32[344,1024]{1,0:T(8,128)S(1)}, bf16[344,1024]{1,0:T(8,128)(2,1)S(1)}) custom-call(bf16[688,1024]{1,0:T(8,128)(2,1)S(1)} %pad_maximum_fusion.4.rows_ref.left_ref, bf16[1024,2048]{1,0:T(8,128)(2,1)S(1)} %bitcast.306, f32[1,2048]{1,0:T(1,128)S(1)} %bitcast.336, ...), custom_call_target="tpu_custom_call" | custom-call | flops 1000 | bytes 1000 | tf_op jit(solution)/shard_map/pallas_call | solution.py:859
  381.6 8.7 %shard_map.305 = (bf16[688,2048]{1,0:T(8,128)(2,1)S(1)}, f32[1,2048]{1,0:T(1,128)S(1)}, f32[344,1024]{1,0:T(8,128)S(1)}, bf16[344,1024]{1,0:T(8,128)(2,1)S(1)}) custom-call(bf16[688,1024]{1,0:T(8,128)(2,1)S(1)} %pad_maximum_fusion.5.grad_ref.other_ref, bf16[2048,1024]{1,0:T(8,128)(2,1)S(1)} %bitcast.309, bf16[688,2048]{1,0:T(8,128)(2,1)S(1)} %get-tuple-element.240.slope_ref, ...), custom_call_target="tpu_custom_call" | custom-call | flops 1000 | bytes 1000 | tf_op jit(solution)/shard_map/pallas_call | solution.py:897
  391.5 10.8 %shard_map.306 = (bf16[4,2,1,128,1024]{4,3,2,1,0:T(8,128)(2,1)S(1)}, bf16[4,2,1,128,1024]{4,3,2,1,0:T(8,128)(2,1)}, bf16[4,1,2,128,1024]{4,3,2,1,0:T(8,128)(2,1)S(1)}, bf16[4,1,2,128,1024]{4,3,2,1,0:T(8,128)(2,1)}) custom-call(s32[2]{0:T(128)S(1)} %pad_add_fusion.2.where_ref, bf16[688,1024]{1,0:T(8,128)(2,1)S(1)} %pad_maximum_fusion.4.rows_ref.left_ref, ...), custom_call_target="tpu_custom_call" | custom-call | flops 1000 | bytes 1000 | tf_op jit(solution)/shard_map/pallas_call | solution.py:369
  404.4 6.0 collective-permute-done.40
  418.0 16.2 %shard_map.307 = (bf16[688,256]{1,0:T(8,128)(2,1)}, bf16[2,688,256]{2,1,0:T(8,128)(2,1)}, bf16[2,688,256]{2,1,0:T(8,128)(2,1)}) custom-call(bf16[688,1536]{1,0:T(8,128)(2,1)} %copy-done.43, bf16[688,1536]{1,0:T(8,128)(2,1)} %copy-done.43, bf16[688,1024]{1,0:T(8,128)(2,1)} %copy-done.48, bf16[688,1536]{1,0:T(8,128)(2,1)} %copy-done.43, ...), custom_call_target="tpu_custom_call" | custom-call | flops 1000 | bytes 1000 | tf_op jit(solution)/shard_map/pallas_call | solution.py:804
  434.2 16.5 %shard_map.308 = (bf16[688,256]{1,0:T(8,128)(2,1)}, bf16[2,688,256]{2,1,0:T(8,128)(2,1)}, bf16[2,688,256]{2,1,0:T(8,128)(2,1)}) custom-call(bf16[688,1536]{1,0:T(8,128)(2,1)} %copy-done.43, bf16[688,1536]{1,0:T(8,128)(2,1)} %copy-done.43, bf16[688,1024]{1,0:T(8,128)(2,1)} %copy-done.48, bf16[688,1536]{1,0:T(8,128)(2,1)} %copy-done.43, ...), custom_call_target="tpu_custom_call" | custom-call | flops 1000 | bytes 1000 | tf_op jit(solution)/shard_map/pallas_call | solution.py:804
  476.9 6.2 shard_map.310
  492.5 9.5 %shard_map.311 = (bf16[688,2048]{1,0:T(8,128)(2,1)S(1)}, f32[1,2048]{1,0:T(1,128)S(1)}, f32[344,1024]{1,0:T(8,128)S(1)}, bf16[344,1024]{1,0:T(8,128)(2,1)}) custom-call(bf16[688,1024]{1,0:T(8,128)(2,1)S(1)} %pad_maximum_fusion.7.grad_ref.other_ref, bf16[2048,1024]{1,0:T(8,128)(2,1)S(1)} %bitcast.305, bf16[688,2048]{1,0:T(8,128)(2,1)S(1)} %copy-done.11, ...), custom_call_target="tpu_custom_call" | custom-call | flops 1000 | bytes 1000 | tf_op jit(solution)/shard_map/pallas_call | solution.py:897
  504.8 10.6 %shard_map.313 = (bf16[4,2,1,128,1024]{4,3,2,1,0:T(8,128)(2,1)S(1)}, bf16[4,2,1,128,1024]{4,3,2,1,0:T(8,128)(2,1)}, bf16[4,1,2,128,1024]{4,3,2,1,0:T(8,128)(2,1)S(1)}, bf16[4,1,2,128,1024]{4,3,2,1,0:T(8,128)(2,1)}) custom-call(s32[2]{0:T(128)S(1)} %pad_add_fusion.2.where_ref, bf16[688,1024]{1,0:T(8,128)(2,1)S(1)} %constant_dynamic-update-slice_fusion.11.rows_ref.left_ref, ...), custom_call_target="tpu_custom_call" | custom-call | flops 1000 | bytes 1000 | tf_op jit(solution)/shard_map/pallas_call | solution.py:369
  516.3 8.7 %collective-permute-done.52.refs_1_ = bf16[4,2,1,64,1024]{4,3,2,1,0:T(8,128)(2,1)S(1)} collective-permute-done((bf16[4,2,1,64,1024]{4,3,2,1,0:T(8,128)(2,1)}, bf16[4,2,1,64,1024]{4,3,2,1,0:T(8,128)(2,1)S(1)}, u32[]{:S(2)}, u32[]{:S(2)}) %collective-permute-start.52) | collective-permute-done | bytes 1048608 | tf_op jit(solution)/shard_map/ppermute | solution.py:63
  545.5 16.4 %shard_map.315 = (bf16[688,256]{1,0:T(8,128)(2,1)}, bf16[2,688,256]{2,1,0:T(8,128)(2,1)}, bf16[2,688,256]{2,1,0:T(8,128)(2,1)}) custom-call(bf16[688,1536]{1,0:T(8,128)(2,1)} %copy-done.42, bf16[688,1536]{1,0:T(8,128)(2,1)} %copy-done.42, bf16[688,1024]{1,0:T(8,128)(2,1)} %copy-done.44, bf16[688,1536]{1,0:T(8,128)(2,1)} %copy-done.42, ...), custom_call_target="tpu_custom_call" | custom-call | flops 1000 | bytes 1000 | tf_op jit(solution)/shard_map/pallas_call | solution.py:804
  570.1 16.4 %shard_map.317 = (bf16[688,256]{1,0:T(8,128)(2,1)}, bf16[2,688,256]{2,1,0:T(8,128)(2,1)}, bf16[2,688,256]{2,1,0:T(8,128)(2,1)}) custom-call(bf16[688,1536]{1,0:T(8,128)(2,1)} %copy-done.42, bf16[688,1536]{1,0:T(8,128)(2,1)} %copy-done.42, bf16[688,1024]{1,0:T(8,128)(2,1)} %copy-done.44, bf16[688,1536]{1,0:T(8,128)(2,1)} %copy-done.42, ...), custom_call_target="tpu_custom_call" | custom-call | flops 1000 | bytes 1000 | tf_op jit(solution)/shard_map/pallas_call | solution.py:804
  602.1 16.2 %collective-permute-done.62 = bf16[2,688,256]{2,1,0:T(8,128)(2,1)S(1)} collective-permute-done((bf16[2,688,256]{2,1,0:T(8,128)(2,1)}, bf16[2,688,256]{2,1,0:T(8,128)(2,1)S(1)}, u32[]{:S(2)}, u32[]{:S(2)}) %collective-permute-start.62) | collective-permute-done | bytes 704544 | tf_op jit(solution)/shard_map/ppermute | solution.py:63
  640.3 13.6 %collective-permute-done.68 = bf16[4,1,2,64,1024]{4,3,2,0,1:T(8,128)(2,1)S(1)} collective-permute-done((bf16[4,1,2,64,1024]{4,3,2,0,1:T(8,128)(2,1)S(1)}, bf16[4,1,2,64,1024]{4,3,2,0,1:T(8,128)(2,1)S(1)}, u32[]{:S(2)}, u32[]{:S(2)}) %collective-permute-start.68) | collective-permute-done | bytes 1048608 | tf_op jit(solution)/shard_map/ppermute | solution.py:63
  660.2 7.0 collective-permute-done.66
  689.5 18.0 %collective-permute-done.91 = bf16[1,1,128,2048]{3,2,1,0:T(8,128)(2,1)S(1)} collective-permute-done((bf16[1,1,128,2048]{3,2,1,0:T(8,128)(2,1)S(1)}, bf16[1,1,128,2048]{3,2,1,0:T(8,128)(2,1)S(1)}, u32[]{:S(2)}, u32[]{:S(2)}) %collective-permute-start.91) | collective-permute-done | bytes 524320 | tf_op jit(solution)/shard_map/ppermute | solution.py:63
  712.9 12.5 %collective-permute-done.77 = bf16[1,1,64,2048]{3,2,1,0:T(8,128)(2,1)S(1)} collective-permute-done((bf16[1,1,64,2048]{3,2,1,0:T(8,128)(2,1)S(1)}, bf16[1,1,64,2048]{3,2,1,0:T(8,128)(2,1)S(1)}, u32[]{:S(2)}, u32[]{:S(2)}) %collective-permute-start.77) | collective-permute-done | bytes 262176 | tf_op jit(solution)/shard_map/ppermute | solution.py:63
  748.9 13.6 %collective-permute-done.89 = bf16[192,2048]{1,0:T(8,128)(2,1)S(1)} collective-permute-done((bf16[192,2048]{1,0:T(8,128)(2,1)S(1)}, bf16[192,2048]{1,0:T(8,128)(2,1)S(1)}, u32[]{:S(2)}, u32[]{:S(2)}) %collective-permute-start.89) | collective-permute-done | bytes 786464 | tf_op jit(solution)/shard_map/ppermute | solution.py:63
  (838 shorter events, 345.9 us)
Async XLA Ops:
  29.6 41.4 %collective-permute-start.7 = (bf16[2,64,2048]{2,1,0:T(8,128)(2,1)S(1)}, bf16[2,64,2048]{2,1,0:T(8,128)(2,1)S(1)}, u32[]{:S(2)}, u32[]{:S(2)}) collective-permute-start(bf16[2,64,2048]{2,1,0:T(8,128)(2,1)S(1)} %get-tuple-element.197), channel_id=1, source_target_pairs={{0,2},{1,3},{2,0},{3,1},{4,6},{5,7},{6,4},{7,5},{8,10},{9,11},{10,... | collective-permute-start | bytes 1572872 | tf_op jit(solution)/shard_map/ppermute | solution.py:63
  80.3 29.9 %collective-permute-start.6 = (bf16[344,1024]{1,0:T(8,128)(2,1)S(1)}, bf16[344,1024]{1,0:T(8,128)(2,1)S(1)}, u32[]{:S(2)}, u32[]{:S(2)}) collective-permute-start(bf16[344,1024]{1,0:T(8,128)(2,1)S(1)} %fusion.9), channel_id=1, source_target_pairs={{0,1},{1,0},{2,3},{3,2},{4,5},{5,4},{6,7},{7,6},{8,9},{9,8},{10,11... | collective-permute-start | bytes 2113544 | tf_op jit(solution)/shard_map/ppermute | solution.py:63
  115.0 30.8 %collective-permute-start.14 = (bf16[688,1024]{1,0:T(8,128)(2,1)S(1)}, bf16[688,1024]{1,0:T(8,128)(2,1)S(1)}, u32[]{:S(2)}, u32[]{:S(2)}) collective-permute-start(bf16[688,1024]{1,0:T(8,128)(2,1)S(1)} %slice.495), channel_id=1, source_target_pairs={{0,2},{1,3},{2,0},{3,1},{4,6},{5,7},{6,4},{7,5},{8,10},{9,11},{10,... | collective-permute-start | bytes 4227080 | tf_op jit(solution)/shard_map/ppermute | solution.py:63
  117.2 54.1 %collective-permute-start.20 = (bf16[4,128,2048]{2,1,0:T(8,128)(2,1)S(1)}, bf16[4,128,2048]{2,1,0:T(8,128)(2,1)S(1)}, u32[]{:S(2)}, u32[]{:S(2)}) collective-permute-start(bf16[4,128,2048]{2,1,0:T(8,128)(2,1)S(1)} %bitcast.341), channel_id=1, source_target_pairs={{0,8},{8,0},{16,24},{24,16},{1,9},{9,1},{17,25},{25,17},{2,10},{10... | collective-permute-start | bytes 6291464 | tf_op jit(solution)/shard_map/ppermute | solution.py:63
  118.8 52.6 %collective-permute-start.21 = (bf16[4,128,2048]{2,1,0:T(8,128)(2,1)S(1)}, bf16[4,128,2048]{2,1,0:T(8,128)(2,1)}, u32[]{:S(2)}, u32[]{:S(2)}) collective-permute-start(bf16[4,128,2048]{2,1,0:T(8,128)(2,1)S(1)} %bitcast.342), channel_id=1, source_target_pairs={{0,16},{8,24},{16,0},{24,8},{1,17},{9,25},{17,1},{25,9},{2,18},{10... | collective-permute-start | bytes 6291464 | tf_op jit(solution)/shard_map/ppermute | solution.py:63
  171.4 31.8 %collective-permute-start.23 = (bf16[4,64,2048]{2,1,0:T(8,128)(2,1)S(1)}, bf16[4,64,2048]{2,1,0:T(8,128)(2,1)S(1)}, u32[]{:S(2)}, u32[]{:S(2)}) collective-permute-start(bf16[4,64,2048]{2,1,0:T(8,128)(2,1)S(1)} %slice.509), channel_id=1, source_target_pairs={{0,16},{8,24},{16,0},{24,8},{1,17},{9,25},{17,1},{25,9},{2,18},{10... | collective-permute-start | bytes 3145736 | tf_op jit(solution)/shard_map/ppermute | solution.py:63
  263.9 32.0 %collective-permute-start.31 = (bf16[688,1024]{1,0:T(8,128)(2,1)S(1)}, bf16[688,1024]{1,0:T(8,128)(2,1)S(1)}, u32[]{:S(2)}, u32[]{:S(2)}) collective-permute-start(bf16[688,1024]{1,0:T(8,128)(2,1)S(1)} %slice.521), channel_id=1, source_target_pairs={{0,2},{1,3},{2,0},{3,1},{4,6},{5,7},{6,4},{7,5},{8,10},{9,11},{10,... | collective-permute-start | bytes 4227080 | tf_op jit(solution)/shard_map/ppermute | solution.py:63
  267.5 52.8 %collective-permute-start.35 = (bf16[4,128,2048]{2,1,0:T(8,128)(2,1)S(1)}, bf16[4,128,2048]{2,1,0:T(8,128)(2,1)}, u32[]{:S(2)}, u32[]{:S(2)}) collective-permute-start(bf16[4,128,2048]{2,1,0:T(8,128)(2,1)S(1)} %bitcast.344), channel_id=1, source_target_pairs={{0,8},{8,0},{16,24},{24,16},{1,9},{9,1},{17,25},{25,17},{2,10},{10... | collective-permute-start | bytes 6291464 | tf_op jit(solution)/shard_map/ppermute | solution.py:63
  268.8 54.0 %collective-permute-start.36 = (bf16[4,128,2048]{2,1,0:T(8,128)(2,1)S(1)}, bf16[4,128,2048]{2,1,0:T(8,128)(2,1)}, u32[]{:S(2)}, u32[]{:S(2)}) collective-permute-start(bf16[4,128,2048]{2,1,0:T(8,128)(2,1)S(1)} %bitcast.345), channel_id=1, source_target_pairs={{0,16},{8,24},{16,0},{24,8},{1,17},{9,25},{17,1},{25,9},{2,18},{10... | collective-permute-start | bytes 6291464 | tf_op jit(solution)/shard_map/ppermute | solution.py:63
  330.9 29.3 %collective-permute-start.34 = (bf16[344,1024]{1,0:T(8,128)(2,1)}, bf16[344,1024]{1,0:T(8,128)(2,1)}, u32[]{:S(2)}, u32[]{:S(2)}) collective-permute-start(bf16[344,1024]{1,0:T(8,128)(2,1)} %add_convert_fusion.7), channel_id=1, source_target_pairs={{0,1},{1,0},{2,3},{3,2},{4,5},{5,4},{6,7},{7,6},{8,9},{9,8},{10,11... | collective-permute-start | bytes 2113544 | tf_op jit(solution)/shard_map/ppermute | solution.py:63
  403.7 50.1 %collective-permute-start.44 = (bf16[4,2,1,128,1024]{4,3,2,1,0:T(8,128)(2,1)}, bf16[4,2,1,128,1024]{4,3,2,1,0:T(8,128)(2,1)}, u32[]{:S(2)}, u32[]{:S(2)}) collective-permute-start(bf16[4,2,1,128,1024]{4,3,2,1,0:T(8,128)(2,1)} %get-tuple-element.244), channel_id=1, source_target_pairs={{0,8},{8,0},{16,24},{24,16},{1,9},{9,1},{17,25},{25,17},{2,10},{10... | collective-permute-start | bytes 6291464 | tf_op jit(solution)/shard_map/ppermute | solution.py:63
  410.4 47.9 %collective-permute-start.45 = (bf16[4,1,2,128,1024]{4,3,2,0,1:T(8,128)(2,1)}, bf16[4,1,2,128,1024]{4,3,2,0,1:T(8,128)(2,1)}, u32[]{:S(2)}, u32[]{:S(2)}) collective-permute-start(bf16[4,1,2,128,1024]{4,3,2,0,1:T(8,128)(2,1)} %bitcast.96), channel_id=1, source_target_pairs={{0,16},{8,24},{16,0},{24,8},{1,17},{9,25},{17,1},{25,9},{2,18},{10... | collective-permute-start | bytes 6291464 | tf_op jit(solution)/shard_map/ppermute | solution.py:63
  490.0 35.0 %collective-permute-start.52 = (bf16[4,2,1,64,1024]{4,3,2,1,0:T(8,128)(2,1)}, bf16[4,2,1,64,1024]{4,3,2,1,0:T(8,128)(2,1)S(1)}, u32[]{:S(2)}, u32[]{:S(2)}) collective-permute-start(bf16[4,2,1,64,1024]{4,3,2,1,0:T(8,128)(2,1)} %get-tuple-element.265), channel_id=1, source_target_pairs={{0,8},{8,0},{16,24},{24,16},{1,9},{9,1},{17,25},{25,17},{2,10},{10... | collective-permute-start | bytes 3145736 | tf_op jit(solution)/shard_map/ppermute | solution.py:63
  491.6 33.5 %collective-permute-start.53 = (bf16[4,1,2,64,1024]{4,3,2,0,1:T(8,128)(2,1)}, bf16[4,1,2,64,1024]{4,3,2,0,1:T(8,128)(2,1)}, u32[]{:S(2)}, u32[]{:S(2)}) collective-permute-start(bf16[4,1,2,64,1024]{4,3,2,0,1:T(8,128)(2,1)} %bitcast.108), channel_id=1, source_target_pairs={{0,16},{8,24},{16,0},{24,8},{1,17},{9,25},{17,1},{25,9},{2,18},{10... | collective-permute-start | bytes 3145736 | tf_op jit(solution)/shard_map/ppermute | solution.py:63
  515.4 73.8 %collective-permute-start.57 = (bf16[4,2,1,128,1024]{4,3,2,1,0:T(8,128)(2,1)}, bf16[4,2,1,128,1024]{4,3,2,1,0:T(8,128)(2,1)}, u32[]{:S(2)}, u32[]{:S(2)}) collective-permute-start(bf16[4,2,1,128,1024]{4,3,2,1,0:T(8,128)(2,1)} %get-tuple-element.280), channel_id=1, source_target_pairs={{0,8},{8,0},{16,24},{24,16},{1,9},{9,1},{17,25},{25,17},{2,10},{10... | collective-permute-start | bytes 6291464 | tf_op jit(solution)/shard_map/ppermute | solution.py:63
  529.1 61.2 %collective-permute-start.58 = (bf16[4,1,2,128,1024]{4,3,2,0,1:T(8,128)(2,1)}, bf16[4,1,2,128,1024]{4,3,2,0,1:T(8,128)(2,1)}, u32[]{:S(2)}, u32[]{:S(2)}) collective-permute-start(bf16[4,1,2,128,1024]{4,3,2,0,1:T(8,128)(2,1)} %bitcast.114), channel_id=1, source_target_pairs={{0,16},{8,24},{16,0},{24,8},{1,17},{9,25},{17,1},{25,9},{2,18},{10... | collective-permute-start | bytes 6291464 | tf_op jit(solution)/shard_map/ppermute | solution.py:63
  565.0 32.3 %collective-permute-start.59 = (bf16[4,1,64,1024]{3,2,1,0:T(8,128)(2,1)}, bf16[4,1,64,1024]{3,2,1,0:T(8,128)(2,1)}, u32[]{:S(2)}, u32[]{:S(2)}) collective-permute-start(bf16[4,1,64,1024]{3,2,1,0:T(8,128)(2,1)} %get-tuple-element.288), channel_id=1, source_target_pairs={{0,16},{8,24},{16,0},{24,8},{1,17},{9,25},{17,1},{25,9},{2,18},{10... | collective-permute-start | bytes 1572872 | tf_op jit(solution)/shard_map/ppermute | solution.py:63
  566.5 31.5 %collective-permute-start.60 = (bf16[4,1,64,1024]{3,2,1,0:T(8,128)(2,1)}, bf16[4,1,64,1024]{3,2,1,0:T(8,128)(2,1)}, u32[]{:S(2)}, u32[]{:S(2)}) collective-permute-start(bf16[4,1,64,1024]{3,2,1,0:T(8,128)(2,1)} %get-tuple-element.289), channel_id=1, source_target_pairs={{0,8},{8,0},{16,24},{24,16},{1,9},{9,1},{17,25},{25,17},{2,10},{10... | collective-permute-start | bytes 1572872 | tf_op jit(solution)/shard_map/ppermute | solution.py:63
  588.1 30.2 %collective-permute-start.62 = (bf16[2,688,256]{2,1,0:T(8,128)(2,1)}, bf16[2,688,256]{2,1,0:T(8,128)(2,1)S(1)}, u32[]{:S(2)}, u32[]{:S(2)}) collective-permute-start(bf16[2,688,256]{2,1,0:T(8,128)(2,1)} %get-tuple-element.318), channel_id=1, source_target_pairs={{0,2},{1,3},{2,0},{3,1},{4,6},{5,7},{6,4},{7,5},{8,10},{9,11},{10,... | collective-permute-start | bytes 2113544 | tf_op jit(solution)/shard_map/ppermute | solution.py:63
  589.2 46.2 %collective-permute-start.82 = (bf16[1,1,128,2048]{3,2,1,0:T(8,128)(2,1)S(1)}, bf16[1,1,128,2048]{3,2,1,0:T(8,128)(2,1)S(1)}, u32[]{:S(2)}, u32[]{:S(2)}) collective-permute-start(bf16[1,1,128,2048]{3,2,1,0:T(8,128)(2,1)S(1)} %copy-done.41), channel_id=1, source_target_pairs={{0,4},{1,5},{2,6},{3,7},{4,0},{5,1},{6,2},{7,3},{8,12},{9,13},{10,... | collective-permute-start | bytes 1572872 | tf_op jit(solution)/shard_map/ppermute | solution.py:63
  595.8 31.2 %collective-permute-start.64 = (bf16[4,1,128,1024]{3,2,1,0:T(8,128)(2,1)S(1)}, bf16[4,1,128,1024]{3,2,1,0:T(8,128)(2,1)S(1)}, u32[]{:S(2)}, u32[]{:S(2)}) collective-permute-start(bf16[4,1,128,1024]{3,2,1,0:T(8,128)(2,1)S(1)} %get-tuple-element.305), channel_id=1, source_target_pairs={{0,8},{8,0},{16,24},{24,16},{1,9},{9,1},{17,25},{25,17},{2,10},{10... | collective-permute-start | bytes 3145736 | tf_op jit(solution)/shard_map/ppermute | solution.py:63
  597.4 31.2 %collective-permute-start.63 = (bf16[4,1,128,1024]{3,2,1,0:T(8,128)(2,1)S(1)}, bf16[4,1,128,1024]{3,2,1,0:T(8,128)(2,1)S(1)}, u32[]{:S(2)}, u32[]{:S(2)}) collective-permute-start(bf16[4,1,128,1024]{3,2,1,0:T(8,128)(2,1)S(1)} %get-tuple-element.304), channel_id=1, source_target_pairs={{0,16},{8,24},{16,0},{24,8},{1,17},{9,25},{17,1},{25,9},{2,18},{10... | collective-permute-start | bytes 3145736 | tf_op jit(solution)/shard_map/ppermute | solution.py:63
  599.5 36.0 %collective-permute-start.84 = (bf16[2,64,2048]{2,1,0:T(8,128)(2,1)S(1)}, bf16[2,64,2048]{2,1,0:T(8,128)(2,1)S(1)}, u32[]{:S(2)}, u32[]{:S(2)}) collective-permute-start(bf16[2,64,2048]{2,1,0:T(8,128)(2,1)S(1)} %get-tuple-element.312), channel_id=1, source_target_pairs={{0,2},{1,3},{2,0},{3,1},{4,6},{5,7},{6,4},{7,5},{8,10},{9,11},{10,... | collective-permute-start | bytes 1572872 | tf_op jit(solution)/shard_map/ppermute | solution.py:63
  630.8 49.9 %collective-permute-start.90 = (bf16[2,128,2048]{2,1,0:T(8,128)(2,1)}, bf16[2,128,2048]{2,1,0:T(8,128)(2,1)S(1)}, u32[]{:S(2)}, u32[]{:S(2)}) collective-permute-start(bf16[2,128,2048]{2,1,0:T(8,128)(2,1)} %get-tuple-element.326), channel_id=1, source_target_pairs={{0,2},{1,3},{2,0},{3,1},{4,6},{5,7},{6,4},{7,5},{8,10},{9,11},{10,... | collective-permute-start | bytes 3145736 | tf_op jit(solution)/shard_map/ppermute | solution.py:63
  636.8 30.4 %collective-permute-start.66 = (bf16[172,1024]{1,0:T(8,128)(2,1)S(1)}, bf16[172,1024]{1,0:T(8,128)(2,1)S(1)}, u32[]{:S(2)}, u32[]{:S(2)}) collective-permute-start(bf16[172,1024]{1,0:T(8,128)(2,1)S(1)} %slice.655), channel_id=1, source_target_pairs={{0,4},{1,5},{2,6},{3,7},{4,0},{5,1},{6,2},{7,3},{8,12},{9,13},{10,... | collective-permute-start | bytes 1056776 | tf_op jit(solution)/shard_map/ppermute | solution.py:63
  685.6 43.9 %collective-permute-start.88 = (bf16[192,2048]{1,0:T(8,128)(2,1)S(1)}, bf16[192,2048]{1,0:T(8,128)(2,1)S(1)}, u32[]{:S(2)}, u32[]{:S(2)}) collective-permute-start(bf16[192,2048]{1,0:T(8,128)(2,1)S(1)} %maximum_maximum_fusion), channel_id=1, source_target_pairs={{0,16},{8,24},{16,0},{24,8},{1,17},{9,25},{17,1},{25,9},{2,18},{10... | collective-permute-start | bytes 2359304 | tf_op jit(solution)/shard_map/ppermute | solution.py:63
  686.8 46.9 %collective-permute-start.87 = (bf16[192,2048]{1,0:T(8,128)(2,1)S(1)}, bf16[192,2048]{1,0:T(8,128)(2,1)S(1)}, u32[]{:S(2)}, u32[]{:S(2)}) collective-permute-start(bf16[192,2048]{1,0:T(8,128)(2,1)S(1)} %maximum_maximum_fusion), channel_id=1, source_target_pairs={{0,8},{8,0},{16,24},{24,16},{1,9},{9,1},{17,25},{25,17},{2,10},{10... | collective-permute-start | bytes 2359304 | tf_op jit(solution)/shard_map/ppermute | solution.py:63
  688.0 39.9 %collective-permute-start.74 = (f32[2,1,1792]{2,0,1:T(2,128)S(1)}, f32[2,1,1792]{2,0,1:T(2,128)S(1)}, u32[]{:S(2)}, u32[]{:S(2)}) collective-permute-start(f32[2,1,1792]{2,0,1:T(2,128)S(1)} %dynamic-slice_add_fusion), channel_id=1, source_target_pairs={{0,8},{8,0},{16,24},{24,16},{1,9},{9,1},{17,25},{25,17},{2,10},{10... | collective-permute-start | bytes 43016 | tf_op jit(solution)/shard_map/ppermute | solution.py:63
  729.5 33.0 %collective-permute-start.89 = (bf16[192,2048]{1,0:T(8,128)(2,1)S(1)}, bf16[192,2048]{1,0:T(8,128)(2,1)S(1)}, u32[]{:S(2)}, u32[]{:S(2)}) collective-permute-start(bf16[192,2048]{1,0:T(8,128)(2,1)S(1)} %collective-permute-done.88), channel_id=1, source_target_pairs={{0,8},{8,0},{16,24},{24,16},{1,9},{9,1},{17,25},{25,17},{2,10},{10... | collective-permute-start | bytes 2359304 | tf_op jit(solution)/shard_map/ppermute | solution.py:63
  733.0 38.2 %collective-permute-start.94 = (bf16[128,2048]{1,0:T(8,128)(2,1)S(1)}, bf16[128,2048]{1,0:T(8,128)(2,1)S(1)}, u32[]{:S(2)}, u32[]{:S(2)}) collective-permute-start(bf16[128,2048]{1,0:T(8,128)(2,1)S(1)} %pad_maximum_fusion.17.refs_0_), channel_id=1, source_target_pairs={{0,16},{8,24},{16,0},{24,8},{1,17},{9,25},{17,1},{25,9},{2,18},{10... | collective-permute-start | bytes 1572872 | tf_op jit(solution)/shard_map/ppermute | solution.py:63
  733.6 34.6 %collective-permute-start.80 = (bf16[64,2048]{1,0:T(8,128)(2,1)S(1)}, bf16[64,2048]{1,0:T(8,128)(2,1)S(1)}, u32[]{:S(2)}, u32[]{:S(2)}) collective-permute-start(bf16[64,2048]{1,0:T(8,128)(2,1)S(1)} %pad_maximum_fusion.18.refs_0_), channel_id=1, source_target_pairs={{0,16},{8,24},{16,0},{24,8},{1,17},{9,25},{17,1},{25,9},{2,18},{10... | collective-permute-start | bytes 786440 | tf_op jit(solution)/shard_map/ppermute | solution.py:63
  740.4 30.8 %collective-permute-start.95 = (bf16[128,2048]{1,0:T(8,128)(2,1)S(1)}, bf16[128,2048]{1,0:T(8,128)(2,1)S(1)}, u32[]{:S(2)}, u32[]{:S(2)}) collective-permute-start(bf16[128,2048]{1,0:T(8,128)(2,1)S(1)} %collective-permute-done.93.refs_1_), channel_id=1, source_target_pairs={{0,16},{8,24},{16,0},{24,8},{1,17},{9,25},{17,1},{25,9},{2,18},{10... | collective-permute-start | bytes 1572872 | tf_op jit(solution)/shard_map/ppermute | solution.py:63
  (271 other events, 2608.4 us)

commit v7 on v6

--- a/solution.py
+++ b/solution.py
@@ -177,7 +177,7 @@
             pltpu.SemaphoreType.DMA((len(pieces),)),
             pltpu.SemaphoreType.DMA((len(blocks), len(pieces), planes)),
         ],
-        compiler_params=params(60),
+        compiler_params=params(20),
         cost_estimate=estimate(0, 4 * sum(piece.size for piece in pieces)),
     )(scalars(plane, member), *pieces)
     return [out.reshape(-1, out.shape[-1]) for out in outs]
@@ -295,7 +295,7 @@
             jnp.moveaxis(whole[:, :, start : start + size], 0, 1).reshape(LAYERS, -1)
         )
         start += size
-    return vectors
+    return vectors, got
 
 
 def link_orders():
@@ -1103,8 +1103,6 @@
     second_query = later.sent(second_query, block)
     if old:
         second_query = later.came(second_query, old[1])
-        later.join(old[3], [old[1]], second_query)
-        second_query = later.sent(second_query, old[3])
     d_query = jnp.concatenate([first_query, second_query], 1)
     d_key = jnp.concatenate([first_kv[0], second_kv[0]], 1)
     d_value = jnp.concatenate([first_kv[1], second_kv[1]], 1)
@@ -1115,6 +1113,7 @@
     later.begin(mixed, mixed_grad, (normed, d_projected, attended, d_branch_both))
     d_projected = later.sent(d_projected, mixed)
     if old:
+        later.join(old[3], [old[1]], d_projected)
         later.join(block_planes, [block], d_projected)
         d_projected = later.sent(d_projected, block_planes)
     d_normed = input_dot(d_projected[:tokens], heads_weight) + widen(got)
@@ -1141,12 +1140,12 @@
 def local(images, cotangent, *all_params):
     owners, count = lax.axis_size("fsdp"), lax.axis_size("rep")
     pieces = message_pieces(all_params)
-    column, planes = gather_planes(pieces[0])
+    small, small_got = gather_small(all_params, pieces[0])
+    column, planes = gather_planes(pieces[0], beside=[small_got])
     own, got = regroup(after(images, planes[0]))
     tok_rows = widen(jnp.concatenate([own, got], 0))
     column = after(column, got)
     next_column, next_planes = gather_planes(pieces[1], got)
-    small = gather_small(all_params, got)
     held, neighbours = gather_neighbours(column, [])
     saved_layers, fetched = [], []
     for layer in range(LAYERS):
@@ -1218,24 +1217,22 @@
     activations = ungroup(activation_rows, activation_got)
     image_got = other_half(low(d_rows[d_rows.shape[0] // 2 :]))
     d_images = ungroup(d_rows, image_got)
-    for name in (old[2], old[3]):
+    while old[2] in later.running:
+        later.step(old[2], d_rows)
+    first = after(block_piece(later, layer + 1), d_rows)
+    later.step(new[1], d_rows)
+    write_block(layer + 1, spread(later.sent(first, new[1]), True))
+    last_gots = later.gots[new[1]] + [image_got]
+    later.join(new[3], [new[1]], d_rows)
+    for name in (new[3], new[2], old[3]):
         while name in later.running:
             later.step(name, d_rows)
-    first = block_piece(later, layer + 1)
-    rows = first.shape[0]
-    first = after(jnp.concatenate([first, mixed_piece(later, layer + 1)], 0), d_rows)
-    later.step(new[1], d_rows)
-    pieces = spread(later.sent(first, new[1]), True)
-    write_block(layer + 1, [piece[:rows] for piece in pieces])
-    write_mixed(layer + 1, [piece[rows:] for piece in pieces])
-    last_gots = later.gots[new[1]] + [image_got]
-    later.join(new[3], [new[1]], d_rows)
-    while new[3] in later.running:
-        later.step(new[3], d_rows)
-    while new[2] in later.running:
-        later.step(new[2], d_rows)
     write_block(layer, spread(block_piece(later, layer), False))
-    write_mixed(layer, spread(mixed_piece(later, layer), False))
+    both = [mixed_piece(later, n) for n in (layer + 1, layer)]
+    rows = both[0].shape[0]
+    pieces = spread(jnp.concatenate(both, 0), True)
+    write_mixed(layer + 1, [piece[:rows] for piece in pieces])
+    write_mixed(layer, [piece[rows:] for piece in pieces])
     stacked = [None] * len(all_params)
     for i, out in zip((10, 12, 2, 5), list(outs["block"]) + list(outs["mixed"])):
         stacked[i] = out.reshape(all_params[i].shape)

time: 785 us -> 790 us (level)
  starting transfers between devices: 84.3 us -> 93.1 us
    ppermute x96, starting transfers between devices: 84.3 us -> 93.1 us  [swap(): return lax.ppermute(tensor, axis, [(i, i ^ offset) for i in range(count)])]
    unnamed x435 -> x433, local copies, waits for them, and re-layouts: 41.3 us -> 46.2 us
  transfers between devices with their start and end apart: 96 -> 96, of which waited for: 43 -> 40; matrix products, arithmetic and copies ran while one was open for 12% -> 11% of each run, Pallas kernels for 27% -> 26%
where the time goes in v7:
time: 790 us; the launch traced here: 780 us
  waiting for transfers between devices  313 us (40%)
  Pallas kernels  231 us (29%)
  starting transfers between devices  93.1 us (12%)
  local copies, waits for them, and re-layouts  69.8 us (9%)
  other arithmetic  44.3 us (6%)
  matrix products  25.2 us (3%)
    ppermute x96, waiting for transfers between devices, swap(): return lax.ppermute(tensor, axis, [(i, i ^ offset) for i in range(count)])  313 us
    ppermute x96, starting transfers between devices, swap(): return lax.ppermute(tensor, axis, [(i, i ^ offset) for i in range(count)])  93.1 us
    pallas_call x4, Pallas kernels, attend_back(): pl.pallas_call(functools.partial(attend_back_kernel, scale * math.log2(ma...  65.8 us
    unnamed x433, local copies, waits for them, and re-layouts  46.2 us
    pallas_call x2, Pallas kernels, attend(): pl.pallas_call(functools.partial(attend_kernel, factor, len(parts)), out_...  36.7 us
    pallas_call x4, Pallas kernels, grad_call(): pl.pallas_call(functools.partial(kernel, shapes), out_shape=out_shapes, g...  32.6 us
    pallas_call x4, Pallas kernels, place(): pl.pallas_call(functools.partial(place_kernel, pieces[0].shape[1] // 2, b...  23.2 us
    pallas_call x2, Pallas kernels, feed_forward(): pl.pallas_call(expand_kernel, out_shape=[jax.ShapeDtypeStruct((tokens, un...  19.6 us
  transfers between devices with their start and end apart: 96, of which 40 were waited for; matrix products, arithmetic and copies ran while one was open for 11% of the time, Pallas kernels for 26%

profile of v7, /device:TPU:0, one launch (start us, length us, event | category | flops | bytes accessed | tf_op | source)
XLA Modules:
  0.0 780.2 jit_solution(13668140244309540)
XLA Ops:
  24.8 9.2 %collective-permute-done.1 = bf16[1,64,2048]{2,1,0:T(8,128)(2,1)S(1)} collective-permute-done((bf16[1,64,2048]{2,1,0:T(8,128)(2,1)S(1)}, bf16[1,64,2048]{2,1,0:T(8,128)(2,1)S(1)}, u32[]{:S(2)}, u32[]{:S(2)}) %collective-permute-start.1) | collective-permute-done | bytes 262176 | tf_op jit(solution)/shard_map/ppermute | solution.py:63
  39.0 13.8 %collective-permute-done.2 = bf16[172,1024]{1,0:T(8,128)(2,1)S(1)} collective-permute-done((bf16[172,1024]{1,0:T(8,128)(2,1)S(1)}, bf16[172,1024]{1,0:T(8,128)(2,1)S(1)}, u32[]{:S(2)}, u32[]{:S(2)}) %collective-permute-start.2) | collective-permute-done | bytes 352288 | tf_op jit(solution)/shard_map/ppermute | solution.py:63
  61.2 16.9 %collective-permute-done.8 = bf16[1,128,2048]{2,1,0:T(8,128)(2,1)S(1)} collective-permute-done((bf16[1,128,2048]{2,1,0:T(8,128)(2,1)S(1)}, bf16[1,128,2048]{2,1,0:T(8,128)(2,1)S(1)}, u32[]{:S(2)}, u32[]{:S(2)}) %collective-permute-start.8) | collective-permute-done | bytes 524320 | tf_op jit(solution)/shard_map/ppermute | solution.py:63
  84.6 18.0 %collective-permute-done.9 = bf16[2,128,2048]{2,1,0:T(8,128)(2,1)S(1)} collective-permute-done((bf16[2,128,2048]{2,1,0:T(8,128)(2,1)S(1)}, bf16[2,128,2048]{2,1,0:T(8,128)(2,1)S(1)}, u32[]{:S(2)}, u32[]{:S(2)}) %collective-permute-start.9) | collective-permute-done | bytes 1048608 | tf_op jit(solution)/shard_map/ppermute | solution.py:63
  115.5 25.8 %collective-permute-done.14.refs_1_.refs_3_ = bf16[688,1024]{1,0:T(8,128)(2,1)} collective-permute-done((bf16[688,1024]{1,0:T(8,128)(2,1)S(1)}, bf16[688,1024]{1,0:T(8,128)(2,1)}, u32[]{:S(2)}, u32[]{:S(2)}) %collective-permute-start.14) | collective-permute-done | bytes 1409056 | tf_op jit(solution)/shard_map/ppermute | solution.py:63
  143.7 18.3 %shard_map.298 = (bf16[688,512]{1,0:T(8,128)(2,1)}, f32[688,512]{1,0:T(8,128)}) custom-call(bf16[688,1536]{1,0:T(8,128)(2,1)} %copy-done.67, bf16[688,1536]{1,0:T(8,128)(2,1)} %copy-done.67, bf16[688,1024]{1,0:T(8,128)(2,1)} %collective-permute-done.14.refs_1_.refs_3_, bf16[688,1536]{1,0:T(8,128)(2,1)} %copy-done.67, ...), custom_call_target="tpu_custom_call" | custom-call | flops 1000 | bytes 1000 | tf_op jit(solution)/shard_map/pallas_call | solution.py:760
  178.7 19.3 %collective-permute-done.18 = bf16[1,128,2048]{2,1,0:T(8,128)(2,1)S(1)} collective-permute-done((bf16[1,128,2048]{2,1,0:T(8,128)(2,1)S(1)}, bf16[1,128,2048]{2,1,0:T(8,128)(2,1)S(1)}, u32[]{:S(2)}, u32[]{:S(2)}) %collective-permute-start.18) | collective-permute-done | bytes 524320 | tf_op jit(solution)/shard_map/ppermute | solution.py:63
  212.4 8.1 %shard_map.299 = (bf16[4,2,4,32,2048]{4,3,2,1,0:T(8,128)(2,1)S(1)}, bf16[4,4,2,64,1024]{4,3,2,1,0:T(8,128)(2,1)S(1)}) custom-call(s32[2]{0:T(128)S(1)} %pad_add_fusion.1.where_ref, bf16[4,128,2048]{2,1,0:T(8,128)(2,1)S(1)} %bitcast.312, bf16[4,128,2048]{2,1,0:T(8,128)(2,1)S(1)} %copy-done.13, bf16[4,128,2048]{2,1,0:T(8,128)(2,1)S(1)} %copy-done.15, ...), custom_call_target="tpu_custom_call" | custom-call | flops 1000 | bytes 1000 | tf_op jit(solution)/shard_map/pallas_call | solution.py:169
  222.2 9.8 %shard_map.300 = (bf16[688,2048]{1,0:T(8,128)(2,1)S(1)}, bf16[688,2048]{1,0:T(8,128)(2,1)S(1)}, f32[344,1024]{1,0:T(8,128)S(1)}, bf16[344,1024]{1,0:T(8,128)(2,1)S(1)}) custom-call(bf16[688,1024]{1,0:T(8,128)(2,1)S(1)} %constant_dynamic-update-slice_fusion.11.rows_ref.left_ref, bf16[1024,2048]{1,0:T(8,128)(2,1)S(1)} %bitcast.302, f32[1,2048]{1,0:T(1,128)S(1)} %bitcast.353, ...), custom_call_target="tpu_custom_call" | custom-call | flops 1000 | bytes 1000 | tf_op jit(solution)/shard_map/pallas_call | solution.py:859
  240.3 11.8 %collective-permute-done.30.refs_4_ = bf16[4,32,2048]{2,1,0:T(8,128)(2,1)S(1)} collective-permute-done((bf16[4,32,2048]{2,1,0:T(8,128)(2,1)S(1)}, bf16[4,32,2048]{2,1,0:T(8,128)(2,1)S(1)}, u32[]{:S(2)}, u32[]{:S(2)}) %collective-permute-start.30) | collective-permute-done | bytes 524320 | tf_op jit(solution)/shard_map/ppermute | solution.py:63
  267.9 26.5 %collective-permute-done.31.refs_1_.refs_3_ = bf16[688,1024]{1,0:T(8,128)(2,1)S(1)} collective-permute-done((bf16[688,1024]{1,0:T(8,128)(2,1)S(1)}, bf16[688,1024]{1,0:T(8,128)(2,1)S(1)}, u32[]{:S(2)}, u32[]{:S(2)}) %collective-permute-start.31) | collective-permute-done | bytes 1409056 | tf_op jit(solution)/shard_map/ppermute | solution.py:63
  296.4 18.5 %shard_map.302 = (bf16[688,512]{1,0:T(8,128)(2,1)}, f32[688,512]{1,0:T(8,128)}) custom-call(bf16[688,1536]{1,0:T(8,128)(2,1)} %copy-done.68, bf16[688,1536]{1,0:T(8,128)(2,1)} %copy-done.68, bf16[688,1024]{1,0:T(8,128)(2,1)} %copy-done.72, bf16[688,1536]{1,0:T(8,128)(2,1)} %copy-done.68, bf16[688,1024]{1,0:T(8,128)(2,1)} %copy-done.72), custom_call_target="tpu_custom_call" | custom-call | flops 1000 | bytes 1000 | tf_op jit(solution)/shard_map/pallas_call | solution.py:760
  323.9 19.9 %collective-permute-done.38.refs_4_ = bf16[4,64,2048]{2,1,0:T(8,128)(2,1)} collective-permute-done((bf16[4,64,2048]{2,1,0:T(8,128)(2,1)}, bf16[4,64,2048]{2,1,0:T(8,128)(2,1)}, u32[]{:S(2)}, u32[]{:S(2)}) %collective-permute-start.38) | collective-permute-done | bytes 1048608 | tf_op jit(solution)/shard_map/ppermute | solution.py:63
  349.1 8.0 %shard_map.303 = (bf16[4,2,4,32,2048]{4,3,2,1,0:T(8,128)(2,1)S(1)}, bf16[4,4,2,64,1024]{4,3,2,1,0:T(8,128)(2,1)S(1)}) custom-call(s32[2]{0:T(128)S(1)} %pad_add_fusion.1.where_ref, bf16[4,128,2048]{2,1,0:T(8,128)(2,1)S(1)} %bitcast.315, bf16[4,128,2048]{2,1,0:T(8,128)(2,1)S(1)} %copy-done.17, bf16[4,128,2048]{2,1,0:T(8,128)(2,1)S(1)} %copy-done.19, ...), custom_call_target="tpu_custom_call" | custom-call | flops 1000 | bytes 1000 | tf_op jit(solution)/shard_map/pallas_call | solution.py:169
  358.6 9.8 %shard_map.304 = (bf16[688,2048]{1,0:T(8,128)(2,1)S(1)}, bf16[688,2048]{1,0:T(8,128)(2,1)S(1)}, f32[344,1024]{1,0:T(8,128)S(1)}, bf16[344,1024]{1,0:T(8,128)(2,1)S(1)}) custom-call(bf16[688,1024]{1,0:T(8,128)(2,1)S(1)} %pad_maximum_fusion.4.rows_ref.left_ref, bf16[1024,2048]{1,0:T(8,128)(2,1)S(1)} %bitcast.306, f32[1,2048]{1,0:T(1,128)S(1)} %bitcast.352, ...), custom_call_target="tpu_custom_call" | custom-call | flops 1000 | bytes 1000 | tf_op jit(solution)/shard_map/pallas_call | solution.py:859
  374.1 9.6 %shard_map.305 = (bf16[688,2048]{1,0:T(8,128)(2,1)S(1)}, f32[1,2048]{1,0:T(1,128)S(1)}, f32[344,1024]{1,0:T(8,128)S(1)}, bf16[344,1024]{1,0:T(8,128)(2,1)}) custom-call(bf16[688,1024]{1,0:T(8,128)(2,1)S(1)} %pad_maximum_fusion.5.grad_ref.other_ref, bf16[2048,1024]{1,0:T(8,128)(2,1)S(1)} %bitcast.309, bf16[688,2048]{1,0:T(8,128)(2,1)S(1)} %get-tuple-element.239.slope_ref, ...), custom_call_target="tpu_custom_call" | custom-call | flops 1000 | bytes 1000 | tf_op jit(solution)/shard_map/pallas_call | solution.py:897
  391.6 10.7 %shard_map.306 = (bf16[4,2,1,128,1024]{4,3,2,1,0:T(8,128)(2,1)S(1)}, bf16[4,2,1,128,1024]{4,3,2,1,0:T(8,128)(2,1)}, bf16[4,1,2,128,1024]{4,3,2,1,0:T(8,128)(2,1)S(1)}, bf16[4,1,2,128,1024]{4,3,2,1,0:T(8,128)(2,1)}) custom-call(s32[2]{0:T(128)S(1)} %pad_add_fusion.2.where_ref, bf16[688,1024]{1,0:T(8,128)(2,1)S(1)} %pad_maximum_fusion.4.rows_ref.left_ref, ...), custom_call_target="tpu_custom_call" | custom-call | flops 1000 | bytes 1000 | tf_op jit(solution)/shard_map/pallas_call | solution.py:369
  417.2 16.3 %shard_map.307 = (bf16[688,256]{1,0:T(8,128)(2,1)}, bf16[2,688,256]{2,1,0:T(8,128)(2,1)}, bf16[2,688,256]{2,1,0:T(8,128)(2,1)}) custom-call(bf16[688,1536]{1,0:T(8,128)(2,1)} %copy-done.68, bf16[688,1536]{1,0:T(8,128)(2,1)} %copy-done.68, bf16[688,1024]{1,0:T(8,128)(2,1)} %copy-done.72, bf16[688,1536]{1,0:T(8,128)(2,1)} %copy-done.68, ...), custom_call_target="tpu_custom_call" | custom-call | flops 1000 | bytes 1000 | tf_op jit(solution)/shard_map/pallas_call | solution.py:804
  433.7 16.6 %shard_map.308 = (bf16[688,256]{1,0:T(8,128)(2,1)}, bf16[2,688,256]{2,1,0:T(8,128)(2,1)}, bf16[2,688,256]{2,1,0:T(8,128)(2,1)}) custom-call(bf16[688,1536]{1,0:T(8,128)(2,1)} %copy-done.68, bf16[688,1536]{1,0:T(8,128)(2,1)} %copy-done.68, bf16[688,1024]{1,0:T(8,128)(2,1)} %copy-done.72, bf16[688,1536]{1,0:T(8,128)(2,1)} %copy-done.68, ...), custom_call_target="tpu_custom_call" | custom-call | flops 1000 | bytes 1000 | tf_op jit(solution)/shard_map/pallas_call | solution.py:804
  461.4 7.3 collective-permute-done.47
  492.9 9.6 %shard_map.311 = (bf16[688,2048]{1,0:T(8,128)(2,1)S(1)}, f32[1,2048]{1,0:T(1,128)S(1)}, f32[344,1024]{1,0:T(8,128)S(1)}, bf16[344,1024]{1,0:T(8,128)(2,1)}) custom-call(bf16[688,1024]{1,0:T(8,128)(2,1)S(1)} %pad_maximum_fusion.7.grad_ref.other_ref, bf16[2048,1024]{1,0:T(8,128)(2,1)S(1)} %bitcast.305, bf16[688,2048]{1,0:T(8,128)(2,1)S(1)} %copy-done.29, ...), custom_call_target="tpu_custom_call" | custom-call | flops 1000 | bytes 1000 | tf_op jit(solution)/shard_map/pallas_call | solution.py:897
  504.3 10.5 %shard_map.313 = (bf16[4,2,1,128,1024]{4,3,2,1,0:T(8,128)(2,1)S(1)}, bf16[4,2,1,128,1024]{4,3,2,1,0:T(8,128)(2,1)}, bf16[4,1,2,128,1024]{4,3,2,1,0:T(8,128)(2,1)S(1)}, bf16[4,1,2,128,1024]{4,3,2,1,0:T(8,128)(2,1)}) custom-call(s32[2]{0:T(128)S(1)} %pad_add_fusion.2.where_ref, bf16[688,1024]{1,0:T(8,128)(2,1)S(1)} %copy-done.5, ...), custom_call_target="tpu_custom_call" | custom-call | flops 1000 | bytes 1000 | tf_op jit(solution)/shard_map/pallas_call | solution.py:369
  516.3 7.4 collective-permute-done.52.refs_1_
  543.7 16.4 %shard_map.315 = (bf16[688,256]{1,0:T(8,128)(2,1)}, bf16[2,688,256]{2,1,0:T(8,128)(2,1)}, bf16[2,688,256]{2,1,0:T(8,128)(2,1)}) custom-call(bf16[688,1536]{1,0:T(8,128)(2,1)} %copy-done.67, bf16[688,1536]{1,0:T(8,128)(2,1)} %copy-done.67, bf16[688,1024]{1,0:T(8,128)(2,1)} %collective-permute-done.14.refs_1_.refs_3_, bf16[688,1536]{1,0:T(8,128)(2,1)} %copy-done.67, ...), custom_call_target="tpu_custom_call" | custom-call | flops 1000 | bytes 1000 | tf_op jit(solution)/shard_map/pallas_call | solution.py:804
  566.5 16.6 %shard_map.317 = (bf16[688,256]{1,0:T(8,128)(2,1)}, bf16[2,688,256]{2,1,0:T(8,128)(2,1)}, bf16[2,688,256]{2,1,0:T(8,128)(2,1)}) custom-call(bf16[688,1536]{1,0:T(8,128)(2,1)} %copy-done.67, bf16[688,1536]{1,0:T(8,128)(2,1)} %copy-done.67, bf16[688,1024]{1,0:T(8,128)(2,1)} %collective-permute-done.14.refs_1_.refs_3_, bf16[688,1536]{1,0:T(8,128)(2,1)} %copy-done.67, ...), custom_call_target="tpu_custom_call" | custom-call | flops 1000 | bytes 1000 | tf_op jit(solution)/shard_map/pallas_call | solution.py:804
  597.1 16.1 %collective-permute-done.62 = bf16[2,688,256]{2,1,0:T(8,128)(2,1)S(1)} collective-permute-done((bf16[2,688,256]{2,1,0:T(8,128)(2,1)}, bf16[2,688,256]{2,1,0:T(8,128)(2,1)S(1)}, u32[]{:S(2)}, u32[]{:S(2)}) %collective-permute-start.62) | collective-permute-done | bytes 704544 | tf_op jit(solution)/shard_map/ppermute | solution.py:63
  644.0 6.9 collective-permute-done.68
  656.1 10.5 %collective-permute-done.80 = bf16[1,1,64,2048]{3,2,1,0:T(8,128)(2,1)S(1)} collective-permute-done((bf16[1,1,64,2048]{3,2,1,0:T(8,128)(2,1)S(1)}, bf16[1,1,64,2048]{3,2,1,0:T(8,128)(2,1)S(1)}, u32[]{:S(2)}, u32[]{:S(2)}) %collective-permute-start.80) | collective-permute-done | bytes 262176 | tf_op jit(solution)/shard_map/ppermute | solution.py:63
  699.9 18.0 %collective-permute-done.86 = bf16[1,1,128,2048]{3,2,1,0:T(8,128)(2,1)S(1)} collective-permute-done((bf16[1,1,128,2048]{3,2,1,0:T(8,128)(2,1)S(1)}, bf16[1,1,128,2048]{3,2,1,0:T(8,128)(2,1)S(1)}, u32[]{:S(2)}, u32[]{:S(2)}) %collective-permute-start.86) | collective-permute-done | bytes 524320 | tf_op jit(solution)/shard_map/ppermute | solution.py:63
  719.9 12.8 %collective-permute-done.77 = bf16[1,1,64,2048]{3,2,1,0:T(8,128)(2,1)S(1)} collective-permute-done((bf16[1,1,64,2048]{3,2,1,0:T(8,128)(2,1)S(1)}, bf16[1,1,64,2048]{3,2,1,0:T(8,128)(2,1)S(1)}, u32[]{:S(2)}, u32[]{:S(2)}) %collective-permute-start.77) | collective-permute-done | bytes 262176 | tf_op jit(solution)/shard_map/ppermute | solution.py:63
  751.0 8.0 %collective-permute-done.82 = bf16[128,2048]{1,0:T(8,128)(2,1)S(1)} collective-permute-done((bf16[128,2048]{1,0:T(8,128)(2,1)S(1)}, bf16[128,2048]{1,0:T(8,128)(2,1)S(1)}, u32[]{:S(2)}, u32[]{:S(2)}) %collective-permute-start.82) | collective-permute-done | bytes 524320 | tf_op jit(solution)/shard_map/ppermute | solution.py:63
  761.1 10.5 %collective-permute-done.90.refs_3_ = bf16[128,2048]{1,0:T(8,128)(2,1)S(1)} collective-permute-done((bf16[128,2048]{1,0:T(8,128)(2,1)S(1)}, bf16[128,2048]{1,0:T(8,128)(2,1)S(1)}, u32[]{:S(2)}, u32[]{:S(2)}) %collective-permute-start.90) | collective-permute-done | bytes 524320 | tf_op jit(solution)/shard_map/ppermute | solution.py:63
  (828 shorter events, 338.7 us)
Async XLA Ops:
  110.1 31.2 %collective-permute-start.14 = (bf16[688,1024]{1,0:T(8,128)(2,1)S(1)}, bf16[688,1024]{1,0:T(8,128)(2,1)}, u32[]{:S(2)}, u32[]{:S(2)}) collective-permute-start(bf16[688,1024]{1,0:T(8,128)(2,1)S(1)} %slice.487), channel_id=1, source_target_pairs={{0,2},{1,3},{2,0},{3,1},{4,6},{5,7},{6,4},{7,5},{8,10},{9,11},{10,... | collective-permute-start | bytes 4227080 | tf_op jit(solution)/shard_map/ppermute | solution.py:63
  111.5 54.6 %collective-permute-start.20 = (bf16[4,128,2048]{2,1,0:T(8,128)(2,1)S(1)}, bf16[4,128,2048]{2,1,0:T(8,128)(2,1)S(1)}, u32[]{:S(2)}, u32[]{:S(2)}) collective-permute-start(bf16[4,128,2048]{2,1,0:T(8,128)(2,1)S(1)} %bitcast.310), channel_id=1, source_target_pairs={{0,8},{8,0},{16,24},{24,16},{1,9},{9,1},{17,25},{25,17},{2,10},{10... | collective-permute-start | bytes 6291464 | tf_op jit(solution)/shard_map/ppermute | solution.py:63
  113.1 53.1 %collective-permute-start.21 = (bf16[4,128,2048]{2,1,0:T(8,128)(2,1)S(1)}, bf16[4,128,2048]{2,1,0:T(8,128)(2,1)S(1)}, u32[]{:S(2)}, u32[]{:S(2)}) collective-permute-start(bf16[4,128,2048]{2,1,0:T(8,128)(2,1)S(1)} %bitcast.311), channel_id=1, source_target_pairs={{0,16},{8,24},{16,0},{24,8},{1,17},{9,25},{17,1},{25,9},{2,18},{10... | collective-permute-start | bytes 6291464 | tf_op jit(solution)/shard_map/ppermute | solution.py:63
  166.2 33.3 %collective-permute-start.23 = (bf16[4,64,2048]{2,1,0:T(8,128)(2,1)S(1)}, bf16[4,64,2048]{2,1,0:T(8,128)(2,1)S(1)}, u32[]{:S(2)}, u32[]{:S(2)}) collective-permute-start(bf16[4,64,2048]{2,1,0:T(8,128)(2,1)S(1)} %slice.501), channel_id=1, source_target_pairs={{0,16},{8,24},{16,0},{24,8},{1,17},{9,25},{17,1},{25,9},{2,18},{10... | collective-permute-start | bytes 3145736 | tf_op jit(solution)/shard_map/ppermute | solution.py:63
  167.9 32.6 %collective-permute-start.22 = (bf16[4,64,2048]{2,1,0:T(8,128)(2,1)S(1)}, bf16[4,64,2048]{2,1,0:T(8,128)(2,1)S(1)}, u32[]{:S(2)}, u32[]{:S(2)}) collective-permute-start(bf16[4,64,2048]{2,1,0:T(8,128)(2,1)S(1)} %slice.500), channel_id=1, source_target_pairs={{0,8},{8,0},{16,24},{24,16},{1,9},{9,1},{17,25},{25,17},{2,10},{10... | collective-permute-start | bytes 3145736 | tf_op jit(solution)/shard_map/ppermute | solution.py:63
  199.5 34.1 %collective-permute-start.26 = (bf16[2,128,2048]{2,1,0:T(8,128)(2,1)}, bf16[2,128,2048]{2,1,0:T(8,128)(2,1)}, u32[]{:S(2)}, u32[]{:S(2)}) collective-permute-start(bf16[2,128,2048]{2,1,0:T(8,128)(2,1)} %get-tuple-element.221), channel_id=1, source_target_pairs={{0,2},{1,3},{2,0},{3,1},{4,6},{5,7},{6,4},{7,5},{8,10},{9,11},{10,... | collective-permute-start | bytes 3145736 | tf_op jit(solution)/shard_map/ppermute | solution.py:63
  201.5 32.2 %collective-permute-start.24 = (bf16[4,64,2048]{2,1,0:T(8,128)(2,1)}, bf16[4,64,2048]{2,1,0:T(8,128)(2,1)S(1)}, u32[]{:S(2)}, u32[]{:S(2)}) collective-permute-start(bf16[4,64,2048]{2,1,0:T(8,128)(2,1)} %bitcast.65.refs_0_), channel_id=1, source_target_pairs={{0,8},{8,0},{16,24},{24,16},{1,9},{9,1},{17,25},{25,17},{2,10},{10... | collective-permute-start | bytes 3145736 | tf_op jit(solution)/shard_map/ppermute | solution.py:63
  203.0 30.7 %collective-permute-start.25 = (bf16[4,64,2048]{2,1,0:T(8,128)(2,1)}, bf16[4,64,2048]{2,1,0:T(8,128)(2,1)}, u32[]{:S(2)}, u32[]{:S(2)}) collective-permute-start(bf16[4,64,2048]{2,1,0:T(8,128)(2,1)} %bitcast.65.refs_0_), channel_id=1, source_target_pairs={{0,16},{8,24},{16,0},{24,8},{1,17},{9,25},{17,1},{25,9},{2,18},{10... | collective-permute-start | bytes 3145736 | tf_op jit(solution)/shard_map/ppermute | solution.py:63
  262.3 32.1 %collective-permute-start.31 = (bf16[688,1024]{1,0:T(8,128)(2,1)S(1)}, bf16[688,1024]{1,0:T(8,128)(2,1)S(1)}, u32[]{:S(2)}, u32[]{:S(2)}) collective-permute-start(bf16[688,1024]{1,0:T(8,128)(2,1)S(1)} %slice.513), channel_id=1, source_target_pairs={{0,2},{1,3},{2,0},{3,1},{4,6},{5,7},{6,4},{7,5},{8,10},{9,11},{10,... | collective-permute-start | bytes 4227080 | tf_op jit(solution)/shard_map/ppermute | solution.py:63
  265.9 50.8 %collective-permute-start.35 = (bf16[4,128,2048]{2,1,0:T(8,128)(2,1)S(1)}, bf16[4,128,2048]{2,1,0:T(8,128)(2,1)S(1)}, u32[]{:S(2)}, u32[]{:S(2)}) collective-permute-start(bf16[4,128,2048]{2,1,0:T(8,128)(2,1)S(1)} %bitcast.313), channel_id=1, source_target_pairs={{0,8},{8,0},{16,24},{24,16},{1,9},{9,1},{17,25},{25,17},{2,10},{10... | collective-permute-start | bytes 6291464 | tf_op jit(solution)/shard_map/ppermute | solution.py:63
  266.5 51.3 %collective-permute-start.36 = (bf16[4,128,2048]{2,1,0:T(8,128)(2,1)S(1)}, bf16[4,128,2048]{2,1,0:T(8,128)(2,1)S(1)}, u32[]{:S(2)}, u32[]{:S(2)}) collective-permute-start(bf16[4,128,2048]{2,1,0:T(8,128)(2,1)S(1)} %bitcast.314), channel_id=1, source_target_pairs={{0,16},{8,24},{16,0},{24,8},{1,17},{9,25},{17,1},{25,9},{2,18},{10... | collective-permute-start | bytes 6291464 | tf_op jit(solution)/shard_map/ppermute | solution.py:63
  323.9 33.3 %collective-permute-start.34 = (bf16[344,1024]{1,0:T(8,128)(2,1)S(1)}, bf16[344,1024]{1,0:T(8,128)(2,1)}, u32[]{:S(2)}, u32[]{:S(2)}) collective-permute-start(bf16[344,1024]{1,0:T(8,128)(2,1)S(1)} %add_convert_fusion.7), channel_id=1, source_target_pairs={{0,1},{1,0},{2,3},{3,2},{4,5},{5,4},{6,7},{7,6},{8,9},{9,8},{10,11... | collective-permute-start | bytes 2113544 | tf_op jit(solution)/shard_map/ppermute | solution.py:63
  403.7 48.5 %collective-permute-start.44 = (bf16[4,2,1,128,1024]{4,3,2,1,0:T(8,128)(2,1)}, bf16[4,2,1,128,1024]{4,3,2,1,0:T(8,128)(2,1)}, u32[]{:S(2)}, u32[]{:S(2)}) collective-permute-start(bf16[4,2,1,128,1024]{4,3,2,1,0:T(8,128)(2,1)} %get-tuple-element.243), channel_id=1, source_target_pairs={{0,8},{8,0},{16,24},{24,16},{1,9},{9,1},{17,25},{25,17},{2,10},{10... | collective-permute-start | bytes 6291464 | tf_op jit(solution)/shard_map/ppermute | solution.py:63
  407.3 47.4 %collective-permute-start.45 = (bf16[4,1,2,128,1024]{4,3,2,0,1:T(8,128)(2,1)}, bf16[4,1,2,128,1024]{4,3,2,0,1:T(8,128)(2,1)}, u32[]{:S(2)}, u32[]{:S(2)}) collective-permute-start(bf16[4,1,2,128,1024]{4,3,2,0,1:T(8,128)(2,1)} %bitcast.96), channel_id=1, source_target_pairs={{0,16},{8,24},{16,0},{24,8},{1,17},{9,25},{17,1},{25,9},{2,18},{10... | collective-permute-start | bytes 6291464 | tf_op jit(solution)/shard_map/ppermute | solution.py:63
  473.7 28.8 %collective-permute-start.50 = (bf16[4,1,128,1024]{3,2,1,0:T(8,128)(2,1)}, bf16[4,1,128,1024]{3,2,1,0:T(8,128)(2,1)S(1)}, u32[]{:S(2)}, u32[]{:S(2)}) collective-permute-start(bf16[4,1,128,1024]{3,2,1,0:T(8,128)(2,1)} %get-tuple-element.256), channel_id=1, source_target_pairs={{0,16},{8,24},{16,0},{24,8},{1,17},{9,25},{17,1},{25,9},{2,18},{10... | collective-permute-start | bytes 3145736 | tf_op jit(solution)/shard_map/ppermute | solution.py:63
  475.2 27.3 %collective-permute-start.51 = (bf16[4,1,128,1024]{3,2,1,0:T(8,128)(2,1)S(1)}, bf16[4,1,128,1024]{3,2,1,0:T(8,128)(2,1)S(1)}, u32[]{:S(2)}, u32[]{:S(2)}) collective-permute-start(bf16[4,1,128,1024]{3,2,1,0:T(8,128)(2,1)S(1)} %get-tuple-element.257), channel_id=1, source_target_pairs={{0,8},{8,0},{16,24},{24,16},{1,9},{9,1},{17,25},{25,17},{2,10},{10... | collective-permute-start | bytes 3145736 | tf_op jit(solution)/shard_map/ppermute | solution.py:63
  490.6 33.2 %collective-permute-start.52 = (bf16[4,2,1,64,1024]{4,3,2,1,0:T(8,128)(2,1)}, bf16[4,2,1,64,1024]{4,3,2,1,0:T(8,128)(2,1)S(1)}, u32[]{:S(2)}, u32[]{:S(2)}) collective-permute-start(bf16[4,2,1,64,1024]{4,3,2,1,0:T(8,128)(2,1)} %get-tuple-element.264), channel_id=1, source_target_pairs={{0,8},{8,0},{16,24},{24,16},{1,9},{9,1},{17,25},{25,17},{2,10},{10... | collective-permute-start | bytes 3145736 | tf_op jit(solution)/shard_map/ppermute | solution.py:63
  492.1 31.7 %collective-permute-start.53 = (bf16[4,1,2,64,1024]{4,3,2,0,1:T(8,128)(2,1)}, bf16[4,1,2,64,1024]{4,3,2,0,1:T(8,128)(2,1)S(1)}, u32[]{:S(2)}, u32[]{:S(2)}) collective-permute-start(bf16[4,1,2,64,1024]{4,3,2,0,1:T(8,128)(2,1)} %bitcast.108), channel_id=1, source_target_pairs={{0,16},{8,24},{16,0},{24,8},{1,17},{9,25},{17,1},{25,9},{2,18},{10... | collective-permute-start | bytes 3145736 | tf_op jit(solution)/shard_map/ppermute | solution.py:63
  514.8 72.0 %collective-permute-start.57 = (bf16[4,2,1,128,1024]{4,3,2,1,0:T(8,128)(2,1)}, bf16[4,2,1,128,1024]{4,3,2,1,0:T(8,128)(2,1)}, u32[]{:S(2)}, u32[]{:S(2)}) collective-permute-start(bf16[4,2,1,128,1024]{4,3,2,1,0:T(8,128)(2,1)} %get-tuple-element.279), channel_id=1, source_target_pairs={{0,8},{8,0},{16,24},{24,16},{1,9},{9,1},{17,25},{25,17},{2,10},{10... | collective-permute-start | bytes 6291464 | tf_op jit(solution)/shard_map/ppermute | solution.py:63
  526.0 63.3 %collective-permute-start.58 = (bf16[4,1,2,128,1024]{4,3,2,0,1:T(8,128)(2,1)}, bf16[4,1,2,128,1024]{4,3,2,0,1:T(8,128)(2,1)}, u32[]{:S(2)}, u32[]{:S(2)}) collective-permute-start(bf16[4,1,2,128,1024]{4,3,2,0,1:T(8,128)(2,1)} %bitcast.114), channel_id=1, source_target_pairs={{0,16},{8,24},{16,0},{24,8},{1,17},{9,25},{17,1},{25,9},{2,18},{10... | collective-permute-start | bytes 6291464 | tf_op jit(solution)/shard_map/ppermute | solution.py:63
  534.5 28.9 %collective-permute-start.56 = (bf16[2,128,2048]{2,1,0:T(8,128)(2,1)}, bf16[2,128,2048]{2,1,0:T(8,128)(2,1)}, u32[]{:S(2)}, u32[]{:S(2)}) collective-permute-start(bf16[2,128,2048]{2,1,0:T(8,128)(2,1)} %get-tuple-element.276), channel_id=1, source_target_pairs={{0,2},{1,3},{2,0},{3,1},{4,6},{5,7},{6,4},{7,5},{8,10},{9,11},{10,... | collective-permute-start | bytes 3145736 | tf_op jit(solution)/shard_map/ppermute | solution.py:63
  562.0 32.8 %collective-permute-start.59 = (bf16[4,1,64,1024]{3,2,1,0:T(8,128)(2,1)}, bf16[4,1,64,1024]{3,2,1,0:T(8,128)(2,1)}, u32[]{:S(2)}, u32[]{:S(2)}) collective-permute-start(bf16[4,1,64,1024]{3,2,1,0:T(8,128)(2,1)} %get-tuple-element.287), channel_id=1, source_target_pairs={{0,16},{8,24},{16,0},{24,8},{1,17},{9,25},{17,1},{25,9},{2,18},{10... | collective-permute-start | bytes 1572872 | tf_op jit(solution)/shard_map/ppermute | solution.py:63
  563.5 32.0 %collective-permute-start.60 = (bf16[4,1,64,1024]{3,2,1,0:T(8,128)(2,1)}, bf16[4,1,64,1024]{3,2,1,0:T(8,128)(2,1)}, u32[]{:S(2)}, u32[]{:S(2)}) collective-permute-start(bf16[4,1,64,1024]{3,2,1,0:T(8,128)(2,1)} %get-tuple-element.288), channel_id=1, source_target_pairs={{0,8},{8,0},{16,24},{24,16},{1,9},{9,1},{17,25},{25,17},{2,10},{10... | collective-permute-start | bytes 1572872 | tf_op jit(solution)/shard_map/ppermute | solution.py:63
  584.6 28.6 %collective-permute-start.62 = (bf16[2,688,256]{2,1,0:T(8,128)(2,1)}, bf16[2,688,256]{2,1,0:T(8,128)(2,1)S(1)}, u32[]{:S(2)}, u32[]{:S(2)}) collective-permute-start(bf16[2,688,256]{2,1,0:T(8,128)(2,1)} %get-tuple-element.311), channel_id=1, source_target_pairs={{0,2},{1,3},{2,0},{3,1},{4,6},{5,7},{6,4},{7,5},{8,10},{9,11},{10,... | collective-permute-start | bytes 2113544 | tf_op jit(solution)/shard_map/ppermute | solution.py:63
  586.9 47.6 %collective-permute-start.91 = (bf16[1,1,128,2048]{3,2,1,0:T(8,128)(2,1)S(1)}, bf16[1,1,128,2048]{3,2,1,0:T(8,128)(2,1)}, u32[]{:S(2)}, u32[]{:S(2)}) collective-permute-start(bf16[1,1,128,2048]{3,2,1,0:T(8,128)(2,1)S(1)} %copy-done.66), channel_id=1, source_target_pairs={{0,4},{1,5},{2,6},{3,7},{4,0},{5,1},{6,2},{7,3},{8,12},{9,13},{10,... | collective-permute-start | bytes 1572872 | tf_op jit(solution)/shard_map/ppermute | solution.py:63
  593.3 32.3 %collective-permute-start.64 = (bf16[4,1,128,1024]{3,2,1,0:T(8,128)(2,1)S(1)}, bf16[4,1,128,1024]{3,2,1,0:T(8,128)(2,1)S(1)}, u32[]{:S(2)}, u32[]{:S(2)}) collective-permute-start(bf16[4,1,128,1024]{3,2,1,0:T(8,128)(2,1)S(1)} %get-tuple-element.304), channel_id=1, source_target_pairs={{0,8},{8,0},{16,24},{24,16},{1,9},{9,1},{17,25},{25,17},{2,10},{10... | collective-permute-start | bytes 3145736 | tf_op jit(solution)/shard_map/ppermute | solution.py:63
  594.8 31.4 %collective-permute-start.63 = (bf16[4,1,128,1024]{3,2,1,0:T(8,128)(2,1)S(1)}, bf16[4,1,128,1024]{3,2,1,0:T(8,128)(2,1)S(1)}, u32[]{:S(2)}, u32[]{:S(2)}) collective-permute-start(bf16[4,1,128,1024]{3,2,1,0:T(8,128)(2,1)S(1)} %get-tuple-element.303), channel_id=1, source_target_pairs={{0,16},{8,24},{16,0},{24,8},{1,17},{9,25},{17,1},{25,9},{2,18},{10... | collective-permute-start | bytes 3145736 | tf_op jit(solution)/shard_map/ppermute | solution.py:63
  622.5 29.7 %collective-permute-start.67 = (bf16[4,2,1,64,1024]{4,3,2,1,0:T(8,128)(2,1)S(1)}, bf16[4,2,1,64,1024]{4,3,2,1,0:T(8,128)(2,1)S(1)}, u32[]{:S(2)}, u32[]{:S(2)}) collective-permute-start(bf16[4,2,1,64,1024]{4,3,2,1,0:T(8,128)(2,1)S(1)} %get-tuple-element.312), channel_id=1, source_target_pairs={{0,8},{8,0},{16,24},{24,16},{1,9},{9,1},{17,25},{25,17},{2,10},{10... | collective-permute-start | bytes 3145736 | tf_op jit(solution)/shard_map/ppermute | solution.py:63
  627.8 63.3 %collective-permute-start.85 = (bf16[2,128,2048]{2,1,0:T(8,128)(2,1)}, bf16[2,128,2048]{2,1,0:T(8,128)(2,1)S(1)}, u32[]{:S(2)}, u32[]{:S(2)}) collective-permute-start(bf16[2,128,2048]{2,1,0:T(8,128)(2,1)} %get-tuple-element.319), channel_id=1, source_target_pairs={{0,2},{1,3},{2,0},{3,1},{4,6},{5,7},{6,4},{7,5},{8,10},{9,11},{10,... | collective-permute-start | bytes 3145736 | tf_op jit(solution)/shard_map/ppermute | solution.py:63
  683.2 55.2 %collective-permute-start.93 = (bf16[128,2048]{1,0:T(8,128)(2,1)S(1)}, bf16[128,2048]{1,0:T(8,128)(2,1)}, u32[]{:S(2)}, u32[]{:S(2)}) collective-permute-start(bf16[128,2048]{1,0:T(8,128)(2,1)S(1)} %pad_maximum_fusion.18.refs_0_), channel_id=1, source_target_pairs={{0,8},{8,0},{16,24},{24,16},{1,9},{9,1},{17,25},{25,17},{2,10},{10... | collective-permute-start | bytes 1572872 | tf_op jit(solution)/shard_map/ppermute | solution.py:63
  697.0 41.3 %collective-permute-start.95 = (bf16[128,2048]{1,0:T(8,128)(2,1)S(1)}, bf16[128,2048]{1,0:T(8,128)(2,1)S(1)}, u32[]{:S(2)}, u32[]{:S(2)}) collective-permute-start(bf16[128,2048]{1,0:T(8,128)(2,1)S(1)} %collective-permute-done.94.refs_2_), channel_id=1, source_target_pairs={{0,8},{8,0},{16,24},{24,16},{1,9},{9,1},{17,25},{25,17},{2,10},{10... | collective-permute-start | bytes 1572872 | tf_op jit(solution)/shard_map/ppermute | solution.py:63
  699.2 36.1 %collective-permute-start.75 = (f32[2,1,1792]{2,0,1:T(2,128)S(1)}, f32[2,1,1792]{2,0,1:T(2,128)S(1)}, u32[]{:S(2)}, u32[]{:S(2)}) collective-permute-start(f32[2,1,1792]{2,0,1:T(2,128)S(1)} %add.406), channel_id=1, source_target_pairs={{0,16},{8,24},{16,0},{24,8},{1,17},{9,25},{17,1},{25,9},{2,18},{10... | collective-permute-start | bytes 43016 | tf_op jit(solution)/shard_map/ppermute | solution.py:63
  (269 other events, 2900.1 us)

commit v8 on v6

--- a/solution.py
+++ b/solution.py
@@ -177,7 +177,7 @@
             pltpu.SemaphoreType.DMA((len(pieces),)),
             pltpu.SemaphoreType.DMA((len(blocks), len(pieces), planes)),
         ],
-        compiler_params=params(60),
+        compiler_params=params(20),
         cost_estimate=estimate(0, 4 * sum(piece.size for piece in pieces)),
     )(scalars(plane, member), *pieces)
     return [out.reshape(-1, out.shape[-1]) for out in outs]
@@ -1097,14 +1097,12 @@
         d_attended = later.sent(d_attended, old[2])
     second_query, d_own, d_others = back(pairs // 2)
     d_others = after(d_others, first_got)
+    if old:
+        d_others = later.came(d_others, old[2])
     second_kv, second_got = collect_rows(d_own, d_others)
     second_query = later.came(second_query, block)
     later.step(block, second_query)
     second_query = later.sent(second_query, block)
-    if old:
-        second_query = later.came(second_query, old[1])
-        later.join(old[3], [old[1]], second_query)
-        second_query = later.sent(second_query, old[3])
     d_query = jnp.concatenate([first_query, second_query], 1)
     d_key = jnp.concatenate([first_kv[0], second_kv[0]], 1)
     d_value = jnp.concatenate([first_kv[1], second_kv[1]], 1)
@@ -1115,6 +1113,8 @@
     later.begin(mixed, mixed_grad, (normed, d_projected, attended, d_branch_both))
     d_projected = later.sent(d_projected, mixed)
     if old:
+        later.join(old[3], [old[1]], d_projected)
+        d_projected = later.sent(d_projected, old[3])
         later.join(block_planes, [block], d_projected)
         d_projected = later.sent(d_projected, block_planes)
     d_normed = input_dot(d_projected[:tokens], heads_weight) + widen(got)

time: 785 us -> 777 us (0.990)
  local copies, waits for them, and re-layouts: 73.8 us -> 63.5 us
  waiting for transfers between devices: 306 us -> 314 us
    ppermute x96, waiting for transfers between devices: 306 us -> 314 us  [swap(): return lax.ppermute(tensor, axis, [(i, i ^ offset) for i in range(count)])]
    unnamed x435 -> x415, local copies, waits for them, and re-layouts: 41.3 us -> 39.7 us
  transfers between devices with their start and end apart: 96 -> 96, of which waited for: 43 -> 42; matrix products, arithmetic and copies ran while one was open for 12% -> 12% of each run, Pallas kernels for 27% -> 26%
where the time goes in v8:
time: 777 us; the launch traced here: 767 us
  waiting for transfers between devices  314 us (40%)
  Pallas kernels  227 us (29%)
  starting transfers between devices  85.4 us (11%)
  local copies, waits for them, and re-layouts  63.5 us (8%)
  other arithmetic  47.5 us (6%)
  matrix products  25.4 us (3%)
    ppermute x96, waiting for transfers between devices, swap(): return lax.ppermute(tensor, axis, [(i, i ^ offset) for i in range(count)])  314 us
    ppermute x96, starting transfers between devices, swap(): return lax.ppermute(tensor, axis, [(i, i ^ offset) for i in range(count)])  85.4 us
    pallas_call x4, Pallas kernels, attend_back(): pl.pallas_call(functools.partial(attend_back_kernel, scale * math.log2(ma...  65.7 us
    unnamed x415, local copies, waits for them, and re-layouts  39.7 us
    pallas_call x2, Pallas kernels, attend(): pl.pallas_call(functools.partial(attend_kernel, factor, len(parts)), out_...  36.8 us
    pallas_call x4, Pallas kernels, grad_call(): pl.pallas_call(functools.partial(kernel, shapes), out_shape=out_shapes, g...  32 us
    pallas_call x4, Pallas kernels, place(): pl.pallas_call(functools.partial(place_kernel, pieces[0].shape[1] // 2, b...  23.2 us
    pallas_call x2, Pallas kernels, feed_forward(): pl.pallas_call(expand_kernel, out_shape=[jax.ShapeDtypeStruct((tokens, un...  19.6 us
  transfers between devices with their start and end apart: 96, of which 42 were waited for; matrix products, arithmetic and copies ran while one was open for 12% of the time, Pallas kernels for 26%

profile of v8, /device:TPU:0, one launch (start us, length us, event | category | flops | bytes accessed | tf_op | source)
XLA Modules:
  0.0 766.6 jit_solution(6030461690791572594)
XLA Ops:
  14.0 12.5 %collective-permute-done.1 = bf16[1,64,2048]{2,1,0:T(8,128)(2,1)S(1)} collective-permute-done((bf16[1,64,2048]{2,1,0:T(8,128)(2,1)S(1)}, bf16[1,64,2048]{2,1,0:T(8,128)(2,1)S(1)}, u32[]{:S(2)}, u32[]{:S(2)}) %collective-permute-start.1) | collective-permute-done | bytes 262176 | tf_op jit(solution)/shard_map/ppermute | solution.py:63
  31.2 14.6 %collective-permute-done.2 = bf16[172,1024]{1,0:T(8,128)(2,1)S(1)} collective-permute-done((bf16[172,1024]{1,0:T(8,128)(2,1)S(1)}, bf16[172,1024]{1,0:T(8,128)(2,1)S(1)}, u32[]{:S(2)}, u32[]{:S(2)}) %collective-permute-start.2) | collective-permute-done | bytes 352288 | tf_op jit(solution)/shard_map/ppermute | solution.py:63
  53.8 13.3 %collective-permute-done.5 = bf16[4,2,1792]{2,1,0:T(2,128)(2,1)S(1)} collective-permute-done((bf16[4,2,1792]{2,1,0:T(2,128)(2,1)S(1)}, bf16[4,2,1792]{2,1,0:T(2,128)(2,1)S(1)}, u32[]{:S(2)}, u32[]{:S(2)}) %collective-permute-start.5) | collective-permute-done | bytes 28704 | tf_op jit(solution)/shard_map/ppermute | solution.py:63
  89.9 11.4 %collective-permute-done.9 = bf16[2,128,2048]{2,1,0:T(8,128)(2,1)S(1)} collective-permute-done((bf16[2,128,2048]{2,1,0:T(8,128)(2,1)S(1)}, bf16[2,128,2048]{2,1,0:T(8,128)(2,1)S(1)}, u32[]{:S(2)}, u32[]{:S(2)}) %collective-permute-start.9) | collective-permute-done | bytes 1048608 | tf_op jit(solution)/shard_map/ppermute | solution.py:63
  112.5 25.5 %collective-permute-done.14.refs_1_.refs_3_ = bf16[688,1024]{1,0:T(8,128)(2,1)} collective-permute-done((bf16[688,1024]{1,0:T(8,128)(2,1)S(1)}, bf16[688,1024]{1,0:T(8,128)(2,1)}, u32[]{:S(2)}, u32[]{:S(2)}) %collective-permute-start.14) | collective-permute-done | bytes 1409056 | tf_op jit(solution)/shard_map/ppermute | solution.py:63
  140.4 18.3 %shard_map.298 = (bf16[688,512]{1,0:T(8,128)(2,1)}, f32[688,512]{1,0:T(8,128)}) custom-call(bf16[688,1536]{1,0:T(8,128)(2,1)} %copy-done.58, bf16[688,1536]{1,0:T(8,128)(2,1)} %copy-done.58, bf16[688,1024]{1,0:T(8,128)(2,1)} %collective-permute-done.14.refs_1_.refs_3_, bf16[688,1536]{1,0:T(8,128)(2,1)} %copy-done.58, ...), custom_call_target="tpu_custom_call" | custom-call | flops 1000 | bytes 1000 | tf_op jit(solution)/shard_map/pallas_call | solution.py:760
  177.9 15.0 %collective-permute-done.18 = bf16[1,128,2048]{2,1,0:T(8,128)(2,1)S(1)} collective-permute-done((bf16[1,128,2048]{2,1,0:T(8,128)(2,1)S(1)}, bf16[1,128,2048]{2,1,0:T(8,128)(2,1)S(1)}, u32[]{:S(2)}, u32[]{:S(2)}) %collective-permute-start.18) | collective-permute-done | bytes 524320 | tf_op jit(solution)/shard_map/ppermute | solution.py:63
  208.1 8.1 %shard_map.299 = (bf16[4,2,4,32,2048]{4,3,2,1,0:T(8,128)(2,1)S(1)}, bf16[4,4,2,64,1024]{4,3,2,1,0:T(8,128)(2,1)S(1)}) custom-call(s32[2]{0:T(128)S(1)} %pad_add_fusion.1.where_ref, bf16[4,128,2048]{2,1,0:T(8,128)(2,1)S(1)} %bitcast.312, bf16[4,128,2048]{2,1,0:T(8,128)(2,1)S(1)} %copy-done.7, bf16[4,128,2048]{2,1,0:T(8,128)(2,1)S(1)} %copy-done.9, ...), custom_call_target="tpu_custom_call" | custom-call | flops 1000 | bytes 1000 | tf_op jit(solution)/shard_map/pallas_call | solution.py:169
  218.0 9.8 %shard_map.300 = (bf16[688,2048]{1,0:T(8,128)(2,1)S(1)}, bf16[688,2048]{1,0:T(8,128)(2,1)S(1)}, f32[344,1024]{1,0:T(8,128)S(1)}, bf16[344,1024]{1,0:T(8,128)(2,1)S(1)}) custom-call(bf16[688,1024]{1,0:T(8,128)(2,1)S(1)} %constant_dynamic-update-slice_fusion.11.rows_ref.left_ref, bf16[1024,2048]{1,0:T(8,128)(2,1)S(1)} %bitcast.302, f32[1,2048]{1,0:T(1,128)S(1)} %bitcast.354, ...), custom_call_target="tpu_custom_call" | custom-call | flops 1000 | bytes 1000 | tf_op jit(solution)/shard_map/pallas_call | solution.py:859
  237.8 11.8 %collective-permute-done.30.refs_4_ = bf16[4,32,2048]{2,1,0:T(8,128)(2,1)S(1)} collective-permute-done((bf16[4,32,2048]{2,1,0:T(8,128)(2,1)S(1)}, bf16[4,32,2048]{2,1,0:T(8,128)(2,1)S(1)}, u32[]{:S(2)}, u32[]{:S(2)}) %collective-permute-start.30) | collective-permute-done | bytes 524320 | tf_op jit(solution)/shard_map/ppermute | solution.py:63
  265.4 26.4 %collective-permute-done.31.refs_1_.refs_3_ = bf16[688,1024]{1,0:T(8,128)(2,1)S(1)} collective-permute-done((bf16[688,1024]{1,0:T(8,128)(2,1)S(1)}, bf16[688,1024]{1,0:T(8,128)(2,1)S(1)}, u32[]{:S(2)}, u32[]{:S(2)}) %collective-permute-start.31) | collective-permute-done | bytes 1409056 | tf_op jit(solution)/shard_map/ppermute | solution.py:63
  296.0 18.5 %shard_map.302 = (bf16[688,512]{1,0:T(8,128)(2,1)}, f32[688,512]{1,0:T(8,128)}) custom-call(bf16[688,1536]{1,0:T(8,128)(2,1)} %copy-done.59, bf16[688,1536]{1,0:T(8,128)(2,1)} %copy-done.59, bf16[688,1024]{1,0:T(8,128)(2,1)} %copy-done.63, bf16[688,1536]{1,0:T(8,128)(2,1)} %copy-done.59, bf16[688,1024]{1,0:T(8,128)(2,1)} %copy-done.63), custom_call_target="tpu_custom_call" | custom-call | flops 1000 | bytes 1000 | tf_op jit(solution)/shard_map/pallas_call | solution.py:760
  326.2 17.6 %collective-permute-done.38.refs_4_ = bf16[4,64,2048]{2,1,0:T(8,128)(2,1)} collective-permute-done((bf16[4,64,2048]{2,1,0:T(8,128)(2,1)}, bf16[4,64,2048]{2,1,0:T(8,128)(2,1)}, u32[]{:S(2)}, u32[]{:S(2)}) %collective-permute-start.38) | collective-permute-done | bytes 1048608 | tf_op jit(solution)/shard_map/ppermute | solution.py:63
  349.3 8.0 %shard_map.303 = (bf16[4,2,4,32,2048]{4,3,2,1,0:T(8,128)(2,1)S(1)}, bf16[4,4,2,64,1024]{4,3,2,1,0:T(8,128)(2,1)S(1)}) custom-call(s32[2]{0:T(128)S(1)} %pad_add_fusion.1.where_ref, bf16[4,128,2048]{2,1,0:T(8,128)(2,1)S(1)} %bitcast.315, bf16[4,128,2048]{2,1,0:T(8,128)(2,1)S(1)} %copy-done.11, bf16[4,128,2048]{2,1,0:T(8,128)(2,1)S(1)} %copy-done.13, ...), custom_call_target="tpu_custom_call" | custom-call | flops 1000 | bytes 1000 | tf_op jit(solution)/shard_map/pallas_call | solution.py:169
  358.7 9.8 %shard_map.304 = (bf16[688,2048]{1,0:T(8,128)(2,1)S(1)}, bf16[688,2048]{1,0:T(8,128)(2,1)S(1)}, f32[344,1024]{1,0:T(8,128)S(1)}, bf16[344,1024]{1,0:T(8,128)(2,1)S(1)}) custom-call(bf16[688,1024]{1,0:T(8,128)(2,1)S(1)} %pad_maximum_fusion.4.rows_ref.left_ref, bf16[1024,2048]{1,0:T(8,128)(2,1)S(1)} %bitcast.306, f32[1,2048]{1,0:T(1,128)S(1)} %bitcast.353, ...), custom_call_target="tpu_custom_call" | custom-call | flops 1000 | bytes 1000 | tf_op jit(solution)/shard_map/pallas_call | solution.py:859
  374.3 8.8 %shard_map.305 = (bf16[688,2048]{1,0:T(8,128)(2,1)S(1)}, f32[1,2048]{1,0:T(1,128)S(1)}, f32[344,1024]{1,0:T(8,128)S(1)}, bf16[344,1024]{1,0:T(8,128)(2,1)S(1)}) custom-call(bf16[688,1024]{1,0:T(8,128)(2,1)S(1)} %pad_maximum_fusion.5.grad_ref.other_ref, bf16[2048,1024]{1,0:T(8,128)(2,1)S(1)} %bitcast.309, bf16[688,2048]{1,0:T(8,128)(2,1)S(1)} %get-tuple-element.240.slope_ref, ...), custom_call_target="tpu_custom_call" | custom-call | flops 1000 | bytes 1000 | tf_op jit(solution)/shard_map/pallas_call | solution.py:897
  384.3 10.4 %shard_map.306 = (bf16[4,2,1,128,1024]{4,3,2,1,0:T(8,128)(2,1)S(1)}, bf16[4,2,1,128,1024]{4,3,2,1,0:T(8,128)(2,1)}, bf16[4,1,2,128,1024]{4,3,2,1,0:T(8,128)(2,1)S(1)}, bf16[4,1,2,128,1024]{4,3,2,1,0:T(8,128)(2,1)}) custom-call(s32[2]{0:T(128)S(1)} %pad_add_fusion.2.where_ref, bf16[688,1024]{1,0:T(8,128)(2,1)S(1)} %pad_maximum_fusion.4.rows_ref.left_ref, ...), custom_call_target="tpu_custom_call" | custom-call | flops 1000 | bytes 1000 | tf_op jit(solution)/shard_map/pallas_call | solution.py:369
  396.6 6.6 collective-permute-done.40
  410.5 16.2 %shard_map.307 = (bf16[688,256]{1,0:T(8,128)(2,1)}, bf16[2,688,256]{2,1,0:T(8,128)(2,1)}, bf16[2,688,256]{2,1,0:T(8,128)(2,1)}) custom-call(bf16[688,1536]{1,0:T(8,128)(2,1)} %copy-done.59, bf16[688,1536]{1,0:T(8,128)(2,1)} %copy-done.59, bf16[688,1024]{1,0:T(8,128)(2,1)} %copy-done.63, bf16[688,1536]{1,0:T(8,128)(2,1)} %copy-done.59, ...), custom_call_target="tpu_custom_call" | custom-call | flops 1000 | bytes 1000 | tf_op jit(solution)/shard_map/pallas_call | solution.py:804
  426.8 16.5 %shard_map.308 = (bf16[688,256]{1,0:T(8,128)(2,1)}, bf16[2,688,256]{2,1,0:T(8,128)(2,1)}, bf16[2,688,256]{2,1,0:T(8,128)(2,1)}) custom-call(bf16[688,1536]{1,0:T(8,128)(2,1)} %copy-done.59, bf16[688,1536]{1,0:T(8,128)(2,1)} %copy-done.59, bf16[688,1024]{1,0:T(8,128)(2,1)} %copy-done.63, bf16[688,1536]{1,0:T(8,128)(2,1)} %copy-done.59, ...), custom_call_target="tpu_custom_call" | custom-call | flops 1000 | bytes 1000 | tf_op jit(solution)/shard_map/pallas_call | solution.py:804
  487.4 8.7 %shard_map.311 = (bf16[688,2048]{1,0:T(8,128)(2,1)S(1)}, f32[1,2048]{1,0:T(1,128)S(1)}, f32[344,1024]{1,0:T(8,128)S(1)}, bf16[344,1024]{1,0:T(8,128)(2,1)S(1)}) custom-call(bf16[688,1024]{1,0:T(8,128)(2,1)S(1)} %pad_maximum_fusion.7.grad_ref.other_ref, bf16[2048,1024]{1,0:T(8,128)(2,1)S(1)} %bitcast.305, bf16[688,2048]{1,0:T(8,128)(2,1)S(1)} %copy-done.22, ...), custom_call_target="tpu_custom_call" | custom-call | flops 1000 | bytes 1000 | tf_op jit(solution)/shard_map/pallas_call | solution.py:897
  497.4 10.4 %shard_map.313 = (bf16[4,2,1,128,1024]{4,3,2,1,0:T(8,128)(2,1)S(1)}, bf16[4,2,1,128,1024]{4,3,2,1,0:T(8,128)(2,1)}, bf16[4,1,2,128,1024]{4,3,2,1,0:T(8,128)(2,1)S(1)}, bf16[4,1,2,128,1024]{4,3,2,1,0:T(8,128)(2,1)}) custom-call(s32[2]{0:T(128)S(1)} %pad_add_fusion.2.where_ref, bf16[688,1024]{1,0:T(8,128)(2,1)S(1)} %constant_dynamic-update-slice_fusion.11.rows_ref.left_ref, ...), custom_call_target="tpu_custom_call" | custom-call | flops 1000 | bytes 1000 | tf_op jit(solution)/shard_map/pallas_call | solution.py:369
  509.4 8.7 %collective-permute-done.52.refs_1_ = bf16[4,2,1,64,1024]{4,3,2,1,0:T(8,128)(2,1)S(1)} collective-permute-done((bf16[4,2,1,64,1024]{4,3,2,1,0:T(8,128)(2,1)}, bf16[4,2,1,64,1024]{4,3,2,1,0:T(8,128)(2,1)S(1)}, u32[]{:S(2)}, u32[]{:S(2)}) %collective-permute-start.52) | collective-permute-done | bytes 1048608 | tf_op jit(solution)/shard_map/ppermute | solution.py:63
  537.7 16.4 %shard_map.315 = (bf16[688,256]{1,0:T(8,128)(2,1)}, bf16[2,688,256]{2,1,0:T(8,128)(2,1)}, bf16[2,688,256]{2,1,0:T(8,128)(2,1)}) custom-call(bf16[688,1536]{1,0:T(8,128)(2,1)} %copy-done.58, bf16[688,1536]{1,0:T(8,128)(2,1)} %copy-done.58, bf16[688,1024]{1,0:T(8,128)(2,1)} %collective-permute-done.14.refs_1_.refs_3_, bf16[688,1536]{1,0:T(8,128)(2,1)} %copy-done.58, ...), custom_call_target="tpu_custom_call" | custom-call | flops 1000 | bytes 1000 | tf_op jit(solution)/shard_map/pallas_call | solution.py:804
  560.0 16.6 %shard_map.317 = (bf16[688,256]{1,0:T(8,128)(2,1)}, bf16[2,688,256]{2,1,0:T(8,128)(2,1)}, bf16[2,688,256]{2,1,0:T(8,128)(2,1)}) custom-call(bf16[688,1536]{1,0:T(8,128)(2,1)} %copy-done.58, bf16[688,1536]{1,0:T(8,128)(2,1)} %copy-done.58, bf16[688,1024]{1,0:T(8,128)(2,1)} %collective-permute-done.14.refs_1_.refs_3_, bf16[688,1536]{1,0:T(8,128)(2,1)} %copy-done.58, ...), custom_call_target="tpu_custom_call" | custom-call | flops 1000 | bytes 1000 | tf_op jit(solution)/shard_map/pallas_call | solution.py:804
  592.5 9.4 %collective-permute-done.61 = bf16[2,688,256]{2,1,0:T(8,128)(2,1)S(1)} collective-permute-done((bf16[2,688,256]{2,1,0:T(8,128)(2,1)}, bf16[2,688,256]{2,1,0:T(8,128)(2,1)S(1)}, u32[]{:S(2)}, u32[]{:S(2)}) %collective-permute-start.61) | collective-permute-done | bytes 704544 | tf_op jit(solution)/shard_map/ppermute | solution.py:63
  633.1 8.4 %collective-permute-done.69 = bf16[4,1,2,64,1024]{4,3,2,0,1:T(8,128)(2,1)S(1)} collective-permute-done((bf16[4,1,2,64,1024]{4,3,2,0,1:T(8,128)(2,1)S(1)}, bf16[4,1,2,64,1024]{4,3,2,0,1:T(8,128)(2,1)S(1)}, u32[]{:S(2)}, u32[]{:S(2)}) %collective-permute-start.69) | collective-permute-done | bytes 1048608 | tf_op jit(solution)/shard_map/ppermute | solution.py:63
  645.8 7.3 collective-permute-done.85
  653.1 7.3 collective-permute-done.67
  682.8 17.4 %collective-permute-done.91 = bf16[1,1,128,2048]{3,2,1,0:T(8,128)(2,1)S(1)} collective-permute-done((bf16[1,1,128,2048]{3,2,1,0:T(8,128)(2,1)S(1)}, bf16[1,1,128,2048]{3,2,1,0:T(8,128)(2,1)S(1)}, u32[]{:S(2)}, u32[]{:S(2)}) %collective-permute-start.91) | collective-permute-done | bytes 524320 | tf_op jit(solution)/shard_map/ppermute | solution.py:63
  704.7 12.9 %collective-permute-done.78 = bf16[1,1,64,2048]{3,2,1,0:T(8,128)(2,1)S(1)} collective-permute-done((bf16[1,1,64,2048]{3,2,1,0:T(8,128)(2,1)S(1)}, bf16[1,1,64,2048]{3,2,1,0:T(8,128)(2,1)S(1)}, u32[]{:S(2)}, u32[]{:S(2)}) %collective-permute-start.78) | collective-permute-done | bytes 262176 | tf_op jit(solution)/shard_map/ppermute | solution.py:63
  740.1 14.6 %collective-permute-done.89 = bf16[192,2048]{1,0:T(8,128)(2,1)S(1)} collective-permute-done((bf16[192,2048]{1,0:T(8,128)(2,1)S(1)}, bf16[192,2048]{1,0:T(8,128)(2,1)S(1)}, u32[]{:S(2)}, u32[]{:S(2)}) %collective-permute-start.89) | collective-permute-done | bytes 786464 | tf_op jit(solution)/shard_map/ppermute | solution.py:63
  (818 shorter events, 345.2 us)
Async XLA Ops:
  27.0 40.9 %collective-permute-start.7 = (bf16[2,64,2048]{2,1,0:T(8,128)(2,1)S(1)}, bf16[2,64,2048]{2,1,0:T(8,128)(2,1)S(1)}, u32[]{:S(2)}, u32[]{:S(2)}) collective-permute-start(bf16[2,64,2048]{2,1,0:T(8,128)(2,1)S(1)} %get-tuple-element.197), channel_id=1, source_target_pairs={{0,2},{1,3},{2,0},{3,1},{4,6},{5,7},{6,4},{7,5},{8,10},{9,11},{10,... | collective-permute-start | bytes 1572872 | tf_op jit(solution)/shard_map/ppermute | solution.py:63
  107.1 30.9 %collective-permute-start.14 = (bf16[688,1024]{1,0:T(8,128)(2,1)S(1)}, bf16[688,1024]{1,0:T(8,128)(2,1)}, u32[]{:S(2)}, u32[]{:S(2)}) collective-permute-start(bf16[688,1024]{1,0:T(8,128)(2,1)S(1)} %slice.495), channel_id=1, source_target_pairs={{0,2},{1,3},{2,0},{3,1},{4,6},{5,7},{6,4},{7,5},{8,10},{9,11},{10,... | collective-permute-start | bytes 4227080 | tf_op jit(solution)/shard_map/ppermute | solution.py:63
  108.5 54.8 %collective-permute-start.20 = (bf16[4,128,2048]{2,1,0:T(8,128)(2,1)S(1)}, bf16[4,128,2048]{2,1,0:T(8,128)(2,1)S(1)}, u32[]{:S(2)}, u32[]{:S(2)}) collective-permute-start(bf16[4,128,2048]{2,1,0:T(8,128)(2,1)S(1)} %bitcast.310), channel_id=1, source_target_pairs={{0,8},{8,0},{16,24},{24,16},{1,9},{9,1},{17,25},{25,17},{2,10},{10... | collective-permute-start | bytes 6291464 | tf_op jit(solution)/shard_map/ppermute | solution.py:63
  110.2 53.2 %collective-permute-start.21 = (bf16[4,128,2048]{2,1,0:T(8,128)(2,1)S(1)}, bf16[4,128,2048]{2,1,0:T(8,128)(2,1)S(1)}, u32[]{:S(2)}, u32[]{:S(2)}) collective-permute-start(bf16[4,128,2048]{2,1,0:T(8,128)(2,1)S(1)} %bitcast.311), channel_id=1, source_target_pairs={{0,16},{8,24},{16,0},{24,8},{1,17},{9,25},{17,1},{25,9},{2,18},{10... | collective-permute-start | bytes 6291464 | tf_op jit(solution)/shard_map/ppermute | solution.py:63
  163.4 31.0 %collective-permute-start.23 = (bf16[4,64,2048]{2,1,0:T(8,128)(2,1)S(1)}, bf16[4,64,2048]{2,1,0:T(8,128)(2,1)S(1)}, u32[]{:S(2)}, u32[]{:S(2)}) collective-permute-start(bf16[4,64,2048]{2,1,0:T(8,128)(2,1)S(1)} %slice.509), channel_id=1, source_target_pairs={{0,16},{8,24},{16,0},{24,8},{1,17},{9,25},{17,1},{25,9},{2,18},{10... | collective-permute-start | bytes 3145736 | tf_op jit(solution)/shard_map/ppermute | solution.py:63
  165.1 30.3 %collective-permute-start.22 = (bf16[4,64,2048]{2,1,0:T(8,128)(2,1)S(1)}, bf16[4,64,2048]{2,1,0:T(8,128)(2,1)S(1)}, u32[]{:S(2)}, u32[]{:S(2)}) collective-permute-start(bf16[4,64,2048]{2,1,0:T(8,128)(2,1)S(1)} %slice.508), channel_id=1, source_target_pairs={{0,8},{8,0},{16,24},{24,16},{1,9},{9,1},{17,25},{25,17},{2,10},{10... | collective-permute-start | bytes 3145736 | tf_op jit(solution)/shard_map/ppermute | solution.py:63
  194.3 35.1 %collective-permute-start.26 = (bf16[2,128,2048]{2,1,0:T(8,128)(2,1)}, bf16[2,128,2048]{2,1,0:T(8,128)(2,1)}, u32[]{:S(2)}, u32[]{:S(2)}) collective-permute-start(bf16[2,128,2048]{2,1,0:T(8,128)(2,1)} %get-tuple-element.222), channel_id=1, source_target_pairs={{0,2},{1,3},{2,0},{3,1},{4,6},{5,7},{6,4},{7,5},{8,10},{9,11},{10,... | collective-permute-start | bytes 3145736 | tf_op jit(solution)/shard_map/ppermute | solution.py:63
  196.3 33.2 %collective-permute-start.24 = (bf16[4,64,2048]{2,1,0:T(8,128)(2,1)}, bf16[4,64,2048]{2,1,0:T(8,128)(2,1)}, u32[]{:S(2)}, u32[]{:S(2)}) collective-permute-start(bf16[4,64,2048]{2,1,0:T(8,128)(2,1)} %bitcast.65.refs_0_), channel_id=1, source_target_pairs={{0,8},{8,0},{16,24},{24,16},{1,9},{9,1},{17,25},{25,17},{2,10},{10... | collective-permute-start | bytes 3145736 | tf_op jit(solution)/shard_map/ppermute | solution.py:63
  197.8 31.7 %collective-permute-start.25 = (bf16[4,64,2048]{2,1,0:T(8,128)(2,1)}, bf16[4,64,2048]{2,1,0:T(8,128)(2,1)}, u32[]{:S(2)}, u32[]{:S(2)}) collective-permute-start(bf16[4,64,2048]{2,1,0:T(8,128)(2,1)} %bitcast.65.refs_0_), channel_id=1, source_target_pairs={{0,16},{8,24},{16,0},{24,8},{1,17},{9,25},{17,1},{25,9},{2,18},{10... | collective-permute-start | bytes 3145736 | tf_op jit(solution)/shard_map/ppermute | solution.py:63
  259.7 32.1 %collective-permute-start.31 = (bf16[688,1024]{1,0:T(8,128)(2,1)S(1)}, bf16[688,1024]{1,0:T(8,128)(2,1)S(1)}, u32[]{:S(2)}, u32[]{:S(2)}) collective-permute-start(bf16[688,1024]{1,0:T(8,128)(2,1)S(1)} %slice.521), channel_id=1, source_target_pairs={{0,2},{1,3},{2,0},{3,1},{4,6},{5,7},{6,4},{7,5},{8,10},{9,11},{10,... | collective-permute-start | bytes 4227080 | tf_op jit(solution)/shard_map/ppermute | solution.py:63
  263.3 53.3 %collective-permute-start.35 = (bf16[4,128,2048]{2,1,0:T(8,128)(2,1)S(1)}, bf16[4,128,2048]{2,1,0:T(8,128)(2,1)S(1)}, u32[]{:S(2)}, u32[]{:S(2)}) collective-permute-start(bf16[4,128,2048]{2,1,0:T(8,128)(2,1)S(1)} %bitcast.313), channel_id=1, source_target_pairs={{0,8},{8,0},{16,24},{24,16},{1,9},{9,1},{17,25},{25,17},{2,10},{10... | collective-permute-start | bytes 6291464 | tf_op jit(solution)/shard_map/ppermute | solution.py:63
  263.9 53.9 %collective-permute-start.36 = (bf16[4,128,2048]{2,1,0:T(8,128)(2,1)S(1)}, bf16[4,128,2048]{2,1,0:T(8,128)(2,1)S(1)}, u32[]{:S(2)}, u32[]{:S(2)}) collective-permute-start(bf16[4,128,2048]{2,1,0:T(8,128)(2,1)S(1)} %bitcast.314), channel_id=1, source_target_pairs={{0,16},{8,24},{16,0},{24,8},{1,17},{9,25},{17,1},{25,9},{2,18},{10... | collective-permute-start | bytes 6291464 | tf_op jit(solution)/shard_map/ppermute | solution.py:63
  324.7 32.5 %collective-permute-start.34 = (bf16[344,1024]{1,0:T(8,128)(2,1)}, bf16[344,1024]{1,0:T(8,128)(2,1)}, u32[]{:S(2)}, u32[]{:S(2)}) collective-permute-start(bf16[344,1024]{1,0:T(8,128)(2,1)} %add_convert_fusion.7), channel_id=1, source_target_pairs={{0,1},{1,0},{2,3},{3,2},{4,5},{5,4},{6,7},{7,6},{8,9},{9,8},{10,11... | collective-permute-start | bytes 2113544 | tf_op jit(solution)/shard_map/ppermute | solution.py:63
  396.0 49.3 %collective-permute-start.44 = (bf16[4,2,1,128,1024]{4,3,2,1,0:T(8,128)(2,1)}, bf16[4,2,1,128,1024]{4,3,2,1,0:T(8,128)(2,1)}, u32[]{:S(2)}, u32[]{:S(2)}) collective-permute-start(bf16[4,2,1,128,1024]{4,3,2,1,0:T(8,128)(2,1)} %get-tuple-element.244), channel_id=1, source_target_pairs={{0,8},{8,0},{16,24},{24,16},{1,9},{9,1},{17,25},{25,17},{2,10},{10... | collective-permute-start | bytes 6291464 | tf_op jit(solution)/shard_map/ppermute | solution.py:63
  403.2 47.9 %collective-permute-start.45 = (bf16[4,1,2,128,1024]{4,3,2,0,1:T(8,128)(2,1)}, bf16[4,1,2,128,1024]{4,3,2,0,1:T(8,128)(2,1)}, u32[]{:S(2)}, u32[]{:S(2)}) collective-permute-start(bf16[4,1,2,128,1024]{4,3,2,0,1:T(8,128)(2,1)} %bitcast.96), channel_id=1, source_target_pairs={{0,16},{8,24},{16,0},{24,8},{1,17},{9,25},{17,1},{25,9},{2,18},{10... | collective-permute-start | bytes 6291464 | tf_op jit(solution)/shard_map/ppermute | solution.py:63
  484.5 33.6 %collective-permute-start.52 = (bf16[4,2,1,64,1024]{4,3,2,1,0:T(8,128)(2,1)}, bf16[4,2,1,64,1024]{4,3,2,1,0:T(8,128)(2,1)S(1)}, u32[]{:S(2)}, u32[]{:S(2)}) collective-permute-start(bf16[4,2,1,64,1024]{4,3,2,1,0:T(8,128)(2,1)} %get-tuple-element.265), channel_id=1, source_target_pairs={{0,8},{8,0},{16,24},{24,16},{1,9},{9,1},{17,25},{25,17},{2,10},{10... | collective-permute-start | bytes 3145736 | tf_op jit(solution)/shard_map/ppermute | solution.py:63
  486.0 32.1 %collective-permute-start.53 = (bf16[4,1,2,64,1024]{4,3,2,0,1:T(8,128)(2,1)S(1)}, bf16[4,1,2,64,1024]{4,3,2,0,1:T(8,128)(2,1)S(1)}, u32[]{:S(2)}, u32[]{:S(2)}) collective-permute-start(bf16[4,1,2,64,1024]{4,3,2,0,1:T(8,128)(2,1)S(1)} %bitcast.364), channel_id=1, source_target_pairs={{0,16},{8,24},{16,0},{24,8},{1,17},{9,25},{17,1},{25,9},{2,18},{10... | collective-permute-start | bytes 3145736 | tf_op jit(solution)/shard_map/ppermute | solution.py:63
  507.9 77.0 %collective-permute-start.57 = (bf16[4,2,1,128,1024]{4,3,2,1,0:T(8,128)(2,1)}, bf16[4,2,1,128,1024]{4,3,2,1,0:T(8,128)(2,1)}, u32[]{:S(2)}, u32[]{:S(2)}) collective-permute-start(bf16[4,2,1,128,1024]{4,3,2,1,0:T(8,128)(2,1)} %get-tuple-element.280), channel_id=1, source_target_pairs={{0,8},{8,0},{16,24},{24,16},{1,9},{9,1},{17,25},{25,17},{2,10},{10... | collective-permute-start | bytes 6291464 | tf_op jit(solution)/shard_map/ppermute | solution.py:63
  520.3 64.6 %collective-permute-start.58 = (bf16[4,1,2,128,1024]{4,3,2,0,1:T(8,128)(2,1)}, bf16[4,1,2,128,1024]{4,3,2,0,1:T(8,128)(2,1)}, u32[]{:S(2)}, u32[]{:S(2)}) collective-permute-start(bf16[4,1,2,128,1024]{4,3,2,0,1:T(8,128)(2,1)} %bitcast.114), channel_id=1, source_target_pairs={{0,16},{8,24},{16,0},{24,8},{1,17},{9,25},{17,1},{25,9},{2,18},{10... | collective-permute-start | bytes 6291464 | tf_op jit(solution)/shard_map/ppermute | solution.py:63
  554.1 29.2 %collective-permute-start.59 = (bf16[2,688,256]{2,1,0:T(8,128)(2,1)}, bf16[2,688,256]{2,1,0:T(8,128)(2,1)}, u32[]{:S(2)}, u32[]{:S(2)}) collective-permute-start(bf16[2,688,256]{2,1,0:T(8,128)(2,1)} %get-tuple-element.308), channel_id=1, source_target_pairs={{0,2},{1,3},{2,0},{3,1},{4,6},{5,7},{6,4},{7,5},{8,10},{9,11},{10,... | collective-permute-start | bytes 2113544 | tf_op jit(solution)/shard_map/ppermute | solution.py:63
  559.5 51.6 %collective-permute-start.63 = (bf16[4,1,64,1024]{3,2,1,0:T(8,128)(2,1)}, bf16[4,1,64,1024]{3,2,1,0:T(8,128)(2,1)}, u32[]{:S(2)}, u32[]{:S(2)}) collective-permute-start(bf16[4,1,64,1024]{3,2,1,0:T(8,128)(2,1)} %get-tuple-element.289), channel_id=1, source_target_pairs={{0,8},{8,0},{16,24},{24,16},{1,9},{9,1},{17,25},{25,17},{2,10},{10... | collective-permute-start | bytes 1572872 | tf_op jit(solution)/shard_map/ppermute | solution.py:63
  589.4 31.3 %collective-permute-start.64 = (bf16[4,1,128,1024]{3,2,1,0:T(8,128)(2,1)S(1)}, bf16[4,1,128,1024]{3,2,1,0:T(8,128)(2,1)S(1)}, u32[]{:S(2)}, u32[]{:S(2)}) collective-permute-start(bf16[4,1,128,1024]{3,2,1,0:T(8,128)(2,1)S(1)} %get-tuple-element.304), channel_id=1, source_target_pairs={{0,16},{8,24},{16,0},{24,8},{1,17},{9,25},{17,1},{25,9},{2,18},{10... | collective-permute-start | bytes 3145736 | tf_op jit(solution)/shard_map/ppermute | solution.py:63
  612.7 28.8 %collective-permute-start.68 = (bf16[4,2,1,64,1024]{4,3,2,1,0:T(8,128)(2,1)S(1)}, bf16[4,2,1,64,1024]{4,3,2,1,0:T(8,128)(2,1)S(1)}, u32[]{:S(2)}, u32[]{:S(2)}) collective-permute-start(bf16[4,2,1,64,1024]{4,3,2,1,0:T(8,128)(2,1)S(1)} %get-tuple-element.313), channel_id=1, source_target_pairs={{0,8},{8,0},{16,24},{24,16},{1,9},{9,1},{17,25},{25,17},{2,10},{10... | collective-permute-start | bytes 3145736 | tf_op jit(solution)/shard_map/ppermute | solution.py:63
  622.2 51.7 %collective-permute-start.90 = (bf16[2,128,2048]{2,1,0:T(8,128)(2,1)}, bf16[2,128,2048]{2,1,0:T(8,128)(2,1)S(1)}, u32[]{:S(2)}, u32[]{:S(2)}) collective-permute-start(bf16[2,128,2048]{2,1,0:T(8,128)(2,1)} %get-tuple-element.326), channel_id=1, source_target_pairs={{0,2},{1,3},{2,0},{3,1},{4,6},{5,7},{6,4},{7,5},{8,10},{9,11},{10,... | collective-permute-start | bytes 3145736 | tf_op jit(solution)/shard_map/ppermute | solution.py:63
  628.5 31.9 %collective-permute-start.67 = (bf16[172,1024]{1,0:T(8,128)(2,1)S(1)}, bf16[172,1024]{1,0:T(8,128)(2,1)S(1)}, u32[]{:S(2)}, u32[]{:S(2)}) collective-permute-start(bf16[172,1024]{1,0:T(8,128)(2,1)S(1)} %slice.655), channel_id=1, source_target_pairs={{0,4},{1,5},{2,6},{3,7},{4,0},{5,1},{6,2},{7,3},{8,12},{9,13},{10,... | collective-permute-start | bytes 1056776 | tf_op jit(solution)/shard_map/ppermute | solution.py:63
  676.7 44.7 %collective-permute-start.88 = (bf16[192,2048]{1,0:T(8,128)(2,1)S(1)}, bf16[192,2048]{1,0:T(8,128)(2,1)S(1)}, u32[]{:S(2)}, u32[]{:S(2)}) collective-permute-start(bf16[192,2048]{1,0:T(8,128)(2,1)S(1)} %maximum_maximum_fusion), channel_id=1, source_target_pairs={{0,16},{8,24},{16,0},{24,8},{1,17},{9,25},{17,1},{25,9},{2,18},{10... | collective-permute-start | bytes 2359304 | tf_op jit(solution)/shard_map/ppermute | solution.py:63
  678.3 48.0 %collective-permute-start.87 = (bf16[192,2048]{1,0:T(8,128)(2,1)S(1)}, bf16[192,2048]{1,0:T(8,128)(2,1)S(1)}, u32[]{:S(2)}, u32[]{:S(2)}) collective-permute-start(bf16[192,2048]{1,0:T(8,128)(2,1)S(1)} %maximum_maximum_fusion), channel_id=1, source_target_pairs={{0,8},{8,0},{16,24},{24,16},{1,9},{9,1},{17,25},{25,17},{2,10},{10... | collective-permute-start | bytes 2359304 | tf_op jit(solution)/shard_map/ppermute | solution.py:63
  681.2 39.5 %collective-permute-start.75 = (f32[2,1,1792]{2,0,1:T(2,128)S(1)}, f32[2,1,1792]{2,0,1:T(2,128)S(1)}, u32[]{:S(2)}, u32[]{:S(2)}) collective-permute-start(f32[2,1,1792]{2,0,1:T(2,128)S(1)} %dynamic-slice_add_fusion), channel_id=1, source_target_pairs={{0,8},{8,0},{16,24},{24,16},{1,9},{9,1},{17,25},{25,17},{2,10},{10... | collective-permute-start | bytes 43016 | tf_op jit(solution)/shard_map/ppermute | solution.py:63
  721.4 33.4 %collective-permute-start.89 = (bf16[192,2048]{1,0:T(8,128)(2,1)S(1)}, bf16[192,2048]{1,0:T(8,128)(2,1)S(1)}, u32[]{:S(2)}, u32[]{:S(2)}) collective-permute-start(bf16[192,2048]{1,0:T(8,128)(2,1)S(1)} %collective-permute-done.88), channel_id=1, source_target_pairs={{0,8},{8,0},{16,24},{24,16},{1,9},{9,1},{17,25},{25,17},{2,10},{10... | collective-permute-start | bytes 2359304 | tf_op jit(solution)/shard_map/ppermute | solution.py:63
  724.7 38.3 %collective-permute-start.94 = (bf16[128,2048]{1,0:T(8,128)(2,1)S(1)}, bf16[128,2048]{1,0:T(8,128)(2,1)S(1)}, u32[]{:S(2)}, u32[]{:S(2)}) collective-permute-start(bf16[128,2048]{1,0:T(8,128)(2,1)S(1)} %pad_maximum_fusion.17.refs_0_), channel_id=1, source_target_pairs={{0,16},{8,24},{16,0},{24,8},{1,17},{9,25},{17,1},{25,9},{2,18},{10... | collective-permute-start | bytes 1572872 | tf_op jit(solution)/shard_map/ppermute | solution.py:63
  726.3 34.2 %collective-permute-start.81 = (bf16[64,2048]{1,0:T(8,128)(2,1)S(1)}, bf16[64,2048]{1,0:T(8,128)(2,1)S(1)}, u32[]{:S(2)}, u32[]{:S(2)}) collective-permute-start(bf16[64,2048]{1,0:T(8,128)(2,1)S(1)} %pad_maximum_fusion.18.refs_0_), channel_id=1, source_target_pairs={{0,16},{8,24},{16,0},{24,8},{1,17},{9,25},{17,1},{25,9},{2,18},{10... | collective-permute-start | bytes 786440 | tf_op jit(solution)/shard_map/ppermute | solution.py:63
  732.7 30.3 %collective-permute-start.95 = (bf16[128,2048]{1,0:T(8,128)(2,1)S(1)}, bf16[128,2048]{1,0:T(8,128)(2,1)S(1)}, u32[]{:S(2)}, u32[]{:S(2)}) collective-permute-start(bf16[128,2048]{1,0:T(8,128)(2,1)S(1)} %collective-permute-done.93.refs_1_), channel_id=1, source_target_pairs={{0,16},{8,24},{16,0},{24,8},{1,17},{9,25},{17,1},{25,9},{2,18},{10... | collective-permute-start | bytes 1572872 | tf_op jit(solution)/shard_map/ppermute | solution.py:63
  (261 other events, 2366.9 us)

commit v9 on v7

--- a/solution.py
+++ b/solution.py
@@ -295,7 +295,7 @@
             jnp.moveaxis(whole[:, :, start : start + size], 0, 1).reshape(LAYERS, -1)
         )
         start += size
-    return vectors, got
+    return vectors
 
 
 def link_orders():
@@ -1097,12 +1097,12 @@
         d_attended = later.sent(d_attended, old[2])
     second_query, d_own, d_others = back(pairs // 2)
     d_others = after(d_others, first_got)
+    if old:
+        d_others = later.came(d_others, old[2])
     second_kv, second_got = collect_rows(d_own, d_others)
     second_query = later.came(second_query, block)
     later.step(block, second_query)
     second_query = later.sent(second_query, block)
-    if old:
-        second_query = later.came(second_query, old[1])
     d_query = jnp.concatenate([first_query, second_query], 1)
     d_key = jnp.concatenate([first_kv[0], second_kv[0]], 1)
     d_value = jnp.concatenate([first_kv[1], second_kv[1]], 1)
@@ -1114,6 +1114,7 @@
     d_projected = later.sent(d_projected, mixed)
     if old:
         later.join(old[3], [old[1]], d_projected)
+        d_projected = later.sent(d_projected, old[3])
         later.join(block_planes, [block], d_projected)
         d_projected = later.sent(d_projected, block_planes)
     d_normed = input_dot(d_projected[:tokens], heads_weight) + widen(got)
@@ -1140,12 +1141,12 @@
 def local(images, cotangent, *all_params):
     owners, count = lax.axis_size("fsdp"), lax.axis_size("rep")
     pieces = message_pieces(all_params)
-    small, small_got = gather_small(all_params, pieces[0])
-    column, planes = gather_planes(pieces[0], beside=[small_got])
+    column, planes = gather_planes(pieces[0])
     own, got = regroup(after(images, planes[0]))
     tok_rows = widen(jnp.concatenate([own, got], 0))
     column = after(column, got)
     next_column, next_planes = gather_planes(pieces[1], got)
+    small = gather_small(all_params, got)
     held, neighbours = gather_neighbours(column, [])
     saved_layers, fetched = [], []
     for layer in range(LAYERS):

time: 790 us -> 778 us (0.985)
  starting transfers between devices: 93.1 us -> 83.9 us
    ppermute x96, starting transfers between devices: 93.1 us -> 83.9 us  [swap(): return lax.ppermute(tensor, axis, [(i, i ^ offset) for i in range(count)])]
    unnamed x433 -> x423, local copies, waits for them, and re-layouts: 46.2 us -> 41.2 us
  transfers between devices with their start and end apart: 96 -> 96, of which waited for: 40 -> 44; matrix products, arithmetic and copies ran while one was open for 11% -> 12% of each run, Pallas kernels for 26% -> 26%
where the time goes in v9:
time: 778 us; the launch traced here: 768 us
  waiting for transfers between devices  314 us (40%)
  Pallas kernels  228 us (29%)
  starting transfers between devices  83.9 us (11%)
  local copies, waits for them, and re-layouts  64.6 us (8%)
  other arithmetic  46.8 us (6%)
  matrix products  26.4 us (3%)
    ppermute x96, waiting for transfers between devices, swap(): return lax.ppermute(tensor, axis, [(i, i ^ offset) for i in range(count)])  314 us
    ppermute x96, starting transfers between devices, swap(): return lax.ppermute(tensor, axis, [(i, i ^ offset) for i in range(count)])  83.9 us
    pallas_call x4, Pallas kernels, attend_back(): pl.pallas_call(functools.partial(attend_back_kernel, scale * math.log2(ma...  65.7 us
    unnamed x423, local copies, waits for them, and re-layouts  41.2 us
    pallas_call x2, Pallas kernels, attend(): pl.pallas_call(functools.partial(attend_kernel, factor, len(parts)), out_...  36.8 us
    pallas_call x4, Pallas kernels, grad_call(): pl.pallas_call(functools.partial(kernel, shapes), out_shape=out_shapes, g...  32 us
    pallas_call x4, Pallas kernels, place(): pl.pallas_call(functools.partial(place_kernel, pieces[0].shape[1] // 2, b...  23.2 us
    pallas_call x2, Pallas kernels, feed_forward(): pl.pallas_call(expand_kernel, out_shape=[jax.ShapeDtypeStruct((tokens, un...  19.6 us
  transfers between devices with their start and end apart: 96, of which 44 were waited for; matrix products, arithmetic and copies ran while one was open for 12% of the time, Pallas kernels for 26%

profile of v9, /device:TPU:0, one launch (start us, length us, event | category | flops | bytes accessed | tf_op | source)
XLA Modules:
  0.0 767.9 jit_solution(16112058402045924750)
XLA Ops:
  14.0 12.5 %collective-permute-done.1 = bf16[1,64,2048]{2,1,0:T(8,128)(2,1)S(1)} collective-permute-done((bf16[1,64,2048]{2,1,0:T(8,128)(2,1)S(1)}, bf16[1,64,2048]{2,1,0:T(8,128)(2,1)S(1)}, u32[]{:S(2)}, u32[]{:S(2)}) %collective-permute-start.1) | collective-permute-done | bytes 262176 | tf_op jit(solution)/shard_map/ppermute | solution.py:63
  31.2 14.6 %collective-permute-done.2 = bf16[172,1024]{1,0:T(8,128)(2,1)S(1)} collective-permute-done((bf16[172,1024]{1,0:T(8,128)(2,1)S(1)}, bf16[172,1024]{1,0:T(8,128)(2,1)S(1)}, u32[]{:S(2)}, u32[]{:S(2)}) %collective-permute-start.2) | collective-permute-done | bytes 352288 | tf_op jit(solution)/shard_map/ppermute | solution.py:63
  53.9 13.3 %collective-permute-done.5 = bf16[4,2,1792]{2,1,0:T(2,128)(2,1)S(1)} collective-permute-done((bf16[4,2,1792]{2,1,0:T(2,128)(2,1)S(1)}, bf16[4,2,1792]{2,1,0:T(2,128)(2,1)S(1)}, u32[]{:S(2)}, u32[]{:S(2)}) %collective-permute-start.5) | collective-permute-done | bytes 28704 | tf_op jit(solution)/shard_map/ppermute | solution.py:63
  89.9 11.4 %collective-permute-done.9 = bf16[2,128,2048]{2,1,0:T(8,128)(2,1)S(1)} collective-permute-done((bf16[2,128,2048]{2,1,0:T(8,128)(2,1)S(1)}, bf16[2,128,2048]{2,1,0:T(8,128)(2,1)S(1)}, u32[]{:S(2)}, u32[]{:S(2)}) %collective-permute-start.9) | collective-permute-done | bytes 1048608 | tf_op jit(solution)/shard_map/ppermute | solution.py:63
  112.6 25.5 %collective-permute-done.14.refs_1_.refs_3_ = bf16[688,1024]{1,0:T(8,128)(2,1)} collective-permute-done((bf16[688,1024]{1,0:T(8,128)(2,1)S(1)}, bf16[688,1024]{1,0:T(8,128)(2,1)}, u32[]{:S(2)}, u32[]{:S(2)}) %collective-permute-start.14) | collective-permute-done | bytes 1409056 | tf_op jit(solution)/shard_map/ppermute | solution.py:63
  140.5 18.3 %shard_map.298 = (bf16[688,512]{1,0:T(8,128)(2,1)}, f32[688,512]{1,0:T(8,128)}) custom-call(bf16[688,1536]{1,0:T(8,128)(2,1)} %copy-done.62, bf16[688,1536]{1,0:T(8,128)(2,1)} %copy-done.62, bf16[688,1024]{1,0:T(8,128)(2,1)} %collective-permute-done.14.refs_1_.refs_3_, bf16[688,1536]{1,0:T(8,128)(2,1)} %copy-done.62, ...), custom_call_target="tpu_custom_call" | custom-call | flops 1000 | bytes 1000 | tf_op jit(solution)/shard_map/pallas_call | solution.py:760
  177.9 15.0 %collective-permute-done.18 = bf16[1,128,2048]{2,1,0:T(8,128)(2,1)S(1)} collective-permute-done((bf16[1,128,2048]{2,1,0:T(8,128)(2,1)S(1)}, bf16[1,128,2048]{2,1,0:T(8,128)(2,1)S(1)}, u32[]{:S(2)}, u32[]{:S(2)}) %collective-permute-start.18) | collective-permute-done | bytes 524320 | tf_op jit(solution)/shard_map/ppermute | solution.py:63
  208.1 8.1 %shard_map.299 = (bf16[4,2,4,32,2048]{4,3,2,1,0:T(8,128)(2,1)S(1)}, bf16[4,4,2,64,1024]{4,3,2,1,0:T(8,128)(2,1)S(1)}) custom-call(s32[2]{0:T(128)S(1)} %pad_add_fusion.1.where_ref, bf16[4,128,2048]{2,1,0:T(8,128)(2,1)S(1)} %bitcast.312, bf16[4,128,2048]{2,1,0:T(8,128)(2,1)S(1)} %copy-done.7, bf16[4,128,2048]{2,1,0:T(8,128)(2,1)S(1)} %copy-done.9, ...), custom_call_target="tpu_custom_call" | custom-call | flops 1000 | bytes 1000 | tf_op jit(solution)/shard_map/pallas_call | solution.py:169
  218.0 9.8 %shard_map.300 = (bf16[688,2048]{1,0:T(8,128)(2,1)S(1)}, bf16[688,2048]{1,0:T(8,128)(2,1)S(1)}, f32[344,1024]{1,0:T(8,128)S(1)}, bf16[344,1024]{1,0:T(8,128)(2,1)S(1)}) custom-call(bf16[688,1024]{1,0:T(8,128)(2,1)S(1)} %constant_dynamic-update-slice_fusion.11.rows_ref.left_ref, bf16[1024,2048]{1,0:T(8,128)(2,1)S(1)} %bitcast.302, f32[1,2048]{1,0:T(1,128)S(1)} %bitcast.354, ...), custom_call_target="tpu_custom_call" | custom-call | flops 1000 | bytes 1000 | tf_op jit(solution)/shard_map/pallas_call | solution.py:859
  237.9 11.8 %collective-permute-done.30.refs_4_ = bf16[4,32,2048]{2,1,0:T(8,128)(2,1)S(1)} collective-permute-done((bf16[4,32,2048]{2,1,0:T(8,128)(2,1)S(1)}, bf16[4,32,2048]{2,1,0:T(8,128)(2,1)S(1)}, u32[]{:S(2)}, u32[]{:S(2)}) %collective-permute-start.30) | collective-permute-done | bytes 524320 | tf_op jit(solution)/shard_map/ppermute | solution.py:63
  265.5 26.4 %collective-permute-done.31.refs_1_.refs_3_ = bf16[688,1024]{1,0:T(8,128)(2,1)S(1)} collective-permute-done((bf16[688,1024]{1,0:T(8,128)(2,1)S(1)}, bf16[688,1024]{1,0:T(8,128)(2,1)S(1)}, u32[]{:S(2)}, u32[]{:S(2)}) %collective-permute-start.31) | collective-permute-done | bytes 1409056 | tf_op jit(solution)/shard_map/ppermute | solution.py:63
  296.1 18.5 %shard_map.302 = (bf16[688,512]{1,0:T(8,128)(2,1)}, f32[688,512]{1,0:T(8,128)}) custom-call(bf16[688,1536]{1,0:T(8,128)(2,1)} %copy-done.63, bf16[688,1536]{1,0:T(8,128)(2,1)} %copy-done.63, bf16[688,1024]{1,0:T(8,128)(2,1)} %copy-done.67, bf16[688,1536]{1,0:T(8,128)(2,1)} %copy-done.63, bf16[688,1024]{1,0:T(8,128)(2,1)} %copy-done.67), custom_call_target="tpu_custom_call" | custom-call | flops 1000 | bytes 1000 | tf_op jit(solution)/shard_map/pallas_call | solution.py:760
  326.2 17.6 %collective-permute-done.38.refs_4_ = bf16[4,64,2048]{2,1,0:T(8,128)(2,1)} collective-permute-done((bf16[4,64,2048]{2,1,0:T(8,128)(2,1)}, bf16[4,64,2048]{2,1,0:T(8,128)(2,1)}, u32[]{:S(2)}, u32[]{:S(2)}) %collective-permute-start.38) | collective-permute-done | bytes 1048608 | tf_op jit(solution)/shard_map/ppermute | solution.py:63
  349.3 8.0 %shard_map.303 = (bf16[4,2,4,32,2048]{4,3,2,1,0:T(8,128)(2,1)S(1)}, bf16[4,4,2,64,1024]{4,3,2,1,0:T(8,128)(2,1)S(1)}) custom-call(s32[2]{0:T(128)S(1)} %pad_add_fusion.1.where_ref, bf16[4,128,2048]{2,1,0:T(8,128)(2,1)S(1)} %bitcast.315, bf16[4,128,2048]{2,1,0:T(8,128)(2,1)S(1)} %copy-done.11, bf16[4,128,2048]{2,1,0:T(8,128)(2,1)S(1)} %copy-done.13, ...), custom_call_target="tpu_custom_call" | custom-call | flops 1000 | bytes 1000 | tf_op jit(solution)/shard_map/pallas_call | solution.py:169
  358.8 9.8 %shard_map.304 = (bf16[688,2048]{1,0:T(8,128)(2,1)S(1)}, bf16[688,2048]{1,0:T(8,128)(2,1)S(1)}, f32[344,1024]{1,0:T(8,128)S(1)}, bf16[344,1024]{1,0:T(8,128)(2,1)S(1)}) custom-call(bf16[688,1024]{1,0:T(8,128)(2,1)S(1)} %pad_maximum_fusion.4.rows_ref.left_ref, bf16[1024,2048]{1,0:T(8,128)(2,1)S(1)} %bitcast.306, f32[1,2048]{1,0:T(1,128)S(1)} %bitcast.353, ...), custom_call_target="tpu_custom_call" | custom-call | flops 1000 | bytes 1000 | tf_op jit(solution)/shard_map/pallas_call | solution.py:859
  374.3 8.8 %shard_map.305 = (bf16[688,2048]{1,0:T(8,128)(2,1)S(1)}, f32[1,2048]{1,0:T(1,128)S(1)}, f32[344,1024]{1,0:T(8,128)S(1)}, bf16[344,1024]{1,0:T(8,128)(2,1)S(1)}) custom-call(bf16[688,1024]{1,0:T(8,128)(2,1)S(1)} %pad_maximum_fusion.5.grad_ref.other_ref, bf16[2048,1024]{1,0:T(8,128)(2,1)S(1)} %bitcast.309, bf16[688,2048]{1,0:T(8,128)(2,1)S(1)} %get-tuple-element.240.slope_ref, ...), custom_call_target="tpu_custom_call" | custom-call | flops 1000 | bytes 1000 | tf_op jit(solution)/shard_map/pallas_call | solution.py:897
  384.3 10.4 %shard_map.306 = (bf16[4,2,1,128,1024]{4,3,2,1,0:T(8,128)(2,1)S(1)}, bf16[4,2,1,128,1024]{4,3,2,1,0:T(8,128)(2,1)}, bf16[4,1,2,128,1024]{4,3,2,1,0:T(8,128)(2,1)S(1)}, bf16[4,1,2,128,1024]{4,3,2,1,0:T(8,128)(2,1)}) custom-call(s32[2]{0:T(128)S(1)} %pad_add_fusion.2.where_ref, bf16[688,1024]{1,0:T(8,128)(2,1)S(1)} %pad_maximum_fusion.4.rows_ref.left_ref, ...), custom_call_target="tpu_custom_call" | custom-call | flops 1000 | bytes 1000 | tf_op jit(solution)/shard_map/pallas_call | solution.py:369
  410.6 16.2 %shard_map.307 = (bf16[688,256]{1,0:T(8,128)(2,1)}, bf16[2,688,256]{2,1,0:T(8,128)(2,1)}, bf16[2,688,256]{2,1,0:T(8,128)(2,1)}) custom-call(bf16[688,1536]{1,0:T(8,128)(2,1)} %copy-done.63, bf16[688,1536]{1,0:T(8,128)(2,1)} %copy-done.63, bf16[688,1024]{1,0:T(8,128)(2,1)} %copy-done.67, bf16[688,1536]{1,0:T(8,128)(2,1)} %copy-done.63, ...), custom_call_target="tpu_custom_call" | custom-call | flops 1000 | bytes 1000 | tf_op jit(solution)/shard_map/pallas_call | solution.py:804
  426.9 16.5 %shard_map.308 = (bf16[688,256]{1,0:T(8,128)(2,1)}, bf16[2,688,256]{2,1,0:T(8,128)(2,1)}, bf16[2,688,256]{2,1,0:T(8,128)(2,1)}) custom-call(bf16[688,1536]{1,0:T(8,128)(2,1)} %copy-done.63, bf16[688,1536]{1,0:T(8,128)(2,1)} %copy-done.63, bf16[688,1024]{1,0:T(8,128)(2,1)} %copy-done.67, bf16[688,1536]{1,0:T(8,128)(2,1)} %copy-done.63, ...), custom_call_target="tpu_custom_call" | custom-call | flops 1000 | bytes 1000 | tf_op jit(solution)/shard_map/pallas_call | solution.py:804
  487.5 8.7 %shard_map.311 = (bf16[688,2048]{1,0:T(8,128)(2,1)S(1)}, f32[1,2048]{1,0:T(1,128)S(1)}, f32[344,1024]{1,0:T(8,128)S(1)}, bf16[344,1024]{1,0:T(8,128)(2,1)S(1)}) custom-call(bf16[688,1024]{1,0:T(8,128)(2,1)S(1)} %pad_maximum_fusion.7.grad_ref.other_ref, bf16[2048,1024]{1,0:T(8,128)(2,1)S(1)} %bitcast.305, bf16[688,2048]{1,0:T(8,128)(2,1)S(1)} %copy-done.22, ...), custom_call_target="tpu_custom_call" | custom-call | flops 1000 | bytes 1000 | tf_op jit(solution)/shard_map/pallas_call | solution.py:897
  497.5 10.4 %shard_map.313 = (bf16[4,2,1,128,1024]{4,3,2,1,0:T(8,128)(2,1)S(1)}, bf16[4,2,1,128,1024]{4,3,2,1,0:T(8,128)(2,1)}, bf16[4,1,2,128,1024]{4,3,2,1,0:T(8,128)(2,1)S(1)}, bf16[4,1,2,128,1024]{4,3,2,1,0:T(8,128)(2,1)}) custom-call(s32[2]{0:T(128)S(1)} %pad_add_fusion.2.where_ref, bf16[688,1024]{1,0:T(8,128)(2,1)S(1)} %constant_dynamic-update-slice_fusion.11.rows_ref.left_ref, ...), custom_call_target="tpu_custom_call" | custom-call | flops 1000 | bytes 1000 | tf_op jit(solution)/shard_map/pallas_call | solution.py:369
  509.5 8.7 %collective-permute-done.52.refs_1_ = bf16[4,2,1,64,1024]{4,3,2,1,0:T(8,128)(2,1)S(1)} collective-permute-done((bf16[4,2,1,64,1024]{4,3,2,1,0:T(8,128)(2,1)}, bf16[4,2,1,64,1024]{4,3,2,1,0:T(8,128)(2,1)S(1)}, u32[]{:S(2)}, u32[]{:S(2)}) %collective-permute-start.52) | collective-permute-done | bytes 1048608 | tf_op jit(solution)/shard_map/ppermute | solution.py:63
  537.8 16.4 %shard_map.315 = (bf16[688,256]{1,0:T(8,128)(2,1)}, bf16[2,688,256]{2,1,0:T(8,128)(2,1)}, bf16[2,688,256]{2,1,0:T(8,128)(2,1)}) custom-call(bf16[688,1536]{1,0:T(8,128)(2,1)} %copy-done.62, bf16[688,1536]{1,0:T(8,128)(2,1)} %copy-done.62, bf16[688,1024]{1,0:T(8,128)(2,1)} %collective-permute-done.14.refs_1_.refs_3_, bf16[688,1536]{1,0:T(8,128)(2,1)} %copy-done.62, ...), custom_call_target="tpu_custom_call" | custom-call | flops 1000 | bytes 1000 | tf_op jit(solution)/shard_map/pallas_call | solution.py:804
  560.1 16.6 %shard_map.317 = (bf16[688,256]{1,0:T(8,128)(2,1)}, bf16[2,688,256]{2,1,0:T(8,128)(2,1)}, bf16[2,688,256]{2,1,0:T(8,128)(2,1)}) custom-call(bf16[688,1536]{1,0:T(8,128)(2,1)} %copy-done.62, bf16[688,1536]{1,0:T(8,128)(2,1)} %copy-done.62, bf16[688,1024]{1,0:T(8,128)(2,1)} %collective-permute-done.14.refs_1_.refs_3_, bf16[688,1536]{1,0:T(8,128)(2,1)} %copy-done.62, ...), custom_call_target="tpu_custom_call" | custom-call | flops 1000 | bytes 1000 | tf_op jit(solution)/shard_map/pallas_call | solution.py:804
  592.6 9.4 %collective-permute-done.61 = bf16[2,688,256]{2,1,0:T(8,128)(2,1)S(1)} collective-permute-done((bf16[2,688,256]{2,1,0:T(8,128)(2,1)}, bf16[2,688,256]{2,1,0:T(8,128)(2,1)S(1)}, u32[]{:S(2)}, u32[]{:S(2)}) %collective-permute-start.61) | collective-permute-done | bytes 704544 | tf_op jit(solution)/shard_map/ppermute | solution.py:63
  632.6 9.0 %collective-permute-done.69 = bf16[4,1,2,64,1024]{4,3,2,0,1:T(8,128)(2,1)S(1)} collective-permute-done((bf16[4,1,2,64,1024]{4,3,2,0,1:T(8,128)(2,1)S(1)}, bf16[4,1,2,64,1024]{4,3,2,0,1:T(8,128)(2,1)S(1)}, u32[]{:S(2)}, u32[]{:S(2)}) %collective-permute-start.69) | collective-permute-done | bytes 1048608 | tf_op jit(solution)/shard_map/ppermute | solution.py:63
  646.4 7.4 collective-permute-done.81
  654.5 10.1 %collective-permute-done.67 = bf16[172,1024]{1,0:T(8,128)(2,1)S(1)} collective-permute-done((bf16[172,1024]{1,0:T(8,128)(2,1)S(1)}, bf16[172,1024]{1,0:T(8,128)(2,1)S(1)}, u32[]{:S(2)}, u32[]{:S(2)}) %collective-permute-start.67) | collective-permute-done | bytes 352288 | tf_op jit(solution)/shard_map/ppermute | solution.py:63
  688.2 18.2 %collective-permute-done.87 = bf16[1,1,128,2048]{3,2,1,0:T(8,128)(2,1)S(1)} collective-permute-done((bf16[1,1,128,2048]{3,2,1,0:T(8,128)(2,1)S(1)}, bf16[1,1,128,2048]{3,2,1,0:T(8,128)(2,1)S(1)}, u32[]{:S(2)}, u32[]{:S(2)}) %collective-permute-start.87) | collective-permute-done | bytes 524320 | tf_op jit(solution)/shard_map/ppermute | solution.py:63
  708.5 12.6 %collective-permute-done.78 = bf16[1,1,64,2048]{3,2,1,0:T(8,128)(2,1)S(1)} collective-permute-done((bf16[1,1,64,2048]{3,2,1,0:T(8,128)(2,1)S(1)}, bf16[1,1,64,2048]{3,2,1,0:T(8,128)(2,1)S(1)}, u32[]{:S(2)}, u32[]{:S(2)}) %collective-permute-start.78) | collective-permute-done | bytes 262176 | tf_op jit(solution)/shard_map/ppermute | solution.py:63
  738.8 8.6 %collective-permute-done.83 = bf16[128,2048]{1,0:T(8,128)(2,1)S(1)} collective-permute-done((bf16[128,2048]{1,0:T(8,128)(2,1)S(1)}, bf16[128,2048]{1,0:T(8,128)(2,1)S(1)}, u32[]{:S(2)}, u32[]{:S(2)}) %collective-permute-start.83) | collective-permute-done | bytes 524320 | tf_op jit(solution)/shard_map/ppermute | solution.py:63
  748.8 10.4 %collective-permute-done.91.refs_3_ = bf16[128,2048]{1,0:T(8,128)(2,1)S(1)} collective-permute-done((bf16[128,2048]{1,0:T(8,128)(2,1)S(1)}, bf16[128,2048]{1,0:T(8,128)(2,1)S(1)}, u32[]{:S(2)}, u32[]{:S(2)}) %collective-permute-start.91) | collective-permute-done | bytes 524320 | tf_op jit(solution)/shard_map/ppermute | solution.py:63
  (822 shorter events, 344.7 us)
Async XLA Ops:
  27.1 40.9 %collective-permute-start.7 = (bf16[2,64,2048]{2,1,0:T(8,128)(2,1)S(1)}, bf16[2,64,2048]{2,1,0:T(8,128)(2,1)S(1)}, u32[]{:S(2)}, u32[]{:S(2)}) collective-permute-start(bf16[2,64,2048]{2,1,0:T(8,128)(2,1)S(1)} %get-tuple-element.197), channel_id=1, source_target_pairs={{0,2},{1,3},{2,0},{3,1},{4,6},{5,7},{6,4},{7,5},{8,10},{9,11},{10,... | collective-permute-start | bytes 1572872 | tf_op jit(solution)/shard_map/ppermute | solution.py:63
  77.8 26.6 %collective-permute-start.6 = (bf16[344,1024]{1,0:T(8,128)(2,1)S(1)}, bf16[344,1024]{1,0:T(8,128)(2,1)S(1)}, u32[]{:S(2)}, u32[]{:S(2)}) collective-permute-start(bf16[344,1024]{1,0:T(8,128)(2,1)S(1)} %fusion.9), channel_id=1, source_target_pairs={{0,1},{1,0},{2,3},{3,2},{4,5},{5,4},{6,7},{7,6},{8,9},{9,8},{10,11... | collective-permute-start | bytes 2113544 | tf_op jit(solution)/shard_map/ppermute | solution.py:63
  107.1 30.9 %collective-permute-start.14 = (bf16[688,1024]{1,0:T(8,128)(2,1)S(1)}, bf16[688,1024]{1,0:T(8,128)(2,1)}, u32[]{:S(2)}, u32[]{:S(2)}) collective-permute-start(bf16[688,1024]{1,0:T(8,128)(2,1)S(1)} %slice.487), channel_id=1, source_target_pairs={{0,2},{1,3},{2,0},{3,1},{4,6},{5,7},{6,4},{7,5},{8,10},{9,11},{10,... | collective-permute-start | bytes 4227080 | tf_op jit(solution)/shard_map/ppermute | solution.py:63
  108.6 54.7 %collective-permute-start.20 = (bf16[4,128,2048]{2,1,0:T(8,128)(2,1)S(1)}, bf16[4,128,2048]{2,1,0:T(8,128)(2,1)S(1)}, u32[]{:S(2)}, u32[]{:S(2)}) collective-permute-start(bf16[4,128,2048]{2,1,0:T(8,128)(2,1)S(1)} %bitcast.310), channel_id=1, source_target_pairs={{0,8},{8,0},{16,24},{24,16},{1,9},{9,1},{17,25},{25,17},{2,10},{10... | collective-permute-start | bytes 6291464 | tf_op jit(solution)/shard_map/ppermute | solution.py:63
  110.2 53.2 %collective-permute-start.21 = (bf16[4,128,2048]{2,1,0:T(8,128)(2,1)S(1)}, bf16[4,128,2048]{2,1,0:T(8,128)(2,1)S(1)}, u32[]{:S(2)}, u32[]{:S(2)}) collective-permute-start(bf16[4,128,2048]{2,1,0:T(8,128)(2,1)S(1)} %bitcast.311), channel_id=1, source_target_pairs={{0,16},{8,24},{16,0},{24,8},{1,17},{9,25},{17,1},{25,9},{2,18},{10... | collective-permute-start | bytes 6291464 | tf_op jit(solution)/shard_map/ppermute | solution.py:63
  163.4 30.9 %collective-permute-start.23 = (bf16[4,64,2048]{2,1,0:T(8,128)(2,1)S(1)}, bf16[4,64,2048]{2,1,0:T(8,128)(2,1)S(1)}, u32[]{:S(2)}, u32[]{:S(2)}) collective-permute-start(bf16[4,64,2048]{2,1,0:T(8,128)(2,1)S(1)} %slice.501), channel_id=1, source_target_pairs={{0,16},{8,24},{16,0},{24,8},{1,17},{9,25},{17,1},{25,9},{2,18},{10... | collective-permute-start | bytes 3145736 | tf_op jit(solution)/shard_map/ppermute | solution.py:63
  165.1 30.2 %collective-permute-start.22 = (bf16[4,64,2048]{2,1,0:T(8,128)(2,1)S(1)}, bf16[4,64,2048]{2,1,0:T(8,128)(2,1)S(1)}, u32[]{:S(2)}, u32[]{:S(2)}) collective-permute-start(bf16[4,64,2048]{2,1,0:T(8,128)(2,1)S(1)} %slice.500), channel_id=1, source_target_pairs={{0,8},{8,0},{16,24},{24,16},{1,9},{9,1},{17,25},{25,17},{2,10},{10... | collective-permute-start | bytes 3145736 | tf_op jit(solution)/shard_map/ppermute | solution.py:63
  194.3 35.1 %collective-permute-start.26 = (bf16[2,128,2048]{2,1,0:T(8,128)(2,1)}, bf16[2,128,2048]{2,1,0:T(8,128)(2,1)}, u32[]{:S(2)}, u32[]{:S(2)}) collective-permute-start(bf16[2,128,2048]{2,1,0:T(8,128)(2,1)} %get-tuple-element.222), channel_id=1, source_target_pairs={{0,2},{1,3},{2,0},{3,1},{4,6},{5,7},{6,4},{7,5},{8,10},{9,11},{10,... | collective-permute-start | bytes 3145736 | tf_op jit(solution)/shard_map/ppermute | solution.py:63
  196.3 33.2 %collective-permute-start.24 = (bf16[4,64,2048]{2,1,0:T(8,128)(2,1)}, bf16[4,64,2048]{2,1,0:T(8,128)(2,1)}, u32[]{:S(2)}, u32[]{:S(2)}) collective-permute-start(bf16[4,64,2048]{2,1,0:T(8,128)(2,1)} %bitcast.65.refs_0_), channel_id=1, source_target_pairs={{0,8},{8,0},{16,24},{24,16},{1,9},{9,1},{17,25},{25,17},{2,10},{10... | collective-permute-start | bytes 3145736 | tf_op jit(solution)/shard_map/ppermute | solution.py:63
  197.8 31.7 %collective-permute-start.25 = (bf16[4,64,2048]{2,1,0:T(8,128)(2,1)}, bf16[4,64,2048]{2,1,0:T(8,128)(2,1)}, u32[]{:S(2)}, u32[]{:S(2)}) collective-permute-start(bf16[4,64,2048]{2,1,0:T(8,128)(2,1)} %bitcast.65.refs_0_), channel_id=1, source_target_pairs={{0,16},{8,24},{16,0},{24,8},{1,17},{9,25},{17,1},{25,9},{2,18},{10... | collective-permute-start | bytes 3145736 | tf_op jit(solution)/shard_map/ppermute | solution.py:63
  259.8 32.1 %collective-permute-start.31 = (bf16[688,1024]{1,0:T(8,128)(2,1)S(1)}, bf16[688,1024]{1,0:T(8,128)(2,1)S(1)}, u32[]{:S(2)}, u32[]{:S(2)}) collective-permute-start(bf16[688,1024]{1,0:T(8,128)(2,1)S(1)} %slice.513), channel_id=1, source_target_pairs={{0,2},{1,3},{2,0},{3,1},{4,6},{5,7},{6,4},{7,5},{8,10},{9,11},{10,... | collective-permute-start | bytes 4227080 | tf_op jit(solution)/shard_map/ppermute | solution.py:63
  263.4 53.3 %collective-permute-start.35 = (bf16[4,128,2048]{2,1,0:T(8,128)(2,1)S(1)}, bf16[4,128,2048]{2,1,0:T(8,128)(2,1)S(1)}, u32[]{:S(2)}, u32[]{:S(2)}) collective-permute-start(bf16[4,128,2048]{2,1,0:T(8,128)(2,1)S(1)} %bitcast.313), channel_id=1, source_target_pairs={{0,8},{8,0},{16,24},{24,16},{1,9},{9,1},{17,25},{25,17},{2,10},{10... | collective-permute-start | bytes 6291464 | tf_op jit(solution)/shard_map/ppermute | solution.py:63
  264.0 53.9 %collective-permute-start.36 = (bf16[4,128,2048]{2,1,0:T(8,128)(2,1)S(1)}, bf16[4,128,2048]{2,1,0:T(8,128)(2,1)S(1)}, u32[]{:S(2)}, u32[]{:S(2)}) collective-permute-start(bf16[4,128,2048]{2,1,0:T(8,128)(2,1)S(1)} %bitcast.314), channel_id=1, source_target_pairs={{0,16},{8,24},{16,0},{24,8},{1,17},{9,25},{17,1},{25,9},{2,18},{10... | collective-permute-start | bytes 6291464 | tf_op jit(solution)/shard_map/ppermute | solution.py:63
  324.7 32.6 %collective-permute-start.34 = (bf16[344,1024]{1,0:T(8,128)(2,1)}, bf16[344,1024]{1,0:T(8,128)(2,1)}, u32[]{:S(2)}, u32[]{:S(2)}) collective-permute-start(bf16[344,1024]{1,0:T(8,128)(2,1)} %add_convert_fusion.7), channel_id=1, source_target_pairs={{0,1},{1,0},{2,3},{3,2},{4,5},{5,4},{6,7},{7,6},{8,9},{9,8},{10,11... | collective-permute-start | bytes 2113544 | tf_op jit(solution)/shard_map/ppermute | solution.py:63
  396.0 49.4 %collective-permute-start.44 = (bf16[4,2,1,128,1024]{4,3,2,1,0:T(8,128)(2,1)}, bf16[4,2,1,128,1024]{4,3,2,1,0:T(8,128)(2,1)}, u32[]{:S(2)}, u32[]{:S(2)}) collective-permute-start(bf16[4,2,1,128,1024]{4,3,2,1,0:T(8,128)(2,1)} %get-tuple-element.244), channel_id=1, source_target_pairs={{0,8},{8,0},{16,24},{24,16},{1,9},{9,1},{17,25},{25,17},{2,10},{10... | collective-permute-start | bytes 6291464 | tf_op jit(solution)/shard_map/ppermute | solution.py:63
  403.2 47.9 %collective-permute-start.45 = (bf16[4,1,2,128,1024]{4,3,2,0,1:T(8,128)(2,1)}, bf16[4,1,2,128,1024]{4,3,2,0,1:T(8,128)(2,1)}, u32[]{:S(2)}, u32[]{:S(2)}) collective-permute-start(bf16[4,1,2,128,1024]{4,3,2,0,1:T(8,128)(2,1)} %bitcast.96), channel_id=1, source_target_pairs={{0,16},{8,24},{16,0},{24,8},{1,17},{9,25},{17,1},{25,9},{2,18},{10... | collective-permute-start | bytes 6291464 | tf_op jit(solution)/shard_map/ppermute | solution.py:63
  468.0 28.1 %collective-permute-start.50 = (bf16[4,1,128,1024]{3,2,1,0:T(8,128)(2,1)S(1)}, bf16[4,1,128,1024]{3,2,1,0:T(8,128)(2,1)S(1)}, u32[]{:S(2)}, u32[]{:S(2)}) collective-permute-start(bf16[4,1,128,1024]{3,2,1,0:T(8,128)(2,1)S(1)} %get-tuple-element.257), channel_id=1, source_target_pairs={{0,16},{8,24},{16,0},{24,8},{1,17},{9,25},{17,1},{25,9},{2,18},{10... | collective-permute-start | bytes 3145736 | tf_op jit(solution)/shard_map/ppermute | solution.py:63
  484.6 33.6 %collective-permute-start.52 = (bf16[4,2,1,64,1024]{4,3,2,1,0:T(8,128)(2,1)}, bf16[4,2,1,64,1024]{4,3,2,1,0:T(8,128)(2,1)S(1)}, u32[]{:S(2)}, u32[]{:S(2)}) collective-permute-start(bf16[4,2,1,64,1024]{4,3,2,1,0:T(8,128)(2,1)} %get-tuple-element.265), channel_id=1, source_target_pairs={{0,8},{8,0},{16,24},{24,16},{1,9},{9,1},{17,25},{25,17},{2,10},{10... | collective-permute-start | bytes 3145736 | tf_op jit(solution)/shard_map/ppermute | solution.py:63
  486.1 32.1 %collective-permute-start.53 = (bf16[4,1,2,64,1024]{4,3,2,0,1:T(8,128)(2,1)S(1)}, bf16[4,1,2,64,1024]{4,3,2,0,1:T(8,128)(2,1)S(1)}, u32[]{:S(2)}, u32[]{:S(2)}) collective-permute-start(bf16[4,1,2,64,1024]{4,3,2,0,1:T(8,128)(2,1)S(1)} %bitcast.364), channel_id=1, source_target_pairs={{0,16},{8,24},{16,0},{24,8},{1,17},{9,25},{17,1},{25,9},{2,18},{10... | collective-permute-start | bytes 3145736 | tf_op jit(solution)/shard_map/ppermute | solution.py:63
  508.0 77.0 %collective-permute-start.57 = (bf16[4,2,1,128,1024]{4,3,2,1,0:T(8,128)(2,1)}, bf16[4,2,1,128,1024]{4,3,2,1,0:T(8,128)(2,1)}, u32[]{:S(2)}, u32[]{:S(2)}) collective-permute-start(bf16[4,2,1,128,1024]{4,3,2,1,0:T(8,128)(2,1)} %get-tuple-element.280), channel_id=1, source_target_pairs={{0,8},{8,0},{16,24},{24,16},{1,9},{9,1},{17,25},{25,17},{2,10},{10... | collective-permute-start | bytes 6291464 | tf_op jit(solution)/shard_map/ppermute | solution.py:63
  520.3 64.6 %collective-permute-start.58 = (bf16[4,1,2,128,1024]{4,3,2,0,1:T(8,128)(2,1)}, bf16[4,1,2,128,1024]{4,3,2,0,1:T(8,128)(2,1)}, u32[]{:S(2)}, u32[]{:S(2)}) collective-permute-start(bf16[4,1,2,128,1024]{4,3,2,0,1:T(8,128)(2,1)} %bitcast.114), channel_id=1, source_target_pairs={{0,16},{8,24},{16,0},{24,8},{1,17},{9,25},{17,1},{25,9},{2,18},{10... | collective-permute-start | bytes 6291464 | tf_op jit(solution)/shard_map/ppermute | solution.py:63
  554.2 29.2 %collective-permute-start.59 = (bf16[2,688,256]{2,1,0:T(8,128)(2,1)}, bf16[2,688,256]{2,1,0:T(8,128)(2,1)}, u32[]{:S(2)}, u32[]{:S(2)}) collective-permute-start(bf16[2,688,256]{2,1,0:T(8,128)(2,1)} %get-tuple-element.308), channel_id=1, source_target_pairs={{0,2},{1,3},{2,0},{3,1},{4,6},{5,7},{6,4},{7,5},{8,10},{9,11},{10,... | collective-permute-start | bytes 2113544 | tf_op jit(solution)/shard_map/ppermute | solution.py:63
  559.5 51.6 %collective-permute-start.63 = (bf16[4,1,64,1024]{3,2,1,0:T(8,128)(2,1)}, bf16[4,1,64,1024]{3,2,1,0:T(8,128)(2,1)}, u32[]{:S(2)}, u32[]{:S(2)}) collective-permute-start(bf16[4,1,64,1024]{3,2,1,0:T(8,128)(2,1)} %get-tuple-element.289), channel_id=1, source_target_pairs={{0,8},{8,0},{16,24},{24,16},{1,9},{9,1},{17,25},{25,17},{2,10},{10... | collective-permute-start | bytes 1572872 | tf_op jit(solution)/shard_map/ppermute | solution.py:63
  583.4 28.4 %collective-permute-start.62 = (bf16[4,1,64,1024]{3,2,1,0:T(8,128)(2,1)S(1)}, bf16[4,1,64,1024]{3,2,1,0:T(8,128)(2,1)S(1)}, u32[]{:S(2)}, u32[]{:S(2)}) collective-permute-start(bf16[4,1,64,1024]{3,2,1,0:T(8,128)(2,1)S(1)} %copy-done.61), channel_id=1, source_target_pairs={{0,16},{8,24},{16,0},{24,8},{1,17},{9,25},{17,1},{25,9},{2,18},{10... | collective-permute-start | bytes 1572872 | tf_op jit(solution)/shard_map/ppermute | solution.py:63
  589.5 31.3 %collective-permute-start.64 = (bf16[4,1,128,1024]{3,2,1,0:T(8,128)(2,1)S(1)}, bf16[4,1,128,1024]{3,2,1,0:T(8,128)(2,1)S(1)}, u32[]{:S(2)}, u32[]{:S(2)}) collective-permute-start(bf16[4,1,128,1024]{3,2,1,0:T(8,128)(2,1)S(1)} %get-tuple-element.304), channel_id=1, source_target_pairs={{0,16},{8,24},{16,0},{24,8},{1,17},{9,25},{17,1},{25,9},{2,18},{10... | collective-permute-start | bytes 3145736 | tf_op jit(solution)/shard_map/ppermute | solution.py:63
  611.2 30.4 %collective-permute-start.68 = (bf16[4,2,1,64,1024]{4,3,2,1,0:T(8,128)(2,1)S(1)}, bf16[4,2,1,64,1024]{4,3,2,1,0:T(8,128)(2,1)S(1)}, u32[]{:S(2)}, u32[]{:S(2)}) collective-permute-start(bf16[4,2,1,64,1024]{4,3,2,1,0:T(8,128)(2,1)S(1)} %get-tuple-element.313), channel_id=1, source_target_pairs={{0,8},{8,0},{16,24},{24,16},{1,9},{9,1},{17,25},{25,17},{2,10},{10... | collective-permute-start | bytes 3145736 | tf_op jit(solution)/shard_map/ppermute | solution.py:63
  613.6 28.0 %collective-permute-start.69 = (bf16[4,1,2,64,1024]{4,3,2,0,1:T(8,128)(2,1)S(1)}, bf16[4,1,2,64,1024]{4,3,2,0,1:T(8,128)(2,1)S(1)}, u32[]{:S(2)}, u32[]{:S(2)}) collective-permute-start(bf16[4,1,2,64,1024]{4,3,2,0,1:T(8,128)(2,1)S(1)} %bitcast.363), channel_id=1, source_target_pairs={{0,16},{8,24},{16,0},{24,8},{1,17},{9,25},{17,1},{25,9},{2,18},{10... | collective-permute-start | bytes 3145736 | tf_op jit(solution)/shard_map/ppermute | solution.py:63
  622.2 57.4 %collective-permute-start.86 = (bf16[2,128,2048]{2,1,0:T(8,128)(2,1)}, bf16[2,128,2048]{2,1,0:T(8,128)(2,1)S(1)}, u32[]{:S(2)}, u32[]{:S(2)}) collective-permute-start(bf16[2,128,2048]{2,1,0:T(8,128)(2,1)} %get-tuple-element.326), channel_id=1, source_target_pairs={{0,2},{1,3},{2,0},{3,1},{4,6},{5,7},{6,4},{7,5},{8,10},{9,11},{10,... | collective-permute-start | bytes 3145736 | tf_op jit(solution)/shard_map/ppermute | solution.py:63
  670.9 55.2 %collective-permute-start.93 = (bf16[128,2048]{1,0:T(8,128)(2,1)S(1)}, bf16[128,2048]{1,0:T(8,128)(2,1)}, u32[]{:S(2)}, u32[]{:S(2)}) collective-permute-start(bf16[128,2048]{1,0:T(8,128)(2,1)S(1)} %pad_maximum_fusion.18.refs_0_), channel_id=1, source_target_pairs={{0,8},{8,0},{16,24},{24,16},{1,9},{9,1},{17,25},{25,17},{2,10},{10... | collective-permute-start | bytes 1572872 | tf_op jit(solution)/shard_map/ppermute | solution.py:63
  679.9 26.6 %collective-permute-start.87 = (bf16[1,1,128,2048]{3,2,1,0:T(8,128)(2,1)S(1)}, bf16[1,1,128,2048]{3,2,1,0:T(8,128)(2,1)S(1)}, u32[]{:S(2)}, u32[]{:S(2)}) collective-permute-start(bf16[1,1,128,2048]{3,2,1,0:T(8,128)(2,1)S(1)} %get-tuple-element.359), channel_id=1, source_target_pairs={{0,4},{1,5},{2,6},{3,7},{4,0},{5,1},{6,2},{7,3},{8,12},{9,13},{10,... | collective-permute-start | bytes 1572872 | tf_op jit(solution)/shard_map/ppermute | solution.py:63
  684.6 41.5 %collective-permute-start.95 = (bf16[128,2048]{1,0:T(8,128)(2,1)S(1)}, bf16[128,2048]{1,0:T(8,128)(2,1)S(1)}, u32[]{:S(2)}, u32[]{:S(2)}) collective-permute-start(bf16[128,2048]{1,0:T(8,128)(2,1)S(1)} %collective-permute-done.94.refs_2_), channel_id=1, source_target_pairs={{0,8},{8,0},{16,24},{24,16},{1,9},{9,1},{17,25},{25,17},{2,10},{10... | collective-permute-start | bytes 1572872 | tf_op jit(solution)/shard_map/ppermute | solution.py:63
  687.0 37.2 %collective-permute-start.76 = (f32[2,1,1792]{2,0,1:T(2,128)S(1)}, f32[2,1,1792]{2,0,1:T(2,128)S(1)}, u32[]{:S(2)}, u32[]{:S(2)}) collective-permute-start(f32[2,1,1792]{2,0,1:T(2,128)S(1)} %add.406), channel_id=1, source_target_pairs={{0,16},{8,24},{16,0},{24,8},{1,17},{9,25},{17,1},{25,9},{2,18},{10... | collective-permute-start | bytes 43016 | tf_op jit(solution)/shard_map/ppermute | solution.py:63
  (264 other events, 2351.0 us)
